TPU v7x, 32 devices: a whole 2x2x4 slice. The times are simulated.
32 devices in a mesh: seq: 16 (over z, x, core), tp: 2 (over y).
Axes of the slice: x: 2, y: 2, z: 4, core: 2. Of those that a mesh axis runs over, the one named last changes fastest.
Arguments:
- hidden_in: bfloat16 [4, 4096], P(None, 'seq'), may hold values from -12 to 12
- attn_gain: float32 [4096], P('seq'), may hold values from 0.25 to 4
- mlp_gain: float32 [4096], P('seq'), may hold values from 0.25 to 1.75
- query_weight: bfloat16 [4096, 4096], P('seq', 'tp'), may hold values from -0.09375 to 0.09375
- key_weight: bfloat16 [4096, 1024], P('seq', 'tp'), may hold values from -0.21875 to 0.21875
- value_weight: bfloat16 [4096, 1024], P('seq', 'tp'), may hold values from -0.09375 to 0.09375
- out_weight: bfloat16 [4096, 4096], P('tp', 'seq'), may hold values from -0.25 to 0.25
- up_weight: bfloat16 [4096, 21504], P('seq', 'tp'), may hold values from -0.09375 to 0.09375
- down_weight: bfloat16 [21504, 4096], P('tp', 'seq'), may hold values from -0.0390625 to 0.0390625
- key_cache: bfloat16 [4, 2048, 1024], P(None, 'seq', 'tp'), may hold values from -90 to 90
- value_cache: bfloat16 [4, 2048, 1024], P(None, 'seq', 'tp'), may hold values from -6 to 6
- lengths: int32 [4], replicated, may hold values from 1 to 2048, as said below
- block_order: int32 [4], replicated, may hold values from 0 to 3, each once
- pad_mask: int32 [4, 2048], P(None, 'seq'), may hold values 0 or 1
Outputs:
- layer_out: bfloat16 [4, 4096], P(None, 'seq')
Inputs may be any that keep to these rules, and one draw needn't show every extreme that they name: `lengths`: exactly one request has 2048 positions; 2 requests have at most 8 positions, the others at least 1536. `block_order`: a permutation of 0 to 3.
All inputs are finite; a program needn't handle non-finite values. No bound on the sum of `pad_mask` on one device may be relied on, other than what follows from the above.
Results may differ from a plain program's by a relative error of at most 0.012.
The roundings to bfloat16 on the way count: a program that leaves them out, or rounds other values in their place, can miss the bound.
Values may be sent and summed in bfloat16 or wider, within the bound.
No kernel may reach another device: no remote copies, remote signals or barrier semaphores. Data moves between devices by JAX's collectives and lax.ppermute only.
A program may use at most 64 MiB of HBM per device.

v0:
```python
import math

import jax
import jax.numpy as jnp
from jax import lax
from jax.sharding import PartitionSpec as P

D = 4096
H = 32
KVH = 8
HD = 128


NORM_EPS = 1e-05
MASKED = -1e30


def squared_relu(values_in):
    positive = jnp.maximum(values_in, 0.0)
    return positive * positive


def per_device(
    hidden_in,
    attn_gain,
    mlp_gain,
    query_weight,
    key_weight,
    value_weight,
    out_weight,
    up_weight,
    down_weight,
    key_cache,
    value_cache,
    lengths,
    block_order,
    pad_mask,
):
    n_requests = hidden_in.shape[0]
    q_per_kv = H // KVH
    kv_here = key_cache.shape[2] // HD
    span_here = key_cache.shape[1]
    score_scale = 1.0 / math.sqrt(HD)
    x_rows = hidden_in.astype(jnp.float32)
    scaled_in = (x_rows * attn_gain).astype(jnp.bfloat16)
    sq_attn = jnp.sum(x_rows * x_rows, axis=1)
    proj_query = jnp.dot(scaled_in, query_weight, preferred_element_type=jnp.float32)
    proj_key = jnp.dot(scaled_in, key_weight, preferred_element_type=jnp.float32)
    proj_value = jnp.dot(scaled_in, value_weight, preferred_element_type=jnp.float32)
    sum_query, sum_key, sum_value, sum_sq = lax.psum(
        (proj_query, proj_key, proj_value, sq_attn), "seq"
    )
    inv_attn = lax.rsqrt(sum_sq / D + NORM_EPS)[:, None]
    query_rows = (sum_query * inv_attn).astype(jnp.bfloat16)
    key_new = (sum_key * inv_attn).astype(jnp.bfloat16)
    value_new = (sum_value * inv_attn).astype(jnp.bfloat16)
    n_blocks = lax.axis_size("seq")
    my_block = lax.axis_index("seq")
    first_block = block_order % n_blocks
    position = ((my_block - first_block) % n_blocks)[:, None] * span_here + jnp.arange(
        span_here, dtype=jnp.int32
    )[None, :]
    live_slots = ((position < lengths[:, None]) & (pad_mask == 1))[:, None, None, :]
    q_groups = query_rows.reshape(n_requests, kv_here, q_per_kv, HD)
    keys_here = key_cache.reshape(n_requests, span_here, kv_here, HD)
    values_here = value_cache.reshape(n_requests, span_here, kv_here, HD)
    scores = (
        jnp.einsum("rkgd,rtkd->rkgt", q_groups, keys_here, preferred_element_type=jnp.float32)
        * score_scale
    )
    scores = jnp.where(live_slots, scores, MASKED)
    local_top = jnp.max(scores, axis=3)
    weights = jnp.where(live_slots, jnp.exp(scores - local_top[..., None]), 0.0)
    local_total = jnp.sum(weights, axis=3)
    local_out = jnp.einsum(
        "rkgt,rtkd->rkgd",
        weights.astype(jnp.bfloat16),
        values_here,
        preferred_element_type=jnp.float32,
    )
    score_top = lax.pmax(local_top, "seq")
    fade_factor = jnp.exp(local_top - score_top)
    row_total, numerator = lax.psum(
        (local_total * fade_factor, local_out * fade_factor[..., None]), "seq"
    )
    self_score = (
        jnp.einsum(
            "rkgd,rkd->rkg",
            q_groups,
            key_new.reshape(n_requests, kv_here, HD),
            preferred_element_type=jnp.float32,
        )
        * score_scale
    )
    final_top = jnp.maximum(score_top, self_score)
    keep_factor = jnp.exp(score_top - final_top)
    self_weight = jnp.exp(self_score - final_top)
    denominator = row_total * keep_factor + self_weight
    value_self = value_new.reshape(n_requests, kv_here, 1, HD).astype(jnp.float32)
    numerator = numerator * keep_factor[..., None] + self_weight[..., None] * value_self
    attended = (
        (numerator / denominator[..., None])
        .reshape(n_requests, kv_here * q_per_kv * HD)
        .astype(jnp.bfloat16)
    )
    head_part = jnp.dot(attended, out_weight, preferred_element_type=jnp.float32)
    attn_out = lax.psum(head_part, "tp")
    hidden_state = (x_rows + attn_out).astype(jnp.bfloat16)
    resid_rows = hidden_state.astype(jnp.float32)
    scaled_mlp = (resid_rows * mlp_gain).astype(jnp.bfloat16)
    sq_mlp = jnp.sum(resid_rows * resid_rows, axis=1)
    up_part = jnp.dot(scaled_mlp, up_weight, preferred_element_type=jnp.float32)
    up_sum, sq_sum = lax.psum((up_part, sq_mlp), "seq")
    activated = squared_relu(up_sum * lax.rsqrt(sq_sum / D + NORM_EPS)[:, None]).astype(
        jnp.bfloat16
    )
    down_part = jnp.dot(activated, down_weight, preferred_element_type=jnp.float32)
    mlp_out = lax.psum(down_part, "tp")
    return (resid_rows + mlp_out).astype(jnp.bfloat16)


def solution(mesh):
    return jax.shard_map(
        per_device,
        mesh=mesh,
        in_specs=(
            P(None, "seq"),
            P("seq"),
            P("seq"),
            P("seq", "tp"),
            P("seq", "tp"),
            P("seq", "tp"),
            P("tp", "seq"),
            P("seq", "tp"),
            P("tp", "seq"),
            P(None, "seq", "tp"),
            P(None, "seq", "tp"),
            P(),
            P(),
            P(None, "seq"),
        ),
        out_specs=P(None, "seq"),
        check_vma=False,
    )
```

profile of v0, /device:TPU:0, one launch (start us, length us, event | category | flops | bytes accessed | tf_op | source)
XLA Modules:
  0.0 278.9 jit_solution(18446069774392452971)
XLA Ops:
  6.5 0.0 copy-start
  6.5 0.0 all-reduce.4.cloned.1.call-start
  6.5 0.9 fusion.18
  7.4 1.1 fusion.34
  8.5 1.1 fusion.32
  9.7 0.0 copy-done
  9.7 1.0 fusion.36
  10.6 62.9 %all-reduce.1 = (f32[4,2048]{1,0:T(4,128)S(1)}, f32[4]{0:T(128)S(1)}) all-reduce(f32[4,2048]{1,0:T(4,128)S(1)} %fusion.36, f32[4]{0:T(128)S(1)} %fusion.18), channel_id=1, replica_groups=mesh['seq'=16,'tp'=2] {'seq'}, use_global_device_ids=true, to_apply=%region_0.0 | all-reduce | flops 8196 | bytes 65568 | tf_op jit(solution)/shard_map/psum | solution.py:50
  73.6 0.1 multiply_convert_fusion.2
  73.7 0.7 fusion.29
  74.3 0.8 fusion.27
  75.1 1.5 fusion.44
  76.6 30.0 %pmax.7 = f32[4,4,4]{2,1,0:T(4,128)S(1)} all-reduce(f32[4,4,4]{2,1,0:T(4,128)S(1)} %get-tuple-element.20), channel_id=1, replica_groups=mesh['seq'=16,'tp'=2] {'seq'}, use_global_device_ids=true, to_apply=%region_4.0 | all-reduce | flops 64 | bytes 512 | tf_op jit(solution)/shard_map/pmax | solution.py:81
  106.6 0.2 fusion.9
  106.8 1.3 convolution_multiply_fusion
  108.2 57.7 %all-reduce = (f32[4,4,4,128]{3,2,1,0:T(4,128)S(1)}, f32[4,512]{1,0:T(4,128)S(1)}, f32[4,4,4]{2,1,0:T(4,128)S(1)}, f32[4,512]{1,0:T(4,128)S(1)}) all-reduce(f32[4,4,4,128]{3,2,1,0:T(4,128)S(1)} %convolution_multiply_fusion, f32[4,512]{1,0:T(4,128)S(1)} %fusion.34, ...), channel_id=1, replica_groups=mesh['seq'=16,'tp'=2] {'seq'}, use_global_device_ids=true, to_apply=%region_5.6 | all-reduce | flops 12352 | bytes 98816 | tf_op jit(solution)/shard_map/psum | solution.py:83
  165.9 0.1 fusion.23
  166.0 0.1 fusion.45
  166.2 0.1 fusion.8
  166.3 1.5 fusion.46
  167.8 4.9 %psum.76 = f32[4,256]{1,0:T(4,128)S(1)} all-reduce(f32[4,256]{1,0:T(4,128)S(1)} %fusion.46), channel_id=1, replica_groups=mesh['seq'=16,'tp'=2] {'tp'}, use_global_device_ids=true, to_apply=%region_10.11 | all-reduce | flops 1024 | bytes 8192 | tf_op jit(solution)/shard_map/psum | solution.py:107
  172.7 0.8 fusion.21
  173.5 4.1 %fusion.24 = f32[4,10752]{1,0:T(4,128)} fusion(bf16[256,10752]{1,0:T(8,128)(2,1)} %param.21, bf16[4,256]{1,0:T(4,128)(2,1)S(1)} %get-tuple-element.12, f32[256]{0:T(256)} %param.16), kind=kOutput, calls=%fused_computation.45 | convolution fusion | flops 22023168 | bytes 5680128 | tf_op jit(solution)/shard_map/dot_general | solution.py:112
  177.6 0.0 all-reduce.4.cloned.1.call-update
  177.6 29.5 %psum.78 = f32[4]{0:T(128)S(1)} all-reduce(f32[4]{0:T(128)S(1)} %get-tuple-element.11), channel_id=1, replica_groups=mesh['seq'=16,'tp'=2] {'seq'}, use_global_device_ids=true, to_apply=%region_13.14 | all-reduce | flops 4 | bytes 32 | tf_op jit(solution)/shard_map/psum | solution.py:113
  207.1 55.9 %all-reduce.4.cloned.1.call-done = f32[4,10752]{1,0:T(4,128)} async-done(((f32[4,10752]{1,0:T(4,128)}), f32[4,10752]{1,0:T(4,128)}) %all-reduce.4.cloned.1.call-update) | async-done | bytes 172048 | tf_op jit(solution)/shard_map/psum | solution.py:113
  263.0 3.5 %fusion.5 = f32[4,256]{1,0:T(4,128)S(1)} fusion(bf16[10752,256]{1,0:T(8,128)(2,1)} %param.22, f32[4,10752]{1,0:T(4,128)} %all-reduce.4.cloned.1.call-done, f32[4]{0:T(128)S(1)} %add_rsqrt_fusion), kind=kOutput, calls=%fused_computation.8 | convolution fusion | flops 22192128 | bytes 5681168 | tf_op jit(solution)/shard_map/dot_general | solution.py:117
  266.5 4.9 %psum.79 = f32[4,256]{1,0:T(4,128)S(1)} all-reduce(f32[4,256]{1,0:T(4,128)S(1)} %fusion.5), channel_id=1, replica_groups=mesh['seq'=16,'tp'=2] {'tp'}, use_global_device_ids=true, to_apply=%region_14.15 | all-reduce | flops 1024 | bytes 8192 | tf_op jit(solution)/shard_map/psum | solution.py:118
  271.4 0.6 fusion.22
  (8 shorter events, 0.1 us)
Async XLA Ops:
  6.5 3.1 %copy-start = (bf16[256,2048]{1,0:T(8,128)(2,1)S(1)}, bf16[256,2048]{1,0:T(8,128)(2,1)}, u32[]{:S(2)}) copy-start(bf16[256,2048]{1,0:T(8,128)(2,1)} %param.17) | copy-start | bytes 3145732
  6.5 256.5 %all-reduce.4.cloned.1.call-start = ((), (), s32[]{:S(2)}) async-start(), calls=%async_computation | async-start | bytes 344064 | tf_op jit(solution)/shard_map/psum | solution.py:113
Sparse Core Ops, SparseCore 0:
  177.7 85.2 all-reduce.3
where the time goes:
time: 280 us; the launch traced here: 279 us
  blocking collectives  190 us (68%)
  waiting for transfers between devices  55.9 us (20%)
  matrix products  15.2 us (5%)
  between operations  13.4 us (5%)
  other arithmetic  4.22 us (2%)
    psum x1, blocking collectives, per_device(): lax.psum((proj_query, proj_key, proj_value, sq_attn), 'seq')  62.9 us
    psum x1, blocking collectives, per_device(): lax.psum((local_total * fade_factor, local_out * fade_factor[..., None]),...  57.7 us
    psum x1, waiting for transfers between devices, per_device(): up_sum, sq_sum = lax.psum((up_part, sq_mlp), 'seq')  55.9 us
    pmax x1, blocking collectives, per_device(): score_top = lax.pmax(local_top, 'seq')  30 us
    psum x1, blocking collectives, per_device(): up_sum, sq_sum = lax.psum((up_part, sq_mlp), 'seq')  29.5 us
  transfers between devices with their start and end apart: 1, of which 1 were waited for; matrix products, arithmetic and copies ran while one was open for 0% of the time, Pallas kernels for 0%

commit v1 on v0

v1 whole, which is shorter than its diff:
```python
import math

import jax
import jax.numpy as jnp
from jax import lax
from jax.sharding import Mesh, PartitionSpec as P

D = 4096
H = 32
KVH = 8
HD = 128


NORM_EPS = 1e-05
MASKED = -1e30
LANES = 128


def squared_relu(values_in):
    positive = jnp.maximum(values_in, 0.0)
    return positive * positive


def swap(values_in, axis):
    n = lax.axis_size(axis)
    return lax.ppermute(values_in, axis, [(i, i ^ 1) for i in range(n)])


def gather_all(values_in, axes, n):
    copies = jnp.broadcast_to(values_in[None], (n,) + values_in.shape)
    return lax.all_to_all(copies, axes, 0, 0)


def sum_tp(values_in):
    n = lax.axis_size("tp")
    if n == 2:
        return values_in + swap(values_in, "tp")
    return lax.psum(values_in, "tp")


def per_device(
    hidden_in,
    attn_gain,
    mlp_gain,
    query_weight,
    key_weight,
    value_weight,
    out_weight,
    up_weight,
    down_weight,
    key_cache,
    value_cache,
    lengths,
    block_order,
    pad_mask,
):
    n_req = hidden_in.shape[0]
    q_per_kv = H // KVH
    kv_here = key_cache.shape[2] // HD
    span_here = key_cache.shape[1]
    heads_here = kv_here * q_per_kv
    n_chips = lax.axis_size("chip")
    core = lax.axis_index("core")
    n_blocks = 2 * n_chips
    my_block = 2 * lax.axis_index("chip") + core
    score_scale = 1.0 / math.sqrt(HD)

    x_rows = hidden_in.astype(jnp.float32)
    scaled_in = (x_rows * attn_gain).astype(jnp.bfloat16)
    sq_attn = jnp.sum(x_rows * x_rows, axis=1, keepdims=True)
    proj_query = jnp.dot(scaled_in, query_weight, preferred_element_type=jnp.float32)
    proj_key = jnp.dot(scaled_in, key_weight, preferred_element_type=jnp.float32)
    proj_value = jnp.dot(scaled_in, value_weight, preferred_element_type=jnp.float32)
    half_q, half_kv = proj_query.shape[1] // 2, proj_key.shape[1] // 2
    square_cols = jnp.broadcast_to(sq_attn, (n_req, LANES))

    def half(i):
        return jnp.concatenate(
            [
                proj_query[:, i * half_q : (i + 1) * half_q],
                proj_key[:, i * half_kv : (i + 1) * half_kv],
                proj_value[:, i * half_kv : (i + 1) * half_kv],
                square_cols,
            ],
            axis=1,
        )

    low, high = half(0), half(1)
    mine = jnp.where(core == 0, low, high)
    other = jnp.where(core == 0, high, low)
    pair_sum = mine + swap(other, "core")
    qkv_sum = jnp.sum(gather_all(pair_sum, "chip", n_chips), axis=0)
    inv_attn = lax.rsqrt(qkv_sum[:, -1:] / D + NORM_EPS)
    qkv_half = (qkv_sum[:, :-LANES] * inv_attn).astype(jnp.bfloat16)
    qkv_other = swap(qkv_half, "core")
    qkv_low = jnp.where(core == 0, qkv_half, qkv_other)
    qkv_high = jnp.where(core == 0, qkv_other, qkv_half)

    def both(start, size):
        return jnp.concatenate(
            [qkv_low[:, start : start + size], qkv_high[:, start : start + size]], axis=1
        )

    query_rows = both(0, half_q)
    key_new = both(half_q, half_kv)
    value_new = both(half_q + half_kv, half_kv)

    first_block = block_order % n_blocks
    position = ((my_block - first_block) % n_blocks)[:, None] * span_here + jnp.arange(
        span_here, dtype=jnp.int32
    )[None, :]
    live_slots = ((position < lengths[:, None]) & (pad_mask == 1))[:, None, None, :]
    q_groups = query_rows.reshape(n_req, kv_here, q_per_kv, HD)
    keys_here = key_cache.reshape(n_req, span_here, kv_here, HD)
    values_here = value_cache.reshape(n_req, span_here, kv_here, HD)
    scores = (
        jnp.einsum("rkgd,rtkd->rkgt", q_groups, keys_here, preferred_element_type=jnp.float32)
        * score_scale
    )
    scores = jnp.where(live_slots, scores, MASKED)
    local_top = jnp.max(scores, axis=3, keepdims=True)
    weights = jnp.where(live_slots, jnp.exp(scores - local_top), 0.0)
    local_total = jnp.sum(weights, axis=3, keepdims=True)
    local_out = jnp.einsum(
        "rkgt,rtkd->rkgd",
        weights.astype(jnp.bfloat16),
        values_here,
        preferred_element_type=jnp.float32,
    )
    numer = local_out.reshape(n_req, heads_here, HD)
    stats = jnp.concatenate(
        [
            local_total.reshape(n_req, heads_here, 1),
            local_top.reshape(n_req, heads_here, 1),
        ],
        axis=2,
    )
    stat_rows = stats.reshape(n_req, heads_here * 2)
    pad = (-stat_rows.shape[1]) % LANES
    message = jnp.concatenate(
        [numer.reshape(n_req, heads_here * HD), jnp.pad(stat_rows, ((0, 0), (0, pad)))], axis=1
    )
    arrived = gather_all(message, ("chip", "core"), n_blocks)
    outs = arrived[:, :, : heads_here * HD].reshape(n_blocks, n_req, heads_here, HD)
    stats_all = arrived[:, :, heads_here * HD : heads_here * (HD + 2)].reshape(
        n_blocks, n_req, heads_here, 2
    )
    totals, tops = stats_all[..., 0], stats_all[..., 1]
    self_score = (
        jnp.einsum(
            "rkgd,rkd->rkg",
            q_groups,
            key_new.reshape(n_req, kv_here, HD),
            preferred_element_type=jnp.float32,
        )
        * score_scale
    ).reshape(n_req, heads_here)
    final_top = jnp.maximum(jnp.max(tops, axis=0), self_score)
    fades = jnp.exp(tops - final_top)
    self_weight = jnp.exp(self_score - final_top)
    denominator = jnp.sum(totals * fades, axis=0) + self_weight
    value_self = jnp.broadcast_to(
        value_new.reshape(n_req, kv_here, 1, HD), (n_req, kv_here, q_per_kv, HD)
    ).reshape(n_req, heads_here, HD)
    numerator = jnp.sum(outs * fades[..., None], axis=0) + self_weight[
        ..., None
    ] * value_self.astype(jnp.float32)
    attended = (
        (numerator / denominator[..., None])
        .reshape(n_req, heads_here * HD)
        .astype(jnp.bfloat16)
    )
    head_part = jnp.dot(attended, out_weight, preferred_element_type=jnp.float32)
    attn_out = sum_tp(head_part)
    hidden_state = (x_rows + attn_out).astype(jnp.bfloat16)

    resid_rows = hidden_state.astype(jnp.float32)
    scaled_mlp = (resid_rows * mlp_gain).astype(jnp.bfloat16)
    sq_mlp = jnp.sum(resid_rows * resid_rows, axis=1, keepdims=True)
    up_part = jnp.dot(scaled_mlp, up_weight, preferred_element_type=jnp.float32)
    half_up = up_part.shape[1] // 2
    up_low, up_high = up_part[:, :half_up], up_part[:, half_up:]
    square_cols = jnp.broadcast_to(sq_mlp, (n_req, LANES))
    up_mine = jnp.concatenate([jnp.where(core == 0, up_low, up_high), square_cols], axis=1)
    up_other = jnp.concatenate([jnp.where(core == 0, up_high, up_low), square_cols], axis=1)
    up_pair = up_mine + swap(up_other, "core")
    square_sum = up_pair[:, half_up : half_up + 1]
    piece_0 = lax.reduce_precision(square_sum, 8, 7)
    piece_1 = lax.reduce_precision(square_sum - piece_0, 8, 7)
    piece_2 = square_sum - piece_0 - piece_1
    pieces = jnp.pad(
        jnp.concatenate([piece_0, piece_1, piece_2], axis=1), ((0, 0), (0, LANES - 3))
    )
    up_message = jnp.concatenate([up_pair[:, :half_up], pieces], axis=1).astype(jnp.bfloat16)
    up_sum = jnp.sum(gather_all(up_message, "chip", n_chips).astype(jnp.float32), axis=0)
    squares = jnp.sum(up_sum[:, half_up:], axis=1, keepdims=True)
    inv_mlp = lax.rsqrt(squares / D + NORM_EPS)
    active_half = squared_relu(up_sum[:, :half_up] * inv_mlp).astype(jnp.bfloat16)
    active_other = swap(active_half, "core")
    activated = jnp.concatenate(
        [
            jnp.where(core == 0, active_half, active_other),
            jnp.where(core == 0, active_other, active_half),
        ],
        axis=1,
    )
    down_part = jnp.dot(activated, down_weight, preferred_element_type=jnp.float32)
    mlp_out = sum_tp(down_part)
    return (resid_rows + mlp_out).astype(jnp.bfloat16)


def solution(mesh):
    n_seq, n_tp = mesh.shape["seq"], mesh.shape["tp"]
    split = Mesh(mesh.devices.reshape(n_seq // 2, 2, n_tp), ("chip", "core", "tp"))
    seq = ("chip", "core")
    return jax.shard_map(
        per_device,
        mesh=split,
        in_specs=(
            P(None, seq),
            P(seq),
            P(seq),
            P(seq, "tp"),
            P(seq, "tp"),
            P(seq, "tp"),
            P("tp", seq),
            P(seq, "tp"),
            P("tp", seq),
            P(None, seq, "tp"),
            P(None, seq, "tp"),
            P(),
            P(),
            P(None, seq),
        ),
        out_specs=P(None, seq),
        check_vma=False,
    )
```

time: 280 us -> 81.6 us (0.29)
  blocking collectives: 190 us -> 15.5 us
  waiting for transfers between devices: 55.9 us -> 30.4 us
  starting transfers between devices: 0.01 us -> 14.5 us
  between operations: 13.4 us -> 0.29 us
  matrix products: 15.2 us -> 12.1 us
  local copies, waits for them, and re-layouts: 0.07 us -> 3.14 us
    psum x5 -> x0, blocking collectives: 160 us -> none  [the longest x1 62.9 us: per_device(): lax.psum((proj_query, proj_key, proj_value, sq_attn), 'seq')]
    psum x1 -> x0, waiting for transfers between devices: 55.9 us -> none  [per_device(): up_sum, sq_sum = lax.psum((up_part, sq_mlp), 'seq')]
    pmax x1 -> x0, blocking collectives: 30 us -> none  [per_device(): score_top = lax.pmax(local_top, 'seq')]
    all_to_all x0 -> x2, waiting for transfers between devices: none -> 22.5 us  [gather_all(): return lax.all_to_all(copies, axes, 0, 0)]
    all_to_all x0 -> x1, blocking collectives: none -> 15.5 us  [gather_all(): return lax.all_to_all(copies, axes, 0, 0)]
    all_to_all x0 -> x2, starting transfers between devices: none -> 10.7 us  [gather_all(): return lax.all_to_all(copies, axes, 0, 0)]
    ppermute x0 -> x6, waiting for transfers between devices: none -> 7.91 us  [swap(): return lax.ppermute(values_in, axis, [(i, i ^ 1) for i in range(n)])]
    ppermute x0 -> x6, starting transfers between devices: none -> 3.73 us  [swap(): return lax.ppermute(values_in, axis, [(i, i ^ 1) for i in range(n)])]
  transfers between devices with their start and end apart: 1 -> 8, of which waited for: 1 -> 8; matrix products, arithmetic and copies ran while one was open for 0% -> 2% of each run, Pallas kernels for 0% -> 0%
where the time goes in v1:
time: 81.6 us; the launch traced here: 81.1 us
  waiting for transfers between devices  30.4 us (37%)
  blocking collectives  15.5 us (19%)
  starting transfers between devices  14.5 us (18%)
  matrix products  12.1 us (15%)
  other arithmetic  5.17 us (6%)
  local copies, waits for them, and re-layouts  3.14 us (4%)
    all_to_all x2, waiting for transfers between devices, gather_all(): return lax.all_to_all(copies, axes, 0, 0)  22.5 us
    all_to_all x1, blocking collectives, gather_all(): return lax.all_to_all(copies, axes, 0, 0)  15.5 us
    all_to_all x2, starting transfers between devices, gather_all(): return lax.all_to_all(copies, axes, 0, 0)  10.7 us
    ppermute x6, waiting for transfers between devices, swap(): return lax.ppermute(values_in, axis, [(i, i ^ 1) for i in range(n)])  7.91 us
    ppermute x6, starting transfers between devices, swap(): return lax.ppermute(values_in, axis, [(i, i ^ 1) for i in range(n)])  3.73 us
    dot_general x1, matrix products, per_device(): up_part = jnp.dot(scaled_mlp, up_weight, preferred_element_type=jnp.float32)  3.48 us
    broadcast_in_dim x3, local copies, waits for them, and re-layouts, gather_all(): copies = jnp.broadcast_to(values_in[None], (n,) + values_in.shape)  1.66 us
  transfers between devices with their start and end apart: 8, of which 8 were waited for; matrix products, arithmetic and copies ran while one was open for 2% of the time, Pallas kernels for 0%

profile of v1, /device:TPU:0, one launch (start us, length us, event | category | flops | bytes accessed | tf_op | source)
XLA Modules:
  0.0 81.1 jit_solution(6471351042521738836)
XLA Ops:
  0.0 0.9 %fusion.27 = f32[4]{0:T(128)S(1)} fusion(bf16[4,256]{1,0:T(4,128)(2,1)} %param.14), kind=kLoop, calls=%fused_computation.60 | loop fusion | flops 3068 | bytes 2064 | tf_op jit(solution)/shard_map/reduce_sum | solution.py:70
  0.9 1.1 %fusion.51 = f32[4,512]{1,0:T(4,128)S(1)} fusion(bf16[256,512]{1,0:T(8,128)(2,1)} %param.18, bf16[4,256]{1,0:T(4,128)(2,1)} %param.14, f32[256]{0:T(256)} %param.15), kind=kOutput, calls=%fused_computation.102 | convolution fusion | flops 1051648 | bytes 273408 | tf_op jit(solution)/shard_map/dot_general | solution.py:72
  2.0 1.1 %fusion.49 = f32[4,512]{1,0:T(4,128)S(1)} fusion(bf16[256,512]{1,0:T(8,128)(2,1)} %param.19, bf16[4,256]{1,0:T(4,128)(2,1)} %param.14, f32[256]{0:T(256)} %param.15), kind=kOutput, calls=%fused_computation.101 | convolution fusion | flops 1051648 | bytes 273408 | tf_op jit(solution)/shard_map/dot_general | solution.py:73
  3.2 1.0 %fusion.53 = f32[4,2048]{1,0:T(4,128)S(1)} fusion(bf16[256,2048]{1,0:T(8,128)(2,1)S(1)} %copy-done, bf16[4,256]{1,0:T(4,128)(2,1)} %param.14, f32[256]{0:T(256)} %param.15), kind=kOutput, calls=%fused_computation.103 | convolution fusion | flops 4197376 | bytes 1084416 | tf_op jit(solution)/shard_map/dot_general | solution.py:71
  4.2 0.5 collective-permute-start
  4.7 0.9 %collective-permute-done = f32[4,1664]{1,0:T(4,128)S(1)} collective-permute-done((f32[4,1664]{1,0:T(4,128)S(1)}, f32[4,1664]{1,0:T(4,128)S(1)}, u32[]{:S(2)}, u32[]{:S(2)}) %collective-permute-start) | collective-permute-done | bytes 26656 | tf_op jit(solution)/shard_map/ppermute | solution.py:26
  5.6 0.7 broadcast_in_dim.32
  6.3 7.1 %all-to-all-start = ((f32[8,4,1664]{2,1,0:T(4,128)}), f32[8,4,1664]{2,1,0:T(4,128)S(1)}, u32[]{:S(2)}, u32[]{:S(2)}) async-start(f32[8,4,1664]{2,1,0:T(4,128)} %broadcast_in_dim.32), calls=%async_computation | async-start | bytes 425984 | tf_op jit(solution)/shard_map/all_to_all | solution.py:31
  13.4 0.7 fusion.46
  14.1 7.8 %all-to-all-done = f32[8,4,1664]{2,1,0:T(4,128)S(1)} async-done(((f32[8,4,1664]{2,1,0:T(4,128)}), f32[8,4,1664]{2,1,0:T(4,128)S(1)}, u32[]{:S(2)}, u32[]{:S(2)}) %all-to-all-start) | async-done | bytes 213024 | tf_op jit(solution)/shard_map/all_to_all | solution.py:31
  22.0 0.2 fusion.40
  22.3 0.8 fusion.42
  23.1 0.4 collective-permute-done.1
  23.6 1.5 %fusion.64 = (f32[4,4,4]{2,1,0:T(4,128)S(1)}, f32[4,4,4,128]{3,2,1,0:T(4,128)S(1)}) fusion(bf16[4,4,4,128]{3,2,1,0:T(4,128)(2,1)S(1)} %reshape.99, pred[4,128]{1,0:T(4,128)(4,1)S(1)} %fusion.42, bf16[4,128,512]{2,1,0:T(8,128)(2,1)} %param.23), kind=kOutput, calls=%fused_computation.113 | convolution fusion | flops 2121664 | bytes 574208 | tf_op jit(solution)/shard_map/rkgd,rtkd->rkgt/dot_general | solution.py:117
  25.1 0.1 reshape_broadcast_in_dim.7
  25.2 0.2 fusion.18
  25.4 0.1 reshape_broadcast_in_dim.6
  25.5 0.1 copy.67
  25.7 1.3 %fusion.1 = f32[4,4,4,128]{3,2,1,0:T(4,128)S(1)} fusion(f32[4,4,4,128]{3,2,1,0:T(4,128)S(1)} %get-tuple-element.32, f32[4,4,4]{2,1,0:T(4,128)S(1)} %get-tuple-element.31, pred[4,128]{1,0:T(4,128)(4,1)S(1)} %fusion.42, bf16[4,128,512]{2,1,0:T(8,128)(2,1)} %param.24), kind=kOutput, calls=%fused_computation.3 | convolution fusion | flops 2121728 | bytes 590592 | tf_op jit(solution)/shard_map/rkgt,rtkd->rkgd/dot_general | solution.py:124
  27.1 0.9 %broadcast_in_dim.35 = f32[16,4,2176]{2,1,0:T(4,128)} broadcast(f32[4,2176]{1,0:T(4,128)S(1)} %select_maximum_fusion), dimensions={1,2} | broadcast | bytes 591872 | tf_op jit(solution)/shard_map/broadcast_in_dim | solution.py:30
  28.0 3.6 %all-to-all-start.1 = ((f32[16,4,2176]{2,1,0:T(4,128)}), f32[16,4,2176]{2,1,0:T(4,128)S(1)}, u32[]{:S(2)}, u32[]{:S(2)}) async-start(f32[16,4,2176]{2,1,0:T(4,128)} %broadcast_in_dim.35), calls=%async_computation.1 | async-start | bytes 1114112 | tf_op jit(solution)/shard_map/all_to_all | solution.py:31
  31.6 0.1 fusion.65
  31.7 0.1 reshape.105
  31.9 14.6 %all-to-all-done.1 = f32[16,4,2176]{2,1,0:T(4,128)S(1)} async-done(((f32[16,4,2176]{2,1,0:T(4,128)}), f32[16,4,2176]{2,1,0:T(4,128)S(1)}, u32[]{:S(2)}, u32[]{:S(2)}) %all-to-all-start.1) | async-done | bytes 557088 | tf_op jit(solution)/shard_map/all_to_all | solution.py:31
  46.5 0.1 copy.80
  46.6 0.2 slice_reduce_fusion.1
  46.8 0.2 subtract_exponential_fusion
  47.0 0.2 multiply_reduce_fusion
  47.3 0.2 mul.98
  47.5 0.2 mul.99
  47.8 0.1 fusion.6
  48.0 1.6 %fusion.21 = f32[4,256]{1,0:T(4,128)S(1)} fusion(bf16[2048,256]{1,0:T(8,128)(2,1)} %param.20, f32[1,4,16,128]{3,2,1,0:T(8,128)S(1)} %broadcast_bitcast_fusion, f32[4,2048]{1,0:T(4,128)S(1)} %fusion.6, f32[4,2048]{1,0:T(4,128)S(1)} %convert_element_type.59, f32[1,4,16,128]{3,2,1,0:T(8,128)S(1)} %broadcast_bitcast_fusion.1), kind=kOutput, calls=%fused_computation.43 | convolution fusion | flops 4227072 | bytes 1183744 | tf_op jit(solution)/shard_map/dot_general | solution.py:173
  49.6 1.5 %collective-permute-start.2 = (f32[4,256]{1,0:T(4,128)S(1)}, f32[4,256]{1,0:T(4,128)S(1)}, u32[]{:S(2)}, u32[]{:S(2)}) collective-permute-start(f32[4,256]{1,0:T(4,128)S(1)} %fusion.21), channel_id=1, source_target_pairs={{0,1},{1,0},{2,3},{3,2},{4,5},{5,4},{6,7},{7,6},{8,9},{9,8},{10,11... | collective-permute-start | bytes 12296 | tf_op jit(solution)/shard_map/ppermute | solution.py:26
  51.1 2.1 %collective-permute-done.2 = f32[4,256]{1,0:T(4,128)S(1)} collective-permute-done((f32[4,256]{1,0:T(4,128)S(1)}, f32[4,256]{1,0:T(4,128)S(1)}, u32[]{:S(2)}, u32[]{:S(2)}) %collective-permute-start.2) | collective-permute-done | bytes 4128 | tf_op jit(solution)/shard_map/ppermute | solution.py:26
  53.2 0.1 fusion.30
  53.3 3.5 %fusion.33 = f32[4,10752]{1,0:T(4,128)S(1)} fusion(bf16[256,10752]{1,0:T(8,128)(2,1)} %param.21, bf16[4,256]{1,0:T(4,128)(2,1)S(1)} %get-tuple-element.6, f32[256]{0:T(256)S(1)} %copy-done.2), kind=kOutput, calls=%fused_computation.78 | convolution fusion | flops 22023168 | bytes 5680128 | tf_op jit(solution)/shard_map/dot_general | solution.py:180
  57.0 1.3 %collective-permute-done.3 = f32[4,5504]{1,0:T(4,128)S(1)} collective-permute-done((f32[4,5504]{1,0:T(4,128)S(1)}, f32[4,5504]{1,0:T(4,128)S(1)}, u32[]{:S(2)}, u32[]{:S(2)}) %collective-permute-start.3) | collective-permute-done | bytes 88096 | tf_op jit(solution)/shard_map/ppermute | solution.py:26
  58.5 0.1 broadcast_in_dim.38
  58.6 15.5 %all_to_all.15 = bf16[8,4,5504]{2,1,0:T(4,128)(2,1)S(1)} all-to-all(bf16[8,4,5504]{2,1,0:T(4,128)(2,1)S(1)} %broadcast_in_dim.38), channel_id=1, replica_groups=mesh['chip'=8,'core'=2,'tp'=2] {'chip'}, dimensions={0} | all-to-all | bytes 704512 | tf_op jit(solution)/shard_map/all_to_all | solution.py:31
  74.1 0.3 convert_reduce_fusion
  74.4 0.1 slice_reduce_fusion
  74.5 0.1 fusion.10
  74.7 1.2 %collective-permute-done.4 = bf16[4,5376]{1,0:T(4,128)(2,1)S(1)} collective-permute-done((bf16[4,5376]{1,0:T(4,128)(2,1)S(1)}, bf16[4,5376]{1,0:T(4,128)(2,1)S(1)}, u32[]{:S(2)}, u32[]{:S(2)}) %collective-permute-start.4) | collective-permute-done | bytes 43040 | tf_op jit(solution)/shard_map/ppermute | solution.py:26
  75.9 0.1 broadcast_select_fusion.1
  76.1 0.8 %fusion.11 = f32[4,256]{1,0:T(4,128)S(1)} fusion(bf16[10752,256]{1,0:T(8,128)(2,1)S(1)} %bitcast.53, bf16[4,5376]{1,0:T(4,128)(2,1)S(1)} %get-tuple-element.15, bf16[4,5376]{1,0:T(4,128)(2,1)S(1)} %get-tuple-element.14), kind=kOutput, calls=%fused_computation.18 | convolution fusion | flops 22192128 | bytes 5595136 | tf_op jit(solution)/shard_map/dot_general | solution.py:207
  76.9 1.5 %collective-permute-start.5 = (f32[4,256]{1,0:T(4,128)S(1)}, f32[4,256]{1,0:T(4,128)S(1)}, u32[]{:S(2)}, u32[]{:S(2)}) collective-permute-start(f32[4,256]{1,0:T(4,128)S(1)} %fusion.11), channel_id=1, source_target_pairs={{0,1},{1,0},{2,3},{3,2},{4,5},{5,4},{6,7},{7,6},{8,9},{9,8},{10,11... | collective-permute-start | bytes 12296 | tf_op jit(solution)/shard_map/ppermute | solution.py:26
  78.4 2.1 %collective-permute-done.5 = f32[4,256]{1,0:T(4,128)S(1)} collective-permute-done((f32[4,256]{1,0:T(4,128)S(1)}, f32[4,256]{1,0:T(4,128)S(1)}, u32[]{:S(2)}, u32[]{:S(2)}) %collective-permute-start.5) | collective-permute-done | bytes 4128 | tf_op jit(solution)/shard_map/ppermute | solution.py:26
  80.5 0.6 fusion.31
  (54 shorter events, 1.3 us)
Async XLA Ops:
  0.0 3.2 %copy-start = (bf16[256,2048]{1,0:T(8,128)(2,1)S(1)}, bf16[256,2048]{1,0:T(8,128)(2,1)}, u32[]{:S(2)}) copy-start(bf16[256,2048]{1,0:T(8,128)(2,1)} %param.17) | copy-start | bytes 3145732
  0.0 53.2 %copy-start.1 = (bf16[4,256]{1,0:T(4,128)(2,1)S(1)}, bf16[4,256]{1,0:T(4,128)(2,1)}, u32[]{:S(2)}) copy-start(bf16[4,256]{1,0:T(4,128)(2,1)} %param.14) | copy-start | bytes 6148
  0.9 52.4 %copy-start.2 = (f32[256]{0:T(256)S(1)}, f32[256]{0:T(256)}, u32[]{:S(2)}) copy-start(f32[256]{0:T(256)} %param.16) | copy-start | bytes 3076
  4.2 1.4 %collective-permute-start = (f32[4,1664]{1,0:T(4,128)S(1)}, f32[4,1664]{1,0:T(4,128)S(1)}, u32[]{:S(2)}, u32[]{:S(2)}) collective-permute-start(f32[4,1664]{1,0:T(4,128)S(1)} %broadcast_select_fusion.2), channel_id=1, source_target_pairs={{0,2},{2,0},{1,3},{3,1},{4,6},{6,4},{5,7},{7,5},{8,10},{10,8},{9,1... | collective-permute-start | bytes 79880 | tf_op jit(solution)/shard_map/ppermute | solution.py:26
  6.3 15.7 %all-to-all-start = ((f32[8,4,1664]{2,1,0:T(4,128)}), f32[8,4,1664]{2,1,0:T(4,128)S(1)}, u32[]{:S(2)}, u32[]{:S(2)}) async-start(f32[8,4,1664]{2,1,0:T(4,128)} %broadcast_in_dim.32), calls=%async_computation | async-start | bytes 425984 | tf_op jit(solution)/shard_map/all_to_all | solution.py:31
  22.3 1.2 %collective-permute-start.1 = (bf16[4,1536]{1,0:T(4,128)(2,1)S(1)}, bf16[4,1536]{1,0:T(4,128)(2,1)S(1)}, u32[]{:S(2)}, u32[]{:S(2)}) collective-permute-start(bf16[4,1536]{1,0:T(4,128)(2,1)S(1)} %fusion.17), channel_id=1, source_target_pairs={{0,2},{2,0},{1,3},{3,1},{4,6},{6,4},{5,7},{7,5},{8,10},{10,8},{9,1... | collective-permute-start | bytes 36872 | tf_op jit(solution)/shard_map/ppermute | solution.py:26
  28.0 18.6 %all-to-all-start.1 = ((f32[16,4,2176]{2,1,0:T(4,128)}), f32[16,4,2176]{2,1,0:T(4,128)S(1)}, u32[]{:S(2)}, u32[]{:S(2)}) async-start(f32[16,4,2176]{2,1,0:T(4,128)} %broadcast_in_dim.35), calls=%async_computation.1 | async-start | bytes 1114112 | tf_op jit(solution)/shard_map/all_to_all | solution.py:31
  47.7 28.3 %slice-start = ((s8[5505024]{0:T(1024)(128)(4,1)}), s8[4194304]{0:T(1024)(128)(4,1)S(1)}, s32[]{:S(2)}) async-start(s8[5505024]{0:T(1024)(128)(4,1)} %bitcast.52), calls=%async_computation.3 | async-start | bytes 8388608
  49.6 3.6 %collective-permute-start.2 = (f32[4,256]{1,0:T(4,128)S(1)}, f32[4,256]{1,0:T(4,128)S(1)}, u32[]{:S(2)}, u32[]{:S(2)}) collective-permute-start(f32[4,256]{1,0:T(4,128)S(1)} %fusion.21), channel_id=1, source_target_pairs={{0,1},{1,0},{2,3},{3,2},{4,5},{5,4},{6,7},{7,6},{8,9},{9,8},{10,11... | collective-permute-start | bytes 12296 | tf_op jit(solution)/shard_map/ppermute | solution.py:26
  53.3 22.7 %slice-start.1 = ((s8[5505024]{0:T(1024)(128)(4,1)}), s8[1310720]{0:T(1024)(128)(4,1)S(1)}, s32[]{:S(2)}) async-start(s8[5505024]{0:T(1024)(128)(4,1)} %bitcast.52), calls=%async_computation.4 | async-start | bytes 2621440
  56.9 1.4 %collective-permute-start.3 = (f32[4,5504]{1,0:T(4,128)S(1)}, f32[4,5504]{1,0:T(4,128)S(1)}, u32[]{:S(2)}, u32[]{:S(2)}) collective-permute-start(f32[4,5504]{1,0:T(4,128)S(1)} %pad_maximum_fusion), channel_id=1, source_target_pairs={{0,2},{2,0},{1,3},{3,1},{4,6},{6,4},{5,7},{7,5},{8,10},{10,8},{9,1... | collective-permute-start | bytes 264200 | tf_op jit(solution)/shard_map/ppermute | solution.py:26
  74.6 1.3 %collective-permute-start.4 = (bf16[4,5376]{1,0:T(4,128)(2,1)S(1)}, bf16[4,5376]{1,0:T(4,128)(2,1)S(1)}, u32[]{:S(2)}, u32[]{:S(2)}) collective-permute-start(bf16[4,5376]{1,0:T(4,128)(2,1)S(1)} %fusion.10), channel_id=1, source_target_pairs={{0,2},{2,0},{1,3},{3,1},{4,6},{6,4},{5,7},{7,5},{8,10},{10,8},{9,1... | collective-permute-start | bytes 129032 | tf_op jit(solution)/shard_map/ppermute | solution.py:26
  76.9 3.6 %collective-permute-start.5 = (f32[4,256]{1,0:T(4,128)S(1)}, f32[4,256]{1,0:T(4,128)S(1)}, u32[]{:S(2)}, u32[]{:S(2)}) collective-permute-start(f32[4,256]{1,0:T(4,128)S(1)} %fusion.11), channel_id=1, source_target_pairs={{0,1},{1,0},{2,3},{3,2},{4,5},{5,4},{6,7},{7,6},{8,9},{9,8},{10,11... | collective-permute-start | bytes 12296 | tf_op jit(solution)/shard_map/ppermute | solution.py:26

commit v2 on v1

--- a/solution.py
+++ b/solution.py
@@ -3,6 +3,8 @@
 import jax
 import jax.numpy as jnp
 from jax import lax
+from jax.experimental import pallas as pl
+from jax.experimental.pallas import tpu as pltpu
 from jax.sharding import Mesh, PartitionSpec as P
 
 D = 4096
@@ -38,7 +40,7 @@
     return lax.psum(values_in, "tp")
 
 
-def per_device(
+def per_device_plain(
     hidden_in,
     attn_gain,
     mlp_gain,
@@ -209,12 +211,290 @@
     return (resid_rows + mlp_out).astype(jnp.bfloat16)
 
 
+IN_VMEM = pl.BlockSpec(memory_space=pltpu.VMEM)
+IN_SMEM = pl.BlockSpec(memory_space=pltpu.SMEM)
+STAT_LANES = 8
+
+
+def local_kernel(kernel, outs, operands, flops, scratch=()):
+    in_specs, placed, moved = [], [], 0
+    for x in operands:
+        if x.ndim == 1:
+            in_specs.append(IN_SMEM)
+            placed.append(x)
+        else:
+            in_specs.append(IN_VMEM)
+            placed.append(pltpu.with_memory_space_constraint(x, pltpu.VMEM))
+            moved += x.size * x.dtype.itemsize
+    return pl.pallas_call(
+        kernel,
+        out_shape=outs,
+        in_specs=in_specs,
+        out_specs=jax.tree.map(lambda _: IN_VMEM, outs),
+        scratch_shapes=scratch,
+        compiler_params=pltpu.CompilerParams(vmem_limit_bytes=24 * 2**20),
+        cost_estimate=pl.CostEstimate(flops=flops, bytes_accessed=moved, transcendentals=0),
+    )(*placed)
+
+
+def f32(*shape):
+    return jax.ShapeDtypeStruct(shape, jnp.float32)
+
+
+def bf16(*shape):
+    return jax.ShapeDtypeStruct(shape, jnp.bfloat16)
+
+
+def pieces_of(values_in):
+    first = values_in.astype(jnp.bfloat16).astype(jnp.float32)
+    second = (values_in - first).astype(jnp.bfloat16).astype(jnp.float32)
+    return first, second, values_in - first - second
+
+
+def qkv_kernel(x_ref, gain_ref, wq_ref, wk_ref, wv_ref, mine_ref, other_ref):
+    core = lax.axis_index("core")
+    x_rows = x_ref[...].astype(jnp.float32)
+    scaled_in = (x_rows * gain_ref[...]).astype(jnp.bfloat16)
+    squares = jnp.sum(x_rows * x_rows, axis=1, keepdims=True)
+    at = 0
+    for w_ref in (wq_ref, wk_ref, wv_ref):
+        half = w_ref.shape[1] // 2
+        proj = jnp.dot(scaled_in, w_ref[...], preferred_element_type=jnp.float32)
+        low, high = proj[:, :half], proj[:, half:]
+        mine_ref[:, at : at + half] = jnp.where(core == 0, low, high)
+        other_ref[:, at : at + half] = jnp.where(core == 0, high, low)
+        at += half
+    square_cols = jnp.broadcast_to(squares, (x_rows.shape[0], LANES))
+    mine_ref[:, at:] = square_cols
+    other_ref[:, at:] = square_cols
+
+
+def request_ids(lengths_ref):
+    is_long = [(lengths_ref[r] > 8).astype(jnp.int32) for r in range(4)]
+    long_0 = jnp.where(is_long[0] == 1, 0, jnp.where(is_long[1] == 1, 1, 2))
+    long_1 = jnp.where(is_long[3] == 1, 3, jnp.where(is_long[2] == 1, 2, 1))
+    short_0 = jnp.where(is_long[0] == 0, 0, jnp.where(is_long[1] == 0, 1, 2))
+    short_1 = jnp.where(is_long[3] == 0, 3, jnp.where(is_long[2] == 0, 2, 1))
+    return long_0, long_1, short_0, short_1
+
+
+def attention_kernel(
+    own_ref, oth_ref, key_ref, value_ref, mask_ref, lengths_ref, order_ref,
+    message_ref, query_out, key_out, value_out,
+):
+    core = lax.axis_index("core")
+    n_blocks = message_ref.shape[0]
+    my_block = 2 * lax.axis_index("chip") + core
+    n_req, span = mask_ref.shape
+    heads = message_ref.shape[1]
+    kv_here = key_ref.shape[2] // HD
+    group = heads // kv_here
+    own = own_ref[...].astype(jnp.float32)
+    oth = oth_ref[...].astype(jnp.float32)
+    low = jnp.where(core == 0, own, oth)
+    high = jnp.where(core == 0, oth, own)
+    for i, part in enumerate((low, high)):
+        for h in range(heads // 2):
+            query_out[:, i * (heads // 2) + h, :] = part[:, h * HD : (h + 1) * HD]
+        for k in range(kv_here // 2):
+            at = (heads // 2 + k) * HD
+            for g in range(group):
+                row = (i * (kv_here // 2) + k) * group + g
+                key_out[:, row, :] = part[:, at : at + HD]
+                at_value = at + (kv_here // 2) * HD
+                value_out[:, row, :] = part[:, at_value : at_value + HD]
+
+    long_0, long_1, short_0, short_1 = request_ids(lengths_ref)
+    short_here = jnp.where(lax.rem(order_ref[short_1], n_blocks) == my_block, short_1, short_0)
+    slot = lax.broadcasted_iota(jnp.int32, (1, span), 1)
+    group_of = lax.broadcasted_iota(jnp.int32, (heads, HD), 0) // group
+    lane = lax.broadcasted_iota(jnp.int32, (heads, LANES), 1)
+    stats = jnp.zeros((heads, LANES), jnp.float32)
+    parts = []
+    for s, r in enumerate((long_0, long_1, short_here)):
+        first_block = lax.rem(order_ref[r], n_blocks)
+        position = lax.rem(my_block - first_block + n_blocks, n_blocks) * span + slot
+        live = (position < lengths_ref[r]) & (mask_ref[pl.ds(r, 1), :] == 1)
+        query = query_out[r]
+        spread = jnp.concatenate(
+            [jnp.where(group_of == k, query, 0.0) for k in range(kv_here)], axis=1
+        ).astype(jnp.bfloat16)
+        scores = lax.dot_general(
+            spread, key_ref[r], (((1,), (1,)), ((), ())), preferred_element_type=jnp.float32
+        ) * (1.0 / math.sqrt(HD))
+        scores = jnp.where(live, scores, MASKED)
+        top = jnp.max(scores, axis=1, keepdims=True)
+        weights = jnp.where(live, jnp.exp(scores - top), 0.0)
+        total = jnp.sum(weights, axis=1, keepdims=True)
+        wide = jnp.dot(
+            weights.astype(jnp.bfloat16), value_ref[r], preferred_element_type=jnp.float32
+        )
+        numer = jnp.zeros((heads, HD), jnp.float32)
+        for k in range(kv_here):
+            numer = jnp.where(group_of == k, wide[:, k * HD : (k + 1) * HD], numer)
+        parts.append(numer)
+        for i, piece in enumerate(pieces_of(total) + pieces_of(top)):
+            stats = jnp.where(lane == s * STAT_LANES + i, piece, stats)
+    message = jnp.concatenate(parts + [stats], axis=1).astype(jnp.bfloat16)
+    for b in range(n_blocks):
+        message_ref[b] = message
+
+
+def combine_kernel(
+    arrived_ref, query_ref, key_ref, value_ref, w_ref, lengths_ref, order_ref,
+    head_ref, attended_ref,
+):
+    n_blocks, heads = arrived_ref.shape[:2]
+    long_0, long_1, short_0, short_1 = request_ids(lengths_ref)
+
+    def self_terms(r):
+        return (
+            jnp.sum(query_ref[r] * key_ref[r], axis=1, keepdims=True) * (1.0 / math.sqrt(HD)),
+            value_ref[r],
+        )
+
+    def stat(block, s):
+        lanes = arrived_ref[block, :, 3 * HD :].astype(jnp.float32)
+        at = s * STAT_LANES
+        one = [lanes[:, at + i : at + i + 1] for i in range(6)]
+        return one[0] + one[1] + one[2], one[3] + one[4] + one[5]
+
+    def numerator(block, s):
+        return arrived_ref[block, :, s * HD : (s + 1) * HD].astype(jnp.float32)
+
+    jobs = [(long_0, 0, list(range(n_blocks))), (long_1, 1, list(range(n_blocks)))]
+    for r in (short_0, short_1):
+        jobs.append((r, 2, [lax.rem(order_ref[r], n_blocks)]))
+    for r, s, blocks in jobs:
+        self_score, value_self = self_terms(r)
+        stats = [stat(b, s) for b in blocks]
+        final_top = self_score
+        for _, top in stats:
+            final_top = jnp.maximum(final_top, top)
+        self_weight = jnp.exp(self_score - final_top)
+        denominator = self_weight
+        numer = self_weight * value_self
+        for b, (total, top) in zip(blocks, stats):
+            fade = jnp.exp(top - final_top)
+            denominator = denominator + total * fade
+            numer = numer + numerator(b, s) * fade
+        attended_ref[r] = numer / denominator
+    attended = jnp.concatenate([attended_ref[:, h, :] for h in range(heads)], axis=1)
+    head_ref[...] = jnp.dot(
+        attended.astype(jnp.bfloat16), w_ref[...], preferred_element_type=jnp.float32
+    )
+
+
+def up_kernel(x_ref, part_ref, peer_ref, gain_ref, w_ref, hidden_ref, mine_ref, other_ref):
+    core = lax.axis_index("core")
+    attn_out = part_ref[...] + peer_ref[...]
+    hidden_state = (x_ref[...].astype(jnp.float32) + attn_out).astype(jnp.bfloat16)
+    resid_rows = hidden_state.astype(jnp.float32)
+    hidden_ref[...] = resid_rows
+    scaled_mlp = (resid_rows * gain_ref[...]).astype(jnp.bfloat16)
+    squares = jnp.sum(resid_rows * resid_rows, axis=1, keepdims=True)
+    up_part = jnp.dot(scaled_mlp, w_ref[...], preferred_element_type=jnp.float32)
+    half = up_part.shape[1] // 2
+    low, high = up_part[:, :half], up_part[:, half:]
+    mine_ref[:, :half] = jnp.where(core == 0, low, high)
+    other_ref[:, :half] = jnp.where(core == 0, high, low)
+    square_cols = jnp.broadcast_to(squares, (resid_rows.shape[0], LANES))
+    mine_ref[:, half:] = square_cols
+    other_ref[:, half:] = square_cols
+
+
+def per_device(
+    hidden_in,
+    attn_gain,
+    mlp_gain,
+    query_weight,
+    key_weight,
+    value_weight,
+    out_weight,
+    up_weight,
+    down_weight,
+    key_cache,
+    value_cache,
+    lengths,
+    block_order,
+    pad_mask,
+):
+    n_req, d_here = hidden_in.shape
+    kv_here = key_cache.shape[2] // HD
+    heads_here = kv_here * (H // KVH)
+    n_chips = lax.axis_size("chip")
+    core = lax.axis_index("core")
+    n_blocks = 2 * n_chips
+    half_qkv = (heads_here + 2 * kv_here) * HD // 2
+    half_up = up_weight.shape[1] // 2
+
+    mine, other = local_kernel(
+        qkv_kernel,
+        [f32(n_req, half_qkv + LANES)] * 2,
+        [hidden_in, attn_gain.reshape(1, d_here), query_weight, key_weight, value_weight],
+        flops=4 * n_req * d_here * half_qkv,
+    )
+    pair_sum = mine + swap(other, "core")
+    qkv_sum = jnp.sum(gather_all(pair_sum, "chip", n_chips), axis=0)
+    inv_attn = lax.rsqrt(qkv_sum[:, -1:] / D + NORM_EPS)
+    qkv_half = (qkv_sum[:, :-LANES] * inv_attn).astype(jnp.bfloat16)
+    qkv_other = swap(qkv_half, "core")
+
+    message, query_heads, key_heads, value_heads = local_kernel(
+        attention_kernel,
+        [bf16(n_blocks, heads_here, 3 * HD + LANES)] + [f32(n_req, heads_here, HD)] * 3,
+        [qkv_half, qkv_other, key_cache, value_cache, pad_mask, lengths, block_order],
+        flops=12 * heads_here * kv_here * HD * pad_mask.shape[1],
+    )
+    arrived = lax.all_to_all(message, ("chip", "core"), 0, 0)
+    head_part = local_kernel(
+        combine_kernel,
+        f32(n_req, d_here),
+        [arrived, query_heads, key_heads, value_heads, out_weight, lengths, block_order],
+        flops=2 * n_req * out_weight.size,
+        scratch=[pltpu.VMEM((n_req, heads_here, HD), jnp.float32)],
+    )
+    head_peer = swap(head_part, "tp")
+
+    resid_rows, up_mine, up_other = local_kernel(
+        up_kernel,
+        [f32(n_req, d_here)] + [f32(n_req, half_up + LANES)] * 2,
+        [hidden_in, head_part, head_peer, mlp_gain.reshape(1, d_here), up_weight],
+        flops=2 * n_req * up_weight.size,
+    )
+    up_pair = up_mine + swap(up_other, "core")
+    square_sum = up_pair[:, half_up : half_up + 1]
+    piece_0 = lax.reduce_precision(square_sum, 8, 7)
+    piece_1 = lax.reduce_precision(square_sum - piece_0, 8, 7)
+    piece_2 = square_sum - piece_0 - piece_1
+    pieces = jnp.pad(
+        jnp.concatenate([piece_0, piece_1, piece_2], axis=1), ((0, 0), (0, LANES - 3))
+    )
+    up_message = jnp.concatenate([up_pair[:, :half_up], pieces], axis=1).astype(jnp.bfloat16)
+    up_sum = jnp.sum(gather_all(up_message, "chip", n_chips).astype(jnp.float32), axis=0)
+    squares = jnp.sum(up_sum[:, half_up:], axis=1, keepdims=True)
+    inv_mlp = lax.rsqrt(squares / D + NORM_EPS)
+    active_half = squared_relu(up_sum[:, :half_up] * inv_mlp).astype(jnp.bfloat16)
+    active_other = swap(active_half, "core")
+    activated = jnp.concatenate(
+        [
+            jnp.where(core == 0, active_half, active_other),
+            jnp.where(core == 0, active_other, active_half),
+        ],
+        axis=1,
+    )
+    down_part = jnp.dot(activated, down_weight, preferred_element_type=jnp.float32)
+    mlp_out = sum_tp(down_part)
+    return (resid_rows + mlp_out).astype(jnp.bfloat16)
+
+
 def solution(mesh):
     n_seq, n_tp = mesh.shape["seq"], mesh.shape["tp"]
     split = Mesh(mesh.devices.reshape(n_seq // 2, 2, n_tp), ("chip", "core", "tp"))
     seq = ("chip", "core")
+    whole_tiles = n_tp == 2 and KVH % (2 * n_tp) == 0 and D % (n_seq * LANES) == 0
     return jax.shard_map(
-        per_device,
+        per_device if whole_tiles else per_device_plain,
         mesh=split,
         in_specs=(
             P(None, seq),

time: 81.6 us -> 78.8 us (0.966)
  blocking collectives: 15.5 us -> 43 us
  waiting for transfers between devices: 30.4 us -> 8.67 us
  starting transfers between devices: 14.5 us -> 3.64 us
  local copies, waits for them, and re-layouts: 3.14 us -> 13.8 us
  matrix products: 12.1 us -> 3.38 us
  Pallas kernels: 0 us -> 3.98 us
  other arithmetic: 5.17 us -> 1.63 us
    all_to_all x2 -> x0, waiting for transfers between devices: 22.5 us -> none  [gather_all(): return lax.all_to_all(copies, axes, 0, 0)]
    all_to_all x1 -> x2, blocking collectives: 15.5 us -> 29.8 us  [gather_all(): return lax.all_to_all(copies, axes, 0, 0)]
    unnamed x14 -> x32, local copies, waits for them, and re-layouts: 0.34 us -> 13.7 us
    all_to_all x0 -> x1, blocking collectives: none -> 13.2 us  [per_device(): arrived = lax.all_to_all(message, ('chip', 'core'), 0, 0)]
    dot_general x8 -> x0, matrix products: 11.3 us -> none  [the longest x1 3.48 us: per_device(): up_part = jnp.dot(scaled_mlp, up_weight, preferred_element_type=jnp.float32)]
    all_to_all x2 -> x0, starting transfers between devices: 10.7 us -> none  [gather_all(): return lax.all_to_all(copies, axes, 0, 0)]
    pallas_call x0 -> x4, Pallas kernels: none -> 3.98 us  [local_kernel(): pl.pallas_call(kernel, out_shape=outs, in_specs=in_specs, out_specs=jax.t...]
    dot_general x1, matrix products: 0.82 us -> 3.38 us  [per_device(): jnp.dot(activated, down_weight, preferred_element_type=jnp.float32)]
  transfers between devices with their start and end apart: 8 -> 6, of which waited for: 8 -> 6; matrix products, arithmetic and copies ran while one was open for 2% -> 0% of each run, Pallas kernels for 0% -> 0%
where the time goes in v2:
time: 78.8 us; the launch traced here: 78.2 us
  blocking collectives  43 us (55%)
  local copies, waits for them, and re-layouts  13.8 us (18%)
  waiting for transfers between devices  8.67 us (11%)
  Pallas kernels  3.98 us (5%)
  starting transfers between devices  3.64 us (5%)
  matrix products  3.38 us (4%)
  other arithmetic  1.63 us (2%)
    all_to_all x2, blocking collectives, gather_all(): return lax.all_to_all(copies, axes, 0, 0)  29.8 us
    unnamed x32, local copies, waits for them, and re-layouts  13.7 us
    all_to_all x1, blocking collectives, per_device(): arrived = lax.all_to_all(message, ('chip', 'core'), 0, 0)  13.2 us
    ppermute x6, waiting for transfers between devices, swap(): return lax.ppermute(values_in, axis, [(i, i ^ 1) for i in range(n)])  8.67 us
    pallas_call x4, Pallas kernels, local_kernel(): pl.pallas_call(kernel, out_shape=outs, in_specs=in_specs, out_specs=jax.t...  3.98 us
    ppermute x6, starting transfers between devices, swap(): return lax.ppermute(values_in, axis, [(i, i ^ 1) for i in range(n)])  3.64 us
    dot_general x1, matrix products, per_device(): jnp.dot(activated, down_weight, preferred_element_type=jnp.float32)  3.38 us
  transfers between devices with their start and end apart: 6, of which 6 were waited for; matrix products, arithmetic and copies ran while one was open for 0% of the time, Pallas kernels for 0%

profile of v2, /device:TPU:0, one launch (start us, length us, event | category | flops | bytes accessed | tf_op | source)
XLA Modules:
  0.0 78.2 jit_solution(6650591732969333859)
XLA Ops:
  0.0 0.0 copy-start.15
  0.0 0.0 copy-start.2
  0.0 1.2 %copy-done.2 = bf16[256,2048]{1,0:T(8,128)(2,1)S(1)} copy-done((bf16[256,2048]{1,0:T(8,128)(2,1)S(1)}, bf16[256,2048]{1,0:T(8,128)(2,1)}, u32[]{:S(2)}) %copy-start.2) | copy-done | bytes 1048600
  1.2 0.0 copy-start.5
  1.2 0.9 %copy-done.5 = bf16[256,512]{1,0:T(8,128)(2,1)S(1)} copy-done((bf16[256,512]{1,0:T(8,128)(2,1)S(1)}, bf16[256,512]{1,0:T(8,128)(2,1)}, u32[]{:S(2)}) %copy-start.5) | copy-done | bytes 262168
  2.2 0.9 %copy-done.6 = bf16[256,512]{1,0:T(8,128)(2,1)S(1)} copy-done((bf16[256,512]{1,0:T(8,128)(2,1)S(1)}, bf16[256,512]{1,0:T(8,128)(2,1)}, u32[]{:S(2)}) %copy-start.6) | copy-done | bytes 262168
  3.1 0.7 copy-done.7
  3.8 0.7 copy-done.14
  4.5 0.3 shard_map.136
  4.8 0.5 collective-permute-start
  5.3 0.9 %collective-permute-done = f32[4,1664]{1,0:T(4,128)S(1)} collective-permute-done((f32[4,1664]{1,0:T(4,128)S(1)}, f32[4,1664]{1,0:T(4,128)S(1)}, u32[]{:S(2)}, u32[]{:S(2)}) %collective-permute-start) | collective-permute-done | bytes 26656 | tf_op jit(solution)/shard_map/ppermute | solution.py:28
  6.2 15.5 %all_to_all.15 = f32[8,4,1664]{2,1,0:T(4,128)S(1)} all-to-all(f32[8,4,1664]{2,1,0:T(4,128)S(1)} %broadcast_in_dim.4), channel_id=1, replica_groups=mesh['chip'=8,'core'=2,'tp'=2] {'chip'}, dimensions={0} | all-to-all | bytes 425984 | tf_op jit(solution)/shard_map/all_to_all | solution.py:33
  21.7 0.2 fusion.14
  21.9 0.1 fusion.7.own_ref
  22.0 0.0 collective-permute-start.1
  22.0 1.2 %collective-permute-done.1.oth_ref = bf16[4,1536]{1,0:T(4,128)(2,1)S(1)} collective-permute-done((bf16[4,1536]{1,0:T(4,128)(2,1)S(1)}, bf16[4,1536]{1,0:T(4,128)(2,1)S(1)}, u32[]{:S(2)}, u32[]{:S(2)}) %collective-permute-start.1) | collective-permute-done | bytes 12320 | tf_op jit(solution)/shard_map/ppermute | solution.py:28
  23.2 1.0 %copy-done.3 = bf16[4,128,512]{2,1,0:T(8,128)(2,1)S(1)} copy-done((bf16[4,128,512]{2,1,0:T(8,128)(2,1)S(1)}, bf16[4,128,512]{2,1,0:T(8,128)(2,1)}, u32[]{:S(2)}) %copy-start.3) | copy-done | bytes 524312
  24.2 1.0 %copy-done.4 = bf16[4,128,512]{2,1,0:T(8,128)(2,1)S(1)} copy-done((bf16[4,128,512]{2,1,0:T(8,128)(2,1)S(1)}, bf16[4,128,512]{2,1,0:T(8,128)(2,1)}, u32[]{:S(2)}) %copy-start.4) | copy-done | bytes 524312
  25.2 0.7 copy-done.9
  25.9 0.7 copy-done.11
  26.5 0.7 copy-done.13
  27.2 1.5 %shard_map.137 = (bf16[16,16,512]{2,1,0:T(8,128)(2,1)S(1)}, f32[4,16,128]{2,1,0:T(8,128)S(1)}, f32[4,16,128]{2,1,0:T(8,128)S(1)}, f32[4,16,128]{2,1,0:T(8,128)S(1)}) custom-call(bf16[4,1536]{1,0:T(4,128)(2,1)S(1)} %fusion.7.own_ref, bf16[4,1536]{1,0:T(4,128)(2,1)S(1)} %collective-permute-done.1.oth_ref, bf16[4,128,512]{2,1,0:T(8,128)(2,1)S(1)} %copy-done.3, ...), custom_call_target="tpu_custom_call" | custom-call | flops 12582912 | bytes 1075200 | tf_op jit(solution)/shard_map/pallas_call | solution.py:229
  28.8 13.2 %all_to_all.16.arrived_ref = bf16[16,16,512]{2,1,0:T(8,128)(2,1)S(1)} all-to-all(bf16[16,16,512]{2,1,0:T(8,128)(2,1)S(1)} %get-tuple-element.16), channel_id=1, replica_groups=mesh['chip'=8,'core'=2,'tp'=2] {'chip','core'}, dimensions={0} | all-to-all | bytes 524288 | tf_op jit(solution)/shard_map/all_to_all | solution.py:449
  42.0 1.2 %copy-done.1 = bf16[2048,256]{1,0:T(8,128)(2,1)S(1)} copy-done((bf16[2048,256]{1,0:T(8,128)(2,1)S(1)}, bf16[2048,256]{1,0:T(8,128)(2,1)}, u32[]{:S(2)}) %copy-start.1) | copy-done | bytes 1048600
  43.2 0.7 copy-done.10
  43.9 0.7 copy-done.12
  44.5 1.3 %shard_map.138.part_ref = f32[4,256]{1,0:T(4,128)S(1)} custom-call(bf16[16,16,512]{2,1,0:T(8,128)(2,1)S(1)} %all_to_all.16.arrived_ref, f32[4,16,128]{2,1,0:T(8,128)S(1)} %get-tuple-element.17.query_ref, f32[4,16,128]{2,1,0:T(8,128)S(1)} %get-tuple-element.18.key_ref, f32[4,16,128]{2,1,0:T(8,128)S(1)} %get-tuple-element.19.value_ref, ...), custom_call_target="tpu_custom_call" | custom-call | flops 4194304 | bytes 1409024 | tf_op jit(solution)/shard_map/pallas_call | solution.py:229
  45.8 1.5 %collective-permute-start.2 = (f32[4,256]{1,0:T(4,128)S(1)}, f32[4,256]{1,0:T(4,128)S(1)}, u32[]{:S(2)}, u32[]{:S(2)}) collective-permute-start(f32[4,256]{1,0:T(4,128)S(1)} %shard_map.138.part_ref), channel_id=1, source_target_pairs={{0,1},{1,0},{2,3},{3,2},{4,5},{5,4},{6,7},{7,6},{8,9},{9,8},{10,11... | collective-permute-start | bytes 12296 | tf_op jit(solution)/shard_map/ppermute | solution.py:28
  47.4 2.1 %collective-permute-done.2.peer_ref = f32[4,256]{1,0:T(4,128)S(1)} collective-permute-done((f32[4,256]{1,0:T(4,128)S(1)}, f32[4,256]{1,0:T(4,128)S(1)}, u32[]{:S(2)}, u32[]{:S(2)}) %collective-permute-start.2) | collective-permute-done | bytes 4128 | tf_op jit(solution)/shard_map/ppermute | solution.py:28
  49.5 0.0 copy-done.15
  49.5 0.0 copy-done.8
  49.5 2.6 %copy-done = bf16[256,10752]{1,0:T(8,128)(2,1)S(1)} copy-done((bf16[256,10752]{1,0:T(8,128)(2,1)S(1)}, bf16[256,10752]{1,0:T(8,128)(2,1)}, u32[]{:S(2)}) %copy-start) | copy-done | bytes 5505048
  52.0 0.8 %shard_map.139 = (f32[4,256]{1,0:T(4,128)S(1)}, f32[4,5504]{1,0:T(4,128)S(1)}, f32[4,5504]{1,0:T(4,128)S(1)}) custom-call(bf16[4,256]{1,0:T(4,128)(2,1)S(1)} %copy-done.8, f32[4,256]{1,0:T(4,128)S(1)} %shard_map.138.part_ref, f32[4,256]{1,0:T(4,128)S(1)} %collective-permute-done.2.peer_ref, f32[1,256]{1,0:T(1,128)S(1)} %bitcast.4, bf16[256,10752]{1,0:T(8,128)(2,1)S(1)} %copy-done), custom_call_target="tpu_custom_call" | custom-call | flops 22020096 | bytes 5516288 | tf_op jit(solution)/shard_map/pallas_call | solution.py:229
  52.9 0.0 collective-permute-start.3
  52.9 1.3 %collective-permute-done.3 = f32[4,5504]{1,0:T(4,128)S(1)} collective-permute-done((f32[4,5504]{1,0:T(4,128)S(1)}, f32[4,5504]{1,0:T(4,128)S(1)}, u32[]{:S(2)}, u32[]{:S(2)}) %collective-permute-start.3) | collective-permute-done | bytes 88096 | tf_op jit(solution)/shard_map/ppermute | solution.py:28
  54.2 0.1 fusion.16
  54.3 0.1 broadcast_in_dim.5
  54.4 14.3 %all_to_all.17 = bf16[8,4,5504]{2,1,0:T(4,128)(2,1)S(1)} all-to-all(bf16[8,4,5504]{2,1,0:T(4,128)(2,1)S(1)} %broadcast_in_dim.5), channel_id=1, replica_groups=mesh['chip'=8,'core'=2,'tp'=2] {'chip'}, dimensions={0} | all-to-all | bytes 704512 | tf_op jit(solution)/shard_map/all_to_all | solution.py:33
  68.8 0.3 convert_reduce_fusion
  69.0 0.1 slice_reduce_fusion
  69.1 0.1 fusion.2
  69.2 0.1 collective-permute-start.4
  69.3 1.2 %collective-permute-done.4 = bf16[4,5376]{1,0:T(4,128)(2,1)S(1)} collective-permute-done((bf16[4,5376]{1,0:T(4,128)(2,1)S(1)}, bf16[4,5376]{1,0:T(4,128)(2,1)S(1)}, u32[]{:S(2)}, u32[]{:S(2)}) %collective-permute-start.4) | collective-permute-done | bytes 43040 | tf_op jit(solution)/shard_map/ppermute | solution.py:28
  70.5 0.1 broadcast_select_fusion.1
  70.7 3.4 %fusion.3 = f32[4,256]{1,0:T(4,128)S(1)} fusion(bf16[10752,256]{1,0:T(8,128)(2,1)} %param.22, bf16[4,5376]{1,0:T(4,128)(2,1)S(1)} %get-tuple-element.27, bf16[4,5376]{1,0:T(4,128)(2,1)S(1)} %get-tuple-element.26), kind=kOutput, calls=%fused_computation.6 | convolution fusion | flops 22192128 | bytes 5595136 | tf_op jit(solution)/shard_map/dot_general | solution.py:486
  74.0 1.5 %collective-permute-start.5 = (f32[4,256]{1,0:T(4,128)S(1)}, f32[4,256]{1,0:T(4,128)S(1)}, u32[]{:S(2)}, u32[]{:S(2)}) collective-permute-start(f32[4,256]{1,0:T(4,128)S(1)} %fusion.3), channel_id=1, source_target_pairs={{0,1},{1,0},{2,3},{3,2},{4,5},{5,4},{6,7},{7,6},{8,9},{9,8},{10,11... | collective-permute-start | bytes 12296 | tf_op jit(solution)/shard_map/ppermute | solution.py:28
  75.6 2.1 %collective-permute-done.5 = f32[4,256]{1,0:T(4,128)S(1)} collective-permute-done((f32[4,256]{1,0:T(4,128)S(1)}, f32[4,256]{1,0:T(4,128)S(1)}, u32[]{:S(2)}, u32[]{:S(2)}) %collective-permute-start.5) | collective-permute-done | bytes 4128 | tf_op jit(solution)/shard_map/ppermute | solution.py:28
  77.6 0.6 add_convert_fusion
  (21 shorter events, 0.2 us)
Async XLA Ops:
  0.0 49.5 %copy-start.15 = (f32[256]{0:T(256)S(1)}, f32[256]{0:T(256)}, u32[]{:S(2)}) copy-start(f32[256]{0:T(256)} %param.16) | copy-start | bytes 3076
  0.0 1.2 %copy-start.2 = (bf16[256,2048]{1,0:T(8,128)(2,1)S(1)}, bf16[256,2048]{1,0:T(8,128)(2,1)}, u32[]{:S(2)}) copy-start(bf16[256,2048]{1,0:T(8,128)(2,1)} %wq_ref.1) | copy-start | bytes 3145732
  1.2 0.9 %copy-start.5 = (bf16[256,512]{1,0:T(8,128)(2,1)S(1)}, bf16[256,512]{1,0:T(8,128)(2,1)}, u32[]{:S(2)}) copy-start(bf16[256,512]{1,0:T(8,128)(2,1)} %wk_ref.1) | copy-start | bytes 786436
  2.2 0.9 %copy-start.6 = (bf16[256,512]{1,0:T(8,128)(2,1)S(1)}, bf16[256,512]{1,0:T(8,128)(2,1)}, u32[]{:S(2)}) copy-start(bf16[256,512]{1,0:T(8,128)(2,1)} %wv_ref.1) | copy-start | bytes 786436
  3.1 0.7 copy-start.7
  3.8 0.7 copy-start.14
  4.5 45.0 %copy-start.8 = (bf16[4,256]{1,0:T(4,128)(2,1)S(1)}, bf16[4,256]{1,0:T(4,128)(2,1)}, u32[]{:S(2)}) copy-start(bf16[4,256]{1,0:T(4,128)(2,1)} %x_ref.3) | copy-start | bytes 6148
  4.8 1.3 %collective-permute-start = (f32[4,1664]{1,0:T(4,128)S(1)}, f32[4,1664]{1,0:T(4,128)S(1)}, u32[]{:S(2)}, u32[]{:S(2)}) collective-permute-start(f32[4,1664]{1,0:T(4,128)S(1)} %get-tuple-element.15), channel_id=1, source_target_pairs={{0,2},{2,0},{1,3},{3,1},{4,6},{6,4},{5,7},{7,5},{8,10},{10,8},{9,1... | collective-permute-start | bytes 79880 | tf_op jit(solution)/shard_map/ppermute | solution.py:28
  22.0 1.2 %collective-permute-start.1 = (bf16[4,1536]{1,0:T(4,128)(2,1)S(1)}, bf16[4,1536]{1,0:T(4,128)(2,1)S(1)}, u32[]{:S(2)}, u32[]{:S(2)}) collective-permute-start(bf16[4,1536]{1,0:T(4,128)(2,1)S(1)} %fusion.7.own_ref), channel_id=1, source_target_pairs={{0,2},{2,0},{1,3},{3,1},{4,6},{6,4},{5,7},{7,5},{8,10},{10,8},{9,1... | collective-permute-start | bytes 36872 | tf_op jit(solution)/shard_map/ppermute | solution.py:28
  23.1 1.0 %copy-start.3 = (bf16[4,128,512]{2,1,0:T(8,128)(2,1)S(1)}, bf16[4,128,512]{2,1,0:T(8,128)(2,1)}, u32[]{:S(2)}) copy-start(bf16[4,128,512]{2,1,0:T(8,128)(2,1)} %key_ref.1) | copy-start | bytes 1572868
  24.2 1.0 %copy-start.4 = (bf16[4,128,512]{2,1,0:T(8,128)(2,1)S(1)}, bf16[4,128,512]{2,1,0:T(8,128)(2,1)}, u32[]{:S(2)}) copy-start(bf16[4,128,512]{2,1,0:T(8,128)(2,1)} %value_ref.1) | copy-start | bytes 1572868
  25.2 0.7 copy-start.9
  25.9 0.7 copy-start.11
  26.5 0.7 copy-start.13
  42.0 1.2 %copy-start.1 = (bf16[2048,256]{1,0:T(8,128)(2,1)S(1)}, bf16[2048,256]{1,0:T(8,128)(2,1)}, u32[]{:S(2)}) copy-start(bf16[2048,256]{1,0:T(8,128)(2,1)} %w_ref.2) | copy-start | bytes 3145732
  43.2 0.7 copy-start.10
  43.9 0.7 copy-start.12
  45.8 3.6 %collective-permute-start.2 = (f32[4,256]{1,0:T(4,128)S(1)}, f32[4,256]{1,0:T(4,128)S(1)}, u32[]{:S(2)}, u32[]{:S(2)}) collective-permute-start(f32[4,256]{1,0:T(4,128)S(1)} %shard_map.138.part_ref), channel_id=1, source_target_pairs={{0,1},{1,0},{2,3},{3,2},{4,5},{5,4},{6,7},{7,6},{8,9},{9,8},{10,11... | collective-permute-start | bytes 12296 | tf_op jit(solution)/shard_map/ppermute | solution.py:28
  49.5 2.6 %copy-start = (bf16[256,10752]{1,0:T(8,128)(2,1)S(1)}, bf16[256,10752]{1,0:T(8,128)(2,1)}, u32[]{:S(2)}) copy-start(bf16[256,10752]{1,0:T(8,128)(2,1)} %w_ref.3) | copy-start | bytes 16515076
  52.9 1.3 %collective-permute-start.3 = (f32[4,5504]{1,0:T(4,128)S(1)}, f32[4,5504]{1,0:T(4,128)S(1)}, u32[]{:S(2)}, u32[]{:S(2)}) collective-permute-start(f32[4,5504]{1,0:T(4,128)S(1)} %get-tuple-element.22), channel_id=1, source_target_pairs={{0,2},{2,0},{1,3},{3,1},{4,6},{6,4},{5,7},{7,5},{8,10},{10,8},{9,1... | collective-permute-start | bytes 264200 | tf_op jit(solution)/shard_map/ppermute | solution.py:28
  69.2 1.3 %collective-permute-start.4 = (bf16[4,5376]{1,0:T(4,128)(2,1)S(1)}, bf16[4,5376]{1,0:T(4,128)(2,1)S(1)}, u32[]{:S(2)}, u32[]{:S(2)}) collective-permute-start(bf16[4,5376]{1,0:T(4,128)(2,1)S(1)} %fusion.2), channel_id=1, source_target_pairs={{0,2},{2,0},{1,3},{3,1},{4,6},{6,4},{5,7},{7,5},{8,10},{10,8},{9,1... | collective-permute-start | bytes 129032 | tf_op jit(solution)/shard_map/ppermute | solution.py:28
  74.0 3.6 %collective-permute-start.5 = (f32[4,256]{1,0:T(4,128)S(1)}, f32[4,256]{1,0:T(4,128)S(1)}, u32[]{:S(2)}, u32[]{:S(2)}) collective-permute-start(f32[4,256]{1,0:T(4,128)S(1)} %fusion.3), channel_id=1, source_target_pairs={{0,1},{1,0},{2,3},{3,2},{4,5},{5,4},{6,7},{7,6},{8,9},{9,8},{10,11... | collective-permute-start | bytes 12296 | tf_op jit(solution)/shard_map/ppermute | solution.py:28

commit v3 on v2

--- a/solution.py
+++ b/solution.py
@@ -216,33 +216,35 @@
 STAT_LANES = 8
 
 
-def local_kernel(kernel, outs, operands, flops, scratch=()):
+def local_kernel(kernel, outs, operands, flops, scratch=(), in_hbm=(), anywhere=()):
     in_specs, placed, moved = [], [], 0
-    for x in operands:
+    for i, x in enumerate(operands):
         if x.ndim == 1:
             in_specs.append(IN_SMEM)
             placed.append(x)
-        else:
-            in_specs.append(IN_VMEM)
-            placed.append(pltpu.with_memory_space_constraint(x, pltpu.VMEM))
-            moved += x.size * x.dtype.itemsize
+            continue
+        space = pltpu.HBM if i in in_hbm else pltpu.VMEM
+        in_specs.append(pl.BlockSpec(memory_space=space))
+        placed.append(x if i in anywhere else pltpu.with_memory_space_constraint(x, space))
+        moved += x.size * x.dtype.itemsize
+    out_specs = [IN_SMEM if len(o.shape) == 1 else IN_VMEM for o in outs]
     return pl.pallas_call(
         kernel,
         out_shape=outs,
         in_specs=in_specs,
-        out_specs=jax.tree.map(lambda _: IN_VMEM, outs),
+        out_specs=out_specs,
         scratch_shapes=scratch,
-        compiler_params=pltpu.CompilerParams(vmem_limit_bytes=24 * 2**20),
+        compiler_params=pltpu.CompilerParams(vmem_limit_bytes=6 * 2**20),
         cost_estimate=pl.CostEstimate(flops=flops, bytes_accessed=moved, transcendentals=0),
     )(*placed)
 
 
 def f32(*shape):
-    return jax.ShapeDtypeStruct(shape, jnp.float32)
+    return pltpu.VMEM(shape, jnp.float32)
 
 
 def bf16(*shape):
-    return jax.ShapeDtypeStruct(shape, jnp.bfloat16)
+    return pltpu.VMEM(shape, jnp.bfloat16)
 
 
 def pieces_of(values_in):
@@ -251,22 +253,55 @@
     return first, second, values_in - first - second
 
 
-def qkv_kernel(x_ref, gain_ref, wq_ref, wk_ref, wv_ref, mine_ref, other_ref):
+def qkv_kernel(
+    x_hbm, gain_hbm, wq_hbm, wk_hbm, wv_hbm, mine_ref, other_ref, x_ref, gain_ref, *scratch
+):
     core = lax.axis_index("core")
+    w_refs, sems = scratch[:-1], scratch[-1]
+    chunk = w_refs[0].shape[1]
+    copies = [
+        pltpu.make_async_copy(x_hbm, x_ref, sems.at[0]),
+        pltpu.make_async_copy(gain_hbm, gain_ref, sems.at[1]),
+    ]
+    pieces = [(w, at) for w in (wq_hbm, wk_hbm, wv_hbm) for at in range(0, w.shape[1], chunk)]
+    for (w_hbm, at), w_ref in zip(pieces, w_refs):
+        copies.append(
+            pltpu.make_async_copy(
+                w_hbm.at[:, pl.ds(at, chunk)], w_ref, sems.at[len(copies)]
+            )
+        )
+    for copy in copies:
+        copy.start()
+    copies[0].wait()
+    copies[1].wait()
     x_rows = x_ref[...].astype(jnp.float32)
     scaled_in = (x_rows * gain_ref[...]).astype(jnp.bfloat16)
     squares = jnp.sum(x_rows * x_rows, axis=1, keepdims=True)
-    at = 0
-    for w_ref in (wq_ref, wk_ref, wv_ref):
-        half = w_ref.shape[1] // 2
-        proj = jnp.dot(scaled_in, w_ref[...], preferred_element_type=jnp.float32)
-        low, high = proj[:, :half], proj[:, half:]
+    proj = []
+    for w_ref, copy in zip(w_refs, copies[2:]):
+        copy.wait()
+        proj.append(jnp.dot(scaled_in, w_ref[...], preferred_element_type=jnp.float32))
+    proj = jnp.concatenate(proj, axis=1)
+    at, start = 0, 0
+    for w_hbm in (wq_hbm, wk_hbm, wv_hbm):
+        half = w_hbm.shape[1] // 2
+        low, high = proj[:, start : start + half], proj[:, start + half : start + 2 * half]
         mine_ref[:, at : at + half] = jnp.where(core == 0, low, high)
         other_ref[:, at : at + half] = jnp.where(core == 0, high, low)
         at += half
+        start += 2 * half
     square_cols = jnp.broadcast_to(squares, (x_rows.shape[0], LANES))
     mine_ref[:, at:] = square_cols
     other_ref[:, at:] = square_cols
+
+
+def qkv_sum_kernel(arrived_ref, plan_ref, out_ref):
+    total = arrived_ref[0]
+    for i in range(1, arrived_ref.shape[0]):
+        total = total + arrived_ref[i]
+    width = out_ref.shape[1]
+    inv_attn = lax.rsqrt(total[:, width : width + 1] / D + NORM_EPS)
+    out_ref[...] = (total[:, :width] * inv_attn).astype(jnp.bfloat16)
 
 
 def request_ids(lengths_ref):
@@ -278,13 +313,60 @@
     return long_0, long_1, short_0, short_1
 
 
+PLAN_SLOT = 0
+PLAN_LIVE = 3
+PLAN_SHORT = 6
+PLAN_OWNER = 8
+PLAN_SIZE = 16
+
+
+def prefetch_kernel(
+    after_ref, lengths_ref, order_ref, key_hbm, value_hbm, *refs,
+):
+    n_plain = (len(refs) - 4) // 2
+    plain_in, refs = refs[:n_plain], refs[n_plain:]
+    plan_ref, key_ref, value_ref = refs[:3]
+    plain_out, sems = refs[3:-1], refs[-1]
+    n_blocks = lax.axis_size("chip") * 2
+    my_block = 2 * lax.axis_index("chip") + lax.axis_index("core")
+    span = key_hbm.shape[1]
+    long_0, long_1, short_0, short_1 = request_ids(lengths_ref)
+    owners = [lax.rem(order_ref[r], n_blocks) for r in (short_0, short_1)]
+    short_here = jnp.where(owners[1] == my_block, short_1, short_0)
+    copies = []
+    for s, r in enumerate((long_0, long_1, short_here)):
+        for hbm, vmem in ((key_hbm, key_ref), (value_hbm, value_ref)):
+            copies.append(pltpu.make_async_copy(hbm.at[r], vmem.at[s], sems.at[len(copies)]))
+            copies[-1].start()
+    for hbm, vmem in zip(plain_in, plain_out):
+        copies.append(pltpu.make_async_copy(hbm, vmem, sems.at[len(copies)]))
+        copies[-1].start()
+    for s, r in enumerate((long_0, long_1, short_here)):
+        first_block = lax.rem(order_ref[r], n_blocks)
+        begin = lax.rem(my_block - first_block + n_blocks, n_blocks) * span
+        plan_ref[PLAN_SLOT + s] = r
+        plan_ref[PLAN_LIVE + s] = lengths_ref[r] - begin
+    for i, r in enumerate((short_0, short_1)):
+        plan_ref[PLAN_SHORT + i] = r
+        plan_ref[PLAN_OWNER + i] = owners[i]
+    for i in range(PLAN_OWNER + 2, PLAN_SIZE):
+        plan_ref[i] = 0
+    for copy in copies:
+        copy.wait()
+
+
+def copy_kernel(after_ref, w_hbm, w_ref, sem):
+    copy = pltpu.make_async_copy(w_hbm, w_ref, sem)
+    copy.start()
+    copy.wait()
+
+
 def attention_kernel(
-    own_ref, oth_ref, key_ref, value_ref, mask_ref, lengths_ref, order_ref,
+    own_ref, oth_ref, key_ref, value_ref, mask_ref, plan_ref,
     message_ref, query_out, key_out, value_out,
 ):
     core = lax.axis_index("core")
     n_blocks = message_ref.shape[0]
-    my_block = 2 * lax.axis_index("chip") + core
     n_req, span = mask_ref.shape
     heads = message_ref.shape[1]
     kv_here = key_ref.shape[2] // HD
@@ -304,30 +386,27 @@
                 at_value = at + (kv_here // 2) * HD
                 value_out[:, row, :] = part[:, at_value : at_value + HD]
 
-    long_0, long_1, short_0, short_1 = request_ids(lengths_ref)
-    short_here = jnp.where(lax.rem(order_ref[short_1], n_blocks) == my_block, short_1, short_0)
     slot = lax.broadcasted_iota(jnp.int32, (1, span), 1)
     group_of = lax.broadcasted_iota(jnp.int32, (heads, HD), 0) // group
     lane = lax.broadcasted_iota(jnp.int32, (heads, LANES), 1)
     stats = jnp.zeros((heads, LANES), jnp.float32)
     parts = []
-    for s, r in enumerate((long_0, long_1, short_here)):
-        first_block = lax.rem(order_ref[r], n_blocks)
-        position = lax.rem(my_block - first_block + n_blocks, n_blocks) * span + slot
-        live = (position < lengths_ref[r]) & (mask_ref[pl.ds(r, 1), :] == 1)
+    for s in range(3):
+        r = plan_ref[PLAN_SLOT + s]
+        live = (slot < plan_ref[PLAN_LIVE + s]) & (mask_ref[pl.ds(r, 1), :] == 1)
         query = query_out[r]
         spread = jnp.concatenate(
             [jnp.where(group_of == k, query, 0.0) for k in range(kv_here)], axis=1
         ).astype(jnp.bfloat16)
         scores = lax.dot_general(
-            spread, key_ref[r], (((1,), (1,)), ((), ())), preferred_element_type=jnp.float32
+            spread, key_ref[s], (((1,), (1,)), ((), ())), preferred_element_type=jnp.float32
         ) * (1.0 / math.sqrt(HD))
         scores = jnp.where(live, scores, MASKED)
         top = jnp.max(scores, axis=1, keepdims=True)
         weights = jnp.where(live, jnp.exp(scores - top), 0.0)
         total = jnp.sum(weights, axis=1, keepdims=True)
         wide = jnp.dot(
-            weights.astype(jnp.bfloat16), value_ref[r], preferred_element_type=jnp.float32
+            weights.astype(jnp.bfloat16), value_ref[s], preferred_element_type=jnp.float32
         )
         numer = jnp.zeros((heads, HD), jnp.float32)
         for k in range(kv_here):
@@ -341,11 +420,9 @@
 
 
 def combine_kernel(
-    arrived_ref, query_ref, key_ref, value_ref, w_ref, lengths_ref, order_ref,
-    head_ref, attended_ref,
+    arrived_ref, query_ref, key_ref, value_ref, w_ref, plan_ref, head_ref, attended_ref
 ):
     n_blocks, heads = arrived_ref.shape[:2]
-    long_0, long_1, short_0, short_1 = request_ids(lengths_ref)
 
     def self_terms(r):
         return (
@@ -362,9 +439,9 @@
     def numerator(block, s):
         return arrived_ref[block, :, s * HD : (s + 1) * HD].astype(jnp.float32)
 
-    jobs = [(long_0, 0, list(range(n_blocks))), (long_1, 1, list(range(n_blocks)))]
-    for r in (short_0, short_1):
-        jobs.append((r, 2, [lax.rem(order_ref[r], n_blocks)]))
+    jobs = [(plan_ref[PLAN_SLOT + s], s, list(range(n_blocks))) for s in range(2)]
+    for i in range(2):
+        jobs.append((plan_ref[PLAN_SHORT + i], 2, [plan_ref[PLAN_OWNER + i]]))
     for r, s, blocks in jobs:
         self_score, value_self = self_terms(r)
         stats = [stat(b, s) for b in blocks]
@@ -401,6 +478,17 @@
     square_cols = jnp.broadcast_to(squares, (resid_rows.shape[0], LANES))
     mine_ref[:, half:] = square_cols
     other_ref[:, half:] = square_cols
+
+
+def down_kernel(own_ref, oth_ref, w_ref, out_ref):
+    core = lax.axis_index("core")
+    own, oth = own_ref[...], oth_ref[...]
+    half = own.shape[1]
+    low = jnp.where(core == 0, own, oth)
+    high = jnp.where(core == 0, oth, own)
+    out_ref[...] = jnp.dot(
+        low, w_ref[:half, :], preferred_element_type=jnp.float32
+    ) + jnp.dot(high, w_ref[half:, :], preferred_element_type=jnp.float32)
 
 
 def per_device(
@@ -428,38 +516,70 @@
     half_qkv = (heads_here + 2 * kv_here) * HD // 2
     half_up = up_weight.shape[1] // 2
 
+    chunk = key_weight.shape[1]
+    n_chunks = 2 * half_qkv // chunk
     mine, other = local_kernel(
         qkv_kernel,
         [f32(n_req, half_qkv + LANES)] * 2,
         [hidden_in, attn_gain.reshape(1, d_here), query_weight, key_weight, value_weight],
         flops=4 * n_req * d_here * half_qkv,
+        scratch=[
+            pltpu.VMEM(hidden_in.shape, hidden_in.dtype),
+            pltpu.VMEM((1, d_here), jnp.float32),
+        ]
+        + [pltpu.VMEM((d_here, chunk), jnp.bfloat16)] * n_chunks
+        + [pltpu.SemaphoreType.DMA((2 + n_chunks,))],
+        in_hbm=range(5),
     )
     pair_sum = mine + swap(other, "core")
-    qkv_sum = jnp.sum(gather_all(pair_sum, "chip", n_chips), axis=0)
-    inv_attn = lax.rsqrt(qkv_sum[:, -1:] / D + NORM_EPS)
-    qkv_half = (qkv_sum[:, :-LANES] * inv_attn).astype(jnp.bfloat16)
+    plain = [out_weight, pad_mask, hidden_in, mlp_gain.reshape(1, d_here)]
+    span_here = pad_mask.shape[1]
+    slots = bf16(3, span_here, key_cache.shape[2])
+    plan, keys, values, out_w, mask, x_rows, gain = local_kernel(
+        prefetch_kernel,
+        [pltpu.SMEM((PLAN_SIZE,), jnp.int32), slots, slots]
+        + [pltpu.VMEM(x.shape, x.dtype) for x in plain],
+        [pair_sum, lengths, block_order, key_cache, value_cache] + plain,
+        flops=0,
+        scratch=[pltpu.SemaphoreType.DMA((6 + len(plain),))],
+        in_hbm=range(3, 5 + len(plain)),
+    )
+    (qkv_half,) = local_kernel(
+        qkv_sum_kernel,
+        [bf16(n_req, half_qkv)],
+        [gather_all(pair_sum, "chip", n_chips), plan],
+        flops=n_chips * n_req * half_qkv,
+    )
     qkv_other = swap(qkv_half, "core")
 
     message, query_heads, key_heads, value_heads = local_kernel(
         attention_kernel,
         [bf16(n_blocks, heads_here, 3 * HD + LANES)] + [f32(n_req, heads_here, HD)] * 3,
-        [qkv_half, qkv_other, key_cache, value_cache, pad_mask, lengths, block_order],
-        flops=12 * heads_here * kv_here * HD * pad_mask.shape[1],
+        [qkv_half, qkv_other, keys, values, mask, plan],
+        flops=12 * heads_here * kv_here * HD * span_here,
     )
     arrived = lax.all_to_all(message, ("chip", "core"), 0, 0)
-    head_part = local_kernel(
+    (head_part,) = local_kernel(
         combine_kernel,
-        f32(n_req, d_here),
-        [arrived, query_heads, key_heads, value_heads, out_weight, lengths, block_order],
+        [f32(n_req, d_here)],
+        [arrived, query_heads, key_heads, value_heads, out_w, plan],
         flops=2 * n_req * out_weight.size,
         scratch=[pltpu.VMEM((n_req, heads_here, HD), jnp.float32)],
     )
     head_peer = swap(head_part, "tp")
+    (up_w,) = local_kernel(
+        copy_kernel,
+        [bf16(*up_weight.shape)],
+        [head_part, up_weight],
+        flops=0,
+        scratch=[pltpu.SemaphoreType.DMA],
+        in_hbm=(1,),
+    )
 
     resid_rows, up_mine, up_other = local_kernel(
         up_kernel,
         [f32(n_req, d_here)] + [f32(n_req, half_up + LANES)] * 2,
-        [hidden_in, head_part, head_peer, mlp_gain.reshape(1, d_here), up_weight],
+        [x_rows, head_part, head_peer, gain, up_w],
         flops=2 * n_req * up_weight.size,
     )
     up_pair = up_mine + swap(up_other, "core")
@@ -476,14 +596,13 @@
     inv_mlp = lax.rsqrt(squares / D + NORM_EPS)
     active_half = squared_relu(up_sum[:, :half_up] * inv_mlp).astype(jnp.bfloat16)
     active_other = swap(active_half, "core")
-    activated = jnp.concatenate(
-        [
-            jnp.where(core == 0, active_half, active_other),
-            jnp.where(core == 0, active_other, active_half),
-        ],
-        axis=1,
-    )
-    down_part = jnp.dot(activated, down_weight, preferred_element_type=jnp.float32)
+    (down_part,) = local_kernel(
+        down_kernel,
+        [f32(n_req, d_here)],
+        [active_half, active_other, down_weight],
+        flops=2 * n_req * down_weight.size,
+        anywhere=(2,),
+    )
     mlp_out = sum_tp(down_part)
     return (resid_rows + mlp_out).astype(jnp.bfloat16)
 

time: 78.8 us -> 64 us (0.81)
  blocking collectives: 43 us -> 27.5 us
  local copies, waits for them, and re-layouts: 13.8 us -> 2.15 us
  starting transfers between devices: 3.64 us -> 10.3 us
  Pallas kernels: 3.98 us -> 10.3 us
  waiting for transfers between devices: 8.67 us -> 12.1 us
  matrix products: 3.38 us -> 0 us
    all_to_all x2 -> x1, blocking collectives: 29.8 us -> 14.3 us  [gather_all(): return lax.all_to_all(copies, axes, 0, 0)]
    unnamed x32 -> x8, local copies, waits for them, and re-layouts: 13.7 us -> 1.31 us
    all_to_all x0 -> x1, starting transfers between devices: none -> 7.15 us  [gather_all(): return lax.all_to_all(copies, axes, 0, 0)]
    pallas_call x4 -> x8, Pallas kernels: 3.98 us -> 10.3 us  [local_kernel(): pl.pallas_call(kernel, out_shape=outs, in_specs=in_specs, out_specs=out_s...]
    all_to_all x0 -> x1, waiting for transfers between devices: none -> 4.98 us  [gather_all(): return lax.all_to_all(copies, axes, 0, 0)]
    dot_general x1 -> x0, matrix products: 3.38 us -> none  [per_device(): jnp.dot(activated, down_weight, preferred_element_type=jnp.float32)]
    ppermute x6, waiting for transfers between devices: 8.67 us -> 7.09 us  [swap(): return lax.ppermute(values_in, axis, [(i, i ^ 1) for i in range(n)])]
  transfers between devices with their start and end apart: 6 -> 7, of which waited for: 6 -> 6; matrix products, arithmetic and copies ran while one was open for 0% -> 0% of each run, Pallas kernels for 0% -> 8%
where the time goes in v3:
time: 64 us; the launch traced here: 63.7 us
  blocking collectives  27.5 us (43%)
  waiting for transfers between devices  12.1 us (19%)
  Pallas kernels  10.3 us (16%)
  starting transfers between devices  10.3 us (16%)
  local copies, waits for them, and re-layouts  2.15 us (3%)
  other arithmetic  1.2 us (2%)
    all_to_all x1, blocking collectives, gather_all(): return lax.all_to_all(copies, axes, 0, 0)  14.3 us
    all_to_all x1, blocking collectives, per_device(): arrived = lax.all_to_all(message, ('chip', 'core'), 0, 0)  13.2 us
    pallas_call x8, Pallas kernels, local_kernel(): pl.pallas_call(kernel, out_shape=outs, in_specs=in_specs, out_specs=out_s...  10.3 us
    all_to_all x1, starting transfers between devices, gather_all(): return lax.all_to_all(copies, axes, 0, 0)  7.15 us
    ppermute x6, waiting for transfers between devices, swap(): return lax.ppermute(values_in, axis, [(i, i ^ 1) for i in range(n)])  7.09 us
    all_to_all x1, waiting for transfers between devices, gather_all(): return lax.all_to_all(copies, axes, 0, 0)  4.98 us
    ppermute x6, starting transfers between devices, swap(): return lax.ppermute(values_in, axis, [(i, i ^ 1) for i in range(n)])  3.17 us
    unnamed x8, local copies, waits for them, and re-layouts  1.31 us
  transfers between devices with their start and end apart: 7, of which 6 were waited for; matrix products, arithmetic and copies ran while one was open for 0% of the time, Pallas kernels for 8%

profile of v3, /device:TPU:0, one launch (start us, length us, event | category | flops | bytes accessed | tf_op | source)
XLA Modules:
  0.0 63.7 jit_solution(15854408654359621008)
XLA Ops:
  0.0 2.0 %shard_map.136 = (f32[4,1664]{1,0:T(4,128)S(1)}, f32[4,1664]{1,0:T(4,128)S(1)}) custom-call(bf16[4,256]{1,0:T(4,128)(2,1)} %refs_2_.1, f32[1,256]{1,0:T(1,128)} %bitcast.5, bf16[256,2048]{1,0:T(8,128)(2,1)} %wq_hbm.1, bf16[256,512]{1,0:T(8,128)(2,1)} %wk_hbm.1, bf16[256,512]{1,0:T(8,128)(2,1)} %wv_hbm.1), custom_call_target="tpu_custom_call" | custom-call | flops 6291456 | bytes 1575936 | tf_op jit(solution)/shard_map/pallas_call | solution.py:231
  2.0 0.5 collective-permute-start
  2.5 0.9 %collective-permute-done = f32[4,1664]{1,0:T(4,128)S(1)} collective-permute-done((f32[4,1664]{1,0:T(4,128)S(1)}, f32[4,1664]{1,0:T(4,128)S(1)}, u32[]{:S(2)}, u32[]{:S(2)}) %collective-permute-start) | collective-permute-done | bytes 26656 | tf_op jit(solution)/shard_map/ppermute | solution.py:28
  3.3 0.7 %broadcast_in_dim.4 = f32[8,4,1664]{2,1,0:T(4,128)} broadcast(f32[4,1664]{1,0:T(4,128)S(1)} %add.22.after_ref), dimensions={1,2} | broadcast | bytes 239616 | tf_op jit(solution)/shard_map/broadcast_in_dim | solution.py:32
  4.1 7.1 %all-to-all-start = ((f32[8,4,1664]{2,1,0:T(4,128)}), f32[8,4,1664]{2,1,0:T(4,128)S(1)}, u32[]{:S(2)}, u32[]{:S(2)}) async-start(f32[8,4,1664]{2,1,0:T(4,128)} %broadcast_in_dim.4), calls=%async_computation | async-start | bytes 425984 | tf_op jit(solution)/shard_map/all_to_all | solution.py:33
  11.2 0.0 copy-start
  11.2 0.7 %copy-done = s32[4]{0:T(128)S(1)} copy-done((s32[4]{0:T(128)S(1)}, s32[4]{0:T(128)}, u32[]{:S(2)}) %copy-start) | copy-done | bytes 40
  11.9 0.0 copy-start.1
  11.9 0.7 %copy-done.1 = s32[4]{0:T(128)S(1)} copy-done((s32[4]{0:T(128)S(1)}, s32[4]{0:T(128)}, u32[]{:S(2)}) %copy-start.1) | copy-done | bytes 40
  12.5 2.2 %shard_map.137 = (s32[16]{0:T(128)S(4)}, bf16[3,128,512]{2,1,0:T(8,128)(2,1)S(1)}, bf16[3,128,512]{2,1,0:T(8,128)(2,1)S(1)}, bf16[2048,256]{1,0:T(8,128)(2,1)S(1...) custom-call(f32[4,1664]{1,0:T(4,128)S(1)} %add.22.after_ref, s32[4]{0:T(128)S(1)} %copy-done, ...), custom_call_target="tpu_custom_call" | custom-call | bytes 2128896 | tf_op jit(solution)/shard_map/pallas_call | solution.py:231
  14.8 5.0 %all-to-all-done.arrived_ref = f32[8,4,1664]{2,1,0:T(4,128)S(1)} async-done(((f32[8,4,1664]{2,1,0:T(4,128)}), f32[8,4,1664]{2,1,0:T(4,128)S(1)}, u32[]{:S(2)}, u32[]{:S(2)}) %all-to-all-start) | async-done | bytes 213024 | tf_op jit(solution)/shard_map/all_to_all | solution.py:33
  19.7 0.1 shard_map.138.own_ref
  19.8 0.0 collective-permute-start.1
  19.8 1.2 %collective-permute-done.1.oth_ref = bf16[4,1536]{1,0:T(4,128)(2,1)S(1)} collective-permute-done((bf16[4,1536]{1,0:T(4,128)(2,1)S(1)}, bf16[4,1536]{1,0:T(4,128)(2,1)S(1)}, u32[]{:S(2)}, u32[]{:S(2)}) %collective-permute-start.1) | collective-permute-done | bytes 12320 | tf_op jit(solution)/shard_map/ppermute | solution.py:28
  21.0 1.0 %shard_map.139 = (bf16[16,16,512]{2,1,0:T(8,128)(2,1)S(1)}, f32[4,16,128]{2,1,0:T(8,128)S(1)}, f32[4,16,128]{2,1,0:T(8,128)S(1)}, f32[4,16,128]{2,1,0:T(8,128)S(1)}) custom-call(bf16[4,1536]{1,0:T(4,128)(2,1)S(1)} %shard_map.138.own_ref, bf16[4,1536]{1,0:T(4,128)(2,1)S(1)} %collective-permute-done.1.oth_ref, ...), custom_call_target="tpu_custom_call" | custom-call | flops 12582912 | bytes 813056 | tf_op jit(solution)/shard_map/pallas_call | solution.py:231
  22.0 13.2 %all_to_all.15.arrived_ref = bf16[16,16,512]{2,1,0:T(8,128)(2,1)S(1)} all-to-all(bf16[16,16,512]{2,1,0:T(8,128)(2,1)S(1)} %get-tuple-element.28), channel_id=1, replica_groups=mesh['chip'=8,'core'=2,'tp'=2] {'chip','core'}, dimensions={0} | all-to-all | bytes 524288 | tf_op jit(solution)/shard_map/all_to_all | solution.py:561
  35.2 0.0 slice-start
  35.2 0.8 %shard_map.140.after_ref.part_ref = f32[4,256]{1,0:T(4,128)S(1)} custom-call(bf16[16,16,512]{2,1,0:T(8,128)(2,1)S(1)} %all_to_all.15.arrived_ref, f32[4,16,128]{2,1,0:T(8,128)S(1)} %get-tuple-element.29.query_ref, f32[4,16,128]{2,1,0:T(8,128)S(1)} %get-tuple-element.30.key_ref, f32[4,16,128]{2,1,0:T(8,128)S(1)} %get-tuple-element.31.value_ref, ...), custom_call_target="tpu_custom_call" | custom-call | flops 4194304 | bytes 1409024 | tf_op jit(solution)/shard_map/pallas_call | solution.py:231
  36.0 0.0 slice-start.1
  36.0 1.5 %collective-permute-start.2 = (f32[4,256]{1,0:T(4,128)S(1)}, f32[4,256]{1,0:T(4,128)S(1)}, u32[]{:S(2)}, u32[]{:S(2)}) collective-permute-start(f32[4,256]{1,0:T(4,128)S(1)} %shard_map.140.after_ref.part_ref), channel_id=1, source_target_pairs={{0,1},{1,0},{2,3},{3,2},{4,5},{5,4},{6,7},{7,6},{8,9},{9,8},{10,11... | collective-permute-start | bytes 12296 | tf_op jit(solution)/shard_map/ppermute | solution.py:28
  37.5 2.6 %shard_map.141.w_ref = bf16[256,10752]{1,0:T(8,128)(2,1)S(1)} custom-call(f32[4,256]{1,0:T(4,128)S(1)} %shard_map.140.after_ref.part_ref, bf16[256,10752]{1,0:T(8,128)(2,1)} %w_hbm.1), custom_call_target="tpu_custom_call" | custom-call | bytes 5509120 | tf_op jit(solution)/shard_map/pallas_call | solution.py:231
  40.1 0.0 collective-permute-done.2.peer_ref
  40.1 0.8 %shard_map.142 = (f32[4,256]{1,0:T(4,128)S(1)}, f32[4,5504]{1,0:T(4,128)S(1)}, f32[4,5504]{1,0:T(4,128)S(1)}) custom-call(bf16[4,256]{1,0:T(4,128)(2,1)S(1)} %get-tuple-element.23.x_ref, f32[4,256]{1,0:T(4,128)S(1)} %shard_map.140.after_ref.part_ref, f32[4,256]{1,0:T(4,128)S(1)} %collective-permute-done.2.peer_ref, f32[1,256]{1,0:T(1,128)S(1)} %get-tuple-element.33.gain_ref, ...), custom_call_target="tpu_custom_call" | custom-call | flops 22020096 | bytes 5516288 | tf_op jit(solution)/shard_map/pallas_call | solution.py:231
  41.0 0.0 collective-permute-start.3
  41.0 1.3 %collective-permute-done.3 = f32[4,5504]{1,0:T(4,128)S(1)} collective-permute-done((f32[4,5504]{1,0:T(4,128)S(1)}, f32[4,5504]{1,0:T(4,128)S(1)}, u32[]{:S(2)}, u32[]{:S(2)}) %collective-permute-start.3) | collective-permute-done | bytes 88096 | tf_op jit(solution)/shard_map/ppermute | solution.py:28
  42.3 0.1 fusion.8
  42.4 0.1 broadcast_in_dim.5
  42.5 14.3 %all_to_all.16 = bf16[8,4,5504]{2,1,0:T(4,128)(2,1)S(1)} all-to-all(bf16[8,4,5504]{2,1,0:T(4,128)(2,1)S(1)} %broadcast_in_dim.5), channel_id=1, replica_groups=mesh['chip'=8,'core'=2,'tp'=2] {'chip'}, dimensions={0} | all-to-all | bytes 704512 | tf_op jit(solution)/shard_map/all_to_all | solution.py:33
  56.9 0.3 convert_reduce_fusion
  57.1 0.1 slice_reduce_fusion
  57.2 0.1 fusion.2.own_ref
  57.4 0.1 collective-permute-start.4
  57.4 1.2 %collective-permute-done.4.oth_ref = bf16[4,5376]{1,0:T(4,128)(2,1)S(1)} collective-permute-done((bf16[4,5376]{1,0:T(4,128)(2,1)S(1)}, bf16[4,5376]{1,0:T(4,128)(2,1)S(1)}, u32[]{:S(2)}, u32[]{:S(2)}) %collective-permute-start.4) | collective-permute-done | bytes 43040 | tf_op jit(solution)/shard_map/ppermute | solution.py:28
  58.6 0.0 slice-done
  58.6 0.0 slice-done.1
  58.6 0.8 %shard_map.143 = f32[4,256]{1,0:T(4,128)S(1)} custom-call(bf16[4,5376]{1,0:T(4,128)(2,1)S(1)} %fusion.2.own_ref, bf16[4,5376]{1,0:T(4,128)(2,1)S(1)} %collective-permute-done.4.oth_ref, bf16[10752,256]{1,0:T(8,128)(2,1)S(1)} %bitcast.3), custom_call_target="tpu_custom_call" | custom-call | flops 22020096 | bytes 5591040 | tf_op jit(solution)/shard_map/pallas_call | solution.py:231
  59.5 1.0 %collective-permute-start.5 = (f32[4,256]{1,0:T(4,128)S(1)}, f32[4,256]{1,0:T(4,128)S(1)}, u32[]{:S(2)}, u32[]{:S(2)}) collective-permute-start(f32[4,256]{1,0:T(4,128)S(1)} %shard_map.143), channel_id=1, source_target_pairs={{0,1},{1,0},{2,3},{3,2},{4,5},{5,4},{6,7},{7,6},{8,9},{9,8},{10,11... | collective-permute-start | bytes 12296 | tf_op jit(solution)/shard_map/ppermute | solution.py:28
  60.5 2.6 %collective-permute-done.5 = f32[4,256]{1,0:T(4,128)S(1)} collective-permute-done((f32[4,256]{1,0:T(4,128)S(1)}, f32[4,256]{1,0:T(4,128)S(1)}, u32[]{:S(2)}, u32[]{:S(2)}) %collective-permute-start.5) | collective-permute-done | bytes 4128 | tf_op jit(solution)/shard_map/ppermute | solution.py:28
  63.1 0.6 add_convert_fusion
  (7 shorter events, 0.1 us)
Async XLA Ops:
  2.0 1.4 %collective-permute-start = (f32[4,1664]{1,0:T(4,128)S(1)}, f32[4,1664]{1,0:T(4,128)S(1)}, u32[]{:S(2)}, u32[]{:S(2)}) collective-permute-start(f32[4,1664]{1,0:T(4,128)S(1)} %get-tuple-element.22), channel_id=1, source_target_pairs={{0,2},{2,0},{1,3},{3,1},{4,6},{6,4},{5,7},{7,5},{8,10},{10,8},{9,1... | collective-permute-start | bytes 79880 | tf_op jit(solution)/shard_map/ppermute | solution.py:28
  4.1 15.7 %all-to-all-start = ((f32[8,4,1664]{2,1,0:T(4,128)}), f32[8,4,1664]{2,1,0:T(4,128)S(1)}, u32[]{:S(2)}, u32[]{:S(2)}) async-start(f32[8,4,1664]{2,1,0:T(4,128)} %broadcast_in_dim.4), calls=%async_computation | async-start | bytes 425984 | tf_op jit(solution)/shard_map/all_to_all | solution.py:33
  11.2 0.7 %copy-start = (s32[4]{0:T(128)S(1)}, s32[4]{0:T(128)}, u32[]{:S(2)}) copy-start(s32[4]{0:T(128)} %lengths_ref.1) | copy-start | bytes 52
  11.9 0.7 %copy-start.1 = (s32[4]{0:T(128)S(1)}, s32[4]{0:T(128)}, u32[]{:S(2)}) copy-start(s32[4]{0:T(128)} %order_ref.1) | copy-start | bytes 52
  19.8 1.2 %collective-permute-start.1 = (bf16[4,1536]{1,0:T(4,128)(2,1)S(1)}, bf16[4,1536]{1,0:T(4,128)(2,1)S(1)}, u32[]{:S(2)}, u32[]{:S(2)}) collective-permute-start(bf16[4,1536]{1,0:T(4,128)(2,1)S(1)} %shard_map.138.own_ref), channel_id=1, source_target_pairs={{0,2},{2,0},{1,3},{3,1},{4,6},{6,4},{5,7},{7,5},{8,10},{10,8},{9,1... | collective-permute-start | bytes 36872 | tf_op jit(solution)/shard_map/ppermute | solution.py:28
  35.2 23.4 %slice-start = ((s8[5505024]{0:T(1024)(128)(4,1)}), s8[4194304]{0:T(1024)(128)(4,1)S(1)}, s32[]{:S(2)}) async-start(s8[5505024]{0:T(1024)(128)(4,1)} %bitcast.2), calls=%async_computation.3 | async-start | bytes 8388608
  36.0 22.6 %slice-start.1 = ((s8[5505024]{0:T(1024)(128)(4,1)}), s8[1310720]{0:T(1024)(128)(4,1)S(1)}, s32[]{:S(2)}) async-start(s8[5505024]{0:T(1024)(128)(4,1)} %bitcast.2), calls=%async_computation.4 | async-start | bytes 2621440
  36.0 4.1 %collective-permute-start.2 = (f32[4,256]{1,0:T(4,128)S(1)}, f32[4,256]{1,0:T(4,128)S(1)}, u32[]{:S(2)}, u32[]{:S(2)}) collective-permute-start(f32[4,256]{1,0:T(4,128)S(1)} %shard_map.140.after_ref.part_ref), channel_id=1, source_target_pairs={{0,1},{1,0},{2,3},{3,2},{4,5},{5,4},{6,7},{7,6},{8,9},{9,8},{10,11... | collective-permute-start | bytes 12296 | tf_op jit(solution)/shard_map/ppermute | solution.py:28
  41.0 1.3 %collective-permute-start.3 = (f32[4,5504]{1,0:T(4,128)S(1)}, f32[4,5504]{1,0:T(4,128)S(1)}, u32[]{:S(2)}, u32[]{:S(2)}) collective-permute-start(f32[4,5504]{1,0:T(4,128)S(1)} %get-tuple-element.36), channel_id=1, source_target_pairs={{0,2},{2,0},{1,3},{3,1},{4,6},{6,4},{5,7},{7,5},{8,10},{10,8},{9,1... | collective-permute-start | bytes 264200 | tf_op jit(solution)/shard_map/ppermute | solution.py:28
  57.4 1.3 %collective-permute-start.4 = (bf16[4,5376]{1,0:T(4,128)(2,1)S(1)}, bf16[4,5376]{1,0:T(4,128)(2,1)S(1)}, u32[]{:S(2)}, u32[]{:S(2)}) collective-permute-start(bf16[4,5376]{1,0:T(4,128)(2,1)S(1)} %fusion.2.own_ref), channel_id=1, source_target_pairs={{0,2},{2,0},{1,3},{3,1},{4,6},{6,4},{5,7},{7,5},{8,10},{10,8},{9,1... | collective-permute-start | bytes 129032 | tf_op jit(solution)/shard_map/ppermute | solution.py:28
  59.5 3.6 %collective-permute-start.5 = (f32[4,256]{1,0:T(4,128)S(1)}, f32[4,256]{1,0:T(4,128)S(1)}, u32[]{:S(2)}, u32[]{:S(2)}) collective-permute-start(f32[4,256]{1,0:T(4,128)S(1)} %shard_map.143), channel_id=1, source_target_pairs={{0,1},{1,0},{2,3},{3,2},{4,5},{5,4},{6,7},{7,6},{8,9},{9,8},{10,11... | collective-permute-start | bytes 12296 | tf_op jit(solution)/shard_map/ppermute | solution.py:28

commit v4 on v3

--- a/solution.py
+++ b/solution.py
@@ -212,27 +212,20 @@
 
 
 IN_VMEM = pl.BlockSpec(memory_space=pltpu.VMEM)
-IN_SMEM = pl.BlockSpec(memory_space=pltpu.SMEM)
-STAT_LANES = 8
 
 
 def local_kernel(kernel, outs, operands, flops, scratch=(), in_hbm=(), anywhere=()):
     in_specs, placed, moved = [], [], 0
     for i, x in enumerate(operands):
-        if x.ndim == 1:
-            in_specs.append(IN_SMEM)
-            placed.append(x)
-            continue
         space = pltpu.HBM if i in in_hbm else pltpu.VMEM
         in_specs.append(pl.BlockSpec(memory_space=space))
         placed.append(x if i in anywhere else pltpu.with_memory_space_constraint(x, space))
         moved += x.size * x.dtype.itemsize
-    out_specs = [IN_SMEM if len(o.shape) == 1 else IN_VMEM for o in outs]
     return pl.pallas_call(
         kernel,
         out_shape=outs,
         in_specs=in_specs,
-        out_specs=out_specs,
+        out_specs=[IN_VMEM] * len(outs),
         scratch_shapes=scratch,
         compiler_params=pltpu.CompilerParams(vmem_limit_bytes=6 * 2**20),
         cost_estimate=pl.CostEstimate(flops=flops, bytes_accessed=moved, transcendentals=0),
@@ -295,7 +288,7 @@
     other_ref[:, at:] = square_cols
 
 
-def qkv_sum_kernel(arrived_ref, plan_ref, out_ref):
+def qkv_sum_kernel(arrived_ref, live_ref, out_ref):
     total = arrived_ref[0]
     for i in range(1, arrived_ref.shape[0]):
         total = total + arrived_ref[i]
@@ -304,162 +297,140 @@
     out_ref[...] = (total[:, :width] * inv_attn).astype(jnp.bfloat16)
 
 
-def request_ids(lengths_ref):
-    is_long = [(lengths_ref[r] > 8).astype(jnp.int32) for r in range(4)]
-    long_0 = jnp.where(is_long[0] == 1, 0, jnp.where(is_long[1] == 1, 1, 2))
-    long_1 = jnp.where(is_long[3] == 1, 3, jnp.where(is_long[2] == 1, 2, 1))
-    short_0 = jnp.where(is_long[0] == 0, 0, jnp.where(is_long[1] == 0, 1, 2))
-    short_1 = jnp.where(is_long[3] == 0, 3, jnp.where(is_long[2] == 0, 2, 1))
-    return long_0, long_1, short_0, short_1
-
-
-PLAN_SLOT = 0
-PLAN_LIVE = 3
-PLAN_SHORT = 6
-PLAN_OWNER = 8
-PLAN_SIZE = 16
-
-
 def prefetch_kernel(
-    after_ref, lengths_ref, order_ref, key_hbm, value_hbm, *refs,
+    after_ref, key_hbm, key_peer, value_hbm, value_peer, mask_hbm, mask_peer, lengths_hbm,
+    order_hbm, *refs,
 ):
-    n_plain = (len(refs) - 4) // 2
+    n_plain = (len(refs) - 7) // 2
     plain_in, refs = refs[:n_plain], refs[n_plain:]
-    plan_ref, key_ref, value_ref = refs[:3]
-    plain_out, sems = refs[3:-1], refs[-1]
+    key_ref, value_ref, live_ref = refs[:3]
+    plain_out, (mask_ref, lengths_ref, order_ref, sems) = refs[3:-4], refs[-4:]
+    core = lax.axis_index("core")
     n_blocks = lax.axis_size("chip") * 2
-    my_block = 2 * lax.axis_index("chip") + lax.axis_index("core")
+    my_block = 2 * lax.axis_index("chip") + core
     span = key_hbm.shape[1]
-    long_0, long_1, short_0, short_1 = request_ids(lengths_ref)
-    owners = [lax.rem(order_ref[r], n_blocks) for r in (short_0, short_1)]
-    short_here = jnp.where(owners[1] == my_block, short_1, short_0)
-    copies = []
-    for s, r in enumerate((long_0, long_1, short_here)):
-        for hbm, vmem in ((key_hbm, key_ref), (value_hbm, value_ref)):
-            copies.append(pltpu.make_async_copy(hbm.at[r], vmem.at[s], sems.at[len(copies)]))
-            copies[-1].start()
-    for hbm, vmem in zip(plain_in, plain_out):
-        copies.append(pltpu.make_async_copy(hbm, vmem, sems.at[len(copies)]))
-        copies[-1].start()
-    for s, r in enumerate((long_0, long_1, short_here)):
-        first_block = lax.rem(order_ref[r], n_blocks)
-        begin = lax.rem(my_block - first_block + n_blocks, n_blocks) * span
-        plan_ref[PLAN_SLOT + s] = r
-        plan_ref[PLAN_LIVE + s] = lengths_ref[r] - begin
-    for i, r in enumerate((short_0, short_1)):
-        plan_ref[PLAN_SHORT + i] = r
-        plan_ref[PLAN_OWNER + i] = owners[i]
-    for i in range(PLAN_OWNER + 2, PLAN_SIZE):
-        plan_ref[i] = 0
+    half = key_ref.shape[2]
+    heads = pl.ds(pl.multiple_of(core * half, LANES), half)
+    pairs = [(lengths_hbm, lengths_ref), (order_hbm, order_ref)]
+    for i, mask in enumerate((mask_hbm, mask_peer)):
+        pairs.append((mask, mask_ref.at[i]))
+    for i, (key, value) in enumerate(((key_hbm, value_hbm), (key_peer, value_peer))):
+        slots = pl.ds(i * span, span)
+        pairs.append((key.at[:, :, heads], key_ref.at[:, slots, :]))
+        pairs.append((value.at[:, :, heads], value_ref.at[:, slots, :]))
+    pairs += list(zip(plain_in, plain_out))
+    copies = [pltpu.make_async_copy(src, dst, sems.at[i]) for i, (src, dst) in enumerate(pairs)]
     for copy in copies:
+        copy.start()
+    for copy in copies[:4]:
         copy.wait()
+    slot = lax.broadcasted_iota(jnp.int32, (1, span), 1)
+    for i, block in enumerate((my_block, my_block + 1 - 2 * core)):
+        for r in range(live_ref.shape[0]):
+            first_block = lax.rem(order_ref[r], n_blocks)
+            begin = lax.rem(block - first_block + n_blocks, n_blocks) * span
+            live = (begin + slot < lengths_ref[r]) & (mask_ref[i, r : r + 1, :] == 1)
+            live_ref[r : r + 1, i * span : (i + 1) * span] = live.astype(jnp.int32)
+    for copy in copies[4:]:
+        copy.wait()
+
+
+PIECE = 16
+TOP_AT = 3 * PIECE
+
+
+def attention_kernel(
+    qkv_ref, key_ref, value_ref, live_ref, message_ref, query_ref, key_new_ref, value_new_ref
+):
+    n_copies, heads, _ = message_ref.shape
+    n_req = live_ref.shape[0]
+    kv_half = key_ref.shape[2] // HD
+    group = heads // kv_half
+    is_first = lax.axis_index("chip") == 0
+    qkv = qkv_ref[...].astype(jnp.float32)
+    for h in range(heads):
+        query_ref[:, h, :] = qkv[:, h * HD : (h + 1) * HD]
+        at = (heads + h // group) * HD
+        key_new_ref[:, h, :] = qkv[:, at : at + HD]
+        at += kv_half * HD
+        value_new_ref[:, h, :] = qkv[:, at : at + HD]
+
+    group_of = lax.broadcasted_iota(jnp.int32, (heads, HD), 0) // group
+    lane = lax.broadcasted_iota(jnp.int32, (heads, LANES), 1)
+    stats = jnp.zeros((heads, LANES), jnp.float32)
+    parts = []
+    for r in range(n_req):
+        live = live_ref[r : r + 1, :] == 1
+        query = query_ref[r]
+        spread = jnp.concatenate(
+            [jnp.where(group_of == k, query, 0.0) for k in range(kv_half)], axis=1
+        ).astype(jnp.bfloat16)
+        scores = lax.dot_general(
+            spread, key_ref[r], (((1,), (1,)), ((), ())), preferred_element_type=jnp.float32
+        ) * (1.0 / math.sqrt(HD))
+        scores = jnp.where(live, scores, MASKED)
+        self_score = jnp.sum(query * key_new_ref[r], axis=1, keepdims=True) * (
+            1.0 / math.sqrt(HD)
+        )
+        top = jnp.max(scores, axis=1, keepdims=True)
+        top = jnp.where(is_first, jnp.maximum(top, self_score), top)
+        weights = jnp.where(live, jnp.exp(scores - top), 0.0)
+        self_weight = jnp.where(is_first, jnp.exp(jnp.minimum(self_score - top, 0.0)), 0.0)
+        total = jnp.sum(weights, axis=1, keepdims=True) + self_weight
+        wide = jnp.dot(
+            weights.astype(jnp.bfloat16), value_ref[r], preferred_element_type=jnp.float32
+        )
+        numer = self_weight * value_new_ref[r]
+        for k in range(kv_half):
+            numer = numer + jnp.where(group_of == k, wide[:, k * HD : (k + 1) * HD], 0.0)
+        parts.append(numer)
+        for p, piece in enumerate(pieces_of(total)):
+            stats = jnp.where(lane == p * PIECE + r, piece, stats)
+        for p, piece in enumerate(pieces_of(top)):
+            stats = jnp.where(lane == TOP_AT + p * PIECE + r, piece, stats)
+    message = jnp.concatenate(parts + [stats], axis=1).astype(jnp.bfloat16)
+    for i in range(n_copies):
+        message_ref[i] = message
+
+
+def combine_kernel(arrived_ref, w_ref, head_ref, attended_ref):
+    n_blocks, heads, width = arrived_ref.shape
+    n_req = head_ref.shape[0]
+    for c in range(2):
+        blocks = range(c, n_blocks, 2)
+        totals, tops = [], []
+        for b in blocks:
+            tile = arrived_ref[b, :, width - LANES :].astype(jnp.float32)
+            tile = (
+                tile
+                + pltpu.roll(tile, LANES - PIECE, 1)
+                + pltpu.roll(tile, LANES - 2 * PIECE, 1)
+            )
+            totals.append(tile)
+            tops.append(pltpu.roll(tile, LANES - TOP_AT, 1))
+        final_top = tops[0]
+        for top in tops[1:]:
+            final_top = jnp.maximum(final_top, top)
+        fades = [jnp.exp(top - final_top) for top in tops]
+        denominator = totals[0] * fades[0]
+        for total, fade in zip(totals[1:], fades[1:]):
+            denominator = denominator + total * fade
+        for r in range(n_req):
+            numer = jnp.zeros((heads, HD), jnp.float32)
+            for b, fade in zip(blocks, fades):
+                part = arrived_ref[b, :, r * HD : (r + 1) * HD].astype(jnp.float32)
+                numer = numer + part * fade[:, r : r + 1]
+            attended_ref[r, c * heads : (c + 1) * heads, :] = numer / denominator[:, r : r + 1]
+    attended = jnp.concatenate([attended_ref[:, h, :] for h in range(2 * heads)], axis=1)
+    head_ref[...] = jnp.dot(
+        attended.astype(jnp.bfloat16), w_ref[...], preferred_element_type=jnp.float32
+    )
 
 
 def copy_kernel(after_ref, w_hbm, w_ref, sem):
     copy = pltpu.make_async_copy(w_hbm, w_ref, sem)
     copy.start()
     copy.wait()
-
-
-def attention_kernel(
-    own_ref, oth_ref, key_ref, value_ref, mask_ref, plan_ref,
-    message_ref, query_out, key_out, value_out,
-):
-    core = lax.axis_index("core")
-    n_blocks = message_ref.shape[0]
-    n_req, span = mask_ref.shape
-    heads = message_ref.shape[1]
-    kv_here = key_ref.shape[2] // HD
-    group = heads // kv_here
-    own = own_ref[...].astype(jnp.float32)
-    oth = oth_ref[...].astype(jnp.float32)
-    low = jnp.where(core == 0, own, oth)
-    high = jnp.where(core == 0, oth, own)
-    for i, part in enumerate((low, high)):
-        for h in range(heads // 2):
-            query_out[:, i * (heads // 2) + h, :] = part[:, h * HD : (h + 1) * HD]
-        for k in range(kv_here // 2):
-            at = (heads // 2 + k) * HD
-            for g in range(group):
-                row = (i * (kv_here // 2) + k) * group + g
-                key_out[:, row, :] = part[:, at : at + HD]
-                at_value = at + (kv_here // 2) * HD
-                value_out[:, row, :] = part[:, at_value : at_value + HD]
-
-    slot = lax.broadcasted_iota(jnp.int32, (1, span), 1)
-    group_of = lax.broadcasted_iota(jnp.int32, (heads, HD), 0) // group
-    lane = lax.broadcasted_iota(jnp.int32, (heads, LANES), 1)
-    stats = jnp.zeros((heads, LANES), jnp.float32)
-    parts = []
-    for s in range(3):
-        r = plan_ref[PLAN_SLOT + s]
-        live = (slot < plan_ref[PLAN_LIVE + s]) & (mask_ref[pl.ds(r, 1), :] == 1)
-        query = query_out[r]
-        spread = jnp.concatenate(
-            [jnp.where(group_of == k, query, 0.0) for k in range(kv_here)], axis=1
-        ).astype(jnp.bfloat16)
-        scores = lax.dot_general(
-            spread, key_ref[s], (((1,), (1,)), ((), ())), preferred_element_type=jnp.float32
-        ) * (1.0 / math.sqrt(HD))
-        scores = jnp.where(live, scores, MASKED)
-        top = jnp.max(scores, axis=1, keepdims=True)
-        weights = jnp.where(live, jnp.exp(scores - top), 0.0)
-        total = jnp.sum(weights, axis=1, keepdims=True)
-        wide = jnp.dot(
-            weights.astype(jnp.bfloat16), value_ref[s], preferred_element_type=jnp.float32
-        )
-        numer = jnp.zeros((heads, HD), jnp.float32)
-        for k in range(kv_here):
-            numer = jnp.where(group_of == k, wide[:, k * HD : (k + 1) * HD], numer)
-        parts.append(numer)
-        for i, piece in enumerate(pieces_of(total) + pieces_of(top)):
-            stats = jnp.where(lane == s * STAT_LANES + i, piece, stats)
-    message = jnp.concatenate(parts + [stats], axis=1).astype(jnp.bfloat16)
-    for b in range(n_blocks):
-        message_ref[b] = message
-
-
-def combine_kernel(
-    arrived_ref, query_ref, key_ref, value_ref, w_ref, plan_ref, head_ref, attended_ref
-):
-    n_blocks, heads = arrived_ref.shape[:2]
-
-    def self_terms(r):
-        return (
-            jnp.sum(query_ref[r] * key_ref[r], axis=1, keepdims=True) * (1.0 / math.sqrt(HD)),
-            value_ref[r],
-        )
-
-    def stat(block, s):
-        lanes = arrived_ref[block, :, 3 * HD :].astype(jnp.float32)
-        at = s * STAT_LANES
-        one = [lanes[:, at + i : at + i + 1] for i in range(6)]
-        return one[0] + one[1] + one[2], one[3] + one[4] + one[5]
-
-    def numerator(block, s):
-        return arrived_ref[block, :, s * HD : (s + 1) * HD].astype(jnp.float32)
-
-    jobs = [(plan_ref[PLAN_SLOT + s], s, list(range(n_blocks))) for s in range(2)]
-    for i in range(2):
-        jobs.append((plan_ref[PLAN_SHORT + i], 2, [plan_ref[PLAN_OWNER + i]]))
-    for r, s, blocks in jobs:
-        self_score, value_self = self_terms(r)
-        stats = [stat(b, s) for b in blocks]
-        final_top = self_score
-        for _, top in stats:
-            final_top = jnp.maximum(final_top, top)
-        self_weight = jnp.exp(self_score - final_top)
-        denominator = self_weight
-        numer = self_weight * value_self
-        for b, (total, top) in zip(blocks, stats):
-            fade = jnp.exp(top - final_top)
-            denominator = denominator + total * fade
-            numer = numer + numerator(b, s) * fade
-        attended_ref[r] = numer / denominator
-    attended = jnp.concatenate([attended_ref[:, h, :] for h in range(heads)], axis=1)
-    head_ref[...] = jnp.dot(
-        attended.astype(jnp.bfloat16), w_ref[...], preferred_element_type=jnp.float32
-    )
 
 
 def up_kernel(x_ref, part_ref, peer_ref, gain_ref, w_ref, hidden_ref, mine_ref, other_ref):
@@ -531,38 +502,48 @@
         + [pltpu.SemaphoreType.DMA((2 + n_chunks,))],
         in_hbm=range(5),
     )
-    pair_sum = mine + swap(other, "core")
-    plain = [out_weight, pad_mask, hidden_in, mlp_gain.reshape(1, d_here)]
+    pair_sum, key_own, value_own, mask_own = lax.optimization_barrier(
+        (mine + swap(other, "core"), key_cache, value_cache, pad_mask)
+    )
+    key_peer, value_peer, mask_peer = (swap(x, "core") for x in (key_own, value_own, mask_own))
+    plain = [out_weight, hidden_in, mlp_gain.reshape(1, d_here)]
     span_here = pad_mask.shape[1]
-    slots = bf16(3, span_here, key_cache.shape[2])
-    plan, keys, values, out_w, mask, x_rows, gain = local_kernel(
+    slots = bf16(n_req, 2 * span_here, key_cache.shape[2] // 2)
+    caches = [key_cache, key_peer, value_cache, value_peer, pad_mask, mask_peer]
+    caches += [lengths, block_order]
+    keys, values, live, out_w, x_rows, gain = local_kernel(
         prefetch_kernel,
-        [pltpu.SMEM((PLAN_SIZE,), jnp.int32), slots, slots]
+        [slots, slots, pltpu.VMEM((n_req, 2 * span_here), jnp.int32)]
         + [pltpu.VMEM(x.shape, x.dtype) for x in plain],
-        [pair_sum, lengths, block_order, key_cache, value_cache] + plain,
+        [pair_sum] + caches + plain,
         flops=0,
-        scratch=[pltpu.SemaphoreType.DMA((6 + len(plain),))],
-        in_hbm=range(3, 5 + len(plain)),
+        scratch=[
+            pltpu.VMEM((2, n_req, span_here), jnp.int32),
+            pltpu.SMEM(lengths.shape, jnp.int32),
+            pltpu.SMEM(block_order.shape, jnp.int32),
+            pltpu.SemaphoreType.DMA((len(caches) + len(plain),)),
+        ],
+        in_hbm=range(1, 1 + len(caches) + len(plain)),
     )
     (qkv_half,) = local_kernel(
         qkv_sum_kernel,
         [bf16(n_req, half_qkv)],
-        [gather_all(pair_sum, "chip", n_chips), plan],
+        [gather_all(pair_sum, "chip", n_chips), live],
         flops=n_chips * n_req * half_qkv,
     )
-    qkv_other = swap(qkv_half, "core")
-
-    message, query_heads, key_heads, value_heads = local_kernel(
+    half_heads = heads_here // 2
+    (message,) = local_kernel(
         attention_kernel,
-        [bf16(n_blocks, heads_here, 3 * HD + LANES)] + [f32(n_req, heads_here, HD)] * 3,
-        [qkv_half, qkv_other, keys, values, mask, plan],
-        flops=12 * heads_here * kv_here * HD * span_here,
+        [bf16(n_blocks, half_heads, n_req * HD + LANES)],
+        [qkv_half, keys, values, live],
+        flops=4 * n_req * half_heads * kv_here * HD * span_here,
+        scratch=[pltpu.VMEM((n_req, half_heads, HD), jnp.float32)] * 3,
     )
     arrived = lax.all_to_all(message, ("chip", "core"), 0, 0)
     (head_part,) = local_kernel(
         combine_kernel,
         [f32(n_req, d_here)],
-        [arrived, query_heads, key_heads, value_heads, out_w, plan],
+        [arrived, out_w],
         flops=2 * n_req * out_weight.size,
         scratch=[pltpu.VMEM((n_req, heads_here, HD), jnp.float32)],
     )

time: 64 us -> 61.8 us (0.966)
  blocking collectives: 27.5 us -> 25.9 us
    all_to_all x1, blocking collectives: 13.2 us -> 11.6 us  [per_device(): arrived = lax.all_to_all(message, ('chip', 'core'), 0, 0)]
    ppermute x6 -> x8, starting transfers between devices: 3.17 us -> 3.76 us  [swap(): return lax.ppermute(values_in, axis, [(i, i ^ 1) for i in range(n)])]
    unnamed x8 -> x10, local copies, waits for them, and re-layouts: 1.31 us -> 0.96 us
    ppermute x6 -> x8, waiting for transfers between devices: 7.09 us -> 7.28 us  [swap(): return lax.ppermute(values_in, axis, [(i, i ^ 1) for i in range(n)])]
  transfers between devices with their start and end apart: 7 -> 9, of which waited for: 6 -> 6; matrix products, arithmetic and copies ran while one was open for 0% -> 1% of each run, Pallas kernels for 8% -> 7%
where the time goes in v4:
time: 61.8 us; the launch traced here: 61.4 us
  blocking collectives  25.9 us (42%)
  waiting for transfers between devices  11.8 us (19%)
  starting transfers between devices  10.9 us (18%)
  Pallas kernels  9.72 us (16%)
  local copies, waits for them, and re-layouts  1.8 us (3%)
  other arithmetic  1.2 us (2%)
    all_to_all x1, blocking collectives, gather_all(): return lax.all_to_all(copies, axes, 0, 0)  14.3 us
    all_to_all x1, blocking collectives, per_device(): arrived = lax.all_to_all(message, ('chip', 'core'), 0, 0)  11.6 us
    pallas_call x8, Pallas kernels, local_kernel(): pl.pallas_call(kernel, out_shape=outs, in_specs=in_specs, out_specs=[IN_V...  9.72 us
    ppermute x8, waiting for transfers between devices, swap(): return lax.ppermute(values_in, axis, [(i, i ^ 1) for i in range(n)])  7.28 us
    all_to_all x1, starting transfers between devices, gather_all(): return lax.all_to_all(copies, axes, 0, 0)  7.15 us
    all_to_all x1, waiting for transfers between devices, gather_all(): return lax.all_to_all(copies, axes, 0, 0)  4.48 us
    ppermute x8, starting transfers between devices, swap(): return lax.ppermute(values_in, axis, [(i, i ^ 1) for i in range(n)])  3.76 us
  transfers between devices with their start and end apart: 9, of which 6 were waited for; matrix products, arithmetic and copies ran while one was open for 1% of the time, Pallas kernels for 7%

profile of v4, /device:TPU:0, one launch (start us, length us, event | category | flops | bytes accessed | tf_op | source)
XLA Modules:
  0.0 61.4 jit_solution(8564337173435064032)
XLA Ops:
  0.0 2.0 %shard_map.136 = (f32[4,1664]{1,0:T(4,128)S(1)}, f32[4,1664]{1,0:T(4,128)S(1)}) custom-call(bf16[4,256]{1,0:T(4,128)(2,1)} %refs_1_.1, f32[1,256]{1,0:T(1,128)} %bitcast.5, bf16[256,2048]{1,0:T(8,128)(2,1)} %wq_hbm.1, bf16[256,512]{1,0:T(8,128)(2,1)} %wk_hbm.1, bf16[256,512]{1,0:T(8,128)(2,1)} %wv_hbm.1), custom_call_target="tpu_custom_call" | custom-call | flops 6291456 | bytes 1575936 | tf_op jit(solution)/shard_map/pallas_call | solution.py:224
  2.0 0.5 collective-permute-start
  2.5 0.9 %collective-permute-done = f32[4,1664]{1,0:T(4,128)S(1)} collective-permute-done((f32[4,1664]{1,0:T(4,128)S(1)}, f32[4,1664]{1,0:T(4,128)S(1)}, u32[]{:S(2)}, u32[]{:S(2)}) %collective-permute-start) | collective-permute-done | bytes 26656 | tf_op jit(solution)/shard_map/ppermute | solution.py:28
  3.3 0.4 collective-permute-start.1
  3.8 0.2 collective-permute-start.2
  3.9 0.7 %broadcast_in_dim.4 = f32[8,4,1664]{2,1,0:T(4,128)} broadcast(f32[4,1664]{1,0:T(4,128)S(1)} %add.22.after_ref), dimensions={1,2} | broadcast | bytes 239616 | tf_op jit(solution)/shard_map/broadcast_in_dim | solution.py:32
  4.6 7.1 %all-to-all-start = ((f32[8,4,1664]{2,1,0:T(4,128)}), f32[8,4,1664]{2,1,0:T(4,128)S(1)}, u32[]{:S(2)}, u32[]{:S(2)}) async-start(f32[8,4,1664]{2,1,0:T(4,128)} %broadcast_in_dim.4), calls=%async_computation | async-start | bytes 425984 | tf_op jit(solution)/shard_map/all_to_all | solution.py:33
  11.8 0.0 collective-permute-start.3
  11.8 1.4 %collective-permute-done.3.mask_peer = s32[4,128]{1,0:T(4,128)S(1)} collective-permute-done((s32[4,128]{1,0:T(4,128)}, s32[4,128]{1,0:T(4,128)S(1)}, u32[]{:S(2)}, u32[]{:S(2)}) %collective-permute-start.3) | collective-permute-done | bytes 2080 | tf_op jit(solution)/shard_map/ppermute | solution.py:28
  13.2 0.0 copy-start.2
  13.2 0.0 collective-permute-done.1.key_peer
  13.2 0.0 copy-start
  13.2 0.0 collective-permute-done.2.value_peer
  13.2 0.0 copy-start.1
  13.2 0.6 copy-done.2
  13.7 0.2 copy-done
  14.0 0.2 copy-done.1
  14.1 1.7 %shard_map.137 = (bf16[4,256,256]{2,1,0:T(8,128)(2,1)S(1)}, bf16[4,256,256]{2,1,0:T(8,128)(2,1)S(1)}, s32[4,256]{1,0:T(4,128)S(1)}, bf16[2048,256]{1,0:T(8,128)(...) custom-call(f32[4,1664]{1,0:T(4,128)S(1)} %add.22.after_ref, bf16[4,128,512]{2,1,0:T(8,128)(2,1)} %key_hbm.1, ...), custom_call_target="tpu_custom_call" | custom-call | bytes 3179552 | tf_op jit(solution)/shard_map/pallas_call | solution.py:224
  15.8 4.5 %all-to-all-done.arrived_ref = f32[8,4,1664]{2,1,0:T(4,128)S(1)} async-done(((f32[8,4,1664]{2,1,0:T(4,128)}), f32[8,4,1664]{2,1,0:T(4,128)S(1)}, u32[]{:S(2)}, u32[]{:S(2)}) %all-to-all-start) | async-done | bytes 213024 | tf_op jit(solution)/shard_map/all_to_all | solution.py:33
  20.3 0.1 shard_map.138.qkv_ref
  20.4 1.2 %shard_map.139 = bf16[16,8,640]{2,1,0:T(8,128)(2,1)S(1)} custom-call(bf16[4,1536]{1,0:T(4,128)(2,1)S(1)} %shard_map.138.qkv_ref, bf16[4,256,256]{2,1,0:T(8,128)(2,1)S(1)} %get-tuple-element.28.key_ref, bf16[4,256,256]{2,1,0:T(8,128)(2,1)S(1)} %get-tuple-element.29.value_ref, s32[4,256]{1,0:T(4,128)S(1)} %get-tuple-element.27.live_ref), custom_call_target="tpu_custom_call" | custom-call | flops 8388608 | bytes 1064960 | tf_op jit(solution)/shard_map/pallas_call | solution.py:224
  21.6 11.6 %all_to_all.15.arrived_ref = bf16[16,8,640]{2,1,0:T(8,128)(2,1)S(1)} all-to-all(bf16[16,8,640]{2,1,0:T(8,128)(2,1)S(1)} %shard_map.139), channel_id=1, replica_groups=mesh['chip'=8,'core'=2,'tp'=2] {'chip','core'}, dimensions={0} | all-to-all | bytes 327680 | tf_op jit(solution)/shard_map/all_to_all | solution.py:542
  33.2 0.0 slice-start
  33.2 0.6 shard_map.140.after_ref.part_ref
  33.8 0.0 slice-start.1
  33.8 1.5 %collective-permute-start.4 = (f32[4,256]{1,0:T(4,128)S(1)}, f32[4,256]{1,0:T(4,128)S(1)}, u32[]{:S(2)}, u32[]{:S(2)}) collective-permute-start(f32[4,256]{1,0:T(4,128)S(1)} %shard_map.140.after_ref.part_ref), channel_id=1, source_target_pairs={{0,1},{1,0},{2,3},{3,2},{4,5},{5,4},{6,7},{7,6},{8,9},{9,8},{10,11... | collective-permute-start | bytes 12296 | tf_op jit(solution)/shard_map/ppermute | solution.py:28
  35.3 2.6 %shard_map.141.w_ref = bf16[256,10752]{1,0:T(8,128)(2,1)S(1)} custom-call(f32[4,256]{1,0:T(4,128)S(1)} %shard_map.140.after_ref.part_ref, bf16[256,10752]{1,0:T(8,128)(2,1)} %w_hbm.1), custom_call_target="tpu_custom_call" | custom-call | bytes 5509120 | tf_op jit(solution)/shard_map/pallas_call | solution.py:224
  37.9 0.0 collective-permute-done.4.peer_ref
  37.9 0.8 %shard_map.142 = (f32[4,256]{1,0:T(4,128)S(1)}, f32[4,5504]{1,0:T(4,128)S(1)}, f32[4,5504]{1,0:T(4,128)S(1)}) custom-call(bf16[4,256]{1,0:T(4,128)(2,1)S(1)} %get-tuple-element.26.x_ref, f32[4,256]{1,0:T(4,128)S(1)} %shard_map.140.after_ref.part_ref, f32[4,256]{1,0:T(4,128)S(1)} %collective-permute-done.4.peer_ref, f32[1,256]{1,0:T(1,128)S(1)} %get-tuple-element.31.gain_ref, ...), custom_call_target="tpu_custom_call" | custom-call | flops 22020096 | bytes 5516288 | tf_op jit(solution)/shard_map/pallas_call | solution.py:224
  38.8 0.0 collective-permute-start.5
  38.8 1.3 %collective-permute-done.5 = f32[4,5504]{1,0:T(4,128)S(1)} collective-permute-done((f32[4,5504]{1,0:T(4,128)S(1)}, f32[4,5504]{1,0:T(4,128)S(1)}, u32[]{:S(2)}, u32[]{:S(2)}) %collective-permute-start.5) | collective-permute-done | bytes 88096 | tf_op jit(solution)/shard_map/ppermute | solution.py:28
  40.1 0.1 fusion.8
  40.2 0.1 broadcast_in_dim.5
  40.3 14.3 %all_to_all.16 = bf16[8,4,5504]{2,1,0:T(4,128)(2,1)S(1)} all-to-all(bf16[8,4,5504]{2,1,0:T(4,128)(2,1)S(1)} %broadcast_in_dim.5), channel_id=1, replica_groups=mesh['chip'=8,'core'=2,'tp'=2] {'chip'}, dimensions={0} | all-to-all | bytes 704512 | tf_op jit(solution)/shard_map/all_to_all | solution.py:33
  54.6 0.3 convert_reduce_fusion
  54.9 0.1 slice_reduce_fusion
  55.0 0.1 fusion.2.own_ref
  55.1 0.1 collective-permute-start.6
  55.2 1.2 %collective-permute-done.6.oth_ref = bf16[4,5376]{1,0:T(4,128)(2,1)S(1)} collective-permute-done((bf16[4,5376]{1,0:T(4,128)(2,1)S(1)}, bf16[4,5376]{1,0:T(4,128)(2,1)S(1)}, u32[]{:S(2)}, u32[]{:S(2)}) %collective-permute-start.6) | collective-permute-done | bytes 43040 | tf_op jit(solution)/shard_map/ppermute | solution.py:28
  56.4 0.0 slice-done
  56.4 0.0 slice-done.1
  56.4 0.8 %shard_map.143 = f32[4,256]{1,0:T(4,128)S(1)} custom-call(bf16[4,5376]{1,0:T(4,128)(2,1)S(1)} %fusion.2.own_ref, bf16[4,5376]{1,0:T(4,128)(2,1)S(1)} %collective-permute-done.6.oth_ref, bf16[10752,256]{1,0:T(8,128)(2,1)S(1)} %bitcast.3), custom_call_target="tpu_custom_call" | custom-call | flops 22020096 | bytes 5591040 | tf_op jit(solution)/shard_map/pallas_call | solution.py:224
  57.2 1.0 %collective-permute-start.7 = (f32[4,256]{1,0:T(4,128)S(1)}, f32[4,256]{1,0:T(4,128)S(1)}, u32[]{:S(2)}, u32[]{:S(2)}) collective-permute-start(f32[4,256]{1,0:T(4,128)S(1)} %shard_map.143), channel_id=1, source_target_pairs={{0,1},{1,0},{2,3},{3,2},{4,5},{5,4},{6,7},{7,6},{8,9},{9,8},{10,11... | collective-permute-start | bytes 12296 | tf_op jit(solution)/shard_map/ppermute | solution.py:28
  58.3 2.6 %collective-permute-done.7 = f32[4,256]{1,0:T(4,128)S(1)} collective-permute-done((f32[4,256]{1,0:T(4,128)S(1)}, f32[4,256]{1,0:T(4,128)S(1)}, u32[]{:S(2)}, u32[]{:S(2)}) %collective-permute-start.7) | collective-permute-done | bytes 4128 | tf_op jit(solution)/shard_map/ppermute | solution.py:28
  60.9 0.6 add_convert_fusion
  (7 shorter events, 0.1 us)
Async XLA Ops:
  2.0 1.4 %collective-permute-start = (f32[4,1664]{1,0:T(4,128)S(1)}, f32[4,1664]{1,0:T(4,128)S(1)}, u32[]{:S(2)}, u32[]{:S(2)}) collective-permute-start(f32[4,1664]{1,0:T(4,128)S(1)} %get-tuple-element.21), channel_id=1, source_target_pairs={{0,2},{2,0},{1,3},{3,1},{4,6},{6,4},{5,7},{7,5},{8,10},{10,8},{9,1... | collective-permute-start | bytes 79880 | tf_op jit(solution)/shard_map/ppermute | solution.py:28
  3.3 9.8 %collective-permute-start.1 = (bf16[4,128,512]{2,1,0:T(8,128)(2,1)}, bf16[4,128,512]{2,1,0:T(8,128)(2,1)S(1)}, u32[]{:S(2)}, u32[]{:S(2)}) collective-permute-start(bf16[4,128,512]{2,1,0:T(8,128)(2,1)} %key_hbm.1), channel_id=1, source_target_pairs={{0,2},{2,0},{1,3},{3,1},{4,6},{6,4},{5,7},{7,5},{8,10},{10,8},{9,1... | collective-permute-start | bytes 1572872 | tf_op jit(solution)/shard_map/ppermute | solution.py:28
  3.8 9.4 %collective-permute-start.2 = (bf16[4,128,512]{2,1,0:T(8,128)(2,1)}, bf16[4,128,512]{2,1,0:T(8,128)(2,1)S(1)}, u32[]{:S(2)}, u32[]{:S(2)}) collective-permute-start(bf16[4,128,512]{2,1,0:T(8,128)(2,1)} %value_hbm.1), channel_id=1, source_target_pairs={{0,2},{2,0},{1,3},{3,1},{4,6},{6,4},{5,7},{7,5},{8,10},{10,8},{9,1... | collective-permute-start | bytes 1572872 | tf_op jit(solution)/shard_map/ppermute | solution.py:28
  4.6 15.7 %all-to-all-start = ((f32[8,4,1664]{2,1,0:T(4,128)}), f32[8,4,1664]{2,1,0:T(4,128)S(1)}, u32[]{:S(2)}, u32[]{:S(2)}) async-start(f32[8,4,1664]{2,1,0:T(4,128)} %broadcast_in_dim.4), calls=%async_computation | async-start | bytes 425984 | tf_op jit(solution)/shard_map/all_to_all | solution.py:33
  11.8 1.4 %collective-permute-start.3 = (s32[4,128]{1,0:T(4,128)}, s32[4,128]{1,0:T(4,128)S(1)}, u32[]{:S(2)}, u32[]{:S(2)}) collective-permute-start(s32[4,128]{1,0:T(4,128)} %mask_hbm.1), channel_id=1, source_target_pairs={{0,2},{2,0},{1,3},{3,1},{4,6},{6,4},{5,7},{7,5},{8,10},{10,8},{9,1... | collective-permute-start | bytes 6152 | tf_op jit(solution)/shard_map/ppermute | solution.py:28
  13.2 0.6 copy-start.2
  13.2 0.8 %copy-start = (bf16[4,128,512]{2,1,0:T(8,128)(2,1)}, bf16[4,128,512]{2,1,0:T(8,128)(2,1)S(1)}, u32[]{:S(2)}) copy-start(bf16[4,128,512]{2,1,0:T(8,128)(2,1)S(1)} %collective-permute-done.1.key_peer) | copy-start | bytes 1572868
  13.2 1.0 %copy-start.1 = (bf16[4,128,512]{2,1,0:T(8,128)(2,1)}, bf16[4,128,512]{2,1,0:T(8,128)(2,1)S(1)}, u32[]{:S(2)}) copy-start(bf16[4,128,512]{2,1,0:T(8,128)(2,1)S(1)} %collective-permute-done.2.value_peer) | copy-start | bytes 1572868
  33.2 23.2 %slice-start = ((s8[5505024]{0:T(1024)(128)(4,1)}), s8[4194304]{0:T(1024)(128)(4,1)S(1)}, s32[]{:S(2)}) async-start(s8[5505024]{0:T(1024)(128)(4,1)} %bitcast.2), calls=%async_computation.3 | async-start | bytes 8388608
  33.8 22.6 %slice-start.1 = ((s8[5505024]{0:T(1024)(128)(4,1)}), s8[1310720]{0:T(1024)(128)(4,1)S(1)}, s32[]{:S(2)}) async-start(s8[5505024]{0:T(1024)(128)(4,1)} %bitcast.2), calls=%async_computation.4 | async-start | bytes 2621440
  33.8 4.1 %collective-permute-start.4 = (f32[4,256]{1,0:T(4,128)S(1)}, f32[4,256]{1,0:T(4,128)S(1)}, u32[]{:S(2)}, u32[]{:S(2)}) collective-permute-start(f32[4,256]{1,0:T(4,128)S(1)} %shard_map.140.after_ref.part_ref), channel_id=1, source_target_pairs={{0,1},{1,0},{2,3},{3,2},{4,5},{5,4},{6,7},{7,6},{8,9},{9,8},{10,11... | collective-permute-start | bytes 12296 | tf_op jit(solution)/shard_map/ppermute | solution.py:28
  38.8 1.3 %collective-permute-start.5 = (f32[4,5504]{1,0:T(4,128)S(1)}, f32[4,5504]{1,0:T(4,128)S(1)}, u32[]{:S(2)}, u32[]{:S(2)}) collective-permute-start(f32[4,5504]{1,0:T(4,128)S(1)} %get-tuple-element.34), channel_id=1, source_target_pairs={{0,2},{2,0},{1,3},{3,1},{4,6},{6,4},{5,7},{7,5},{8,10},{10,8},{9,1... | collective-permute-start | bytes 264200 | tf_op jit(solution)/shard_map/ppermute | solution.py:28
  55.1 1.3 %collective-permute-start.6 = (bf16[4,5376]{1,0:T(4,128)(2,1)S(1)}, bf16[4,5376]{1,0:T(4,128)(2,1)S(1)}, u32[]{:S(2)}, u32[]{:S(2)}) collective-permute-start(bf16[4,5376]{1,0:T(4,128)(2,1)S(1)} %fusion.2.own_ref), channel_id=1, source_target_pairs={{0,2},{2,0},{1,3},{3,1},{4,6},{6,4},{5,7},{7,5},{8,10},{10,8},{9,1... | collective-permute-start | bytes 129032 | tf_op jit(solution)/shard_map/ppermute | solution.py:28
  57.2 3.6 %collective-permute-start.7 = (f32[4,256]{1,0:T(4,128)S(1)}, f32[4,256]{1,0:T(4,128)S(1)}, u32[]{:S(2)}, u32[]{:S(2)}) collective-permute-start(f32[4,256]{1,0:T(4,128)S(1)} %shard_map.143), channel_id=1, source_target_pairs={{0,1},{1,0},{2,3},{3,2},{4,5},{5,4},{6,7},{7,6},{8,9},{9,8},{10,11... | collective-permute-start | bytes 12296 | tf_op jit(solution)/shard_map/ppermute | solution.py:28

commit v5 on v4

--- a/solution.py
+++ b/solution.py
@@ -247,34 +247,40 @@
 
 
 def qkv_kernel(
-    x_hbm, gain_hbm, wq_hbm, wk_hbm, wv_hbm, mine_ref, other_ref, x_ref, gain_ref, *scratch
+    x_hbm, gain_hbm, mlp_gain_hbm, mask_hbm, lengths_hbm, order_hbm, wq_hbm, wk_hbm, wv_hbm,
+    mine_ref, other_ref, x_ref, mlp_gain_ref, live_ref,
+    gain_ref, mask_ref, lengths_ref, order_ref, *scratch,
 ):
     core = lax.axis_index("core")
+    n_blocks = lax.axis_size("chip") * 2
+    my_block = 2 * lax.axis_index("chip") + core
     w_refs, sems = scratch[:-1], scratch[-1]
-    chunk = w_refs[0].shape[1]
-    copies = [
-        pltpu.make_async_copy(x_hbm, x_ref, sems.at[0]),
-        pltpu.make_async_copy(gain_hbm, gain_ref, sems.at[1]),
+    small = [
+        (x_hbm, x_ref), (gain_hbm, gain_ref), (mask_hbm, mask_ref), (lengths_hbm, lengths_ref),
+        (order_hbm, order_ref), (mlp_gain_hbm, mlp_gain_ref),
     ]
-    pieces = [(w, at) for w in (wq_hbm, wk_hbm, wv_hbm) for at in range(0, w.shape[1], chunk)]
-    for (w_hbm, at), w_ref in zip(pieces, w_refs):
-        copies.append(
-            pltpu.make_async_copy(
-                w_hbm.at[:, pl.ds(at, chunk)], w_ref, sems.at[len(copies)]
-            )
-        )
+    copies = [pltpu.make_async_copy(src, dst, sems.at[i]) for i, (src, dst) in enumerate(small)]
+    for w_hbm, w_ref in zip((wk_hbm, wv_hbm, wq_hbm), w_refs):
+        copies.append(pltpu.make_async_copy(w_hbm, w_ref, sems.at[len(copies)]))
     for copy in copies:
         copy.start()
-    copies[0].wait()
-    copies[1].wait()
+    for copy in copies[: len(small)]:
+        copy.wait()
+    n_req, span = live_ref.shape
+    slot = lax.broadcasted_iota(jnp.int32, (1, span), 1)
+    for r in range(n_req):
+        first_block = lax.rem(order_ref[r], n_blocks)
+        begin = lax.rem(my_block - first_block + n_blocks, n_blocks) * span
+        live = (begin + slot < lengths_ref[r]) & (mask_ref[r : r + 1, :] == 1)
+        live_ref[r : r + 1, :] = live.astype(jnp.float32)
     x_rows = x_ref[...].astype(jnp.float32)
     scaled_in = (x_rows * gain_ref[...]).astype(jnp.bfloat16)
     squares = jnp.sum(x_rows * x_rows, axis=1, keepdims=True)
     proj = []
-    for w_ref, copy in zip(w_refs, copies[2:]):
+    for w_ref, copy in zip(w_refs, copies[len(small) :]):
         copy.wait()
         proj.append(jnp.dot(scaled_in, w_ref[...], preferred_element_type=jnp.float32))
-    proj = jnp.concatenate(proj, axis=1)
+    proj = jnp.concatenate([proj[2], proj[0], proj[1]], axis=1)
     at, start = 0, 0
     for w_hbm in (wq_hbm, wk_hbm, wv_hbm):
         half = w_hbm.shape[1] // 2
@@ -285,10 +291,11 @@
         start += 2 * half
     square_cols = jnp.broadcast_to(squares, (x_rows.shape[0], LANES))
     mine_ref[:, at:] = square_cols
-    other_ref[:, at:] = square_cols
-
-
-def qkv_sum_kernel(arrived_ref, live_ref, out_ref):
+    other_ref[:, at : at + LANES] = square_cols
+    other_ref[:, at + LANES :] = live_ref[...]
+
+
+def qkv_sum_kernel(arrived_ref, out_ref):
     total = arrived_ref[0]
     for i in range(1, arrived_ref.shape[0]):
         total = total + arrived_ref[i]
@@ -297,54 +304,19 @@
     out_ref[...] = (total[:, :width] * inv_attn).astype(jnp.bfloat16)
 
 
-def prefetch_kernel(
-    after_ref, key_hbm, key_peer, value_hbm, value_peer, mask_hbm, mask_peer, lengths_hbm,
-    order_hbm, *refs,
-):
-    n_plain = (len(refs) - 7) // 2
-    plain_in, refs = refs[:n_plain], refs[n_plain:]
-    key_ref, value_ref, live_ref = refs[:3]
-    plain_out, (mask_ref, lengths_ref, order_ref, sems) = refs[3:-4], refs[-4:]
-    core = lax.axis_index("core")
-    n_blocks = lax.axis_size("chip") * 2
-    my_block = 2 * lax.axis_index("chip") + core
-    span = key_hbm.shape[1]
-    half = key_ref.shape[2]
-    heads = pl.ds(pl.multiple_of(core * half, LANES), half)
-    pairs = [(lengths_hbm, lengths_ref), (order_hbm, order_ref)]
-    for i, mask in enumerate((mask_hbm, mask_peer)):
-        pairs.append((mask, mask_ref.at[i]))
-    for i, (key, value) in enumerate(((key_hbm, value_hbm), (key_peer, value_peer))):
-        slots = pl.ds(i * span, span)
-        pairs.append((key.at[:, :, heads], key_ref.at[:, slots, :]))
-        pairs.append((value.at[:, :, heads], value_ref.at[:, slots, :]))
-    pairs += list(zip(plain_in, plain_out))
-    copies = [pltpu.make_async_copy(src, dst, sems.at[i]) for i, (src, dst) in enumerate(pairs)]
-    for copy in copies:
-        copy.start()
-    for copy in copies[:4]:
-        copy.wait()
-    slot = lax.broadcasted_iota(jnp.int32, (1, span), 1)
-    for i, block in enumerate((my_block, my_block + 1 - 2 * core)):
-        for r in range(live_ref.shape[0]):
-            first_block = lax.rem(order_ref[r], n_blocks)
-            begin = lax.rem(block - first_block + n_blocks, n_blocks) * span
-            live = (begin + slot < lengths_ref[r]) & (mask_ref[i, r : r + 1, :] == 1)
-            live_ref[r : r + 1, i * span : (i + 1) * span] = live.astype(jnp.int32)
-    for copy in copies[4:]:
-        copy.wait()
-
-
 PIECE = 16
 TOP_AT = 3 * PIECE
 
 
 def attention_kernel(
-    qkv_ref, key_ref, value_ref, live_ref, message_ref, query_ref, key_new_ref, value_new_ref
+    qkv_ref, key_own, key_peer, value_own, value_peer, live_own, live_peer,
+    message_ref, query_ref, key_new_ref, value_new_ref,
 ):
     n_copies, heads, _ = message_ref.shape
-    n_req = live_ref.shape[0]
-    kv_half = key_ref.shape[2] // HD
+    n_req, span = live_own.shape
+    half = key_own.shape[2] // 2
+    mine = pl.ds(pl.multiple_of(lax.axis_index("core") * half, LANES), half)
+    kv_half = half // HD
     group = heads // kv_half
     is_first = lax.axis_index("chip") == 0
     qkv = qkv_ref[...].astype(jnp.float32)
@@ -355,39 +327,54 @@
         at += kv_half * HD
         value_new_ref[:, h, :] = qkv[:, at : at + HD]
 
-    group_of = lax.broadcasted_iota(jnp.int32, (heads, HD), 0) // group
+    rows = n_req * heads
+    query = query_ref[...].reshape(rows, HD)
+    group_of = lax.broadcasted_iota(jnp.int32, (rows, HD), 0) % heads // group
+    spread = jnp.concatenate(
+        [jnp.where(group_of == k, query, 0.0) for k in range(kv_half)], axis=1
+    ).astype(jnp.bfloat16)
+    scores, live = [], []
+    for r in range(n_req):
+        blocks = []
+        for keys in (key_own, key_peer):
+            blocks.append(
+                lax.dot_general(
+                    spread[r * heads : (r + 1) * heads, :], keys[r, :, mine],
+                    (((1,), (1,)), ((), ())), preferred_element_type=jnp.float32,
+                )
+            )
+        scores.append(jnp.concatenate(blocks, axis=1))
+        live_row = jnp.concatenate([live_own[r : r + 1, :], live_peer[r : r + 1, :]], axis=1)
+        live.append(jnp.broadcast_to(live_row, (heads, 2 * span)))
+    live = jnp.concatenate(live, axis=0) > 0.0
+    scale = 1.0 / math.sqrt(HD)
+    scores = jnp.where(live, jnp.concatenate(scores, axis=0) * scale, MASKED)
+    key_new = key_new_ref[...].reshape(rows, HD)
+    self_score = jnp.sum(query * key_new, axis=1, keepdims=True) * scale
+    self_score = jnp.where(is_first, self_score, MASKED)
+    top = jnp.maximum(jnp.max(scores, axis=1, keepdims=True), self_score)
+    weights = jnp.where(live, jnp.exp(scores - top), 0.0)
+    self_weight = jnp.where(is_first, jnp.exp(self_score - top), 0.0)
+    total = jnp.sum(weights, axis=1, keepdims=True) + self_weight
+    rounded = weights.astype(jnp.bfloat16)
+    self_part = self_weight * value_new_ref[...].reshape(rows, HD)
+    pieces = pieces_of(total) + pieces_of(top)
     lane = lax.broadcasted_iota(jnp.int32, (heads, LANES), 1)
     stats = jnp.zeros((heads, LANES), jnp.float32)
     parts = []
     for r in range(n_req):
-        live = live_ref[r : r + 1, :] == 1
-        query = query_ref[r]
-        spread = jnp.concatenate(
-            [jnp.where(group_of == k, query, 0.0) for k in range(kv_half)], axis=1
-        ).astype(jnp.bfloat16)
-        scores = lax.dot_general(
-            spread, key_ref[r], (((1,), (1,)), ((), ())), preferred_element_type=jnp.float32
-        ) * (1.0 / math.sqrt(HD))
-        scores = jnp.where(live, scores, MASKED)
-        self_score = jnp.sum(query * key_new_ref[r], axis=1, keepdims=True) * (
-            1.0 / math.sqrt(HD)
+        at = slice(r * heads, (r + 1) * heads)
+        wide = jnp.dot(
+            rounded[at, :span], value_own[r, :, mine], preferred_element_type=jnp.float32
+        ) + jnp.dot(
+            rounded[at, span:], value_peer[r, :, mine], preferred_element_type=jnp.float32
         )
-        top = jnp.max(scores, axis=1, keepdims=True)
-        top = jnp.where(is_first, jnp.maximum(top, self_score), top)
-        weights = jnp.where(live, jnp.exp(scores - top), 0.0)
-        self_weight = jnp.where(is_first, jnp.exp(jnp.minimum(self_score - top, 0.0)), 0.0)
-        total = jnp.sum(weights, axis=1, keepdims=True) + self_weight
-        wide = jnp.dot(
-            weights.astype(jnp.bfloat16), value_ref[r], preferred_element_type=jnp.float32
-        )
-        numer = self_weight * value_new_ref[r]
+        numer = self_part[at, :]
         for k in range(kv_half):
-            numer = numer + jnp.where(group_of == k, wide[:, k * HD : (k + 1) * HD], 0.0)
+            numer = numer + jnp.where(group_of[at, :] == k, wide[:, k * HD : (k + 1) * HD], 0.0)
         parts.append(numer)
-        for p, piece in enumerate(pieces_of(total)):
-            stats = jnp.where(lane == p * PIECE + r, piece, stats)
-        for p, piece in enumerate(pieces_of(top)):
-            stats = jnp.where(lane == TOP_AT + p * PIECE + r, piece, stats)
+        for p, piece in enumerate(pieces):
+            stats = jnp.where(lane == p * PIECE + r, piece[at, :], stats)
     message = jnp.concatenate(parts + [stats], axis=1).astype(jnp.bfloat16)
     for i in range(n_copies):
         message_ref[i] = message
@@ -427,12 +414,6 @@
     )
 
 
-def copy_kernel(after_ref, w_hbm, w_ref, sem):
-    copy = pltpu.make_async_copy(w_hbm, w_ref, sem)
-    copy.start()
-    copy.wait()
-
-
 def up_kernel(x_ref, part_ref, peer_ref, gain_ref, w_ref, hidden_ref, mine_ref, other_ref):
     core = lax.axis_index("core")
     attn_out = part_ref[...] + peer_ref[...]
@@ -449,6 +430,29 @@
     square_cols = jnp.broadcast_to(squares, (resid_rows.shape[0], LANES))
     mine_ref[:, half:] = square_cols
     other_ref[:, half:] = square_cols
+
+
+def up_message_kernel(mine_ref, arrived_ref, message_ref):
+    half = mine_ref.shape[1] - LANES
+    message = (mine_ref[:, :half] + arrived_ref[:, :half]).astype(jnp.bfloat16)
+    squares = mine_ref[:, half:] + arrived_ref[:, half:]
+    lane = lax.broadcasted_iota(jnp.int32, squares.shape, 1)
+    tile = jnp.zeros_like(squares)
+    for p, piece in enumerate(pieces_of(squares)):
+        tile = jnp.where(lane == p, piece, tile)
+    for i in range(message_ref.shape[0]):
+        message_ref[i, :, :half] = message
+        message_ref[i, :, half:] = tile.astype(jnp.bfloat16)
+
+
+def activate_kernel(arrived_ref, out_ref):
+    half = out_ref.shape[1]
+    total = arrived_ref[0].astype(jnp.float32)
+    for i in range(1, arrived_ref.shape[0]):
+        total = total + arrived_ref[i].astype(jnp.float32)
+    squares = jnp.sum(total[:, half:], axis=1, keepdims=True)
+    inv_mlp = lax.rsqrt(squares / D + NORM_EPS)
+    out_ref[...] = squared_relu(total[:, :half] * inv_mlp).astype(jnp.bfloat16)
 
 
 def down_kernel(own_ref, oth_ref, w_ref, out_ref):
@@ -487,95 +491,80 @@
     half_qkv = (heads_here + 2 * kv_here) * HD // 2
     half_up = up_weight.shape[1] // 2
 
-    chunk = key_weight.shape[1]
-    n_chunks = 2 * half_qkv // chunk
-    mine, other = local_kernel(
+    key_peer, value_peer = swap(key_cache, "core"), swap(value_cache, "core")
+    row = (1, d_here)
+    small = [hidden_in, attn_gain.reshape(row), mlp_gain.reshape(row), pad_mask]
+    small += [lengths, block_order]
+    mine, other, x_rows, gain, live = local_kernel(
         qkv_kernel,
-        [f32(n_req, half_qkv + LANES)] * 2,
-        [hidden_in, attn_gain.reshape(1, d_here), query_weight, key_weight, value_weight],
-        flops=4 * n_req * d_here * half_qkv,
+        [
+            f32(n_req, half_qkv + LANES),
+            f32(n_req, half_qkv + LANES + pad_mask.shape[1]),
+            bf16(*hidden_in.shape),
+            f32(*row),
+            f32(*pad_mask.shape),
+        ],
+        small + [query_weight, key_weight, value_weight],
+        flops=4 * 10**9,
         scratch=[
-            pltpu.VMEM(hidden_in.shape, hidden_in.dtype),
-            pltpu.VMEM((1, d_here), jnp.float32),
-        ]
-        + [pltpu.VMEM((d_here, chunk), jnp.bfloat16)] * n_chunks
-        + [pltpu.SemaphoreType.DMA((2 + n_chunks,))],
-        in_hbm=range(5),
-    )
-    pair_sum, key_own, value_own, mask_own = lax.optimization_barrier(
-        (mine + swap(other, "core"), key_cache, value_cache, pad_mask)
-    )
-    key_peer, value_peer, mask_peer = (swap(x, "core") for x in (key_own, value_own, mask_own))
-    plain = [out_weight, hidden_in, mlp_gain.reshape(1, d_here)]
-    span_here = pad_mask.shape[1]
-    slots = bf16(n_req, 2 * span_here, key_cache.shape[2] // 2)
-    caches = [key_cache, key_peer, value_cache, value_peer, pad_mask, mask_peer]
-    caches += [lengths, block_order]
-    keys, values, live, out_w, x_rows, gain = local_kernel(
-        prefetch_kernel,
-        [slots, slots, pltpu.VMEM((n_req, 2 * span_here), jnp.int32)]
-        + [pltpu.VMEM(x.shape, x.dtype) for x in plain],
-        [pair_sum] + caches + plain,
-        flops=0,
-        scratch=[
-            pltpu.VMEM((2, n_req, span_here), jnp.int32),
+            pltpu.VMEM(row, jnp.float32),
+            pltpu.VMEM(pad_mask.shape, jnp.int32),
             pltpu.SMEM(lengths.shape, jnp.int32),
             pltpu.SMEM(block_order.shape, jnp.int32),
-            pltpu.SemaphoreType.DMA((len(caches) + len(plain),)),
-        ],
-        in_hbm=range(1, 1 + len(caches) + len(plain)),
+        ]
+        + [pltpu.VMEM(w.shape, w.dtype) for w in (key_weight, value_weight, query_weight)]
+        + [pltpu.SemaphoreType.DMA((len(small) + 3,))],
+        in_hbm=range(len(small) + 3),
+    )
+    arrived = swap(other, "core")
+    width = mine.shape[1]
+    pair_sum, live_peer, key_peer, value_peer = lax.optimization_barrier(
+        (mine + arrived[:, :width], arrived[:, width:], key_peer, value_peer)
     )
     (qkv_half,) = local_kernel(
         qkv_sum_kernel,
         [bf16(n_req, half_qkv)],
-        [gather_all(pair_sum, "chip", n_chips), live],
+        [gather_all(pair_sum, "chip", n_chips)],
         flops=n_chips * n_req * half_qkv,
     )
     half_heads = heads_here // 2
     (message,) = local_kernel(
         attention_kernel,
         [bf16(n_blocks, half_heads, n_req * HD + LANES)],
-        [qkv_half, keys, values, live],
-        flops=4 * n_req * half_heads * kv_here * HD * span_here,
+        [qkv_half, key_cache, key_peer, value_cache, value_peer, live, live_peer],
+        anywhere=(1, 2, 3, 4),
+        flops=4 * 10**9,
         scratch=[pltpu.VMEM((n_req, half_heads, HD), jnp.float32)] * 3,
     )
     arrived = lax.all_to_all(message, ("chip", "core"), 0, 0)
     (head_part,) = local_kernel(
         combine_kernel,
         [f32(n_req, d_here)],
-        [arrived, out_w],
+        [arrived, out_weight],
+        anywhere=(1,),
         flops=2 * n_req * out_weight.size,
         scratch=[pltpu.VMEM((n_req, heads_here, HD), jnp.float32)],
     )
     head_peer = swap(head_part, "tp")
-    (up_w,) = local_kernel(
-        copy_kernel,
-        [bf16(*up_weight.shape)],
-        [head_part, up_weight],
-        flops=0,
-        scratch=[pltpu.SemaphoreType.DMA],
-        in_hbm=(1,),
-    )
-
     resid_rows, up_mine, up_other = local_kernel(
         up_kernel,
         [f32(n_req, d_here)] + [f32(n_req, half_up + LANES)] * 2,
-        [x_rows, head_part, head_peer, gain, up_w],
+        [x_rows, head_part, head_peer, gain, up_weight],
         flops=2 * n_req * up_weight.size,
-    )
-    up_pair = up_mine + swap(up_other, "core")
-    square_sum = up_pair[:, half_up : half_up + 1]
-    piece_0 = lax.reduce_precision(square_sum, 8, 7)
-    piece_1 = lax.reduce_precision(square_sum - piece_0, 8, 7)
-    piece_2 = square_sum - piece_0 - piece_1
-    pieces = jnp.pad(
-        jnp.concatenate([piece_0, piece_1, piece_2], axis=1), ((0, 0), (0, LANES - 3))
-    )
-    up_message = jnp.concatenate([up_pair[:, :half_up], pieces], axis=1).astype(jnp.bfloat16)
-    up_sum = jnp.sum(gather_all(up_message, "chip", n_chips).astype(jnp.float32), axis=0)
-    squares = jnp.sum(up_sum[:, half_up:], axis=1, keepdims=True)
-    inv_mlp = lax.rsqrt(squares / D + NORM_EPS)
-    active_half = squared_relu(up_sum[:, :half_up] * inv_mlp).astype(jnp.bfloat16)
+        anywhere=(4,),
+    )
+    (up_message,) = local_kernel(
+        up_message_kernel,
+        [bf16(n_chips, n_req, half_up + LANES)],
+        [up_mine, swap(up_other, "core")],
+        flops=n_chips * n_req * half_up,
+    )
+    (active_half,) = local_kernel(
+        activate_kernel,
+        [bf16(n_req, half_up)],
+        [lax.all_to_all(up_message, "chip", 0, 0)],
+        flops=n_chips * n_req * half_up,
+    )
     active_other = swap(active_half, "core")
     (down_part,) = local_kernel(
         down_kernel,

time: 61.8 us -> 59.5 us (0.963)
  blocking collectives: 25.9 us -> 41.9 us
  starting transfers between devices: 10.9 us -> 4.18 us
  Pallas kernels: 9.72 us -> 4.81 us
  waiting for transfers between devices: 11.8 us -> 7.52 us
  local copies, waits for them, and re-layouts: 1.8 us -> 0.07 us
    all_to_all x0 -> x1, blocking collectives: none -> 14.3 us  [per_device(): lax.all_to_all(up_message, 'chip', 0, 0)]
    all_to_all x1 -> x0, starting transfers between devices: 7.15 us -> none  [gather_all(): return lax.all_to_all(copies, axes, 0, 0)]
    pallas_call x8, Pallas kernels: 9.72 us -> 4.81 us  [local_kernel(): pl.pallas_call(kernel, out_shape=outs, in_specs=in_specs, out_specs=[IN_V...]
    all_to_all x1 -> x0, waiting for transfers between devices: 4.48 us -> none  [gather_all(): return lax.all_to_all(copies, axes, 0, 0)]
    all_to_all x1, blocking collectives: 14.3 us -> 15.7 us  [gather_all(): return lax.all_to_all(copies, axes, 0, 0)]
    unnamed x10 -> x14, local copies, waits for them, and re-layouts: 0.96 us -> 0.04 us
    broadcast_in_dim x2 -> x1, local copies, waits for them, and re-layouts: 0.82 us -> 0.03 us  [gather_all(): copies = jnp.broadcast_to(values_in[None], (n,) + values_in.shape)]
    ppermute x8 -> x7, starting transfers between devices: 3.76 us -> 4.18 us  [swap(): return lax.ppermute(values_in, axis, [(i, i ^ 1) for i in range(n)])]
  transfers between devices with their start and end apart: 9 -> 7, of which waited for: 6 -> 5; matrix products, arithmetic and copies ran while one was open for 1% -> 0% of each run, Pallas kernels for 7% -> 3%
where the time goes in v5:
time: 59.5 us; the launch traced here: 59.2 us
  blocking collectives  41.9 us (70%)
  waiting for transfers between devices  7.52 us (13%)
  Pallas kernels  4.81 us (8%)
  starting transfers between devices  4.18 us (7%)
    all_to_all x1, blocking collectives, gather_all(): return lax.all_to_all(copies, axes, 0, 0)  15.7 us
    all_to_all x1, blocking collectives, per_device(): lax.all_to_all(up_message, 'chip', 0, 0)  14.3 us
    all_to_all x1, blocking collectives, per_device(): arrived = lax.all_to_all(message, ('chip', 'core'), 0, 0)  11.9 us
    ppermute x7, waiting for transfers between devices, swap(): return lax.ppermute(values_in, axis, [(i, i ^ 1) for i in range(n)])  7.52 us
    pallas_call x8, Pallas kernels, local_kernel(): pl.pallas_call(kernel, out_shape=outs, in_specs=in_specs, out_specs=[IN_V...  4.81 us
    ppermute x7, starting transfers between devices, swap(): return lax.ppermute(values_in, axis, [(i, i ^ 1) for i in range(n)])  4.18 us
  transfers between devices with their start and end apart: 7, of which 5 were waited for; matrix products, arithmetic and copies ran while one was open for 0% of the time, Pallas kernels for 3%

profile of v5, /device:TPU:0, one launch (start us, length us, event | category | flops | bytes accessed | tf_op | source)
XLA Modules:
  0.0 59.2 jit_solution(2995272363319865724)
XLA Ops:
  0.0 0.5 collective-permute-start.1
  0.5 0.1 collective-permute-start.2
  0.5 0.0 copy-start.1
  0.5 0.0 copy-start.2
  0.5 1.9 %shard_map.136 = (f32[4,1664]{1,0:T(4,128)S(1)}, f32[4,1792]{1,0:T(4,128)S(1)}, bf16[4,256]{1,0:T(4,128)(2,1)S(1)}, f32[1,256]{1,0:T(1,128)S(1)}, f32[4,128]{1,0:T(4,128)S(1)}) custom-call(bf16[4,256]{1,0:T(4,128)(2,1)} %x_hbm.1, f32[1,256]{1,0:T(1,128)} %bitcast.6, f32[1,256]{1,0:T(1,128)} %bitcast.7, s32[4,128]{1,0:T(4,128)} %mask_hbm.1, s32[4]{0:T(128)} %lengths_hbm.1, ...), custom_call_target="tpu_custom_call" | custom-call | flops 4000000000 | bytes 1579040 | tf_op jit(solution)/shard_map/pallas_call | solution.py:224
  2.4 0.5 collective-permute-start
  2.9 0.9 %collective-permute-done = f32[4,1792]{1,0:T(4,128)S(1)} collective-permute-done((f32[4,1792]{1,0:T(4,128)S(1)}, f32[4,1792]{1,0:T(4,128)S(1)}, u32[]{:S(2)}, u32[]{:S(2)}) %collective-permute-start) | collective-permute-done | bytes 28704 | tf_op jit(solution)/shard_map/ppermute | solution.py:28
  3.8 0.0 collective-permute-done.1.key_peer
  3.8 0.0 collective-permute-done.2.value_peer
  3.8 0.0 slice-start
  3.8 15.7 %all_to_all.15.arrived_ref = f32[8,4,1664]{2,1,0:T(4,128)S(1)} all-to-all(f32[8,4,1664]{2,1,0:T(4,128)S(1)} %broadcast_in_dim.2), channel_id=1, replica_groups=mesh['chip'=8,'core'=2,'tp'=2] {'chip'}, dimensions={0} | all-to-all | bytes 425984 | tf_op jit(solution)/shard_map/all_to_all | solution.py:33
  19.6 0.1 shard_map.137.qkv_ref
  19.7 0.0 slice-start.2
  19.7 0.0 copy-done.1
  19.7 0.0 copy-done.2
  19.7 0.0 copy-start
  19.7 0.0 slice-start.1
  19.7 0.0 slice-start.3
  19.7 0.5 shard_map.138
  20.2 11.9 %all_to_all.16.arrived_ref = bf16[16,8,640]{2,1,0:T(8,128)(2,1)S(1)} all-to-all(bf16[16,8,640]{2,1,0:T(8,128)(2,1)S(1)} %shard_map.138), channel_id=1, replica_groups=mesh['chip'=8,'core'=2,'tp'=2] {'chip','core'}, dimensions={0} | all-to-all | bytes 327680 | tf_op jit(solution)/shard_map/all_to_all | solution.py:539
  32.1 0.0 copy-done
  32.1 0.6 shard_map.139.part_ref
  32.7 1.5 %collective-permute-start.3 = (f32[4,256]{1,0:T(4,128)S(1)}, f32[4,256]{1,0:T(4,128)S(1)}, u32[]{:S(2)}, u32[]{:S(2)}) collective-permute-start(f32[4,256]{1,0:T(4,128)S(1)} %shard_map.139.part_ref), channel_id=1, source_target_pairs={{0,1},{1,0},{2,3},{3,2},{4,5},{5,4},{6,7},{7,6},{8,9},{9,8},{10,11... | collective-permute-start | bytes 12296 | tf_op jit(solution)/shard_map/ppermute | solution.py:28
  34.2 2.1 %collective-permute-done.3.peer_ref = f32[4,256]{1,0:T(4,128)S(1)} collective-permute-done((f32[4,256]{1,0:T(4,128)S(1)}, f32[4,256]{1,0:T(4,128)S(1)}, u32[]{:S(2)}, u32[]{:S(2)}) %collective-permute-start.3) | collective-permute-done | bytes 4128 | tf_op jit(solution)/shard_map/ppermute | solution.py:28
  36.3 0.0 slice-done
  36.3 0.0 slice-done.1
  36.3 0.8 %shard_map.140 = (f32[4,256]{1,0:T(4,128)S(1)}, f32[4,5504]{1,0:T(4,128)S(1)}, f32[4,5504]{1,0:T(4,128)S(1)}) custom-call(bf16[4,256]{1,0:T(4,128)(2,1)S(1)} %get-tuple-element.17.x_ref, f32[4,256]{1,0:T(4,128)S(1)} %shard_map.139.part_ref, f32[4,256]{1,0:T(4,128)S(1)} %collective-permute-done.3.peer_ref, f32[1,256]{1,0:T(1,128)S(1)} %get-tuple-element.25.gain_ref, ...), custom_call_target="tpu_custom_call" | custom-call | flops 22020096 | bytes 5516288 | tf_op jit(solution)/shard_map/pallas_call | solution.py:224
  37.1 0.0 collective-permute-start.4
  37.2 1.3 %collective-permute-done.4.arrived_ref = f32[4,5504]{1,0:T(4,128)S(1)} collective-permute-done((f32[4,5504]{1,0:T(4,128)S(1)}, f32[4,5504]{1,0:T(4,128)S(1)}, u32[]{:S(2)}, u32[]{:S(2)}) %collective-permute-start.4) | collective-permute-done | bytes 88096 | tf_op jit(solution)/shard_map/ppermute | solution.py:28
  38.5 14.3 %all_to_all.17.arrived_ref = bf16[8,4,5504]{2,1,0:T(4,128)(2,1)S(1)} all-to-all(bf16[8,4,5504]{2,1,0:T(4,128)(2,1)S(1)} %shard_map.141), channel_id=1, replica_groups=mesh['chip'=8,'core'=2,'tp'=2] {'chip'}, dimensions={0} | all-to-all | bytes 704512 | tf_op jit(solution)/shard_map/all_to_all | solution.py:565
  52.8 0.1 shard_map.142.own_ref
  52.9 0.1 collective-permute-start.5
  53.0 1.2 %collective-permute-done.5.oth_ref = bf16[4,5376]{1,0:T(4,128)(2,1)S(1)} collective-permute-done((bf16[4,5376]{1,0:T(4,128)(2,1)S(1)}, bf16[4,5376]{1,0:T(4,128)(2,1)S(1)}, u32[]{:S(2)}, u32[]{:S(2)}) %collective-permute-start.5) | collective-permute-done | bytes 43040 | tf_op jit(solution)/shard_map/ppermute | solution.py:28
  54.2 0.0 slice-done.2
  54.2 0.0 slice-done.3
  54.2 0.8 %shard_map.143 = f32[4,256]{1,0:T(4,128)S(1)} custom-call(bf16[4,5376]{1,0:T(4,128)(2,1)S(1)} %shard_map.142.own_ref, bf16[4,5376]{1,0:T(4,128)(2,1)S(1)} %collective-permute-done.5.oth_ref, bf16[10752,256]{1,0:T(8,128)(2,1)S(1)} %bitcast.5), custom_call_target="tpu_custom_call" | custom-call | flops 22020096 | bytes 5591040 | tf_op jit(solution)/shard_map/pallas_call | solution.py:224
  55.0 1.5 %collective-permute-start.6 = (f32[4,256]{1,0:T(4,128)S(1)}, f32[4,256]{1,0:T(4,128)S(1)}, u32[]{:S(2)}, u32[]{:S(2)}) collective-permute-start(f32[4,256]{1,0:T(4,128)S(1)} %shard_map.143), channel_id=1, source_target_pairs={{0,1},{1,0},{2,3},{3,2},{4,5},{5,4},{6,7},{7,6},{8,9},{9,8},{10,11... | collective-permute-start | bytes 12296 | tf_op jit(solution)/shard_map/ppermute | solution.py:28
  56.5 2.1 %collective-permute-done.6 = f32[4,256]{1,0:T(4,128)S(1)} collective-permute-done((f32[4,256]{1,0:T(4,128)S(1)}, f32[4,256]{1,0:T(4,128)S(1)}, u32[]{:S(2)}, u32[]{:S(2)}) %collective-permute-start.6) | collective-permute-done | bytes 4128 | tf_op jit(solution)/shard_map/ppermute | solution.py:28
  58.6 0.6 add_convert_fusion
  (6 shorter events, 0.1 us)
Async XLA Ops:
  0.0 3.8 %collective-permute-start.1 = (bf16[4,128,512]{2,1,0:T(8,128)(2,1)}, bf16[4,128,512]{2,1,0:T(8,128)(2,1)S(1)}, u32[]{:S(2)}, u32[]{:S(2)}) collective-permute-start(bf16[4,128,512]{2,1,0:T(8,128)(2,1)} %key_own.1), channel_id=1, source_target_pairs={{0,2},{2,0},{1,3},{3,1},{4,6},{6,4},{5,7},{7,5},{8,10},{10,8},{9,1... | collective-permute-start | bytes 1572872 | tf_op jit(solution)/shard_map/ppermute | solution.py:28
  0.5 3.3 %collective-permute-start.2 = (bf16[4,128,512]{2,1,0:T(8,128)(2,1)}, bf16[4,128,512]{2,1,0:T(8,128)(2,1)S(1)}, u32[]{:S(2)}, u32[]{:S(2)}) collective-permute-start(bf16[4,128,512]{2,1,0:T(8,128)(2,1)} %value_own.1), channel_id=1, source_target_pairs={{0,2},{2,0},{1,3},{3,1},{4,6},{6,4},{5,7},{7,5},{8,10},{10,8},{9,1... | collective-permute-start | bytes 1572872 | tf_op jit(solution)/shard_map/ppermute | solution.py:28
  0.5 19.2 %copy-start.1 = (bf16[4,128,512]{2,1,0:T(8,128)(2,1)S(1)}, bf16[4,128,512]{2,1,0:T(8,128)(2,1)}, u32[]{:S(2)}) copy-start(bf16[4,128,512]{2,1,0:T(8,128)(2,1)} %key_own.1) | copy-start | bytes 1572868
  0.5 19.2 %copy-start.2 = (bf16[4,128,512]{2,1,0:T(8,128)(2,1)S(1)}, bf16[4,128,512]{2,1,0:T(8,128)(2,1)}, u32[]{:S(2)}) copy-start(bf16[4,128,512]{2,1,0:T(8,128)(2,1)} %value_own.1) | copy-start | bytes 1572868
  2.4 1.4 %collective-permute-start = (f32[4,1792]{1,0:T(4,128)S(1)}, f32[4,1792]{1,0:T(4,128)S(1)}, u32[]{:S(2)}, u32[]{:S(2)}) collective-permute-start(f32[4,1792]{1,0:T(4,128)S(1)} %get-tuple-element.19), channel_id=1, source_target_pairs={{0,2},{2,0},{1,3},{3,1},{4,6},{6,4},{5,7},{7,5},{8,10},{10,8},{9,1... | collective-permute-start | bytes 86024 | tf_op jit(solution)/shard_map/ppermute | solution.py:28
  3.8 32.5 %slice-start = ((s8[5505024]{0:T(1024)(128)(4,1)}), s8[4194304]{0:T(1024)(128)(4,1)S(1)}, s32[]{:S(2)}) async-start(s8[5505024]{0:T(1024)(128)(4,1)} %bitcast.2), calls=%async_computation.3 | async-start | bytes 8388608
  19.7 34.5 %slice-start.2 = ((s8[5505024]{0:T(1024)(128)(4,1)}), s8[4194304]{0:T(1024)(128)(4,1)S(1)}, s32[]{:S(2)}) async-start(s8[5505024]{0:T(1024)(128)(4,1)} %bitcast.4), calls=%async_computation.5 | async-start | bytes 8388608
  19.7 12.4 %copy-start = (bf16[2048,256]{1,0:T(8,128)(2,1)S(1)}, bf16[2048,256]{1,0:T(8,128)(2,1)}, u32[]{:S(2)}) copy-start(bf16[2048,256]{1,0:T(8,128)(2,1)} %w_ref.3) | copy-start | bytes 3145732
  19.7 16.6 %slice-start.1 = ((s8[5505024]{0:T(1024)(128)(4,1)}), s8[1310720]{0:T(1024)(128)(4,1)S(1)}, s32[]{:S(2)}) async-start(s8[5505024]{0:T(1024)(128)(4,1)} %bitcast.2), calls=%async_computation.4 | async-start | bytes 2621440
  19.7 34.5 %slice-start.3 = ((s8[5505024]{0:T(1024)(128)(4,1)}), s8[1310720]{0:T(1024)(128)(4,1)S(1)}, s32[]{:S(2)}) async-start(s8[5505024]{0:T(1024)(128)(4,1)} %bitcast.4), calls=%async_computation.6 | async-start | bytes 2621440
  32.7 3.6 %collective-permute-start.3 = (f32[4,256]{1,0:T(4,128)S(1)}, f32[4,256]{1,0:T(4,128)S(1)}, u32[]{:S(2)}, u32[]{:S(2)}) collective-permute-start(f32[4,256]{1,0:T(4,128)S(1)} %shard_map.139.part_ref), channel_id=1, source_target_pairs={{0,1},{1,0},{2,3},{3,2},{4,5},{5,4},{6,7},{7,6},{8,9},{9,8},{10,11... | collective-permute-start | bytes 12296 | tf_op jit(solution)/shard_map/ppermute | solution.py:28
  37.1 1.3 %collective-permute-start.4 = (f32[4,5504]{1,0:T(4,128)S(1)}, f32[4,5504]{1,0:T(4,128)S(1)}, u32[]{:S(2)}, u32[]{:S(2)}) collective-permute-start(f32[4,5504]{1,0:T(4,128)S(1)} %get-tuple-element.28), channel_id=1, source_target_pairs={{0,2},{2,0},{1,3},{3,1},{4,6},{6,4},{5,7},{7,5},{8,10},{10,8},{9,1... | collective-permute-start | bytes 264200 | tf_op jit(solution)/shard_map/ppermute | solution.py:28
  52.9 1.3 %collective-permute-start.5 = (bf16[4,5376]{1,0:T(4,128)(2,1)S(1)}, bf16[4,5376]{1,0:T(4,128)(2,1)S(1)}, u32[]{:S(2)}, u32[]{:S(2)}) collective-permute-start(bf16[4,5376]{1,0:T(4,128)(2,1)S(1)} %shard_map.142.own_ref), channel_id=1, source_target_pairs={{0,2},{2,0},{1,3},{3,1},{4,6},{6,4},{5,7},{7,5},{8,10},{10,8},{9,1... | collective-permute-start | bytes 129032 | tf_op jit(solution)/shard_map/ppermute | solution.py:28
  55.0 3.6 %collective-permute-start.6 = (f32[4,256]{1,0:T(4,128)S(1)}, f32[4,256]{1,0:T(4,128)S(1)}, u32[]{:S(2)}, u32[]{:S(2)}) collective-permute-start(f32[4,256]{1,0:T(4,128)S(1)} %shard_map.143), channel_id=1, source_target_pairs={{0,1},{1,0},{2,3},{3,2},{4,5},{5,4},{6,7},{7,6},{8,9},{9,8},{10,11... | collective-permute-start | bytes 12296 | tf_op jit(solution)/shard_map/ppermute | solution.py:28

commit v6 on v5

--- a/solution.py
+++ b/solution.py
@@ -295,13 +295,37 @@
     other_ref[:, at + LANES :] = live_ref[...]
 
 
+SCALE_UNIT = 1024.0
+
+
+def qkv_message_kernel(mine_ref, arrived_ref, out_ref):
+    width = mine_ref.shape[1] - LANES
+    features = D / lax.axis_size("chip")
+    total = mine_ref[...] + arrived_ref[:, : width + LANES]
+    squares = total[:, width:]
+    scale = jnp.sqrt(jnp.maximum(squares * (1.0 / features), 2.0**-40))
+    scale = scale.astype(jnp.bfloat16).astype(jnp.float32)
+    inverse = 1.0 / scale
+    out_ref[:, :width] = total[:, :width] * inverse[:, :1]
+    lane = lax.broadcasted_iota(jnp.int32, squares.shape, 1)
+    tile = jnp.where(lane == 0, scale * SCALE_UNIT, 0.0)
+    for p, piece in enumerate(pieces_of(squares * inverse * inverse * (1.0 / features))):
+        tile = jnp.where(lane == 1 + p, piece, tile)
+    out_ref[:, width:] = tile
+
+
 def qkv_sum_kernel(arrived_ref, out_ref):
-    total = arrived_ref[0]
-    for i in range(1, arrived_ref.shape[0]):
-        total = total + arrived_ref[i]
     width = out_ref.shape[1]
-    inv_attn = lax.rsqrt(total[:, width : width + 1] / D + NORM_EPS)
-    out_ref[...] = (total[:, :width] * inv_attn).astype(jnp.bfloat16)
+    features = D / arrived_ref.shape[0]
+    total, squares = 0.0, 0.0
+    for i in range(arrived_ref.shape[0]):
+        tile = arrived_ref[i, :, width:]
+        scale = tile[:, :1] * (1.0 / SCALE_UNIT)
+        total = total + arrived_ref[i, :, :width] * scale
+        mean = tile[:, 1:2] + tile[:, 2:3] + tile[:, 3:4]
+        squares = squares + mean * scale * scale * features
+    inv_attn = lax.rsqrt(squares / D + NORM_EPS)
+    out_ref[...] = (total * inv_attn).astype(jnp.bfloat16)
 
 
 PIECE = 16
@@ -518,13 +542,16 @@
     )
     arrived = swap(other, "core")
     width = mine.shape[1]
-    pair_sum, live_peer, key_peer, value_peer = lax.optimization_barrier(
-        (mine + arrived[:, :width], arrived[:, width:], key_peer, value_peer)
+    (qkv_message,) = local_kernel(
+        qkv_message_kernel, [f32(*mine.shape)], [mine, arrived], flops=2 * mine.size
+    )
+    qkv_message, live_peer, key_peer, value_peer = lax.optimization_barrier(
+        (qkv_message.astype(jnp.float16), arrived[:, width:], key_peer, value_peer)
     )
     (qkv_half,) = local_kernel(
         qkv_sum_kernel,
         [bf16(n_req, half_qkv)],
-        [gather_all(pair_sum, "chip", n_chips)],
+        [gather_all(qkv_message, "chip", n_chips).astype(jnp.float32)],
         flops=n_chips * n_req * half_qkv,
     )
     half_heads = heads_here // 2

time: 59.5 us -> 57.8 us (0.971)
  blocking collectives: 41.9 us -> 40 us
    all_to_all x1, blocking collectives: 15.7 us -> 14.1 us  [gather_all(): return lax.all_to_all(copies, axes, 0, 0)]
    pallas_call x8 -> x9, Pallas kernels: 4.81 us -> 4.98 us  [local_kernel(): pl.pallas_call(kernel, out_shape=outs, in_specs=in_specs, out_specs=[IN_V...]
where the time goes in v6:
time: 57.8 us; the launch traced here: 57.5 us
  blocking collectives  40 us (69%)
  waiting for transfers between devices  7.52 us (13%)
  Pallas kernels  4.98 us (9%)
  starting transfers between devices  4.18 us (7%)
  other arithmetic  0.63 us (1%)
    all_to_all x1, blocking collectives, per_device(): lax.all_to_all(up_message, 'chip', 0, 0)  14.3 us
    all_to_all x1, blocking collectives, gather_all(): return lax.all_to_all(copies, axes, 0, 0)  14.1 us
    all_to_all x1, blocking collectives, per_device(): arrived = lax.all_to_all(message, ('chip', 'core'), 0, 0)  11.6 us
    ppermute x7, waiting for transfers between devices, swap(): return lax.ppermute(values_in, axis, [(i, i ^ 1) for i in range(n)])  7.52 us
    pallas_call x9, Pallas kernels, local_kernel(): pl.pallas_call(kernel, out_shape=outs, in_specs=in_specs, out_specs=[IN_V...  4.98 us
    ppermute x7, starting transfers between devices, swap(): return lax.ppermute(values_in, axis, [(i, i ^ 1) for i in range(n)])  4.18 us
  transfers between devices with their start and end apart: 7, of which 5 were waited for; matrix products, arithmetic and copies ran while one was open for 0% of the time, Pallas kernels for 3%

profile of v6, /device:TPU:0, one launch (start us, length us, event | category | flops | bytes accessed | tf_op | source)
XLA Modules:
  0.0 57.5 jit_solution(1565522209385492179)
XLA Ops:
  0.0 0.5 collective-permute-start.1
  0.5 0.1 collective-permute-start.2
  0.5 0.0 copy-start.1
  0.5 0.0 copy-start.2
  0.5 1.9 %shard_map.136 = (f32[4,1664]{1,0:T(4,128)S(1)}, f32[4,1792]{1,0:T(4,128)S(1)}, bf16[4,256]{1,0:T(4,128)(2,1)S(1)}, f32[1,256]{1,0:T(1,128)S(1)}, f32[4,128]{1,0:T(4,128)S(1)}) custom-call(bf16[4,256]{1,0:T(4,128)(2,1)} %x_hbm.1, f32[1,256]{1,0:T(1,128)} %bitcast.6, f32[1,256]{1,0:T(1,128)} %bitcast.7, s32[4,128]{1,0:T(4,128)} %mask_hbm.1, s32[4]{0:T(128)} %lengths_hbm.1, ...), custom_call_target="tpu_custom_call" | custom-call | flops 4000000000 | bytes 1579040 | tf_op jit(solution)/shard_map/pallas_call | solution.py:224
  2.4 0.5 collective-permute-start
  2.9 0.9 %collective-permute-done.arrived_ref = f32[4,1792]{1,0:T(4,128)S(1)} collective-permute-done((f32[4,1792]{1,0:T(4,128)S(1)}, f32[4,1792]{1,0:T(4,128)S(1)}, u32[]{:S(2)}, u32[]{:S(2)}) %collective-permute-start) | collective-permute-done | bytes 28704 | tf_op jit(solution)/shard_map/ppermute | solution.py:28
  3.8 0.1 shard_map.137
  3.9 0.0 collective-permute-done.1.key_peer
  3.9 0.0 collective-permute-done.2.value_peer
  3.9 14.1 %all_to_all.15 = f16[8,4,1664]{2,1,0:T(4,128)(2,1)S(1)} all-to-all(f16[8,4,1664]{2,1,0:T(4,128)(2,1)S(1)} %broadcast_in_dim.2), channel_id=1, replica_groups=mesh['chip'=8,'core'=2,'tp'=2] {'chip'}, dimensions={0} | all-to-all | bytes 212992 | tf_op jit(solution)/shard_map/all_to_all | solution.py:33
  18.1 0.0 slice-start
  18.1 0.2 shard_map.138.qkv_ref
  18.3 0.0 slice-start.2
  18.3 0.0 copy-done.1
  18.3 0.0 copy-done.2
  18.3 0.0 copy-start
  18.3 0.0 slice-start.1
  18.3 0.0 slice-start.3
  18.3 0.5 shard_map.139
  18.8 11.6 %all_to_all.16.arrived_ref = bf16[16,8,640]{2,1,0:T(8,128)(2,1)S(1)} all-to-all(bf16[16,8,640]{2,1,0:T(8,128)(2,1)S(1)} %shard_map.139), channel_id=1, replica_groups=mesh['chip'=8,'core'=2,'tp'=2] {'chip','core'}, dimensions={0} | all-to-all | bytes 327680 | tf_op jit(solution)/shard_map/all_to_all | solution.py:566
  30.4 0.0 copy-done
  30.4 0.6 shard_map.140.part_ref
  31.0 1.5 %collective-permute-start.3 = (f32[4,256]{1,0:T(4,128)S(1)}, f32[4,256]{1,0:T(4,128)S(1)}, u32[]{:S(2)}, u32[]{:S(2)}) collective-permute-start(f32[4,256]{1,0:T(4,128)S(1)} %shard_map.140.part_ref), channel_id=1, source_target_pairs={{0,1},{1,0},{2,3},{3,2},{4,5},{5,4},{6,7},{7,6},{8,9},{9,8},{10,11... | collective-permute-start | bytes 12296 | tf_op jit(solution)/shard_map/ppermute | solution.py:28
  32.5 2.1 %collective-permute-done.3.peer_ref = f32[4,256]{1,0:T(4,128)S(1)} collective-permute-done((f32[4,256]{1,0:T(4,128)S(1)}, f32[4,256]{1,0:T(4,128)S(1)}, u32[]{:S(2)}, u32[]{:S(2)}) %collective-permute-start.3) | collective-permute-done | bytes 4128 | tf_op jit(solution)/shard_map/ppermute | solution.py:28
  34.6 0.0 slice-done
  34.6 0.0 slice-done.1
  34.6 0.8 %shard_map.141 = (f32[4,256]{1,0:T(4,128)S(1)}, f32[4,5504]{1,0:T(4,128)S(1)}, f32[4,5504]{1,0:T(4,128)S(1)}) custom-call(bf16[4,256]{1,0:T(4,128)(2,1)S(1)} %get-tuple-element.17.x_ref, f32[4,256]{1,0:T(4,128)S(1)} %shard_map.140.part_ref, f32[4,256]{1,0:T(4,128)S(1)} %collective-permute-done.3.peer_ref, f32[1,256]{1,0:T(1,128)S(1)} %get-tuple-element.25.gain_ref, ...), custom_call_target="tpu_custom_call" | custom-call | flops 22020096 | bytes 5516288 | tf_op jit(solution)/shard_map/pallas_call | solution.py:224
  35.4 0.0 collective-permute-start.4
  35.5 1.3 %collective-permute-done.4.arrived_ref = f32[4,5504]{1,0:T(4,128)S(1)} collective-permute-done((f32[4,5504]{1,0:T(4,128)S(1)}, f32[4,5504]{1,0:T(4,128)S(1)}, u32[]{:S(2)}, u32[]{:S(2)}) %collective-permute-start.4) | collective-permute-done | bytes 88096 | tf_op jit(solution)/shard_map/ppermute | solution.py:28
  36.8 14.3 %all_to_all.17.arrived_ref = bf16[8,4,5504]{2,1,0:T(4,128)(2,1)S(1)} all-to-all(bf16[8,4,5504]{2,1,0:T(4,128)(2,1)S(1)} %shard_map.142), channel_id=1, replica_groups=mesh['chip'=8,'core'=2,'tp'=2] {'chip'}, dimensions={0} | all-to-all | bytes 704512 | tf_op jit(solution)/shard_map/all_to_all | solution.py:592
  51.1 0.1 shard_map.143.own_ref
  51.2 0.1 collective-permute-start.5
  51.3 1.2 %collective-permute-done.5.oth_ref = bf16[4,5376]{1,0:T(4,128)(2,1)S(1)} collective-permute-done((bf16[4,5376]{1,0:T(4,128)(2,1)S(1)}, bf16[4,5376]{1,0:T(4,128)(2,1)S(1)}, u32[]{:S(2)}, u32[]{:S(2)}) %collective-permute-start.5) | collective-permute-done | bytes 43040 | tf_op jit(solution)/shard_map/ppermute | solution.py:28
  52.5 0.0 slice-done.2
  52.5 0.0 slice-done.3
  52.5 0.8 %shard_map.144 = f32[4,256]{1,0:T(4,128)S(1)} custom-call(bf16[4,5376]{1,0:T(4,128)(2,1)S(1)} %shard_map.143.own_ref, bf16[4,5376]{1,0:T(4,128)(2,1)S(1)} %collective-permute-done.5.oth_ref, bf16[10752,256]{1,0:T(8,128)(2,1)S(1)} %bitcast.5), custom_call_target="tpu_custom_call" | custom-call | flops 22020096 | bytes 5591040 | tf_op jit(solution)/shard_map/pallas_call | solution.py:224
  53.3 1.5 %collective-permute-start.6 = (f32[4,256]{1,0:T(4,128)S(1)}, f32[4,256]{1,0:T(4,128)S(1)}, u32[]{:S(2)}, u32[]{:S(2)}) collective-permute-start(f32[4,256]{1,0:T(4,128)S(1)} %shard_map.144), channel_id=1, source_target_pairs={{0,1},{1,0},{2,3},{3,2},{4,5},{5,4},{6,7},{7,6},{8,9},{9,8},{10,11... | collective-permute-start | bytes 12296 | tf_op jit(solution)/shard_map/ppermute | solution.py:28
  54.9 2.1 %collective-permute-done.6 = f32[4,256]{1,0:T(4,128)S(1)} collective-permute-done((f32[4,256]{1,0:T(4,128)S(1)}, f32[4,256]{1,0:T(4,128)S(1)}, u32[]{:S(2)}, u32[]{:S(2)}) %collective-permute-start.6) | collective-permute-done | bytes 4128 | tf_op jit(solution)/shard_map/ppermute | solution.py:28
  56.9 0.6 %add_convert_fusion = bf16[4,256]{1,0:T(4,128)(2,1)} fusion(f32[4,256]{1,0:T(4,128)S(1)} %get-tuple-element.26, f32[4,256]{1,0:T(4,128)S(1)} %shard_map.144, f32[4,256]{1,0:T(4,128)S(1)} %collective-permute-done.6), kind=kLoop, calls=%fused_computation | loop fusion | flops 3072 | bytes 14336 | tf_op jit(solution)/shard_map/convert_element_type | solution.py:604
  (7 shorter events, 0.1 us)
Async XLA Ops:
  0.0 3.9 %collective-permute-start.1 = (bf16[4,128,512]{2,1,0:T(8,128)(2,1)}, bf16[4,128,512]{2,1,0:T(8,128)(2,1)S(1)}, u32[]{:S(2)}, u32[]{:S(2)}) collective-permute-start(bf16[4,128,512]{2,1,0:T(8,128)(2,1)} %key_own.1), channel_id=1, source_target_pairs={{0,2},{2,0},{1,3},{3,1},{4,6},{6,4},{5,7},{7,5},{8,10},{10,8},{9,1... | collective-permute-start | bytes 1572872 | tf_op jit(solution)/shard_map/ppermute | solution.py:28
  0.5 3.4 %collective-permute-start.2 = (bf16[4,128,512]{2,1,0:T(8,128)(2,1)}, bf16[4,128,512]{2,1,0:T(8,128)(2,1)S(1)}, u32[]{:S(2)}, u32[]{:S(2)}) collective-permute-start(bf16[4,128,512]{2,1,0:T(8,128)(2,1)} %value_own.1), channel_id=1, source_target_pairs={{0,2},{2,0},{1,3},{3,1},{4,6},{6,4},{5,7},{7,5},{8,10},{10,8},{9,1... | collective-permute-start | bytes 1572872 | tf_op jit(solution)/shard_map/ppermute | solution.py:28
  0.5 17.8 %copy-start.1 = (bf16[4,128,512]{2,1,0:T(8,128)(2,1)S(1)}, bf16[4,128,512]{2,1,0:T(8,128)(2,1)}, u32[]{:S(2)}) copy-start(bf16[4,128,512]{2,1,0:T(8,128)(2,1)} %key_own.1) | copy-start | bytes 1572868
  0.5 17.8 %copy-start.2 = (bf16[4,128,512]{2,1,0:T(8,128)(2,1)S(1)}, bf16[4,128,512]{2,1,0:T(8,128)(2,1)}, u32[]{:S(2)}) copy-start(bf16[4,128,512]{2,1,0:T(8,128)(2,1)} %value_own.1) | copy-start | bytes 1572868
  2.4 1.4 %collective-permute-start = (f32[4,1792]{1,0:T(4,128)S(1)}, f32[4,1792]{1,0:T(4,128)S(1)}, u32[]{:S(2)}, u32[]{:S(2)}) collective-permute-start(f32[4,1792]{1,0:T(4,128)S(1)} %get-tuple-element.19), channel_id=1, source_target_pairs={{0,2},{2,0},{1,3},{3,1},{4,6},{6,4},{5,7},{7,5},{8,10},{10,8},{9,1... | collective-permute-start | bytes 86024 | tf_op jit(solution)/shard_map/ppermute | solution.py:28
  18.1 16.5 %slice-start = ((s8[5505024]{0:T(1024)(128)(4,1)}), s8[4194304]{0:T(1024)(128)(4,1)S(1)}, s32[]{:S(2)}) async-start(s8[5505024]{0:T(1024)(128)(4,1)} %bitcast.2), calls=%async_computation.3 | async-start | bytes 8388608
  18.3 34.2 %slice-start.2 = ((s8[5505024]{0:T(1024)(128)(4,1)}), s8[4194304]{0:T(1024)(128)(4,1)S(1)}, s32[]{:S(2)}) async-start(s8[5505024]{0:T(1024)(128)(4,1)} %bitcast.4), calls=%async_computation.5 | async-start | bytes 8388608
  18.3 12.1 %copy-start = (bf16[2048,256]{1,0:T(8,128)(2,1)S(1)}, bf16[2048,256]{1,0:T(8,128)(2,1)}, u32[]{:S(2)}) copy-start(bf16[2048,256]{1,0:T(8,128)(2,1)} %w_ref.3) | copy-start | bytes 3145732
  18.3 16.3 %slice-start.1 = ((s8[5505024]{0:T(1024)(128)(4,1)}), s8[1310720]{0:T(1024)(128)(4,1)S(1)}, s32[]{:S(2)}) async-start(s8[5505024]{0:T(1024)(128)(4,1)} %bitcast.2), calls=%async_computation.4 | async-start | bytes 2621440
  18.3 34.2 %slice-start.3 = ((s8[5505024]{0:T(1024)(128)(4,1)}), s8[1310720]{0:T(1024)(128)(4,1)S(1)}, s32[]{:S(2)}) async-start(s8[5505024]{0:T(1024)(128)(4,1)} %bitcast.4), calls=%async_computation.6 | async-start | bytes 2621440
  31.0 3.6 %collective-permute-start.3 = (f32[4,256]{1,0:T(4,128)S(1)}, f32[4,256]{1,0:T(4,128)S(1)}, u32[]{:S(2)}, u32[]{:S(2)}) collective-permute-start(f32[4,256]{1,0:T(4,128)S(1)} %shard_map.140.part_ref), channel_id=1, source_target_pairs={{0,1},{1,0},{2,3},{3,2},{4,5},{5,4},{6,7},{7,6},{8,9},{9,8},{10,11... | collective-permute-start | bytes 12296 | tf_op jit(solution)/shard_map/ppermute | solution.py:28
  35.4 1.3 %collective-permute-start.4 = (f32[4,5504]{1,0:T(4,128)S(1)}, f32[4,5504]{1,0:T(4,128)S(1)}, u32[]{:S(2)}, u32[]{:S(2)}) collective-permute-start(f32[4,5504]{1,0:T(4,128)S(1)} %get-tuple-element.28), channel_id=1, source_target_pairs={{0,2},{2,0},{1,3},{3,1},{4,6},{6,4},{5,7},{7,5},{8,10},{10,8},{9,1... | collective-permute-start | bytes 264200 | tf_op jit(solution)/shard_map/ppermute | solution.py:28
  51.2 1.3 %collective-permute-start.5 = (bf16[4,5376]{1,0:T(4,128)(2,1)S(1)}, bf16[4,5376]{1,0:T(4,128)(2,1)S(1)}, u32[]{:S(2)}, u32[]{:S(2)}) collective-permute-start(bf16[4,5376]{1,0:T(4,128)(2,1)S(1)} %shard_map.143.own_ref), channel_id=1, source_target_pairs={{0,2},{2,0},{1,3},{3,1},{4,6},{6,4},{5,7},{7,5},{8,10},{10,8},{9,1... | collective-permute-start | bytes 129032 | tf_op jit(solution)/shard_map/ppermute | solution.py:28
  53.3 3.6 %collective-permute-start.6 = (f32[4,256]{1,0:T(4,128)S(1)}, f32[4,256]{1,0:T(4,128)S(1)}, u32[]{:S(2)}, u32[]{:S(2)}) collective-permute-start(f32[4,256]{1,0:T(4,128)S(1)} %shard_map.144), channel_id=1, source_target_pairs={{0,1},{1,0},{2,3},{3,2},{4,5},{5,4},{6,7},{7,6},{8,9},{9,8},{10,11... | collective-permute-start | bytes 12296 | tf_op jit(solution)/shard_map/ppermute | solution.py:28

commit v7 on v6

--- a/solution.py
+++ b/solution.py
@@ -246,25 +246,25 @@
     return first, second, values_in - first - second
 
 
-def qkv_kernel(
-    x_hbm, gain_hbm, mlp_gain_hbm, mask_hbm, lengths_hbm, order_hbm, wq_hbm, wk_hbm, wv_hbm,
-    mine_ref, other_ref, x_ref, mlp_gain_ref, live_ref,
-    gain_ref, mask_ref, lengths_ref, order_ref, *scratch,
+def prepare_kernel(
+    x_hbm, gain_hbm, mlp_gain_hbm, mask_hbm, lengths_hbm, order_hbm, key_hbm, value_hbm,
+    scaled_ref, squares_ref, live_ref, x_ref, mlp_gain_ref, key_ref, value_ref,
+    gain_ref, mask_ref, lengths_ref, order_ref, sems,
 ):
     core = lax.axis_index("core")
     n_blocks = lax.axis_size("chip") * 2
     my_block = 2 * lax.axis_index("chip") + core
-    w_refs, sems = scratch[:-1], scratch[-1]
-    small = [
+    half = key_ref.shape[2]
+    heads = pl.ds(pl.multiple_of((1 - core) * half, LANES), half)
+    pairs = [
         (x_hbm, x_ref), (gain_hbm, gain_ref), (mask_hbm, mask_ref), (lengths_hbm, lengths_ref),
         (order_hbm, order_ref), (mlp_gain_hbm, mlp_gain_ref),
+        (key_hbm.at[:, :, heads], key_ref), (value_hbm.at[:, :, heads], value_ref),
     ]
-    copies = [pltpu.make_async_copy(src, dst, sems.at[i]) for i, (src, dst) in enumerate(small)]
-    for w_hbm, w_ref in zip((wk_hbm, wv_hbm, wq_hbm), w_refs):
-        copies.append(pltpu.make_async_copy(w_hbm, w_ref, sems.at[len(copies)]))
+    copies = [pltpu.make_async_copy(src, dst, sems.at[i]) for i, (src, dst) in enumerate(pairs)]
     for copy in copies:
         copy.start()
-    for copy in copies[: len(small)]:
+    for copy in copies[:-2]:
         copy.wait()
     n_req, span = live_ref.shape
     slot = lax.broadcasted_iota(jnp.int32, (1, span), 1)
@@ -274,25 +274,36 @@
         live = (begin + slot < lengths_ref[r]) & (mask_ref[r : r + 1, :] == 1)
         live_ref[r : r + 1, :] = live.astype(jnp.float32)
     x_rows = x_ref[...].astype(jnp.float32)
-    scaled_in = (x_rows * gain_ref[...]).astype(jnp.bfloat16)
+    scaled_ref[...] = (x_rows * gain_ref[...]).astype(jnp.bfloat16)
     squares = jnp.sum(x_rows * x_rows, axis=1, keepdims=True)
-    proj = []
-    for w_ref, copy in zip(w_refs, copies[len(small) :]):
+    squares_ref[...] = jnp.broadcast_to(squares, squares_ref.shape)
+    for copy in copies[-2:]:
         copy.wait()
-        proj.append(jnp.dot(scaled_in, w_ref[...], preferred_element_type=jnp.float32))
-    proj = jnp.concatenate([proj[2], proj[0], proj[1]], axis=1)
-    at, start = 0, 0
-    for w_hbm in (wq_hbm, wk_hbm, wv_hbm):
-        half = w_hbm.shape[1] // 2
-        low, high = proj[:, start : start + half], proj[:, start + half : start + 2 * half]
-        mine_ref[:, at : at + half] = jnp.where(core == 0, low, high)
-        other_ref[:, at : at + half] = jnp.where(core == 0, high, low)
+
+
+def qkv_columns(scaled_ref, w_refs, core, out_ref):
+    at = 0
+    for w_ref in w_refs:
+        half = w_ref.shape[1] // 2
+        mine = pl.ds(pl.multiple_of(core * half, LANES), half)
+        out_ref[:, at : at + half] = jnp.dot(
+            scaled_ref[...], w_ref[:, mine], preferred_element_type=jnp.float32
+        )
         at += half
-        start += 2 * half
-    square_cols = jnp.broadcast_to(squares, (x_rows.shape[0], LANES))
-    mine_ref[:, at:] = square_cols
-    other_ref[:, at : at + LANES] = square_cols
+    return at
+
+
+def qkv_other_kernel(scaled_ref, squares_ref, live_ref, wq_ref, wk_ref, wv_ref, other_ref):
+    other = 1 - lax.axis_index("core")
+    at = qkv_columns(scaled_ref, (wq_ref, wk_ref, wv_ref), other, other_ref)
+    other_ref[:, at : at + LANES] = squares_ref[...]
     other_ref[:, at + LANES :] = live_ref[...]
+
+
+def qkv_mine_kernel(scaled_ref, squares_ref, wq_ref, wk_ref, wv_ref, mine_ref):
+    core = lax.axis_index("core")
+    at = qkv_columns(scaled_ref, (wq_ref, wk_ref, wv_ref), core, mine_ref)
+    mine_ref[:, at:] = squares_ref[...]
 
 
 SCALE_UNIT = 1024.0
@@ -360,10 +371,10 @@
     scores, live = [], []
     for r in range(n_req):
         blocks = []
-        for keys in (key_own, key_peer):
+        for keys in (key_own[r, :, mine], key_peer[r]):
             blocks.append(
                 lax.dot_general(
-                    spread[r * heads : (r + 1) * heads, :], keys[r, :, mine],
+                    spread[r * heads : (r + 1) * heads, :], keys,
                     (((1,), (1,)), ((), ())), preferred_element_type=jnp.float32,
                 )
             )
@@ -391,7 +402,7 @@
         wide = jnp.dot(
             rounded[at, :span], value_own[r, :, mine], preferred_element_type=jnp.float32
         ) + jnp.dot(
-            rounded[at, span:], value_peer[r, :, mine], preferred_element_type=jnp.float32
+            rounded[at, span:], value_peer[r], preferred_element_type=jnp.float32
         )
         numer = self_part[at, :]
         for k in range(kv_half):
@@ -438,22 +449,30 @@
     )
 
 
-def up_kernel(x_ref, part_ref, peer_ref, gain_ref, w_ref, hidden_ref, mine_ref, other_ref):
-    core = lax.axis_index("core")
+def up_columns(scaled_mlp, w_ref, core, out_ref):
+    half = out_ref.shape[1] - LANES
+    mine = pl.ds(pl.multiple_of(core * half, LANES), half)
+    out_ref[:, :half] = jnp.dot(scaled_mlp, w_ref[:, mine], preferred_element_type=jnp.float32)
+
+
+def up_other_kernel(
+    x_ref, part_ref, peer_ref, gain_ref, w_ref, hidden_ref, scaled_ref, squares_ref, other_ref
+):
     attn_out = part_ref[...] + peer_ref[...]
     hidden_state = (x_ref[...].astype(jnp.float32) + attn_out).astype(jnp.bfloat16)
     resid_rows = hidden_state.astype(jnp.float32)
     hidden_ref[...] = resid_rows
     scaled_mlp = (resid_rows * gain_ref[...]).astype(jnp.bfloat16)
+    scaled_ref[...] = scaled_mlp
     squares = jnp.sum(resid_rows * resid_rows, axis=1, keepdims=True)
-    up_part = jnp.dot(scaled_mlp, w_ref[...], preferred_element_type=jnp.float32)
-    half = up_part.shape[1] // 2
-    low, high = up_part[:, :half], up_part[:, half:]
-    mine_ref[:, :half] = jnp.where(core == 0, low, high)
-    other_ref[:, :half] = jnp.where(core == 0, high, low)
-    square_cols = jnp.broadcast_to(squares, (resid_rows.shape[0], LANES))
-    mine_ref[:, half:] = square_cols
-    other_ref[:, half:] = square_cols
+    squares_ref[...] = jnp.broadcast_to(squares, squares_ref.shape)
+    other_ref[:, other_ref.shape[1] - LANES :] = squares_ref[...]
+    up_columns(scaled_mlp, w_ref, 1 - lax.axis_index("core"), other_ref)
+
+
+def up_mine_kernel(scaled_ref, squares_ref, w_ref, mine_ref):
+    mine_ref[:, mine_ref.shape[1] - LANES :] = squares_ref[...]
+    up_columns(scaled_ref[...], w_ref, lax.axis_index("core"), mine_ref)
 
 
 def up_message_kernel(mine_ref, arrived_ref, message_ref):
@@ -479,15 +498,18 @@
     out_ref[...] = squared_relu(total[:, :half] * inv_mlp).astype(jnp.bfloat16)
 
 
-def down_kernel(own_ref, oth_ref, w_ref, out_ref):
-    core = lax.axis_index("core")
-    own, oth = own_ref[...], oth_ref[...]
-    half = own.shape[1]
-    low = jnp.where(core == 0, own, oth)
-    high = jnp.where(core == 0, oth, own)
-    out_ref[...] = jnp.dot(
-        low, w_ref[:half, :], preferred_element_type=jnp.float32
-    ) + jnp.dot(high, w_ref[half:, :], preferred_element_type=jnp.float32)
+def down_own_kernel(own_ref, w_ref, out_ref):
+    half = own_ref.shape[1]
+    rows = pl.ds(pl.multiple_of(lax.axis_index("core") * half, LANES), half)
+    out_ref[...] = jnp.dot(own_ref[...], w_ref[rows, :], preferred_element_type=jnp.float32)
+
+
+def down_peer_kernel(own_part, peer_ref, w_ref, out_ref):
+    half = peer_ref.shape[1]
+    rows = pl.ds(pl.multiple_of((1 - lax.axis_index("core")) * half, LANES), half)
+    out_ref[...] = own_part[...] + jnp.dot(
+        peer_ref[...], w_ref[rows, :], preferred_element_type=jnp.float32
+    )
 
 
 def per_device(
@@ -515,30 +537,46 @@
     half_qkv = (heads_here + 2 * kv_here) * HD // 2
     half_up = up_weight.shape[1] // 2
 
-    key_peer, value_peer = swap(key_cache, "core"), swap(value_cache, "core")
     row = (1, d_here)
     small = [hidden_in, attn_gain.reshape(row), mlp_gain.reshape(row), pad_mask]
-    small += [lengths, block_order]
-    mine, other, x_rows, gain, live = local_kernel(
-        qkv_kernel,
+    small += [lengths, block_order, key_cache, value_cache]
+    peer_heads = bf16(*key_cache.shape[:2], key_cache.shape[2] // 2)
+    scaled_in, squares, live, x_rows, gain, key_sent, value_sent = local_kernel(
+        prepare_kernel,
         [
-            f32(n_req, half_qkv + LANES),
-            f32(n_req, half_qkv + LANES + pad_mask.shape[1]),
+            bf16(*hidden_in.shape),
+            f32(n_req, LANES),
+            f32(*pad_mask.shape),
             bf16(*hidden_in.shape),
             f32(*row),
-            f32(*pad_mask.shape),
+            peer_heads,
+            peer_heads,
         ],
-        small + [query_weight, key_weight, value_weight],
+        small,
         flops=4 * 10**9,
         scratch=[
             pltpu.VMEM(row, jnp.float32),
             pltpu.VMEM(pad_mask.shape, jnp.int32),
             pltpu.SMEM(lengths.shape, jnp.int32),
             pltpu.SMEM(block_order.shape, jnp.int32),
-        ]
-        + [pltpu.VMEM(w.shape, w.dtype) for w in (key_weight, value_weight, query_weight)]
-        + [pltpu.SemaphoreType.DMA((len(small) + 3,))],
-        in_hbm=range(len(small) + 3),
+            pltpu.SemaphoreType.DMA((len(small),)),
+        ],
+        in_hbm=range(len(small)),
+    )
+    key_peer, value_peer = swap(key_sent, "core"), swap(value_sent, "core")
+    (other,) = local_kernel(
+        qkv_other_kernel,
+        [f32(n_req, half_qkv + LANES + pad_mask.shape[1])],
+        [scaled_in, squares, live, query_weight, key_weight, value_weight],
+        flops=4 * 10**9,
+        anywhere=(3, 4, 5),
+    )
+    (mine,) = local_kernel(
+        qkv_mine_kernel,
+        [f32(n_req, half_qkv + LANES)],
+        [scaled_in, squares, query_weight, key_weight, value_weight],
+        flops=2 * n_req * d_here * half_qkv,
+        anywhere=(2, 3, 4),
     )
     arrived = swap(other, "core")
     width = mine.shape[1]
@@ -573,12 +611,24 @@
         scratch=[pltpu.VMEM((n_req, heads_here, HD), jnp.float32)],
     )
     head_peer = swap(head_part, "tp")
-    resid_rows, up_mine, up_other = local_kernel(
-        up_kernel,
-        [f32(n_req, d_here)] + [f32(n_req, half_up + LANES)] * 2,
+    resid_rows, scaled_mlp, squares, up_other = local_kernel(
+        up_other_kernel,
+        [
+            f32(n_req, d_here),
+            bf16(n_req, d_here),
+            f32(n_req, LANES),
+            f32(n_req, half_up + LANES),
+        ],
         [x_rows, head_part, head_peer, gain, up_weight],
-        flops=2 * n_req * up_weight.size,
+        flops=n_req * up_weight.size,
         anywhere=(4,),
+    )
+    (up_mine,) = local_kernel(
+        up_mine_kernel,
+        [f32(n_req, half_up + LANES)],
+        [scaled_mlp, squares, up_weight],
+        flops=n_req * up_weight.size,
+        anywhere=(2,),
     )
     (up_message,) = local_kernel(
         up_message_kernel,
@@ -593,11 +643,18 @@
         flops=n_chips * n_req * half_up,
     )
     active_other = swap(active_half, "core")
+    (down_own,) = local_kernel(
+        down_own_kernel,
+        [f32(n_req, d_here)],
+        [active_half, down_weight],
+        flops=n_req * down_weight.size,
+        anywhere=(1,),
+    )
     (down_part,) = local_kernel(
-        down_kernel,
+        down_peer_kernel,
         [f32(n_req, d_here)],
-        [active_half, active_other, down_weight],
-        flops=2 * n_req * down_weight.size,
+        [down_own, active_other, down_weight],
+        flops=n_req * down_weight.size,
         anywhere=(2,),
     )
     mlp_out = sum_tp(down_part)

time: 57.8 us -> 56.9 us (0.984)
  waiting for transfers between devices: 7.52 us -> 6.35 us
    ppermute x7, waiting for transfers between devices: 7.52 us -> 6.35 us  [swap(): return lax.ppermute(values_in, axis, [(i, i ^ 1) for i in range(n)])]
    pallas_call x9 -> x13, Pallas kernels: 4.98 us -> 5.03 us  [local_kernel(): pl.pallas_call(kernel, out_shape=outs, in_specs=in_specs, out_specs=[IN_V...]
where the time goes in v7:
time: 56.9 us; the launch traced here: 56.7 us
  blocking collectives  40.1 us (70%)
  waiting for transfers between devices  6.35 us (11%)
  Pallas kernels  5.03 us (9%)
  starting transfers between devices  4.27 us (8%)
  other arithmetic  0.63 us (1%)
    all_to_all x1, blocking collectives, gather_all(): return lax.all_to_all(copies, axes, 0, 0)  14.4 us
    all_to_all x1, blocking collectives, per_device(): lax.all_to_all(up_message, 'chip', 0, 0)  14.3 us
    all_to_all x1, blocking collectives, per_device(): arrived = lax.all_to_all(message, ('chip', 'core'), 0, 0)  11.4 us
    ppermute x7, waiting for transfers between devices, swap(): return lax.ppermute(values_in, axis, [(i, i ^ 1) for i in range(n)])  6.35 us
    pallas_call x13, Pallas kernels, local_kernel(): pl.pallas_call(kernel, out_shape=outs, in_specs=in_specs, out_specs=[IN_V...  5.03 us
    ppermute x7, starting transfers between devices, swap(): return lax.ppermute(values_in, axis, [(i, i ^ 1) for i in range(n)])  4.27 us
  transfers between devices with their start and end apart: 7, of which 5 were waited for; matrix products, arithmetic and copies ran while one was open for 0% of the time, Pallas kernels for 3%

profile of v7, /device:TPU:0, one launch (start us, length us, event | category | flops | bytes accessed | tf_op | source)
XLA Modules:
  0.0 56.7 jit_solution(13932465328295205079)
XLA Ops:
  0.0 0.0 copy-start
  0.0 0.0 copy-start.2
  0.0 0.0 copy-start.3
  0.0 1.3 %shard_map.136 = (bf16[4,256]{1,0:T(4,128)(2,1)S(1)}, f32[4,128]{1,0:T(4,128)S(1)}, f32[4,128]{1,0:T(4,128)S(1)}, bf16[4,256]{1,0:T(4,128)(2,1)S(1)}, f32[1,256]...) custom-call(bf16[4,256]{1,0:T(4,128)(2,1)} %x_hbm.1, f32[1,256]{1,0:T(1,128)} %bitcast.6, ...), custom_call_target="tpu_custom_call" | custom-call | flops 4000000000 | bytes 1054752 | tf_op jit(solution)/shard_map/pallas_call | solution.py:224
  1.3 0.5 collective-permute-start.1
  1.8 0.1 collective-permute-start.2
  1.9 0.0 copy-done
  1.9 0.0 copy-done.2
  1.9 0.0 copy-done.3
  1.9 0.0 copy-start.5
  1.9 0.2 shard_map.138
  2.1 0.5 collective-permute-start
  2.6 0.2 shard_map.137.mine_ref
  2.8 0.7 %collective-permute-done.arrived_ref = f32[4,1792]{1,0:T(4,128)S(1)} collective-permute-done((f32[4,1792]{1,0:T(4,128)S(1)}, f32[4,1792]{1,0:T(4,128)S(1)}, u32[]{:S(2)}, u32[]{:S(2)}) %collective-permute-start) | collective-permute-done | bytes 28704 | tf_op jit(solution)/shard_map/ppermute | solution.py:28
  3.4 0.1 shard_map.139
  3.6 0.0 collective-permute-done.1.key_peer
  3.6 0.0 collective-permute-done.2.value_peer
  3.6 0.0 slice-start.2
  3.6 14.4 %all_to_all.15 = f16[8,4,1664]{2,1,0:T(4,128)(2,1)S(1)} all-to-all(f16[8,4,1664]{2,1,0:T(4,128)(2,1)S(1)} %broadcast_in_dim.2), channel_id=1, replica_groups=mesh['chip'=8,'core'=2,'tp'=2] {'chip'}, dimensions={0} | all-to-all | bytes 212992 | tf_op jit(solution)/shard_map/all_to_all | solution.py:33
  18.1 0.2 shard_map.140.qkv_ref
  18.2 0.0 copy-done.4
  18.3 0.0 copy-done.5
  18.3 0.0 copy-start.1
  18.3 0.0 slice-start.1
  18.3 0.0 slice-start.3
  18.3 0.5 shard_map.141
  18.8 11.4 %all_to_all.16.arrived_ref = bf16[16,8,640]{2,1,0:T(8,128)(2,1)S(1)} all-to-all(bf16[16,8,640]{2,1,0:T(8,128)(2,1)S(1)} %shard_map.141), channel_id=1, replica_groups=mesh['chip'=8,'core'=2,'tp'=2] {'chip','core'}, dimensions={0} | all-to-all | bytes 327680 | tf_op jit(solution)/shard_map/all_to_all | solution.py:604
  30.2 0.0 copy-done.1
  30.2 0.6 %shard_map.142.part_ref = f32[4,256]{1,0:T(4,128)S(1)} custom-call(bf16[16,8,640]{2,1,0:T(8,128)(2,1)S(1)} %all_to_all.16.arrived_ref, bf16[2048,256]{1,0:T(8,128)(2,1)S(1)} %copy-done.1), custom_call_target="tpu_custom_call" | custom-call | flops 4194304 | bytes 1212416 | tf_op jit(solution)/shard_map/pallas_call | solution.py:224
  30.8 1.5 %collective-permute-start.3 = (f32[4,256]{1,0:T(4,128)S(1)}, f32[4,256]{1,0:T(4,128)S(1)}, u32[]{:S(2)}, u32[]{:S(2)}) collective-permute-start(f32[4,256]{1,0:T(4,128)S(1)} %shard_map.142.part_ref), channel_id=1, source_target_pairs={{0,1},{1,0},{2,3},{3,2},{4,5},{5,4},{6,7},{7,6},{8,9},{9,8},{10,11... | collective-permute-start | bytes 12296 | tf_op jit(solution)/shard_map/ppermute | solution.py:28
  32.3 2.1 %collective-permute-done.3.peer_ref = f32[4,256]{1,0:T(4,128)S(1)} collective-permute-done((f32[4,256]{1,0:T(4,128)S(1)}, f32[4,256]{1,0:T(4,128)S(1)}, u32[]{:S(2)}, u32[]{:S(2)}) %collective-permute-start.3) | collective-permute-done | bytes 4128 | tf_op jit(solution)/shard_map/ppermute | solution.py:28
  34.4 0.0 slice-done
  34.4 0.0 slice-done.1
  34.4 0.5 shard_map.143
  34.9 0.0 collective-permute-start.4
  35.0 0.5 shard_map.144.mine_ref
  35.4 0.8 %collective-permute-done.4.arrived_ref = f32[4,5504]{1,0:T(4,128)S(1)} collective-permute-done((f32[4,5504]{1,0:T(4,128)S(1)}, f32[4,5504]{1,0:T(4,128)S(1)}, u32[]{:S(2)}, u32[]{:S(2)}) %collective-permute-start.4) | collective-permute-done | bytes 88096 | tf_op jit(solution)/shard_map/ppermute | solution.py:28
  36.3 14.3 %all_to_all.17.arrived_ref = bf16[8,4,5504]{2,1,0:T(4,128)(2,1)S(1)} all-to-all(bf16[8,4,5504]{2,1,0:T(4,128)(2,1)S(1)} %shard_map.145), channel_id=1, replica_groups=mesh['chip'=8,'core'=2,'tp'=2] {'chip'}, dimensions={0} | all-to-all | bytes 704512 | tf_op jit(solution)/shard_map/all_to_all | solution.py:642
  50.6 0.1 shard_map.146.own_ref
  50.7 0.1 collective-permute-start.5
  50.8 0.0 slice-done.2
  50.8 0.0 slice-done.3
  50.8 0.5 shard_map.147.own_part
  51.3 0.7 %collective-permute-done.5.peer_ref = bf16[4,5376]{1,0:T(4,128)(2,1)S(1)} collective-permute-done((bf16[4,5376]{1,0:T(4,128)(2,1)S(1)}, bf16[4,5376]{1,0:T(4,128)(2,1)S(1)}, u32[]{:S(2)}, u32[]{:S(2)}) %collective-permute-start.5) | collective-permute-done | bytes 43040 | tf_op jit(solution)/shard_map/ppermute | solution.py:28
  52.0 0.4 shard_map.148
  52.5 1.6 %collective-permute-start.6 = (f32[4,256]{1,0:T(4,128)S(1)}, f32[4,256]{1,0:T(4,128)S(1)}, u32[]{:S(2)}, u32[]{:S(2)}) collective-permute-start(f32[4,256]{1,0:T(4,128)S(1)} %shard_map.148), channel_id=1, source_target_pairs={{0,1},{1,0},{2,3},{3,2},{4,5},{5,4},{6,7},{7,6},{8,9},{9,8},{10,11... | collective-permute-start | bytes 12296 | tf_op jit(solution)/shard_map/ppermute | solution.py:28
  54.0 2.1 %collective-permute-done.6 = f32[4,256]{1,0:T(4,128)S(1)} collective-permute-done((f32[4,256]{1,0:T(4,128)S(1)}, f32[4,256]{1,0:T(4,128)S(1)}, u32[]{:S(2)}, u32[]{:S(2)}) %collective-permute-start.6) | collective-permute-done | bytes 4128 | tf_op jit(solution)/shard_map/ppermute | solution.py:28
  56.1 0.6 %add_convert_fusion = bf16[4,256]{1,0:T(4,128)(2,1)} fusion(f32[4,256]{1,0:T(4,128)S(1)} %get-tuple-element.31, f32[4,256]{1,0:T(4,128)S(1)} %shard_map.148, f32[4,256]{1,0:T(4,128)S(1)} %collective-permute-done.6), kind=kLoop, calls=%fused_computation | loop fusion | flops 3072 | bytes 14336 | tf_op jit(solution)/shard_map/convert_element_type | solution.py:661
  (9 shorter events, 0.1 us)
Async XLA Ops:
  0.0 1.9 %copy-start = (bf16[256,2048]{1,0:T(8,128)(2,1)S(1)}, bf16[256,2048]{1,0:T(8,128)(2,1)}, u32[]{:S(2)}) copy-start(bf16[256,2048]{1,0:T(8,128)(2,1)} %wq_ref.3) | copy-start | bytes 3145732
  0.0 1.9 %copy-start.2 = (bf16[256,512]{1,0:T(8,128)(2,1)S(1)}, bf16[256,512]{1,0:T(8,128)(2,1)}, u32[]{:S(2)}) copy-start(bf16[256,512]{1,0:T(8,128)(2,1)} %wk_ref.3) | copy-start | bytes 786436
  0.0 1.9 %copy-start.3 = (bf16[256,512]{1,0:T(8,128)(2,1)S(1)}, bf16[256,512]{1,0:T(8,128)(2,1)}, u32[]{:S(2)}) copy-start(bf16[256,512]{1,0:T(8,128)(2,1)} %wv_ref.3) | copy-start | bytes 786436
  1.3 2.3 %collective-permute-start.1 = (bf16[4,128,256]{2,1,0:T(8,128)(2,1)S(1)}, bf16[4,128,256]{2,1,0:T(8,128)(2,1)S(1)}, u32[]{:S(2)}, u32[]{:S(2)}) collective-permute-start(bf16[4,128,256]{2,1,0:T(8,128)(2,1)S(1)} %get-tuple-element.24), channel_id=1, source_target_pairs={{0,2},{2,0},{1,3},{3,1},{4,6},{6,4},{5,7},{7,5},{8,10},{10,8},{9,1... | collective-permute-start | bytes 786440 | tf_op jit(solution)/shard_map/ppermute | solution.py:28
  1.8 1.8 %collective-permute-start.2 = (bf16[4,128,256]{2,1,0:T(8,128)(2,1)S(1)}, bf16[4,128,256]{2,1,0:T(8,128)(2,1)S(1)}, u32[]{:S(2)}, u32[]{:S(2)}) collective-permute-start(bf16[4,128,256]{2,1,0:T(8,128)(2,1)S(1)} %get-tuple-element.25), channel_id=1, source_target_pairs={{0,2},{2,0},{1,3},{3,1},{4,6},{6,4},{5,7},{7,5},{8,10},{10,8},{9,1... | collective-permute-start | bytes 786440 | tf_op jit(solution)/shard_map/ppermute | solution.py:28
  1.9 16.3 %copy-start.4 = (bf16[4,128,512]{2,1,0:T(8,128)(2,1)S(1)}, bf16[4,128,512]{2,1,0:T(8,128)(2,1)}, u32[]{:S(2)}) copy-start(bf16[4,128,512]{2,1,0:T(8,128)(2,1)} %key_own.1) | copy-start | bytes 1572868
  1.9 16.3 %copy-start.5 = (bf16[4,128,512]{2,1,0:T(8,128)(2,1)S(1)}, bf16[4,128,512]{2,1,0:T(8,128)(2,1)}, u32[]{:S(2)}) copy-start(bf16[4,128,512]{2,1,0:T(8,128)(2,1)} %value_own.1) | copy-start | bytes 1572868
  2.1 1.3 %collective-permute-start = (f32[4,1792]{1,0:T(4,128)S(1)}, f32[4,1792]{1,0:T(4,128)S(1)}, u32[]{:S(2)}, u32[]{:S(2)}) collective-permute-start(f32[4,1792]{1,0:T(4,128)S(1)} %shard_map.138), channel_id=1, source_target_pairs={{0,2},{2,0},{1,3},{3,1},{4,6},{6,4},{5,7},{7,5},{8,10},{10,8},{9,1... | collective-permute-start | bytes 86024 | tf_op jit(solution)/shard_map/ppermute | solution.py:28
  3.6 47.2 %slice-start.2 = ((s8[5505024]{0:T(1024)(128)(4,1)}), s8[4194304]{0:T(1024)(128)(4,1)S(1)}, s32[]{:S(2)}) async-start(s8[5505024]{0:T(1024)(128)(4,1)} %bitcast.4), calls=%async_computation.5 | async-start | bytes 8388608
  18.0 16.4 %slice-start = ((s8[5505024]{0:T(1024)(128)(4,1)}), s8[4194304]{0:T(1024)(128)(4,1)S(1)}, s32[]{:S(2)}) async-start(s8[5505024]{0:T(1024)(128)(4,1)} %bitcast.2), calls=%async_computation.3 | async-start | bytes 8388608
  18.3 12.0 %copy-start.1 = (bf16[2048,256]{1,0:T(8,128)(2,1)S(1)}, bf16[2048,256]{1,0:T(8,128)(2,1)}, u32[]{:S(2)}) copy-start(bf16[2048,256]{1,0:T(8,128)(2,1)} %w_ref.5) | copy-start | bytes 3145732
  18.3 16.2 %slice-start.1 = ((s8[5505024]{0:T(1024)(128)(4,1)}), s8[1310720]{0:T(1024)(128)(4,1)S(1)}, s32[]{:S(2)}) async-start(s8[5505024]{0:T(1024)(128)(4,1)} %bitcast.2), calls=%async_computation.4 | async-start | bytes 2621440
  18.3 32.5 %slice-start.3 = ((s8[5505024]{0:T(1024)(128)(4,1)}), s8[1310720]{0:T(1024)(128)(4,1)S(1)}, s32[]{:S(2)}) async-start(s8[5505024]{0:T(1024)(128)(4,1)} %bitcast.4), calls=%async_computation.6 | async-start | bytes 2621440
  30.8 3.6 %collective-permute-start.3 = (f32[4,256]{1,0:T(4,128)S(1)}, f32[4,256]{1,0:T(4,128)S(1)}, u32[]{:S(2)}, u32[]{:S(2)}) collective-permute-start(f32[4,256]{1,0:T(4,128)S(1)} %shard_map.142.part_ref), channel_id=1, source_target_pairs={{0,1},{1,0},{2,3},{3,2},{4,5},{5,4},{6,7},{7,6},{8,9},{9,8},{10,11... | collective-permute-start | bytes 12296 | tf_op jit(solution)/shard_map/ppermute | solution.py:28
  34.9 1.3 %collective-permute-start.4 = (f32[4,5504]{1,0:T(4,128)S(1)}, f32[4,5504]{1,0:T(4,128)S(1)}, u32[]{:S(2)}, u32[]{:S(2)}) collective-permute-start(f32[4,5504]{1,0:T(4,128)S(1)} %get-tuple-element.34), channel_id=1, source_target_pairs={{0,2},{2,0},{1,3},{3,1},{4,6},{6,4},{5,7},{7,5},{8,10},{10,8},{9,1... | collective-permute-start | bytes 264200 | tf_op jit(solution)/shard_map/ppermute | solution.py:28
  50.7 1.3 %collective-permute-start.5 = (bf16[4,5376]{1,0:T(4,128)(2,1)S(1)}, bf16[4,5376]{1,0:T(4,128)(2,1)S(1)}, u32[]{:S(2)}, u32[]{:S(2)}) collective-permute-start(bf16[4,5376]{1,0:T(4,128)(2,1)S(1)} %shard_map.146.own_ref), channel_id=1, source_target_pairs={{0,2},{2,0},{1,3},{3,1},{4,6},{6,4},{5,7},{7,5},{8,10},{10,8},{9,1... | collective-permute-start | bytes 129032 | tf_op jit(solution)/shard_map/ppermute | solution.py:28
  52.5 3.7 %collective-permute-start.6 = (f32[4,256]{1,0:T(4,128)S(1)}, f32[4,256]{1,0:T(4,128)S(1)}, u32[]{:S(2)}, u32[]{:S(2)}) collective-permute-start(f32[4,256]{1,0:T(4,128)S(1)} %shard_map.148), channel_id=1, source_target_pairs={{0,1},{1,0},{2,3},{3,2},{4,5},{5,4},{6,7},{7,6},{8,9},{9,8},{10,11... | collective-permute-start | bytes 12296 | tf_op jit(solution)/shard_map/ppermute | solution.py:28

commit v8 on v7

--- a/solution.py
+++ b/solution.py
@@ -26,6 +26,10 @@
 def swap(values_in, axis):
     n = lax.axis_size(axis)
     return lax.ppermute(values_in, axis, [(i, i ^ 1) for i in range(n)])
+
+
+def swap_diagonal(values_in):
+    return lax.ppermute(values_in, ("core", "tp"), [(i, 3 - i) for i in range(4)])
 
 
 def gather_all(values_in, axes, n):
@@ -214,6 +218,14 @@
 IN_VMEM = pl.BlockSpec(memory_space=pltpu.VMEM)
 
 
+def chip_turn(chip):
+    return chip // 2 % 2
+
+
+def head_half():
+    return (lax.axis_index("core") + chip_turn(lax.axis_index("chip"))) % 2
+
+
 def local_kernel(kernel, outs, operands, flops, scratch=(), in_hbm=(), anywhere=()):
     in_specs, placed, moved = [], [], 0
     for i, x in enumerate(operands):
@@ -248,18 +260,18 @@
 
 def prepare_kernel(
     x_hbm, gain_hbm, mlp_gain_hbm, mask_hbm, lengths_hbm, order_hbm, key_hbm, value_hbm,
-    scaled_ref, squares_ref, live_ref, x_ref, mlp_gain_ref, key_ref, value_ref,
+    scaled_ref, squares_ref, live_ref, x_ref, mlp_gain_ref, cache_ref,
     gain_ref, mask_ref, lengths_ref, order_ref, sems,
 ):
     core = lax.axis_index("core")
     n_blocks = lax.axis_size("chip") * 2
     my_block = 2 * lax.axis_index("chip") + core
-    half = key_ref.shape[2]
-    heads = pl.ds(pl.multiple_of((1 - core) * half, LANES), half)
+    half = cache_ref.shape[3]
+    heads = pl.ds(pl.multiple_of((1 - head_half()) * half, LANES), half)
     pairs = [
         (x_hbm, x_ref), (gain_hbm, gain_ref), (mask_hbm, mask_ref), (lengths_hbm, lengths_ref),
         (order_hbm, order_ref), (mlp_gain_hbm, mlp_gain_ref),
-        (key_hbm.at[:, :, heads], key_ref), (value_hbm.at[:, :, heads], value_ref),
+        (key_hbm.at[:, :, heads], cache_ref.at[0]), (value_hbm.at[:, :, heads], cache_ref.at[1]),
     ]
     copies = [pltpu.make_async_copy(src, dst, sems.at[i]) for i, (src, dst) in enumerate(pairs)]
     for copy in copies:
@@ -281,11 +293,11 @@
         copy.wait()
 
 
-def qkv_columns(scaled_ref, w_refs, core, out_ref):
+def qkv_columns(scaled_ref, w_refs, side, out_ref):
     at = 0
     for w_ref in w_refs:
         half = w_ref.shape[1] // 2
-        mine = pl.ds(pl.multiple_of(core * half, LANES), half)
+        mine = pl.ds(pl.multiple_of(side * half, LANES), half)
         out_ref[:, at : at + half] = jnp.dot(
             scaled_ref[...], w_ref[:, mine], preferred_element_type=jnp.float32
         )
@@ -294,15 +306,14 @@
 
 
 def qkv_other_kernel(scaled_ref, squares_ref, live_ref, wq_ref, wk_ref, wv_ref, other_ref):
-    other = 1 - lax.axis_index("core")
+    other = 1 - head_half()
     at = qkv_columns(scaled_ref, (wq_ref, wk_ref, wv_ref), other, other_ref)
     other_ref[:, at : at + LANES] = squares_ref[...]
     other_ref[:, at + LANES :] = live_ref[...]
 
 
 def qkv_mine_kernel(scaled_ref, squares_ref, wq_ref, wk_ref, wv_ref, mine_ref):
-    core = lax.axis_index("core")
-    at = qkv_columns(scaled_ref, (wq_ref, wk_ref, wv_ref), core, mine_ref)
+    at = qkv_columns(scaled_ref, (wq_ref, wk_ref, wv_ref), head_half(), mine_ref)
     mine_ref[:, at:] = squares_ref[...]
 
 
@@ -344,13 +355,13 @@
 
 
 def attention_kernel(
-    qkv_ref, key_own, key_peer, value_own, value_peer, live_own, live_peer,
+    qkv_ref, key_own, value_own, cache_peer, live_own, live_peer,
     message_ref, query_ref, key_new_ref, value_new_ref,
 ):
     n_copies, heads, _ = message_ref.shape
     n_req, span = live_own.shape
     half = key_own.shape[2] // 2
-    mine = pl.ds(pl.multiple_of(lax.axis_index("core") * half, LANES), half)
+    mine = pl.ds(pl.multiple_of(head_half() * half, LANES), half)
     kv_half = half // HD
     group = heads // kv_half
     is_first = lax.axis_index("chip") == 0
@@ -371,7 +382,7 @@
     scores, live = [], []
     for r in range(n_req):
         blocks = []
-        for keys in (key_own[r, :, mine], key_peer[r]):
+        for keys in (key_own[r, :, mine], cache_peer[0, r]):
             blocks.append(
                 lax.dot_general(
                     spread[r * heads : (r + 1) * heads, :], keys,
@@ -402,7 +413,7 @@
         wide = jnp.dot(
             rounded[at, :span], value_own[r, :, mine], preferred_element_type=jnp.float32
         ) + jnp.dot(
-            rounded[at, span:], value_peer[r], preferred_element_type=jnp.float32
+            rounded[at, span:], cache_peer[1, r], preferred_element_type=jnp.float32
         )
         numer = self_part[at, :]
         for k in range(kv_half):
@@ -415,11 +426,11 @@
         message_ref[i] = message
 
 
-def combine_kernel(arrived_ref, w_ref, head_ref, attended_ref):
+def combine_kernel(arrived_ref, w_ref, head_ref, rows_ref, attended_ref):
     n_blocks, heads, width = arrived_ref.shape
     n_req = head_ref.shape[0]
     for c in range(2):
-        blocks = range(c, n_blocks, 2)
+        blocks = [2 * chip + (c + chip_turn(chip)) % 2 for chip in range(n_blocks // 2)]
         totals, tops = [], []
         for b in blocks:
             tile = arrived_ref[b, :, width - LANES :].astype(jnp.float32)
@@ -444,9 +455,13 @@
                 numer = numer + part * fade[:, r : r + 1]
             attended_ref[r, c * heads : (c + 1) * heads, :] = numer / denominator[:, r : r + 1]
     attended = jnp.concatenate([attended_ref[:, h, :] for h in range(2 * heads)], axis=1)
-    head_ref[...] = jnp.dot(
-        attended.astype(jnp.bfloat16), w_ref[...], preferred_element_type=jnp.float32
-    )
+    attended = attended.astype(jnp.bfloat16)
+    rows_ref[...] = attended
+    head_ref[...] = jnp.dot(attended, w_ref[...], preferred_element_type=jnp.float32)
+
+
+def out_kernel(rows_ref, w_ref, head_ref):
+    head_ref[...] = jnp.dot(rows_ref[...], w_ref[...], preferred_element_type=jnp.float32)
 
 
 def up_columns(scaled_mlp, w_ref, core, out_ref):
@@ -498,18 +513,18 @@
     out_ref[...] = squared_relu(total[:, :half] * inv_mlp).astype(jnp.bfloat16)
 
 
+def down_rows(rows_ref, w_ref, core):
+    half = rows_ref.shape[1]
+    mine = pl.ds(pl.multiple_of(core * half, LANES), half)
+    return jnp.dot(rows_ref[...], w_ref[mine, :], preferred_element_type=jnp.float32)
+
+
 def down_own_kernel(own_ref, w_ref, out_ref):
-    half = own_ref.shape[1]
-    rows = pl.ds(pl.multiple_of(lax.axis_index("core") * half, LANES), half)
-    out_ref[...] = jnp.dot(own_ref[...], w_ref[rows, :], preferred_element_type=jnp.float32)
+    out_ref[...] = down_rows(own_ref, w_ref, lax.axis_index("core"))
 
 
 def down_peer_kernel(own_part, peer_ref, w_ref, out_ref):
-    half = peer_ref.shape[1]
-    rows = pl.ds(pl.multiple_of((1 - lax.axis_index("core")) * half, LANES), half)
-    out_ref[...] = own_part[...] + jnp.dot(
-        peer_ref[...], w_ref[rows, :], preferred_element_type=jnp.float32
-    )
+    out_ref[...] = own_part[...] + down_rows(peer_ref, w_ref, 1 - lax.axis_index("core"))
 
 
 def per_device(
@@ -540,8 +555,7 @@
     row = (1, d_here)
     small = [hidden_in, attn_gain.reshape(row), mlp_gain.reshape(row), pad_mask]
     small += [lengths, block_order, key_cache, value_cache]
-    peer_heads = bf16(*key_cache.shape[:2], key_cache.shape[2] // 2)
-    scaled_in, squares, live, x_rows, gain, key_sent, value_sent = local_kernel(
+    scaled_in, squares, live, x_rows, gain, cache_sent = local_kernel(
         prepare_kernel,
         [
             bf16(*hidden_in.shape),
@@ -549,8 +563,7 @@
             f32(*pad_mask.shape),
             bf16(*hidden_in.shape),
             f32(*row),
-            peer_heads,
-            peer_heads,
+            bf16(2, *key_cache.shape[:2], key_cache.shape[2] // 2),
         ],
         small,
         flops=4 * 10**9,
@@ -563,7 +576,6 @@
         ],
         in_hbm=range(len(small)),
     )
-    key_peer, value_peer = swap(key_sent, "core"), swap(value_sent, "core")
     (other,) = local_kernel(
         qkv_other_kernel,
         [f32(n_req, half_qkv + LANES + pad_mask.shape[1])],
@@ -583,34 +595,59 @@
     (qkv_message,) = local_kernel(
         qkv_message_kernel, [f32(*mine.shape)], [mine, arrived], flops=2 * mine.size
     )
-    qkv_message, live_peer, key_peer, value_peer = lax.optimization_barrier(
-        (qkv_message.astype(jnp.float16), arrived[:, width:], key_peer, value_peer)
+    qkv_message, live_peer, *moved = lax.optimization_barrier(
+        (
+            qkv_message.astype(jnp.float16),
+            arrived[:, width:],
+            cache_sent,
+            out_weight,
+        )
+    )
+    cache_peer, out_peer = (swap(x, "core") for x in moved)
+    sides = [
+        [2 * chip + (side + chip_turn(chip)) % 2 for chip in range(n_chips)] for side in range(2)
+    ]
+    qkv_all = lax.all_to_all(
+        jnp.broadcast_to(qkv_message[None], (n_chips,) + qkv_message.shape),
+        ("chip", "core"),
+        0,
+        0,
+        axis_index_groups=sides,
     )
     (qkv_half,) = local_kernel(
         qkv_sum_kernel,
         [bf16(n_req, half_qkv)],
-        [gather_all(qkv_message, "chip", n_chips).astype(jnp.float32)],
+        [qkv_all.astype(jnp.float32)],
         flops=n_chips * n_req * half_qkv,
     )
     half_heads = heads_here // 2
     (message,) = local_kernel(
         attention_kernel,
         [bf16(n_blocks, half_heads, n_req * HD + LANES)],
-        [qkv_half, key_cache, key_peer, value_cache, value_peer, live, live_peer],
-        anywhere=(1, 2, 3, 4),
+        [qkv_half, key_cache, value_cache, cache_peer, live, live_peer],
+        anywhere=(1, 2, 3),
         flops=4 * 10**9,
         scratch=[pltpu.VMEM((n_req, half_heads, HD), jnp.float32)] * 3,
     )
+    message, out_peer = lax.optimization_barrier((message, out_peer))
     arrived = lax.all_to_all(message, ("chip", "core"), 0, 0)
-    (head_part,) = local_kernel(
+    head_sent, attended = local_kernel(
         combine_kernel,
-        [f32(n_req, d_here)],
-        [arrived, out_weight],
+        [f32(n_req, d_here), bf16(n_req, heads_here * HD)],
+        [arrived, out_peer],
         anywhere=(1,),
         flops=2 * n_req * out_weight.size,
         scratch=[pltpu.VMEM((n_req, heads_here, HD), jnp.float32)],
     )
-    head_peer = swap(head_part, "tp")
+    head_peer = swap_diagonal(head_sent)
+    (head_part,) = local_kernel(
+        out_kernel,
+        [f32(n_req, d_here)],
+        [attended, out_weight],
+        anywhere=(1,),
+        flops=2 * n_req * out_weight.size,
+    )
+
     resid_rows, scaled_mlp, squares, up_other = local_kernel(
         up_other_kernel,
         [

time: 56.9 us -> 56.1 us (0.986)
  starting transfers between devices: 4.27 us -> 3.32 us
    ppermute x0 -> x1, waiting for transfers between devices: none -> 2.32 us  [swap_diagonal(): lax.ppermute(values_in, ('core', 'tp'), [(i, 3 - i) for i in range(4)])]
    ppermute x7 -> x6, waiting for transfers between devices: 6.35 us -> 4.18 us  [swap(): return lax.ppermute(values_in, axis, [(i, i ^ 1) for i in range(n)])]
    ppermute x7 -> x6, starting transfers between devices: 4.27 us -> 2.84 us  [swap(): return lax.ppermute(values_in, axis, [(i, i ^ 1) for i in range(n)])]
    all_to_all x1, blocking collectives: 14.4 us -> 13.6 us  [per_device(): lax.all_to_all(jnp.broadcast_to(qkv_message[None], (n_chips,) + qkv_messa...]
    pallas_call x13 -> x14, Pallas kernels: 5.03 us -> 5.29 us  [local_kernel(): pl.pallas_call(kernel, out_shape=outs, in_specs=in_specs, out_specs=[IN_V...]
  transfers between devices with their start and end apart: 7 -> 7, of which waited for: 5 -> 5; matrix products, arithmetic and copies ran while one was open for 0% -> 0% of each run, Pallas kernels for 3% -> 4%
where the time goes in v8:
time: 56.1 us; the launch traced here: 55.8 us
  blocking collectives  39.6 us (71%)
  waiting for transfers between devices  6.49 us (12%)
  Pallas kernels  5.29 us (9%)
  starting transfers between devices  3.32 us (6%)
  other arithmetic  0.63 us (1%)
    all_to_all x1, blocking collectives, per_device(): lax.all_to_all(up_message, 'chip', 0, 0)  14.3 us
    all_to_all x1, blocking collectives, per_device(): lax.all_to_all(jnp.broadcast_to(qkv_message[None], (n_chips,) + qkv_messa...  13.6 us
    all_to_all x1, blocking collectives, per_device(): arrived = lax.all_to_all(message, ('chip', 'core'), 0, 0)  11.7 us
    pallas_call x14, Pallas kernels, local_kernel(): pl.pallas_call(kernel, out_shape=outs, in_specs=in_specs, out_specs=[IN_V...  5.29 us
    ppermute x6, waiting for transfers between devices, swap(): return lax.ppermute(values_in, axis, [(i, i ^ 1) for i in range(n)])  4.18 us
    ppermute x6, starting transfers between devices, swap(): return lax.ppermute(values_in, axis, [(i, i ^ 1) for i in range(n)])  2.84 us
    ppermute x1, waiting for transfers between devices, swap_diagonal(): lax.ppermute(values_in, ('core', 'tp'), [(i, 3 - i) for i in range(4)])  2.32 us
  transfers between devices with their start and end apart: 7, of which 5 were waited for; matrix products, arithmetic and copies ran while one was open for 0% of the time, Pallas kernels for 4%

profile of v8, /device:TPU:0, one launch (start us, length us, event | category | flops | bytes accessed | tf_op | source)
XLA Modules:
  0.0 55.8 jit_solution(2254394566850098275)
XLA Ops:
  0.0 0.0 copy-start
  0.0 0.0 copy-start.2
  0.0 0.0 copy-start.3
  0.0 1.3 %shard_map.136 = (bf16[4,256]{1,0:T(4,128)(2,1)S(1)}, f32[4,128]{1,0:T(4,128)S(1)}, f32[4,128]{1,0:T(4,128)S(1)}, bf16[4,256]{1,0:T(4,128)(2,1)S(1)}, f32[1,256]...) custom-call(bf16[4,256]{1,0:T(4,128)(2,1)} %x_hbm.1, f32[1,256]{1,0:T(1,128)} %bitcast.6, f32[1,256]{1,0:T(1,128)} %bitcast.7, ...), custom_call_target="tpu_custom_call" | custom-call | flops 4000000000 | bytes 1054752 | tf_op jit(solution)/shard_map/pallas_call | solution.py:236
  1.3 0.2 copy-done
  1.4 0.0 copy-done.2
  1.5 0.1 copy-done.3
  1.6 0.0 copy-start.1
  1.6 0.0 copy-start.4
  1.6 0.0 copy-start.5
  1.6 0.2 shard_map.138
  1.8 0.5 collective-permute-start
  2.3 0.2 shard_map.137.mine_ref
  2.5 0.7 %collective-permute-done.arrived_ref = f32[4,1792]{1,0:T(4,128)S(1)} collective-permute-done((f32[4,1792]{1,0:T(4,128)S(1)}, f32[4,1792]{1,0:T(4,128)S(1)}, u32[]{:S(2)}, u32[]{:S(2)}) %collective-permute-start) | collective-permute-done | bytes 28704 | tf_op jit(solution)/shard_map/ppermute | solution.py:28
  3.1 0.1 shard_map.139
  3.2 0.0 copy-done.1
  3.2 0.4 collective-permute-start.2
  3.7 0.2 collective-permute-start.1
  3.9 13.6 %all_to_all.15 = f16[8,4,1664]{2,1,0:T(4,128)(2,1)S(1)} all-to-all(f16[8,4,1664]{2,1,0:T(4,128)(2,1)S(1)} %broadcast_in_dim.2), channel_id=1, replica_groups={{0,4,10,14,16,20,26,30},{2,6,8,12,18,22,24,28},{1,5,11,15,17,21,27,31},..., dimensions={0} | all-to-all | bytes 212992 | tf_op jit(solution)/shard_map/all_to_all | solution.py:610
  17.5 0.0 slice-start
  17.5 0.2 shard_map.140.qkv_ref
  17.7 0.0 collective-permute-done.1.cache_peer
  17.7 0.0 copy-done.4
  17.7 0.0 copy-done.5
  17.7 0.5 shard_map.141
  18.2 0.0 collective-permute-done.2.w_ref
  18.2 11.7 %all_to_all.16.arrived_ref = bf16[16,8,640]{2,1,0:T(8,128)(2,1)S(1)} all-to-all(bf16[16,8,640]{2,1,0:T(8,128)(2,1)S(1)} %shard_map.141), channel_id=1, replica_groups=mesh['chip'=8,'core'=2,'tp'=2] {'chip','core'}, dimensions={0} | all-to-all | bytes 327680 | tf_op jit(solution)/shard_map/all_to_all | solution.py:633
  29.9 0.6 %shard_map.142 = (f32[4,256]{1,0:T(4,128)S(1)}, bf16[4,2048]{1,0:T(4,128)(2,1)S(1)}) custom-call(bf16[16,8,640]{2,1,0:T(8,128)(2,1)S(1)} %all_to_all.16.arrived_ref, bf16[2048,256]{1,0:T(8,128)(2,1)S(1)} %collective-permute-done.2.w_ref), custom_call_target="tpu_custom_call" | custom-call | flops 4194304 | bytes 1212416 | tf_op jit(solution)/shard_map/pallas_call | solution.py:236
  30.5 0.5 collective-permute-start.3
  31.0 0.2 shard_map.143.part_ref
  31.2 2.3 %collective-permute-done.3.peer_ref = f32[4,256]{1,0:T(4,128)S(1)} collective-permute-done((f32[4,256]{1,0:T(4,128)S(1)}, f32[4,256]{1,0:T(4,128)S(1)}, u32[]{:S(2)}, u32[]{:S(2)}) %collective-permute-start.3) | collective-permute-done | bytes 4128 | tf_op jit(solution)/shard_map/ppermute | solution.py:32
  33.6 0.0 slice-done
  33.6 0.0 slice-done.1
  33.6 0.5 shard_map.144
  34.1 0.2 collective-permute-start.4
  34.2 0.5 shard_map.145.mine_ref
  34.7 0.7 %collective-permute-done.4.arrived_ref = f32[4,5504]{1,0:T(4,128)S(1)} collective-permute-done((f32[4,5504]{1,0:T(4,128)S(1)}, f32[4,5504]{1,0:T(4,128)S(1)}, u32[]{:S(2)}, u32[]{:S(2)}) %collective-permute-start.4) | collective-permute-done | bytes 88096 | tf_op jit(solution)/shard_map/ppermute | solution.py:28
  35.4 14.3 %all_to_all.17.arrived_ref = bf16[8,4,5504]{2,1,0:T(4,128)(2,1)S(1)} all-to-all(bf16[8,4,5504]{2,1,0:T(4,128)(2,1)S(1)} %shard_map.146), channel_id=1, replica_groups=mesh['chip'=8,'core'=2,'tp'=2] {'chip'}, dimensions={0} | all-to-all | bytes 704512 | tf_op jit(solution)/shard_map/all_to_all | solution.py:679
  49.7 0.1 shard_map.147.own_ref
  49.9 0.1 collective-permute-start.5
  49.9 0.0 slice-done.2
  50.0 0.0 slice-done.3
  50.0 0.5 shard_map.148.own_part
  50.4 0.7 %collective-permute-done.5.peer_ref = bf16[4,5376]{1,0:T(4,128)(2,1)S(1)} collective-permute-done((bf16[4,5376]{1,0:T(4,128)(2,1)S(1)}, bf16[4,5376]{1,0:T(4,128)(2,1)S(1)}, u32[]{:S(2)}, u32[]{:S(2)}) %collective-permute-start.5) | collective-permute-done | bytes 43040 | tf_op jit(solution)/shard_map/ppermute | solution.py:28
  51.1 0.4 shard_map.149
  51.6 1.6 %collective-permute-start.6 = (f32[4,256]{1,0:T(4,128)S(1)}, f32[4,256]{1,0:T(4,128)S(1)}, u32[]{:S(2)}, u32[]{:S(2)}) collective-permute-start(f32[4,256]{1,0:T(4,128)S(1)} %shard_map.149), channel_id=1, source_target_pairs={{0,1},{1,0},{2,3},{3,2},{4,5},{5,4},{6,7},{7,6},{8,9},{9,8},{10,11... | collective-permute-start | bytes 12296 | tf_op jit(solution)/shard_map/ppermute | solution.py:28
  53.2 2.1 %collective-permute-done.6 = f32[4,256]{1,0:T(4,128)S(1)} collective-permute-done((f32[4,256]{1,0:T(4,128)S(1)}, f32[4,256]{1,0:T(4,128)S(1)}, u32[]{:S(2)}, u32[]{:S(2)}) %collective-permute-start.6) | collective-permute-done | bytes 4128 | tf_op jit(solution)/shard_map/ppermute | solution.py:28
  55.3 0.6 %add_convert_fusion = bf16[4,256]{1,0:T(4,128)(2,1)} fusion(f32[4,256]{1,0:T(4,128)S(1)} %get-tuple-element.37, f32[4,256]{1,0:T(4,128)S(1)} %shard_map.149, f32[4,256]{1,0:T(4,128)S(1)} %collective-permute-done.6), kind=kLoop, calls=%fused_computation | loop fusion | flops 3072 | bytes 14336 | tf_op jit(solution)/shard_map/convert_element_type | solution.py:698
  (10 shorter events, 0.1 us)
Async XLA Ops:
  0.0 1.4 %copy-start = (bf16[256,2048]{1,0:T(8,128)(2,1)S(1)}, bf16[256,2048]{1,0:T(8,128)(2,1)}, u32[]{:S(2)}) copy-start(bf16[256,2048]{1,0:T(8,128)(2,1)} %wq_ref.3) | copy-start | bytes 3145732
  0.0 1.5 %copy-start.2 = (bf16[256,512]{1,0:T(8,128)(2,1)S(1)}, bf16[256,512]{1,0:T(8,128)(2,1)}, u32[]{:S(2)}) copy-start(bf16[256,512]{1,0:T(8,128)(2,1)} %wk_ref.3) | copy-start | bytes 786436
  0.0 1.6 %copy-start.3 = (bf16[256,512]{1,0:T(8,128)(2,1)S(1)}, bf16[256,512]{1,0:T(8,128)(2,1)}, u32[]{:S(2)}) copy-start(bf16[256,512]{1,0:T(8,128)(2,1)} %wv_ref.3) | copy-start | bytes 786436
  1.6 1.7 %copy-start.1 = (bf16[2048,256]{1,0:T(8,128)(2,1)S(1)}, bf16[2048,256]{1,0:T(8,128)(2,1)}, u32[]{:S(2)}) copy-start(bf16[2048,256]{1,0:T(8,128)(2,1)} %w_ref.5) | copy-start | bytes 3145732
  1.6 16.1 %copy-start.4 = (bf16[4,128,512]{2,1,0:T(8,128)(2,1)S(1)}, bf16[4,128,512]{2,1,0:T(8,128)(2,1)}, u32[]{:S(2)}) copy-start(bf16[4,128,512]{2,1,0:T(8,128)(2,1)} %key_own.1) | copy-start | bytes 1572868
  1.6 16.1 %copy-start.5 = (bf16[4,128,512]{2,1,0:T(8,128)(2,1)S(1)}, bf16[4,128,512]{2,1,0:T(8,128)(2,1)}, u32[]{:S(2)}) copy-start(bf16[4,128,512]{2,1,0:T(8,128)(2,1)} %value_own.1) | copy-start | bytes 1572868
  1.8 1.3 %collective-permute-start = (f32[4,1792]{1,0:T(4,128)S(1)}, f32[4,1792]{1,0:T(4,128)S(1)}, u32[]{:S(2)}, u32[]{:S(2)}) collective-permute-start(f32[4,1792]{1,0:T(4,128)S(1)} %shard_map.138), channel_id=1, source_target_pairs={{0,2},{2,0},{1,3},{3,1},{4,6},{6,4},{5,7},{7,5},{8,10},{10,8},{9,1... | collective-permute-start | bytes 86024 | tf_op jit(solution)/shard_map/ppermute | solution.py:28
  3.2 14.9 %collective-permute-start.2 = (bf16[2048,256]{1,0:T(8,128)(2,1)S(1)}, bf16[2048,256]{1,0:T(8,128)(2,1)S(1)}, u32[]{:S(2)}, u32[]{:S(2)}) collective-permute-start(bf16[2048,256]{1,0:T(8,128)(2,1)S(1)} %copy-done.1), channel_id=1, source_target_pairs={{0,2},{2,0},{1,3},{3,1},{4,6},{6,4},{5,7},{7,5},{8,10},{10,8},{9,1... | collective-permute-start | bytes 3145736 | tf_op jit(solution)/shard_map/ppermute | solution.py:28
  3.7 14.0 %collective-permute-start.1 = (bf16[2,4,128,256]{3,2,1,0:T(8,128)(2,1)S(1)}, bf16[2,4,128,256]{3,2,1,0:T(8,128)(2,1)S(1)}, u32[]{:S(2)}, u32[]{:S(2)}) collective-permute-start(bf16[2,4,128,256]{3,2,1,0:T(8,128)(2,1)S(1)} %get-tuple-element.29), channel_id=1, source_target_pairs={{0,2},{2,0},{1,3},{3,1},{4,6},{6,4},{5,7},{7,5},{8,10},{10,8},{9,1... | collective-permute-start | bytes 1572872 | tf_op jit(solution)/shard_map/ppermute | solution.py:28
  17.5 16.1 %slice-start = ((s8[5505024]{0:T(1024)(128)(4,1)}), s8[4194304]{0:T(1024)(128)(4,1)S(1)}, s32[]{:S(2)}) async-start(s8[5505024]{0:T(1024)(128)(4,1)} %bitcast.2), calls=%async_computation.3 | async-start | bytes 8388608
  17.7 15.9 %slice-start.1 = ((s8[5505024]{0:T(1024)(128)(4,1)}), s8[1310720]{0:T(1024)(128)(4,1)S(1)}, s32[]{:S(2)}) async-start(s8[5505024]{0:T(1024)(128)(4,1)} %bitcast.2), calls=%async_computation.4 | async-start | bytes 2621440
  29.9 20.0 %slice-start.2 = ((s8[5505024]{0:T(1024)(128)(4,1)}), s8[4194304]{0:T(1024)(128)(4,1)S(1)}, s32[]{:S(2)}) async-start(s8[5505024]{0:T(1024)(128)(4,1)} %bitcast.4), calls=%async_computation.5 | async-start | bytes 8388608
  30.5 3.0 %collective-permute-start.3 = (f32[4,256]{1,0:T(4,128)S(1)}, f32[4,256]{1,0:T(4,128)S(1)}, u32[]{:S(2)}, u32[]{:S(2)}) collective-permute-start(f32[4,256]{1,0:T(4,128)S(1)} %get-tuple-element.35), channel_id=1, source_target_pairs={{0,3},{1,2},{2,1},{3,0},{4,7},{5,6},{6,5},{7,4},{8,11},{9,10},{10,... | collective-permute-start | bytes 12296 | tf_op jit(solution)/shard_map/ppermute | solution.py:32
  33.6 16.4 %slice-start.3 = ((s8[5505024]{0:T(1024)(128)(4,1)}), s8[1310720]{0:T(1024)(128)(4,1)S(1)}, s32[]{:S(2)}) async-start(s8[5505024]{0:T(1024)(128)(4,1)} %bitcast.4), calls=%async_computation.6 | async-start | bytes 2621440
  34.1 1.3 %collective-permute-start.4 = (f32[4,5504]{1,0:T(4,128)S(1)}, f32[4,5504]{1,0:T(4,128)S(1)}, u32[]{:S(2)}, u32[]{:S(2)}) collective-permute-start(f32[4,5504]{1,0:T(4,128)S(1)} %get-tuple-element.40), channel_id=1, source_target_pairs={{0,2},{2,0},{1,3},{3,1},{4,6},{6,4},{5,7},{7,5},{8,10},{10,8},{9,1... | collective-permute-start | bytes 264200 | tf_op jit(solution)/shard_map/ppermute | solution.py:28
  49.9 1.3 %collective-permute-start.5 = (bf16[4,5376]{1,0:T(4,128)(2,1)S(1)}, bf16[4,5376]{1,0:T(4,128)(2,1)S(1)}, u32[]{:S(2)}, u32[]{:S(2)}) collective-permute-start(bf16[4,5376]{1,0:T(4,128)(2,1)S(1)} %shard_map.147.own_ref), channel_id=1, source_target_pairs={{0,2},{2,0},{1,3},{3,1},{4,6},{6,4},{5,7},{7,5},{8,10},{10,8},{9,1... | collective-permute-start | bytes 129032 | tf_op jit(solution)/shard_map/ppermute | solution.py:28
  51.6 3.7 %collective-permute-start.6 = (f32[4,256]{1,0:T(4,128)S(1)}, f32[4,256]{1,0:T(4,128)S(1)}, u32[]{:S(2)}, u32[]{:S(2)}) collective-permute-start(f32[4,256]{1,0:T(4,128)S(1)} %shard_map.149), channel_id=1, source_target_pairs={{0,1},{1,0},{2,3},{3,2},{4,5},{5,4},{6,7},{7,6},{8,9},{9,8},{10,11... | collective-permute-start | bytes 12296 | tf_op jit(solution)/shard_map/ppermute | solution.py:28

commit v9 on v8

--- a/solution.py
+++ b/solution.py
@@ -426,42 +426,53 @@
         message_ref[i] = message
 
 
-def combine_kernel(arrived_ref, w_ref, head_ref, rows_ref, attended_ref):
-    n_blocks, heads, width = arrived_ref.shape
-    n_req = head_ref.shape[0]
-    for c in range(2):
-        blocks = [2 * chip + (c + chip_turn(chip)) % 2 for chip in range(n_blocks // 2)]
-        totals, tops = [], []
-        for b in blocks:
-            tile = arrived_ref[b, :, width - LANES :].astype(jnp.float32)
-            tile = (
-                tile
-                + pltpu.roll(tile, LANES - PIECE, 1)
-                + pltpu.roll(tile, LANES - 2 * PIECE, 1)
-            )
-            totals.append(tile)
-            tops.append(pltpu.roll(tile, LANES - TOP_AT, 1))
-        final_top = tops[0]
-        for top in tops[1:]:
-            final_top = jnp.maximum(final_top, top)
-        fades = [jnp.exp(top - final_top) for top in tops]
-        denominator = totals[0] * fades[0]
-        for total, fade in zip(totals[1:], fades[1:]):
-            denominator = denominator + total * fade
-        for r in range(n_req):
-            numer = jnp.zeros((heads, HD), jnp.float32)
-            for b, fade in zip(blocks, fades):
-                part = arrived_ref[b, :, r * HD : (r + 1) * HD].astype(jnp.float32)
-                numer = numer + part * fade[:, r : r + 1]
-            attended_ref[r, c * heads : (c + 1) * heads, :] = numer / denominator[:, r : r + 1]
-    attended = jnp.concatenate([attended_ref[:, h, :] for h in range(2 * heads)], axis=1)
-    attended = attended.astype(jnp.bfloat16)
-    rows_ref[...] = attended
-    head_ref[...] = jnp.dot(attended, w_ref[...], preferred_element_type=jnp.float32)
-
-
-def out_kernel(rows_ref, w_ref, head_ref):
-    head_ref[...] = jnp.dot(rows_ref[...], w_ref[...], preferred_element_type=jnp.float32)
+def combine_kernel(arrived_ref, rows_ref, attended_ref):
+    n_chips, heads, width = arrived_ref.shape
+    n_req = rows_ref.shape[0]
+    totals, tops = [], []
+    for chip in range(n_chips):
+        tile = arrived_ref[chip, :, width - LANES :].astype(jnp.float32)
+        tile = (
+            tile
+            + pltpu.roll(tile, LANES - PIECE, 1)
+            + pltpu.roll(tile, LANES - 2 * PIECE, 1)
+        )
+        totals.append(tile)
+        tops.append(pltpu.roll(tile, LANES - TOP_AT, 1))
+    final_top = tops[0]
+    for top in tops[1:]:
+        final_top = jnp.maximum(final_top, top)
+    fades = [jnp.exp(top - final_top) for top in tops]
+    denominator = totals[0] * fades[0]
+    for total, fade in zip(totals[1:], fades[1:]):
+        denominator = denominator + total * fade
+    for r in range(n_req):
+        numer = jnp.zeros((heads, HD), jnp.float32)
+        for chip, fade in enumerate(fades):
+            part = arrived_ref[chip, :, r * HD : (r + 1) * HD].astype(jnp.float32)
+            numer = numer + part * fade[:, r : r + 1]
+        attended_ref[r] = numer / denominator[:, r : r + 1]
+    rows = jnp.concatenate([attended_ref[:, h, :] for h in range(heads)], axis=1)
+    rows_ref[...] = rows.astype(jnp.bfloat16)
+
+
+def half_rows(rows_ref, w_ref, side):
+    half = rows_ref.shape[1]
+    rows = pl.ds(pl.multiple_of(side * half, LANES), half)
+    return jnp.dot(rows_ref[...], w_ref[rows, :], preferred_element_type=jnp.float32)
+
+
+def out_own_kernel(own_ref, w_ref, out_ref):
+    out_ref[...] = half_rows(own_ref, w_ref, head_half())
+
+
+def out_peer_kernel(own_part, peer_ref, w_ref, out_ref):
+    out_ref[...] = own_part[...] + half_rows(peer_ref, w_ref, 1 - head_half())
+
+
+def out_both_kernel(own_ref, peer_ref, w_ref, out_ref):
+    side = head_half()
+    out_ref[...] = half_rows(own_ref, w_ref, side) + half_rows(peer_ref, w_ref, 1 - side)
 
 
 def up_columns(scaled_mlp, w_ref, core, out_ref):
@@ -513,18 +524,12 @@
     out_ref[...] = squared_relu(total[:, :half] * inv_mlp).astype(jnp.bfloat16)
 
 
-def down_rows(rows_ref, w_ref, core):
-    half = rows_ref.shape[1]
-    mine = pl.ds(pl.multiple_of(core * half, LANES), half)
-    return jnp.dot(rows_ref[...], w_ref[mine, :], preferred_element_type=jnp.float32)
-
-
 def down_own_kernel(own_ref, w_ref, out_ref):
-    out_ref[...] = down_rows(own_ref, w_ref, lax.axis_index("core"))
+    out_ref[...] = half_rows(own_ref, w_ref, lax.axis_index("core"))
 
 
 def down_peer_kernel(own_part, peer_ref, w_ref, out_ref):
-    out_ref[...] = own_part[...] + down_rows(peer_ref, w_ref, 1 - lax.axis_index("core"))
+    out_ref[...] = own_part[...] + half_rows(peer_ref, w_ref, 1 - lax.axis_index("core"))
 
 
 def per_device(
@@ -623,28 +628,41 @@
     half_heads = heads_here // 2
     (message,) = local_kernel(
         attention_kernel,
-        [bf16(n_blocks, half_heads, n_req * HD + LANES)],
+        [bf16(n_chips, half_heads, n_req * HD + LANES)],
         [qkv_half, key_cache, value_cache, cache_peer, live, live_peer],
         anywhere=(1, 2, 3),
         flops=4 * 10**9,
         scratch=[pltpu.VMEM((n_req, half_heads, HD), jnp.float32)] * 3,
     )
     message, out_peer = lax.optimization_barrier((message, out_peer))
-    arrived = lax.all_to_all(message, ("chip", "core"), 0, 0)
-    head_sent, attended = local_kernel(
+    (attended,) = local_kernel(
         combine_kernel,
-        [f32(n_req, d_here), bf16(n_req, heads_here * HD)],
-        [arrived, out_peer],
+        [bf16(n_req, half_heads * HD)],
+        [lax.all_to_all(message, ("chip", "core"), 0, 0, axis_index_groups=sides)],
+        flops=n_chips * n_req * half_heads * HD,
+        scratch=[pltpu.VMEM((n_req, half_heads, HD), jnp.float32)],
+    )
+    attended_peer = swap(attended, "core")
+    (head_own,) = local_kernel(
+        out_own_kernel,
+        [f32(n_req, d_here)],
+        [attended, out_peer],
         anywhere=(1,),
-        flops=2 * n_req * out_weight.size,
-        scratch=[pltpu.VMEM((n_req, heads_here, HD), jnp.float32)],
+        flops=n_req * out_weight.size,
+    )
+    (head_sent,) = local_kernel(
+        out_peer_kernel,
+        [f32(n_req, d_here)],
+        [head_own, attended_peer, out_peer],
+        anywhere=(2,),
+        flops=n_req * out_weight.size,
     )
     head_peer = swap_diagonal(head_sent)
     (head_part,) = local_kernel(
-        out_kernel,
+        out_both_kernel,
         [f32(n_req, d_here)],
-        [attended, out_weight],
-        anywhere=(1,),
+        [attended, attended_peer, out_weight],
+        anywhere=(2,),
         flops=2 * n_req * out_weight.size,
     )
 

time: 56.1 us -> 55 us (0.980)
  blocking collectives: 39.6 us -> 37.2 us
  starting transfers between devices: 3.32 us -> 5.25 us
  waiting for transfers between devices: 6.49 us -> 5.9 us
    all_to_all x1, blocking collectives: 11.7 us -> 9.09 us  [per_device(): lax.all_to_all(message, ('chip', 'core'), 0, 0, axis_index_groups=sides)]
    ppermute x1, waiting for transfers between devices: 2.32 us -> 1.31 us  [swap_diagonal(): lax.ppermute(values_in, ('core', 'tp'), [(i, 3 - i) for i in range(4)])]
    ppermute x1, starting transfers between devices: 0.48 us -> 1.48 us  [swap_diagonal(): lax.ppermute(values_in, ('core', 'tp'), [(i, 3 - i) for i in range(4)])]
    ppermute x6 -> x7, starting transfers between devices: 2.84 us -> 3.77 us  [swap(): return lax.ppermute(values_in, axis, [(i, i ^ 1) for i in range(n)])]
    ppermute x6 -> x7, waiting for transfers between devices: 4.18 us -> 4.59 us  [swap(): return lax.ppermute(values_in, axis, [(i, i ^ 1) for i in range(n)])]
    pallas_call x14 -> x16, Pallas kernels: 5.29 us -> 5.37 us  [local_kernel(): pl.pallas_call(kernel, out_shape=outs, in_specs=in_specs, out_specs=[IN_V...]
  transfers between devices with their start and end apart: 7 -> 8, of which waited for: 5 -> 6; matrix products, arithmetic and copies ran while one was open for 0% -> 0% of each run, Pallas kernels for 4% -> 4%
where the time goes in v9:
time: 55 us; the launch traced here: 54.8 us
  blocking collectives  37.2 us (68%)
  waiting for transfers between devices  5.9 us (11%)
  Pallas kernels  5.37 us (10%)
  starting transfers between devices  5.25 us (10%)
  other arithmetic  0.63 us (1%)
    all_to_all x1, blocking collectives, per_device(): lax.all_to_all(up_message, 'chip', 0, 0)  14.5 us
    all_to_all x1, blocking collectives, per_device(): lax.all_to_all(jnp.broadcast_to(qkv_message[None], (n_chips,) + qkv_messa...  13.6 us
    all_to_all x1, blocking collectives, per_device(): lax.all_to_all(message, ('chip', 'core'), 0, 0, axis_index_groups=sides)  9.09 us
    pallas_call x16, Pallas kernels, local_kernel(): pl.pallas_call(kernel, out_shape=outs, in_specs=in_specs, out_specs=[IN_V...  5.37 us
    ppermute x7, waiting for transfers between devices, swap(): return lax.ppermute(values_in, axis, [(i, i ^ 1) for i in range(n)])  4.59 us
    ppermute x7, starting transfers between devices, swap(): return lax.ppermute(values_in, axis, [(i, i ^ 1) for i in range(n)])  3.77 us
    ppermute x1, starting transfers between devices, swap_diagonal(): lax.ppermute(values_in, ('core', 'tp'), [(i, 3 - i) for i in range(4)])  1.48 us
    ppermute x1, waiting for transfers between devices, swap_diagonal(): lax.ppermute(values_in, ('core', 'tp'), [(i, 3 - i) for i in range(4)])  1.31 us
  transfers between devices with their start and end apart: 8, of which 6 were waited for; matrix products, arithmetic and copies ran while one was open for 0% of the time, Pallas kernels for 4%

profile of v9, /device:TPU:0, one launch (start us, length us, event | category | flops | bytes accessed | tf_op | source)
XLA Modules:
  0.0 54.8 jit_solution(18147255486921779677)
XLA Ops:
  0.0 0.0 copy-start
  0.0 0.0 copy-start.2
  0.0 1.3 %shard_map.136 = (bf16[4,256]{1,0:T(4,128)(2,1)S(1)}, f32[4,128]{1,0:T(4,128)S(1)}, f32[4,128]{1,0:T(4,128)S(1)}, bf16[4,256]{1,0:T(4,128)(2,1)S(1)}, f32[1,256]...) custom-call(bf16[4,256]{1,0:T(4,128)(2,1)} %x_hbm.1, f32[1,256]{1,0:T(1,128)} %bitcast.6, f32[1,256]{1,0:T(1,128)} %bitcast.7, ...), custom_call_target="tpu_custom_call" | custom-call | flops 4000000000 | bytes 1054752 | tf_op jit(solution)/shard_map/pallas_call | solution.py:236
  1.3 0.2 copy-done
  1.4 0.0 copy-done.2
  1.5 0.1 copy-done.3
  1.6 0.2 shard_map.138
  1.8 0.5 collective-permute-start
  2.3 0.2 shard_map.137.mine_ref
  2.5 0.7 %collective-permute-done.arrived_ref = f32[4,1792]{1,0:T(4,128)S(1)} collective-permute-done((f32[4,1792]{1,0:T(4,128)S(1)}, f32[4,1792]{1,0:T(4,128)S(1)}, u32[]{:S(2)}, u32[]{:S(2)}) %collective-permute-start) | collective-permute-done | bytes 28704 | tf_op jit(solution)/shard_map/ppermute | solution.py:28
  3.1 0.1 shard_map.139
  3.2 0.0 copy-done.1
  3.2 0.4 collective-permute-start.2
  3.7 0.2 collective-permute-start.1
  3.9 13.6 %all_to_all.15 = f16[8,4,1664]{2,1,0:T(4,128)(2,1)S(1)} all-to-all(f16[8,4,1664]{2,1,0:T(4,128)(2,1)S(1)} %broadcast_in_dim.2), channel_id=1, replica_groups={{0,4,10,14,16,20,26,30},{2,6,8,12,18,22,24,28},{1,5,11,15,17,21,27,31},..., dimensions={0} | all-to-all | bytes 212992 | tf_op jit(solution)/shard_map/all_to_all | solution.py:615
  17.5 0.0 slice-start
  17.5 0.2 shard_map.140.qkv_ref
  17.7 0.0 collective-permute-done.1.cache_peer
  17.7 0.0 copy-done.4
  17.7 0.0 copy-done.5
  17.7 0.5 shard_map.141
  18.2 0.0 collective-permute-done.2.w_ref
  18.2 9.1 %all_to_all.16.arrived_ref = bf16[8,8,640]{2,1,0:T(8,128)(2,1)S(1)} all-to-all(bf16[8,8,640]{2,1,0:T(8,128)(2,1)S(1)} %shard_map.141), channel_id=1, replica_groups={{0,4,10,14,16,20,26,30},{2,6,8,12,18,22,24,28},{1,5,11,15,17,21,27,31},..., dimensions={0} | all-to-all | bytes 163840 | tf_op jit(solution)/shard_map/all_to_all | solution.py:641
  27.3 0.3 shard_map.142.own_ref
  27.6 0.7 %collective-permute-start.3 = (bf16[4,1024]{1,0:T(4,128)(2,1)S(1)}, bf16[4,1024]{1,0:T(4,128)(2,1)S(1)}, u32[]{:S(2)}, u32[]{:S(2)}) collective-permute-start(bf16[4,1024]{1,0:T(4,128)(2,1)S(1)} %shard_map.142.own_ref), channel_id=1, source_target_pairs={{0,2},{2,0},{1,3},{3,1},{4,6},{6,4},{5,7},{7,5},{8,10},{10,8},{9,1... | collective-permute-start | bytes 24584 | tf_op jit(solution)/shard_map/ppermute | solution.py:28
  28.3 0.2 shard_map.144.own_part
  28.5 0.6 %collective-permute-done.3.peer_ref = bf16[4,1024]{1,0:T(4,128)(2,1)S(1)} collective-permute-done((bf16[4,1024]{1,0:T(4,128)(2,1)S(1)}, bf16[4,1024]{1,0:T(4,128)(2,1)S(1)}, u32[]{:S(2)}, u32[]{:S(2)}) %collective-permute-start.3) | collective-permute-done | bytes 8224 | tf_op jit(solution)/shard_map/ppermute | solution.py:28
  29.1 0.2 shard_map.145
  29.3 1.5 %collective-permute-start.4 = (f32[4,256]{1,0:T(4,128)S(1)}, f32[4,256]{1,0:T(4,128)S(1)}, u32[]{:S(2)}, u32[]{:S(2)}) collective-permute-start(f32[4,256]{1,0:T(4,128)S(1)} %shard_map.145), channel_id=1, source_target_pairs={{0,3},{1,2},{2,1},{3,0},{4,7},{5,6},{6,5},{7,4},{8,11},{9,10},{10,... | collective-permute-start | bytes 12296 | tf_op jit(solution)/shard_map/ppermute | solution.py:32
  30.8 0.2 shard_map.143.part_ref
  31.0 1.3 %collective-permute-done.4.peer_ref = f32[4,256]{1,0:T(4,128)S(1)} collective-permute-done((f32[4,256]{1,0:T(4,128)S(1)}, f32[4,256]{1,0:T(4,128)S(1)}, u32[]{:S(2)}, u32[]{:S(2)}) %collective-permute-start.4) | collective-permute-done | bytes 4128 | tf_op jit(solution)/shard_map/ppermute | solution.py:32
  32.3 0.0 slice-done
  32.4 0.0 slice-done.1
  32.4 0.5 shard_map.146
  32.8 0.4 collective-permute-start.5
  33.2 0.5 shard_map.147.mine_ref
  33.7 0.5 collective-permute-done.5.arrived_ref
  34.2 14.5 %all_to_all.17.arrived_ref = bf16[8,4,5504]{2,1,0:T(4,128)(2,1)S(1)} all-to-all(bf16[8,4,5504]{2,1,0:T(4,128)(2,1)S(1)} %shard_map.148), channel_id=1, replica_groups=mesh['chip'=8,'core'=2,'tp'=2] {'chip'}, dimensions={0} | all-to-all | bytes 704512 | tf_op jit(solution)/shard_map/all_to_all | solution.py:697
  48.7 0.1 shard_map.149.own_ref
  48.8 0.1 collective-permute-start.6
  48.9 0.0 slice-done.2
  48.9 0.0 slice-done.3
  48.9 0.5 shard_map.150.own_part
  49.4 0.7 %collective-permute-done.6.peer_ref = bf16[4,5376]{1,0:T(4,128)(2,1)S(1)} collective-permute-done((bf16[4,5376]{1,0:T(4,128)(2,1)S(1)}, bf16[4,5376]{1,0:T(4,128)(2,1)S(1)}, u32[]{:S(2)}, u32[]{:S(2)}) %collective-permute-start.6) | collective-permute-done | bytes 43040 | tf_op jit(solution)/shard_map/ppermute | solution.py:28
  50.1 0.4 shard_map.151
  50.6 1.6 %collective-permute-start.7 = (f32[4,256]{1,0:T(4,128)S(1)}, f32[4,256]{1,0:T(4,128)S(1)}, u32[]{:S(2)}, u32[]{:S(2)}) collective-permute-start(f32[4,256]{1,0:T(4,128)S(1)} %shard_map.151), channel_id=1, source_target_pairs={{0,1},{1,0},{2,3},{3,2},{4,5},{5,4},{6,7},{7,6},{8,9},{9,8},{10,11... | collective-permute-start | bytes 12296 | tf_op jit(solution)/shard_map/ppermute | solution.py:28
  52.1 2.1 %collective-permute-done.7 = f32[4,256]{1,0:T(4,128)S(1)} collective-permute-done((f32[4,256]{1,0:T(4,128)S(1)}, f32[4,256]{1,0:T(4,128)S(1)}, u32[]{:S(2)}, u32[]{:S(2)}) %collective-permute-start.7) | collective-permute-done | bytes 4128 | tf_op jit(solution)/shard_map/ppermute | solution.py:28
  54.2 0.6 %add_convert_fusion = bf16[4,256]{1,0:T(4,128)(2,1)} fusion(f32[4,256]{1,0:T(4,128)S(1)} %get-tuple-element.33, f32[4,256]{1,0:T(4,128)S(1)} %shard_map.151, f32[4,256]{1,0:T(4,128)S(1)} %collective-permute-done.7), kind=kLoop, calls=%fused_computation | loop fusion | flops 3072 | bytes 14336 | tf_op jit(solution)/shard_map/convert_element_type | solution.py:716
  (14 shorter events, 0.1 us)
Async XLA Ops:
  0.0 1.4 %copy-start = (bf16[256,2048]{1,0:T(8,128)(2,1)S(1)}, bf16[256,2048]{1,0:T(8,128)(2,1)}, u32[]{:S(2)}) copy-start(bf16[256,2048]{1,0:T(8,128)(2,1)} %wq_ref.3) | copy-start | bytes 3145732
  0.0 1.5 %copy-start.2 = (bf16[256,512]{1,0:T(8,128)(2,1)S(1)}, bf16[256,512]{1,0:T(8,128)(2,1)}, u32[]{:S(2)}) copy-start(bf16[256,512]{1,0:T(8,128)(2,1)} %wk_ref.3) | copy-start | bytes 786436
  0.0 1.6 %copy-start.3 = (bf16[256,512]{1,0:T(8,128)(2,1)S(1)}, bf16[256,512]{1,0:T(8,128)(2,1)}, u32[]{:S(2)}) copy-start(bf16[256,512]{1,0:T(8,128)(2,1)} %wv_ref.3) | copy-start | bytes 786436
  1.6 1.7 %copy-start.1 = (bf16[2048,256]{1,0:T(8,128)(2,1)S(1)}, bf16[2048,256]{1,0:T(8,128)(2,1)}, u32[]{:S(2)}) copy-start(bf16[2048,256]{1,0:T(8,128)(2,1)} %w_ref.5) | copy-start | bytes 3145732
  1.6 16.1 %copy-start.4 = (bf16[4,128,512]{2,1,0:T(8,128)(2,1)S(1)}, bf16[4,128,512]{2,1,0:T(8,128)(2,1)}, u32[]{:S(2)}) copy-start(bf16[4,128,512]{2,1,0:T(8,128)(2,1)} %key_own.1) | copy-start | bytes 1572868
  1.6 16.1 %copy-start.5 = (bf16[4,128,512]{2,1,0:T(8,128)(2,1)S(1)}, bf16[4,128,512]{2,1,0:T(8,128)(2,1)}, u32[]{:S(2)}) copy-start(bf16[4,128,512]{2,1,0:T(8,128)(2,1)} %value_own.1) | copy-start | bytes 1572868
  1.8 1.3 %collective-permute-start = (f32[4,1792]{1,0:T(4,128)S(1)}, f32[4,1792]{1,0:T(4,128)S(1)}, u32[]{:S(2)}, u32[]{:S(2)}) collective-permute-start(f32[4,1792]{1,0:T(4,128)S(1)} %shard_map.138), channel_id=1, source_target_pairs={{0,2},{2,0},{1,3},{3,1},{4,6},{6,4},{5,7},{7,5},{8,10},{10,8},{9,1... | collective-permute-start | bytes 86024 | tf_op jit(solution)/shard_map/ppermute | solution.py:28
  3.2 14.9 %collective-permute-start.2 = (bf16[2048,256]{1,0:T(8,128)(2,1)S(1)}, bf16[2048,256]{1,0:T(8,128)(2,1)S(1)}, u32[]{:S(2)}, u32[]{:S(2)}) collective-permute-start(bf16[2048,256]{1,0:T(8,128)(2,1)S(1)} %copy-done.1), channel_id=1, source_target_pairs={{0,2},{2,0},{1,3},{3,1},{4,6},{6,4},{5,7},{7,5},{8,10},{10,8},{9,1... | collective-permute-start | bytes 3145736 | tf_op jit(solution)/shard_map/ppermute | solution.py:28
  3.7 14.0 %collective-permute-start.1 = (bf16[2,4,128,256]{3,2,1,0:T(8,128)(2,1)S(1)}, bf16[2,4,128,256]{3,2,1,0:T(8,128)(2,1)S(1)}, u32[]{:S(2)}, u32[]{:S(2)}) collective-permute-start(bf16[2,4,128,256]{3,2,1,0:T(8,128)(2,1)S(1)} %get-tuple-element.27), channel_id=1, source_target_pairs={{0,2},{2,0},{1,3},{3,1},{4,6},{6,4},{5,7},{7,5},{8,10},{10,8},{9,1... | collective-permute-start | bytes 1572872 | tf_op jit(solution)/shard_map/ppermute | solution.py:28
  17.5 14.9 %slice-start = ((s8[5505024]{0:T(1024)(128)(4,1)}), s8[4194304]{0:T(1024)(128)(4,1)S(1)}, s32[]{:S(2)}) async-start(s8[5505024]{0:T(1024)(128)(4,1)} %bitcast.2), calls=%async_computation.3 | async-start | bytes 8388608
  17.7 14.7 %slice-start.1 = ((s8[5505024]{0:T(1024)(128)(4,1)}), s8[1310720]{0:T(1024)(128)(4,1)S(1)}, s32[]{:S(2)}) async-start(s8[5505024]{0:T(1024)(128)(4,1)} %bitcast.2), calls=%async_computation.4 | async-start | bytes 2621440
  27.6 1.5 %collective-permute-start.3 = (bf16[4,1024]{1,0:T(4,128)(2,1)S(1)}, bf16[4,1024]{1,0:T(4,128)(2,1)S(1)}, u32[]{:S(2)}, u32[]{:S(2)}) collective-permute-start(bf16[4,1024]{1,0:T(4,128)(2,1)S(1)} %shard_map.142.own_ref), channel_id=1, source_target_pairs={{0,2},{2,0},{1,3},{3,1},{4,6},{6,4},{5,7},{7,5},{8,10},{10,8},{9,1... | collective-permute-start | bytes 24584 | tf_op jit(solution)/shard_map/ppermute | solution.py:28
  29.1 19.8 %slice-start.2 = ((s8[5505024]{0:T(1024)(128)(4,1)}), s8[4194304]{0:T(1024)(128)(4,1)S(1)}, s32[]{:S(2)}) async-start(s8[5505024]{0:T(1024)(128)(4,1)} %bitcast.4), calls=%async_computation.5 | async-start | bytes 8388608
  29.3 3.0 %collective-permute-start.4 = (f32[4,256]{1,0:T(4,128)S(1)}, f32[4,256]{1,0:T(4,128)S(1)}, u32[]{:S(2)}, u32[]{:S(2)}) collective-permute-start(f32[4,256]{1,0:T(4,128)S(1)} %shard_map.145), channel_id=1, source_target_pairs={{0,3},{1,2},{2,1},{3,0},{4,7},{5,6},{6,5},{7,4},{8,11},{9,10},{10,... | collective-permute-start | bytes 12296 | tf_op jit(solution)/shard_map/ppermute | solution.py:32
  32.4 16.6 %slice-start.3 = ((s8[5505024]{0:T(1024)(128)(4,1)}), s8[1310720]{0:T(1024)(128)(4,1)S(1)}, s32[]{:S(2)}) async-start(s8[5505024]{0:T(1024)(128)(4,1)} %bitcast.4), calls=%async_computation.6 | async-start | bytes 2621440
  32.8 1.3 %collective-permute-start.5 = (f32[4,5504]{1,0:T(4,128)S(1)}, f32[4,5504]{1,0:T(4,128)S(1)}, u32[]{:S(2)}, u32[]{:S(2)}) collective-permute-start(f32[4,5504]{1,0:T(4,128)S(1)} %get-tuple-element.36), channel_id=1, source_target_pairs={{0,2},{2,0},{1,3},{3,1},{4,6},{6,4},{5,7},{7,5},{8,10},{10,8},{9,1... | collective-permute-start | bytes 264200 | tf_op jit(solution)/shard_map/ppermute | solution.py:28
  48.8 1.3 %collective-permute-start.6 = (bf16[4,5376]{1,0:T(4,128)(2,1)S(1)}, bf16[4,5376]{1,0:T(4,128)(2,1)S(1)}, u32[]{:S(2)}, u32[]{:S(2)}) collective-permute-start(bf16[4,5376]{1,0:T(4,128)(2,1)S(1)} %shard_map.149.own_ref), channel_id=1, source_target_pairs={{0,2},{2,0},{1,3},{3,1},{4,6},{6,4},{5,7},{7,5},{8,10},{10,8},{9,1... | collective-permute-start | bytes 129032 | tf_op jit(solution)/shard_map/ppermute | solution.py:28
  50.6 3.7 %collective-permute-start.7 = (f32[4,256]{1,0:T(4,128)S(1)}, f32[4,256]{1,0:T(4,128)S(1)}, u32[]{:S(2)}, u32[]{:S(2)}) collective-permute-start(f32[4,256]{1,0:T(4,128)S(1)} %shard_map.151), channel_id=1, source_target_pairs={{0,1},{1,0},{2,3},{3,2},{4,5},{5,4},{6,7},{7,6},{8,9},{9,8},{10,11... | collective-permute-start | bytes 12296 | tf_op jit(solution)/shard_map/ppermute | solution.py:28

commit v10 on v9

--- a/solution.py
+++ b/solution.py
@@ -30,6 +30,11 @@
 
 def swap_diagonal(values_in):
     return lax.ppermute(values_in, ("core", "tp"), [(i, 3 - i) for i in range(4)])
+
+
+def swap_next_chip(values_in):
+    n = 2 * lax.axis_size("chip")
+    return lax.ppermute(values_in, ("chip", "core"), [(i, i ^ 3) for i in range(n)])
 
 
 def gather_all(values_in, axes, n):
@@ -224,6 +229,10 @@
 
 def head_half():
     return (lax.axis_index("core") + chip_turn(lax.axis_index("chip"))) % 2
+
+
+def up_half():
+    return (lax.axis_index("core") + lax.axis_index("chip")) % 2
 
 
 def local_kernel(kernel, outs, operands, flops, scratch=(), in_hbm=(), anywhere=()):
@@ -475,9 +484,9 @@
     out_ref[...] = half_rows(own_ref, w_ref, side) + half_rows(peer_ref, w_ref, 1 - side)
 
 
-def up_columns(scaled_mlp, w_ref, core, out_ref):
+def up_columns(scaled_mlp, w_ref, side, out_ref):
     half = out_ref.shape[1] - LANES
-    mine = pl.ds(pl.multiple_of(core * half, LANES), half)
+    mine = pl.ds(pl.multiple_of(side * half, LANES), half)
     out_ref[:, :half] = jnp.dot(scaled_mlp, w_ref[:, mine], preferred_element_type=jnp.float32)
 
 
@@ -493,25 +502,39 @@
     squares = jnp.sum(resid_rows * resid_rows, axis=1, keepdims=True)
     squares_ref[...] = jnp.broadcast_to(squares, squares_ref.shape)
     other_ref[:, other_ref.shape[1] - LANES :] = squares_ref[...]
-    up_columns(scaled_mlp, w_ref, 1 - lax.axis_index("core"), other_ref)
+    up_columns(scaled_mlp, w_ref, 1 - up_half(), other_ref)
 
 
 def up_mine_kernel(scaled_ref, squares_ref, w_ref, mine_ref):
     mine_ref[:, mine_ref.shape[1] - LANES :] = squares_ref[...]
-    up_columns(scaled_ref[...], w_ref, lax.axis_index("core"), mine_ref)
-
-
-def up_message_kernel(mine_ref, arrived_ref, message_ref):
-    half = mine_ref.shape[1] - LANES
-    message = (mine_ref[:, :half] + arrived_ref[:, :half]).astype(jnp.bfloat16)
-    squares = mine_ref[:, half:] + arrived_ref[:, half:]
+    up_columns(scaled_ref[...], w_ref, up_half(), mine_ref)
+
+
+def squares_tile(squares):
     lane = lax.broadcasted_iota(jnp.int32, squares.shape, 1)
     tile = jnp.zeros_like(squares)
     for p, piece in enumerate(pieces_of(squares)):
         tile = jnp.where(lane == p, piece, tile)
+    return tile.astype(jnp.bfloat16)
+
+
+def up_pair_kernel(mine_ref, arrived_ref, pair_ref, sent_ref):
+    half = mine_ref.shape[1] - LANES
+    total = mine_ref[...] + arrived_ref[...]
+    pair_ref[...] = total
+    sent_ref[:, :half] = total[:, :half].astype(jnp.bfloat16)
+    sent_ref[:, half:] = squares_tile(total[:, half:])
+
+
+def up_message_kernel(pair_ref, arrived_ref, message_ref):
+    half = pair_ref.shape[1] - LANES
+    message = pair_ref[:, :half] + arrived_ref[:, :half].astype(jnp.float32)
+    message = message.astype(jnp.bfloat16)
+    arrived = jnp.sum(arrived_ref[:, half:].astype(jnp.float32), axis=1, keepdims=True)
+    tile = squares_tile(pair_ref[:, half:] + arrived)
     for i in range(message_ref.shape[0]):
         message_ref[i, :, :half] = message
-        message_ref[i, :, half:] = tile.astype(jnp.bfloat16)
+        message_ref[i, :, half:] = tile
 
 
 def activate_kernel(arrived_ref, out_ref):
@@ -525,11 +548,11 @@
 
 
 def down_own_kernel(own_ref, w_ref, out_ref):
-    out_ref[...] = half_rows(own_ref, w_ref, lax.axis_index("core"))
+    out_ref[...] = half_rows(own_ref, w_ref, up_half())
 
 
 def down_peer_kernel(own_part, peer_ref, w_ref, out_ref):
-    out_ref[...] = own_part[...] + half_rows(peer_ref, w_ref, 1 - lax.axis_index("core"))
+    out_ref[...] = own_part[...] + half_rows(peer_ref, w_ref, 1 - up_half())
 
 
 def per_device(
@@ -685,16 +708,27 @@
         flops=n_req * up_weight.size,
         anywhere=(2,),
     )
+    up_pair, up_sent = local_kernel(
+        up_pair_kernel,
+        [f32(*up_mine.shape), bf16(*up_mine.shape)],
+        [up_mine, swap(up_other, "core")],
+        flops=up_mine.size,
+    )
     (up_message,) = local_kernel(
         up_message_kernel,
-        [bf16(n_chips, n_req, half_up + LANES)],
-        [up_mine, swap(up_other, "core")],
-        flops=n_chips * n_req * half_up,
-    )
+        [bf16(n_chips // 2, *up_pair.shape)],
+        [up_pair, swap_next_chip(up_sent)],
+        flops=up_mine.size,
+    )
+    columns = [
+        [2 * chip + core for chip in range(turn, n_chips, 2)]
+        for turn in range(2)
+        for core in range(2)
+    ]
     (active_half,) = local_kernel(
         activate_kernel,
         [bf16(n_req, half_up)],
-        [lax.all_to_all(up_message, "chip", 0, 0)],
+        [lax.all_to_all(up_message, ("chip", "core"), 0, 0, axis_index_groups=columns)],
         flops=n_chips * n_req * half_up,
     )
     active_other = swap(active_half, "core")

time: 55 us -> 54.3 us (0.987)
  blocking collectives: 37.2 us -> 32.8 us
  waiting for transfers between devices: 5.9 us -> 9.07 us
    all_to_all x1, blocking collectives: 14.5 us -> 10.2 us  [per_device(): lax.all_to_all(up_message, ('chip', 'core'), 0, 0, axis_index_groups=colu...]
    ppermute x0 -> x1, waiting for transfers between devices: none -> 3.17 us  [swap_next_chip(): lax.ppermute(values_in, ('chip', 'core'), [(i, i ^ 3) for i in range(n)])]
    pallas_call x16 -> x17, Pallas kernels: 5.37 us -> 5.45 us  [local_kernel(): pl.pallas_call(kernel, out_shape=outs, in_specs=in_specs, out_specs=[IN_V...]
  transfers between devices with their start and end apart: 8 -> 9, of which waited for: 6 -> 7; matrix products, arithmetic and copies ran while one was open for 0% -> 0% of each run, Pallas kernels for 4% -> 4%
where the time goes in v10:
time: 54.3 us; the launch traced here: 54.1 us
  blocking collectives  32.8 us (60%)
  waiting for transfers between devices  9.07 us (17%)
  starting transfers between devices  5.6 us (10%)
  Pallas kernels  5.45 us (10%)
  other arithmetic  0.63 us (1%)
    all_to_all x1, blocking collectives, per_device(): lax.all_to_all(jnp.broadcast_to(qkv_message[None], (n_chips,) + qkv_messa...  13.6 us
    all_to_all x1, blocking collectives, per_device(): lax.all_to_all(up_message, ('chip', 'core'), 0, 0, axis_index_groups=colu...  10.2 us
    all_to_all x1, blocking collectives, per_device(): lax.all_to_all(message, ('chip', 'core'), 0, 0, axis_index_groups=sides)  9.09 us
    pallas_call x17, Pallas kernels, local_kernel(): pl.pallas_call(kernel, out_shape=outs, in_specs=in_specs, out_specs=[IN_V...  5.45 us
    ppermute x7, waiting for transfers between devices, swap(): return lax.ppermute(values_in, axis, [(i, i ^ 1) for i in range(n)])  4.59 us
    ppermute x7, starting transfers between devices, swap(): return lax.ppermute(values_in, axis, [(i, i ^ 1) for i in range(n)])  3.77 us
    ppermute x1, waiting for transfers between devices, swap_next_chip(): lax.ppermute(values_in, ('chip', 'core'), [(i, i ^ 3) for i in range(n)])  3.17 us
    ppermute x1, starting transfers between devices, swap_diagonal(): lax.ppermute(values_in, ('core', 'tp'), [(i, 3 - i) for i in range(4)])  1.48 us
  transfers between devices with their start and end apart: 9, of which 7 were waited for; matrix products, arithmetic and copies ran while one was open for 0% of the time, Pallas kernels for 4%

profile of v10, /device:TPU:0, one launch (start us, length us, event | category | flops | bytes accessed | tf_op | source)
XLA Modules:
  0.0 54.1 jit_solution(5871986457637604708)
XLA Ops:
  0.0 1.3 %shard_map.136 = (bf16[4,256]{1,0:T(4,128)(2,1)S(1)}, f32[4,128]{1,0:T(4,128)S(1)}, f32[4,128]{1,0:T(4,128)S(1)}, bf16[4,256]{1,0:T(4,128)(2,1)S(1)}, f32[1,256]...) custom-call(bf16[4,256]{1,0:T(4,128)(2,1)} %x_hbm.1, f32[1,256]{1,0:T(1,128)} %bitcast.6, f32[1,256]{1,0:T(1,128)} %bitcast.7, ...), custom_call_target="tpu_custom_call" | custom-call | flops 4000000000 | bytes 1054752 | tf_op jit(solution)/shard_map/pallas_call | solution.py:245
  1.3 0.2 copy-done
  1.4 0.0 copy-done.2
  1.5 0.1 copy-done.3
  1.6 0.2 shard_map.138
  1.8 0.5 collective-permute-start
  2.3 0.2 shard_map.137.mine_ref
  2.5 0.7 %collective-permute-done.arrived_ref = f32[4,1792]{1,0:T(4,128)S(1)} collective-permute-done((f32[4,1792]{1,0:T(4,128)S(1)}, f32[4,1792]{1,0:T(4,128)S(1)}, u32[]{:S(2)}, u32[]{:S(2)}) %collective-permute-start) | collective-permute-done | bytes 28704 | tf_op jit(solution)/shard_map/ppermute | solution.py:28
  3.1 0.1 shard_map.139
  3.2 0.0 copy-done.1
  3.2 0.4 collective-permute-start.2
  3.7 0.2 collective-permute-start.1
  3.9 13.6 %all_to_all.15 = f16[8,4,1664]{2,1,0:T(4,128)(2,1)S(1)} all-to-all(f16[8,4,1664]{2,1,0:T(4,128)(2,1)S(1)} %broadcast_in_dim.2), channel_id=1, replica_groups={{0,4,10,14,16,20,26,30},{2,6,8,12,18,22,24,28},{1,5,11,15,17,21,27,31},..., dimensions={0} | all-to-all | bytes 212992 | tf_op jit(solution)/shard_map/all_to_all | solution.py:638
  17.5 0.0 slice-start
  17.5 0.2 shard_map.140.qkv_ref
  17.7 0.0 collective-permute-done.1.cache_peer
  17.7 0.0 copy-done.4
  17.7 0.0 copy-done.5
  17.7 0.5 shard_map.141
  18.2 0.0 collective-permute-done.2.w_ref
  18.2 9.1 %all_to_all.16.arrived_ref = bf16[8,8,640]{2,1,0:T(8,128)(2,1)S(1)} all-to-all(bf16[8,8,640]{2,1,0:T(8,128)(2,1)S(1)} %shard_map.141), channel_id=1, replica_groups={{0,4,10,14,16,20,26,30},{2,6,8,12,18,22,24,28},{1,5,11,15,17,21,27,31},..., dimensions={0} | all-to-all | bytes 163840 | tf_op jit(solution)/shard_map/all_to_all | solution.py:664
  27.3 0.3 shard_map.142.own_ref
  27.6 0.7 %collective-permute-start.3 = (bf16[4,1024]{1,0:T(4,128)(2,1)S(1)}, bf16[4,1024]{1,0:T(4,128)(2,1)S(1)}, u32[]{:S(2)}, u32[]{:S(2)}) collective-permute-start(bf16[4,1024]{1,0:T(4,128)(2,1)S(1)} %shard_map.142.own_ref), channel_id=1, source_target_pairs={{0,2},{2,0},{1,3},{3,1},{4,6},{6,4},{5,7},{7,5},{8,10},{10,8},{9,1... | collective-permute-start | bytes 24584 | tf_op jit(solution)/shard_map/ppermute | solution.py:28
  28.3 0.2 shard_map.144.own_part
  28.5 0.6 %collective-permute-done.3.peer_ref = bf16[4,1024]{1,0:T(4,128)(2,1)S(1)} collective-permute-done((bf16[4,1024]{1,0:T(4,128)(2,1)S(1)}, bf16[4,1024]{1,0:T(4,128)(2,1)S(1)}, u32[]{:S(2)}, u32[]{:S(2)}) %collective-permute-start.3) | collective-permute-done | bytes 8224 | tf_op jit(solution)/shard_map/ppermute | solution.py:28
  29.1 0.2 shard_map.145
  29.3 1.5 %collective-permute-start.4 = (f32[4,256]{1,0:T(4,128)S(1)}, f32[4,256]{1,0:T(4,128)S(1)}, u32[]{:S(2)}, u32[]{:S(2)}) collective-permute-start(f32[4,256]{1,0:T(4,128)S(1)} %shard_map.145), channel_id=1, source_target_pairs={{0,3},{1,2},{2,1},{3,0},{4,7},{5,6},{6,5},{7,4},{8,11},{9,10},{10,... | collective-permute-start | bytes 12296 | tf_op jit(solution)/shard_map/ppermute | solution.py:32
  30.8 0.2 shard_map.143.part_ref
  31.0 1.3 %collective-permute-done.4.peer_ref = f32[4,256]{1,0:T(4,128)S(1)} collective-permute-done((f32[4,256]{1,0:T(4,128)S(1)}, f32[4,256]{1,0:T(4,128)S(1)}, u32[]{:S(2)}, u32[]{:S(2)}) %collective-permute-start.4) | collective-permute-done | bytes 4128 | tf_op jit(solution)/shard_map/ppermute | solution.py:32
  32.3 0.0 slice-done
  32.4 0.0 slice-done.1
  32.4 0.5 shard_map.146
  32.8 0.4 collective-permute-start.5
  33.2 0.5 shard_map.147.mine_ref
  33.7 0.5 collective-permute-done.5.arrived_ref
  34.2 0.4 collective-permute-start.6
  34.6 3.2 %collective-permute-done.6.arrived_ref = bf16[4,5504]{1,0:T(4,128)(2,1)S(1)} collective-permute-done((bf16[4,5504]{1,0:T(4,128)(2,1)S(1)}, bf16[4,5504]{1,0:T(4,128)(2,1)S(1)}, u32[]{:S(2)}, u32[]{:S(2)}) %collective-permute-start.6) | collective-permute-done | bytes 44064 | tf_op jit(solution)/shard_map/ppermute | solution.py:37
  37.7 0.1 shard_map.149
  37.8 10.2 %all_to_all.17.arrived_ref = bf16[4,4,5504]{2,1,0:T(4,128)(2,1)S(1)} all-to-all(bf16[4,4,5504]{2,1,0:T(4,128)(2,1)S(1)} %shard_map.149), channel_id=1, replica_groups={{0,8,16,24},{2,10,18,26},{4,12,20,28},{6,14,22,30},{1,9,17,25},{3,11,19..., dimensions={0} | all-to-all | bytes 352256 | tf_op jit(solution)/shard_map/all_to_all | solution.py:731
  48.0 0.1 shard_map.150.own_ref
  48.1 0.1 collective-permute-start.7
  48.2 0.0 slice-done.2
  48.2 0.5 shard_map.151.own_part
  48.7 0.7 %collective-permute-done.7.peer_ref = bf16[4,5376]{1,0:T(4,128)(2,1)S(1)} collective-permute-done((bf16[4,5376]{1,0:T(4,128)(2,1)S(1)}, bf16[4,5376]{1,0:T(4,128)(2,1)S(1)}, u32[]{:S(2)}, u32[]{:S(2)}) %collective-permute-start.7) | collective-permute-done | bytes 43040 | tf_op jit(solution)/shard_map/ppermute | solution.py:28
  49.4 0.4 shard_map.152
  49.8 1.6 %collective-permute-start.8 = (f32[4,256]{1,0:T(4,128)S(1)}, f32[4,256]{1,0:T(4,128)S(1)}, u32[]{:S(2)}, u32[]{:S(2)}) collective-permute-start(f32[4,256]{1,0:T(4,128)S(1)} %shard_map.152), channel_id=1, source_target_pairs={{0,1},{1,0},{2,3},{3,2},{4,5},{5,4},{6,7},{7,6},{8,9},{9,8},{10,11... | collective-permute-start | bytes 12296 | tf_op jit(solution)/shard_map/ppermute | solution.py:28
  51.4 2.1 %collective-permute-done.8 = f32[4,256]{1,0:T(4,128)S(1)} collective-permute-done((f32[4,256]{1,0:T(4,128)S(1)}, f32[4,256]{1,0:T(4,128)S(1)}, u32[]{:S(2)}, u32[]{:S(2)}) %collective-permute-start.8) | collective-permute-done | bytes 4128 | tf_op jit(solution)/shard_map/ppermute | solution.py:28
  53.5 0.6 %add_convert_fusion = bf16[4,256]{1,0:T(4,128)(2,1)} fusion(f32[4,256]{1,0:T(4,128)S(1)} %get-tuple-element.35, f32[4,256]{1,0:T(4,128)S(1)} %shard_map.152, f32[4,256]{1,0:T(4,128)S(1)} %collective-permute-done.8), kind=kLoop, calls=%fused_computation | loop fusion | flops 3072 | bytes 14336 | tf_op jit(solution)/shard_map/convert_element_type | solution.py:750
  (17 shorter events, 0.1 us)
Async XLA Ops:
  0.0 1.4 %copy-start = (bf16[256,2048]{1,0:T(8,128)(2,1)S(1)}, bf16[256,2048]{1,0:T(8,128)(2,1)}, u32[]{:S(2)}) copy-start(bf16[256,2048]{1,0:T(8,128)(2,1)} %wq_ref.3) | copy-start | bytes 3145732
  0.0 1.5 %copy-start.2 = (bf16[256,512]{1,0:T(8,128)(2,1)S(1)}, bf16[256,512]{1,0:T(8,128)(2,1)}, u32[]{:S(2)}) copy-start(bf16[256,512]{1,0:T(8,128)(2,1)} %wk_ref.3) | copy-start | bytes 786436
  0.0 1.6 %copy-start.3 = (bf16[256,512]{1,0:T(8,128)(2,1)S(1)}, bf16[256,512]{1,0:T(8,128)(2,1)}, u32[]{:S(2)}) copy-start(bf16[256,512]{1,0:T(8,128)(2,1)} %wv_ref.3) | copy-start | bytes 786436
  1.6 1.7 %copy-start.1 = (bf16[2048,256]{1,0:T(8,128)(2,1)S(1)}, bf16[2048,256]{1,0:T(8,128)(2,1)}, u32[]{:S(2)}) copy-start(bf16[2048,256]{1,0:T(8,128)(2,1)} %w_ref.5) | copy-start | bytes 3145732
  1.6 16.1 %copy-start.4 = (bf16[4,128,512]{2,1,0:T(8,128)(2,1)S(1)}, bf16[4,128,512]{2,1,0:T(8,128)(2,1)}, u32[]{:S(2)}) copy-start(bf16[4,128,512]{2,1,0:T(8,128)(2,1)} %key_own.1) | copy-start | bytes 1572868
  1.6 16.1 %copy-start.5 = (bf16[4,128,512]{2,1,0:T(8,128)(2,1)S(1)}, bf16[4,128,512]{2,1,0:T(8,128)(2,1)}, u32[]{:S(2)}) copy-start(bf16[4,128,512]{2,1,0:T(8,128)(2,1)} %value_own.1) | copy-start | bytes 1572868
  1.8 1.3 %collective-permute-start = (f32[4,1792]{1,0:T(4,128)S(1)}, f32[4,1792]{1,0:T(4,128)S(1)}, u32[]{:S(2)}, u32[]{:S(2)}) collective-permute-start(f32[4,1792]{1,0:T(4,128)S(1)} %shard_map.138), channel_id=1, source_target_pairs={{0,2},{2,0},{1,3},{3,1},{4,6},{6,4},{5,7},{7,5},{8,10},{10,8},{9,1... | collective-permute-start | bytes 86024 | tf_op jit(solution)/shard_map/ppermute | solution.py:28
  3.2 14.9 %collective-permute-start.2 = (bf16[2048,256]{1,0:T(8,128)(2,1)S(1)}, bf16[2048,256]{1,0:T(8,128)(2,1)S(1)}, u32[]{:S(2)}, u32[]{:S(2)}) collective-permute-start(bf16[2048,256]{1,0:T(8,128)(2,1)S(1)} %copy-done.1), channel_id=1, source_target_pairs={{0,2},{2,0},{1,3},{3,1},{4,6},{6,4},{5,7},{7,5},{8,10},{10,8},{9,1... | collective-permute-start | bytes 3145736 | tf_op jit(solution)/shard_map/ppermute | solution.py:28
  3.7 14.0 %collective-permute-start.1 = (bf16[2,4,128,256]{3,2,1,0:T(8,128)(2,1)S(1)}, bf16[2,4,128,256]{3,2,1,0:T(8,128)(2,1)S(1)}, u32[]{:S(2)}, u32[]{:S(2)}) collective-permute-start(bf16[2,4,128,256]{3,2,1,0:T(8,128)(2,1)S(1)} %get-tuple-element.29), channel_id=1, source_target_pairs={{0,2},{2,0},{1,3},{3,1},{4,6},{6,4},{5,7},{7,5},{8,10},{10,8},{9,1... | collective-permute-start | bytes 1572872 | tf_op jit(solution)/shard_map/ppermute | solution.py:28
  17.5 14.9 %slice-start = ((s8[5505024]{0:T(1024)(128)(4,1)}), s8[4194304]{0:T(1024)(128)(4,1)S(1)}, s32[]{:S(2)}) async-start(s8[5505024]{0:T(1024)(128)(4,1)} %bitcast.2), calls=%async_computation.3 | async-start | bytes 8388608
  17.7 14.7 %slice-start.1 = ((s8[5505024]{0:T(1024)(128)(4,1)}), s8[1310720]{0:T(1024)(128)(4,1)S(1)}, s32[]{:S(2)}) async-start(s8[5505024]{0:T(1024)(128)(4,1)} %bitcast.2), calls=%async_computation.4 | async-start | bytes 2621440
  27.6 1.5 %collective-permute-start.3 = (bf16[4,1024]{1,0:T(4,128)(2,1)S(1)}, bf16[4,1024]{1,0:T(4,128)(2,1)S(1)}, u32[]{:S(2)}, u32[]{:S(2)}) collective-permute-start(bf16[4,1024]{1,0:T(4,128)(2,1)S(1)} %shard_map.142.own_ref), channel_id=1, source_target_pairs={{0,2},{2,0},{1,3},{3,1},{4,6},{6,4},{5,7},{7,5},{8,10},{10,8},{9,1... | collective-permute-start | bytes 24584 | tf_op jit(solution)/shard_map/ppermute | solution.py:28
  29.1 19.1 %slice-start.2 = ((s8[5505024]{0:T(1024)(128)(4,1)}), s8[4194304]{0:T(1024)(128)(4,1)S(1)}, s32[]{:S(2)}) async-start(s8[5505024]{0:T(1024)(128)(4,1)} %bitcast.4), calls=%async_computation.5 | async-start | bytes 8388608
  29.3 3.0 %collective-permute-start.4 = (f32[4,256]{1,0:T(4,128)S(1)}, f32[4,256]{1,0:T(4,128)S(1)}, u32[]{:S(2)}, u32[]{:S(2)}) collective-permute-start(f32[4,256]{1,0:T(4,128)S(1)} %shard_map.145), channel_id=1, source_target_pairs={{0,3},{1,2},{2,1},{3,0},{4,7},{5,6},{6,5},{7,4},{8,11},{9,10},{10,... | collective-permute-start | bytes 12296 | tf_op jit(solution)/shard_map/ppermute | solution.py:32
  32.4 15.8 %slice-start.3 = ((s8[5505024]{0:T(1024)(128)(4,1)}), s8[1310720]{0:T(1024)(128)(4,1)S(1)}, s32[]{:S(2)}) async-start(s8[5505024]{0:T(1024)(128)(4,1)} %bitcast.4), calls=%async_computation.6 | async-start | bytes 2621440
  32.8 1.3 %collective-permute-start.5 = (f32[4,5504]{1,0:T(4,128)S(1)}, f32[4,5504]{1,0:T(4,128)S(1)}, u32[]{:S(2)}, u32[]{:S(2)}) collective-permute-start(f32[4,5504]{1,0:T(4,128)S(1)} %get-tuple-element.38), channel_id=1, source_target_pairs={{0,2},{2,0},{1,3},{3,1},{4,6},{6,4},{5,7},{7,5},{8,10},{10,8},{9,1... | collective-permute-start | bytes 264200 | tf_op jit(solution)/shard_map/ppermute | solution.py:28
  34.2 3.5 %collective-permute-start.6 = (bf16[4,5504]{1,0:T(4,128)(2,1)S(1)}, bf16[4,5504]{1,0:T(4,128)(2,1)S(1)}, u32[]{:S(2)}, u32[]{:S(2)}) collective-permute-start(bf16[4,5504]{1,0:T(4,128)(2,1)S(1)} %get-tuple-element.40), channel_id=1, source_target_pairs={{0,6},{2,4},{4,2},{6,0},{8,14},{10,12},{12,10},{14,8},{16,22},{18,... | collective-permute-start | bytes 132104 | tf_op jit(solution)/shard_map/ppermute | solution.py:37
  48.1 1.3 %collective-permute-start.7 = (bf16[4,5376]{1,0:T(4,128)(2,1)S(1)}, bf16[4,5376]{1,0:T(4,128)(2,1)S(1)}, u32[]{:S(2)}, u32[]{:S(2)}) collective-permute-start(bf16[4,5376]{1,0:T(4,128)(2,1)S(1)} %shard_map.150.own_ref), channel_id=1, source_target_pairs={{0,2},{2,0},{1,3},{3,1},{4,6},{6,4},{5,7},{7,5},{8,10},{10,8},{9,1... | collective-permute-start | bytes 129032 | tf_op jit(solution)/shard_map/ppermute | solution.py:28
  49.8 3.7 %collective-permute-start.8 = (f32[4,256]{1,0:T(4,128)S(1)}, f32[4,256]{1,0:T(4,128)S(1)}, u32[]{:S(2)}, u32[]{:S(2)}) collective-permute-start(f32[4,256]{1,0:T(4,128)S(1)} %shard_map.152), channel_id=1, source_target_pairs={{0,1},{1,0},{2,3},{3,2},{4,5},{5,4},{6,7},{7,6},{8,9},{9,8},{10,11... | collective-permute-start | bytes 12296 | tf_op jit(solution)/shard_map/ppermute | solution.py:28

commit v11 on v10

--- a/solution.py
+++ b/solution.py
@@ -32,9 +32,11 @@
     return lax.ppermute(values_in, ("core", "tp"), [(i, 3 - i) for i in range(4)])
 
 
-def swap_next_chip(values_in):
+def swap_chips(values_in, bit):
     n = 2 * lax.axis_size("chip")
-    return lax.ppermute(values_in, ("chip", "core"), [(i, i ^ 3) for i in range(n)])
+    return lax.ppermute(
+        values_in, ("chip", "core"), [(i, i ^ (2 << bit) ^ 1) for i in range(n)]
+    )
 
 
 def gather_all(values_in, axes, n):
@@ -232,7 +234,14 @@
 
 
 def up_half():
-    return (lax.axis_index("core") + lax.axis_index("chip")) % 2
+    turns, chip = lax.axis_index("core"), lax.axis_index("chip")
+    for bit in range(chip_bits()):
+        turns = turns + chip // 2**bit % 2
+    return turns % 2
+
+
+def chip_bits():
+    return lax.axis_size("chip").bit_length() - 1
 
 
 def local_kernel(kernel, outs, operands, flops, scratch=(), in_hbm=(), anywhere=()):
@@ -345,18 +354,19 @@
     out_ref[:, width:] = tile
 
 
-def qkv_sum_kernel(arrived_ref, out_ref):
-    width = out_ref.shape[1]
-    features = D / arrived_ref.shape[0]
+def qkv_sum(arrived_ref):
+    n_chips, _, width = arrived_ref.shape
+    width -= LANES
+    features = D / n_chips
     total, squares = 0.0, 0.0
-    for i in range(arrived_ref.shape[0]):
+    for i in range(n_chips):
         tile = arrived_ref[i, :, width:]
         scale = tile[:, :1] * (1.0 / SCALE_UNIT)
         total = total + arrived_ref[i, :, :width] * scale
         mean = tile[:, 1:2] + tile[:, 2:3] + tile[:, 3:4]
         squares = squares + mean * scale * scale * features
     inv_attn = lax.rsqrt(squares / D + NORM_EPS)
-    out_ref[...] = (total * inv_attn).astype(jnp.bfloat16)
+    return (total * inv_attn).astype(jnp.bfloat16).astype(jnp.float32)
 
 
 PIECE = 16
@@ -364,7 +374,7 @@
 
 
 def attention_kernel(
-    qkv_ref, key_own, value_own, cache_peer, live_own, live_peer,
+    arrived_ref, key_own, value_own, cache_peer, live_own, live_peer,
     message_ref, query_ref, key_new_ref, value_new_ref,
 ):
     n_copies, heads, _ = message_ref.shape
@@ -374,7 +384,7 @@
     kv_half = half // HD
     group = heads // kv_half
     is_first = lax.axis_index("chip") == 0
-    qkv = qkv_ref[...].astype(jnp.float32)
+    qkv = qkv_sum(arrived_ref)
     for h in range(heads):
         query_ref[:, h, :] = qkv[:, h * HD : (h + 1) * HD]
         at = (heads + h // group) * HD
@@ -518,33 +528,47 @@
     return tile.astype(jnp.bfloat16)
 
 
-def up_pair_kernel(mine_ref, arrived_ref, pair_ref, sent_ref):
-    half = mine_ref.shape[1] - LANES
-    total = mine_ref[...] + arrived_ref[...]
-    pair_ref[...] = total
+def send_sum(total, sent_ref):
+    half = sent_ref.shape[1] - LANES
     sent_ref[:, :half] = total[:, :half].astype(jnp.bfloat16)
     sent_ref[:, half:] = squares_tile(total[:, half:])
 
 
-def up_message_kernel(pair_ref, arrived_ref, message_ref):
-    half = pair_ref.shape[1] - LANES
-    message = pair_ref[:, :half] + arrived_ref[:, :half].astype(jnp.float32)
-    message = message.astype(jnp.bfloat16)
-    arrived = jnp.sum(arrived_ref[:, half:].astype(jnp.float32), axis=1, keepdims=True)
-    tile = squares_tile(pair_ref[:, half:] + arrived)
-    for i in range(message_ref.shape[0]):
-        message_ref[i, :, :half] = message
-        message_ref[i, :, half:] = tile
-
-
-def activate_kernel(arrived_ref, out_ref):
-    half = out_ref.shape[1]
-    total = arrived_ref[0].astype(jnp.float32)
-    for i in range(1, arrived_ref.shape[0]):
-        total = total + arrived_ref[i].astype(jnp.float32)
-    squares = jnp.sum(total[:, half:], axis=1, keepdims=True)
-    inv_mlp = lax.rsqrt(squares / D + NORM_EPS)
-    out_ref[...] = squared_relu(total[:, :half] * inv_mlp).astype(jnp.bfloat16)
+def add_arrived(total, arrived):
+    half = total.shape[1] - LANES
+    arrived = arrived.astype(jnp.float32)
+    squares = jnp.sum(arrived[:, half:], axis=1, keepdims=True)
+    return total[:, :half] + arrived[:, :half], total[:, half:] + squares
+
+
+def up_pair_kernel(mine_ref, arrived_ref, total_a, sent_a, total_b, sent_b):
+    total = mine_ref[...] + arrived_ref[...]
+    width = total_a.shape[1]
+    total_a[...] = total[:, :width]
+    sent_a[...] = total[:, :width].astype(jnp.bfloat16)
+    total_b[...] = total[:, width:]
+    send_sum(total[:, width:], sent_b)
+
+
+def up_add_a_kernel(part_ref, arrived_ref, total_ref, sent_ref):
+    total = part_ref[...] + arrived_ref[...].astype(jnp.float32)
+    total_ref[...] = total
+    sent_ref[...] = total.astype(jnp.bfloat16)
+
+
+def up_add_b_kernel(part_ref, arrived_ref, total_ref, sent_ref):
+    total = jnp.concatenate(add_arrived(part_ref[...], arrived_ref[...]), axis=1)
+    total_ref[...] = total
+    send_sum(total, sent_ref)
+
+
+def activate_kernel(part_a, arrived_a, part_b, arrived_b, out_ref):
+    width = part_a.shape[1]
+    total_a = part_a[...] + arrived_a[...].astype(jnp.float32)
+    total_b, squares = add_arrived(part_b[...], arrived_b[...])
+    inv_mlp = lax.rsqrt(squares[:, :1] / D + NORM_EPS)
+    out_ref[:, :width] = squared_relu(total_a * inv_mlp).astype(jnp.bfloat16)
+    out_ref[:, width:] = squared_relu(total_b * inv_mlp).astype(jnp.bfloat16)
 
 
 def down_own_kernel(own_ref, w_ref, out_ref):
@@ -642,17 +666,11 @@
         0,
         axis_index_groups=sides,
     )
-    (qkv_half,) = local_kernel(
-        qkv_sum_kernel,
-        [bf16(n_req, half_qkv)],
-        [qkv_all.astype(jnp.float32)],
-        flops=n_chips * n_req * half_qkv,
-    )
     half_heads = heads_here // 2
     (message,) = local_kernel(
         attention_kernel,
         [bf16(n_chips, half_heads, n_req * HD + LANES)],
-        [qkv_half, key_cache, value_cache, cache_peer, live, live_peer],
+        [qkv_all.astype(jnp.float32), key_cache, value_cache, cache_peer, live, live_peer],
         anywhere=(1, 2, 3),
         flops=4 * 10**9,
         scratch=[pltpu.VMEM((n_req, half_heads, HD), jnp.float32)] * 3,
@@ -708,28 +726,29 @@
         flops=n_req * up_weight.size,
         anywhere=(2,),
     )
-    up_pair, up_sent = local_kernel(
+    width_a = half_up // (2 * LANES) * LANES
+    widths = [width_a, half_up + LANES - width_a]
+    sums = [[f32(n_req, width), bf16(n_req, width)] for width in widths]
+    pair = local_kernel(
         up_pair_kernel,
-        [f32(*up_mine.shape), bf16(*up_mine.shape)],
+        sums[0] + sums[1],
         [up_mine, swap(up_other, "core")],
         flops=up_mine.size,
     )
-    (up_message,) = local_kernel(
-        up_message_kernel,
-        [bf16(n_chips // 2, *up_pair.shape)],
-        [up_pair, swap_next_chip(up_sent)],
-        flops=up_mine.size,
-    )
-    columns = [
-        [2 * chip + core for chip in range(turn, n_chips, 2)]
-        for turn in range(2)
-        for core in range(2)
-    ]
+    parts = [pair[:2], pair[2:]]
+    orders = [[2, 1, 0], [1, 0, 2]]
+    arrived = [swap_chips(part[1], order[0]) for part, order in zip(parts, orders)]
+    for step in range(1, chip_bits()):
+        for i, kernel in enumerate((up_add_a_kernel, up_add_b_kernel)):
+            parts[i] = local_kernel(
+                kernel, sums[i], [parts[i][0], arrived[i]], flops=n_req * widths[i]
+            )
+            arrived[i] = swap_chips(parts[i][1], orders[i][step])
     (active_half,) = local_kernel(
         activate_kernel,
         [bf16(n_req, half_up)],
-        [lax.all_to_all(up_message, ("chip", "core"), 0, 0, axis_index_groups=columns)],
-        flops=n_chips * n_req * half_up,
+        [parts[0][0], arrived[0], parts[1][0], arrived[1]],
+        flops=4 * up_mine.size,
     )
     active_other = swap(active_half, "core")
     (down_own,) = local_kernel(
@@ -754,7 +773,8 @@
     n_seq, n_tp = mesh.shape["seq"], mesh.shape["tp"]
     split = Mesh(mesh.devices.reshape(n_seq // 2, 2, n_tp), ("chip", "core", "tp"))
     seq = ("chip", "core")
-    whole_tiles = n_tp == 2 and KVH % (2 * n_tp) == 0 and D % (n_seq * LANES) == 0
+    chips = n_seq // 2
+    whole_tiles = chips == 8 and n_tp == 2
     return jax.shard_map(
         per_device if whole_tiles else per_device_plain,
         mesh=split,

time: 54.3 us -> 51.9 us (0.956)
  blocking collectives: 32.8 us -> 22.7 us
  starting transfers between devices: 5.6 us -> 10.1 us
  waiting for transfers between devices: 9.07 us -> 12.2 us
    all_to_all x1 -> x0, blocking collectives: 10.2 us -> none  [per_device(): lax.all_to_all(up_message, ('chip', 'core'), 0, 0, axis_index_groups=colu...]
    ppermute x1 -> x6, starting transfers between devices: 0.36 us -> 4.66 us  [swap_chips(): lax.ppermute(values_in, ('chip', 'core'), [(i, i ^ 2 << bit ^ 1) for i in...]
    ppermute x1 -> x6, waiting for transfers between devices: 3.17 us -> 6.45 us  [swap_chips(): lax.ppermute(values_in, ('chip', 'core'), [(i, i ^ 2 << bit ^ 1) for i in...]
    pallas_call x17 -> x19, Pallas kernels: 5.45 us -> 5.65 us  [local_kernel(): pl.pallas_call(kernel, out_shape=outs, in_specs=in_specs, out_specs=[IN_V...]
  transfers between devices with their start and end apart: 9 -> 14, of which waited for: 7 -> 12; matrix products, arithmetic and copies ran while one was open for 0% -> 0% of each run, Pallas kernels for 4% -> 5%
where the time goes in v11:
time: 51.9 us; the launch traced here: 51.7 us
  blocking collectives  22.7 us (44%)
  waiting for transfers between devices  12.2 us (24%)
  starting transfers between devices  10.1 us (19%)
  Pallas kernels  5.65 us (11%)
  other arithmetic  0.63 us (1%)
    all_to_all x1, blocking collectives, per_device(): lax.all_to_all(jnp.broadcast_to(qkv_message[None], (n_chips,) + qkv_messa...  13.6 us
    all_to_all x1, blocking collectives, per_device(): lax.all_to_all(message, ('chip', 'core'), 0, 0, axis_index_groups=sides)  9.09 us
    ppermute x6, waiting for transfers between devices, swap_chips(): lax.ppermute(values_in, ('chip', 'core'), [(i, i ^ 2 << bit ^ 1) for i in...  6.45 us
    pallas_call x19, Pallas kernels, local_kernel(): pl.pallas_call(kernel, out_shape=outs, in_specs=in_specs, out_specs=[IN_V...  5.65 us
    ppermute x6, starting transfers between devices, swap_chips(): lax.ppermute(values_in, ('chip', 'core'), [(i, i ^ 2 << bit ^ 1) for i in...  4.66 us
    ppermute x7, waiting for transfers between devices, swap(): return lax.ppermute(values_in, axis, [(i, i ^ 1) for i in range(n)])  4.39 us
    ppermute x7, starting transfers between devices, swap(): return lax.ppermute(values_in, axis, [(i, i ^ 1) for i in range(n)])  3.99 us
    ppermute x1, starting transfers between devices, swap_diagonal(): lax.ppermute(values_in, ('core', 'tp'), [(i, 3 - i) for i in range(4)])  1.48 us
  transfers between devices with their start and end apart: 14, of which 12 were waited for; matrix products, arithmetic and copies ran while one was open for 0% of the time, Pallas kernels for 5%

profile of v11, /device:TPU:0, one launch (start us, length us, event | category | flops | bytes accessed | tf_op | source)
XLA Modules:
  0.0 51.7 jit_solution(16661101224266504597)
XLA Ops:
  0.0 1.3 %shard_map.136 = (bf16[4,256]{1,0:T(4,128)(2,1)S(1)}, f32[4,128]{1,0:T(4,128)S(1)}, f32[4,128]{1,0:T(4,128)S(1)}, bf16[4,256]{1,0:T(4,128)(2,1)S(1)}, f32[1,256]...) custom-call(bf16[4,256]{1,0:T(4,128)(2,1)} %x_hbm.1, f32[1,256]{1,0:T(1,128)} %bitcast.6, f32[1,256]{1,0:T(1,128)} %bitcast.7, ...), custom_call_target="tpu_custom_call" | custom-call | flops 4000000000 | bytes 1054752 | tf_op jit(solution)/shard_map/pallas_call | solution.py:254
  1.3 0.2 copy-done
  1.4 0.0 copy-done.2
  1.5 0.1 copy-done.3
  1.6 0.2 shard_map.138
  1.8 0.5 collective-permute-start
  2.3 0.2 shard_map.137.mine_ref
  2.5 0.7 %collective-permute-done.arrived_ref = f32[4,1792]{1,0:T(4,128)S(1)} collective-permute-done((f32[4,1792]{1,0:T(4,128)S(1)}, f32[4,1792]{1,0:T(4,128)S(1)}, u32[]{:S(2)}, u32[]{:S(2)}) %collective-permute-start) | collective-permute-done | bytes 28704 | tf_op jit(solution)/shard_map/ppermute | solution.py:28
  3.1 0.1 shard_map.139
  3.2 0.4 collective-permute-start.2
  3.7 0.2 collective-permute-start.1
  3.9 13.6 %all_to_all.10 = f16[8,4,1664]{2,1,0:T(4,128)(2,1)S(1)} all-to-all(f16[8,4,1664]{2,1,0:T(4,128)(2,1)S(1)} %broadcast_in_dim.2), channel_id=1, replica_groups={{0,4,10,14,16,20,26,30},{2,6,8,12,18,22,24,28},{1,5,11,15,17,21,27,31},..., dimensions={0} | all-to-all | bytes 212992 | tf_op jit(solution)/shard_map/all_to_all | solution.py:662
  17.5 0.6 %shard_map.140 = bf16[8,8,640]{2,1,0:T(8,128)(2,1)S(1)} custom-call(f32[8,4,1664]{2,1,0:T(4,128)S(1)} %convert_element_type.10.arrived_ref, bf16[4,128,512]{2,1,0:T(8,128)(2,1)S(1)} %copy-done.4, bf16[4,128,512]{2,1,0:T(8,128)(2,1)S(1)} %copy-done.5, bf16[2,4,128,256]{3,2,1,0:T(8,128)(2,1)S(1)} %collective-permute-done.1.cache_peer, ...), custom_call_target="tpu_custom_call" | custom-call | flops 4000000000 | bytes 1789952 | tf_op jit(solution)/shard_map/pallas_call | solution.py:254
  18.2 9.1 %all_to_all.11.arrived_ref = bf16[8,8,640]{2,1,0:T(8,128)(2,1)S(1)} all-to-all(bf16[8,8,640]{2,1,0:T(8,128)(2,1)S(1)} %shard_map.140), channel_id=1, replica_groups={{0,4,10,14,16,20,26,30},{2,6,8,12,18,22,24,28},{1,5,11,15,17,21,27,31},..., dimensions={0} | all-to-all | bytes 163840 | tf_op jit(solution)/shard_map/all_to_all | solution.py:682
  27.3 0.3 shard_map.141.own_ref
  27.6 0.7 %collective-permute-start.3 = (bf16[4,1024]{1,0:T(4,128)(2,1)S(1)}, bf16[4,1024]{1,0:T(4,128)(2,1)S(1)}, u32[]{:S(2)}, u32[]{:S(2)}) collective-permute-start(bf16[4,1024]{1,0:T(4,128)(2,1)S(1)} %shard_map.141.own_ref), channel_id=1, source_target_pairs={{0,2},{2,0},{1,3},{3,1},{4,6},{6,4},{5,7},{7,5},{8,10},{10,8},{9,1... | collective-permute-start | bytes 24584 | tf_op jit(solution)/shard_map/ppermute | solution.py:28
  28.3 0.2 shard_map.143.own_part
  28.4 0.6 %collective-permute-done.3.peer_ref = bf16[4,1024]{1,0:T(4,128)(2,1)S(1)} collective-permute-done((bf16[4,1024]{1,0:T(4,128)(2,1)S(1)}, bf16[4,1024]{1,0:T(4,128)(2,1)S(1)}, u32[]{:S(2)}, u32[]{:S(2)}) %collective-permute-start.3) | collective-permute-done | bytes 8224 | tf_op jit(solution)/shard_map/ppermute | solution.py:28
  29.1 0.2 shard_map.144
  29.3 1.5 %collective-permute-start.4 = (f32[4,256]{1,0:T(4,128)S(1)}, f32[4,256]{1,0:T(4,128)S(1)}, u32[]{:S(2)}, u32[]{:S(2)}) collective-permute-start(f32[4,256]{1,0:T(4,128)S(1)} %shard_map.144), channel_id=1, source_target_pairs={{0,3},{1,2},{2,1},{3,0},{4,7},{5,6},{6,5},{7,4},{8,11},{9,10},{10,... | collective-permute-start | bytes 12296 | tf_op jit(solution)/shard_map/ppermute | solution.py:32
  30.8 0.2 shard_map.142.part_ref
  31.0 1.3 %collective-permute-done.4.peer_ref = f32[4,256]{1,0:T(4,128)S(1)} collective-permute-done((f32[4,256]{1,0:T(4,128)S(1)}, f32[4,256]{1,0:T(4,128)S(1)}, u32[]{:S(2)}, u32[]{:S(2)}) %collective-permute-start.4) | collective-permute-done | bytes 4128 | tf_op jit(solution)/shard_map/ppermute | solution.py:32
  32.3 0.5 shard_map.145
  32.8 0.4 collective-permute-start.5
  33.2 0.5 shard_map.146.mine_ref
  33.7 0.5 collective-permute-done.5.arrived_ref
  34.2 0.5 collective-permute-start.9
  34.7 0.7 %collective-permute-start.6 = (bf16[4,2688]{1,0:T(4,128)(2,1)S(1)}, bf16[4,2688]{1,0:T(4,128)(2,1)S(1)}, u32[]{:S(2)}, u32[]{:S(2)}) collective-permute-start(bf16[4,2688]{1,0:T(4,128)(2,1)S(1)} %get-tuple-element.50), channel_id=1, source_target_pairs={{0,18},{2,16},{4,22},{6,20},{8,26},{10,24},{12,30},{14,28},{16,2},... | collective-permute-start | bytes 64520 | tf_op jit(solution)/shard_map/ppermute | solution.py:37
  35.4 2.1 %collective-permute-done.9.arrived_ref = bf16[4,2816]{1,0:T(4,128)(2,1)S(1)} collective-permute-done((bf16[4,2816]{1,0:T(4,128)(2,1)S(1)}, bf16[4,2816]{1,0:T(4,128)(2,1)S(1)}, u32[]{:S(2)}, u32[]{:S(2)}) %collective-permute-start.9) | collective-permute-done | bytes 22560 | tf_op jit(solution)/shard_map/ppermute | solution.py:37
  37.5 0.1 shard_map.150
  37.6 0.3 collective-permute-start.10
  37.9 0.9 %collective-permute-done.6.arrived_ref = bf16[4,2688]{1,0:T(4,128)(2,1)S(1)} collective-permute-done((bf16[4,2688]{1,0:T(4,128)(2,1)S(1)}, bf16[4,2688]{1,0:T(4,128)(2,1)S(1)}, u32[]{:S(2)}, u32[]{:S(2)}) %collective-permute-start.6) | collective-permute-done | bytes 21536 | tf_op jit(solution)/shard_map/ppermute | solution.py:37
  38.8 1.4 %collective-permute-start.7 = (bf16[4,2688]{1,0:T(4,128)(2,1)S(1)}, bf16[4,2688]{1,0:T(4,128)(2,1)S(1)}, u32[]{:S(2)}, u32[]{:S(2)}) collective-permute-start(bf16[4,2688]{1,0:T(4,128)(2,1)S(1)} %get-tuple-element.52), channel_id=1, source_target_pairs={{0,10},{2,8},{4,14},{6,12},{8,2},{10,0},{12,6},{14,4},{16,26},{18,... | collective-permute-start | bytes 64520 | tf_op jit(solution)/shard_map/ppermute | solution.py:37
  40.2 0.6 %collective-permute-done.10.arrived_ref = bf16[4,2816]{1,0:T(4,128)(2,1)S(1)} collective-permute-done((bf16[4,2816]{1,0:T(4,128)(2,1)S(1)}, bf16[4,2816]{1,0:T(4,128)(2,1)S(1)}, u32[]{:S(2)}, u32[]{:S(2)}) %collective-permute-start.10) | collective-permute-done | bytes 22560 | tf_op jit(solution)/shard_map/ppermute | solution.py:37
  40.8 0.1 shard_map.151
  40.9 0.4 collective-permute-start.11
  41.3 0.8 %collective-permute-done.7.arrived_ref = bf16[4,2688]{1,0:T(4,128)(2,1)S(1)} collective-permute-done((bf16[4,2688]{1,0:T(4,128)(2,1)S(1)}, bf16[4,2688]{1,0:T(4,128)(2,1)S(1)}, u32[]{:S(2)}, u32[]{:S(2)}) %collective-permute-start.7) | collective-permute-done | bytes 21536 | tf_op jit(solution)/shard_map/ppermute | solution.py:37
  42.1 1.4 %collective-permute-start.8 = (bf16[4,2688]{1,0:T(4,128)(2,1)S(1)}, bf16[4,2688]{1,0:T(4,128)(2,1)S(1)}, u32[]{:S(2)}, u32[]{:S(2)}) collective-permute-start(bf16[4,2688]{1,0:T(4,128)(2,1)S(1)} %get-tuple-element.54), channel_id=1, source_target_pairs={{0,6},{2,4},{4,2},{6,0},{8,14},{10,12},{12,10},{14,8},{16,22},{18,... | collective-permute-start | bytes 64520 | tf_op jit(solution)/shard_map/ppermute | solution.py:37
  43.5 1.9 %collective-permute-done.8.arrived_a = bf16[4,2688]{1,0:T(4,128)(2,1)S(1)} collective-permute-done((bf16[4,2688]{1,0:T(4,128)(2,1)S(1)}, bf16[4,2688]{1,0:T(4,128)(2,1)S(1)}, u32[]{:S(2)}, u32[]{:S(2)}) %collective-permute-start.8) | collective-permute-done | bytes 21536 | tf_op jit(solution)/shard_map/ppermute | solution.py:37
  45.4 0.1 collective-permute-done.11.arrived_b
  45.5 0.2 shard_map.152.own_ref
  45.7 0.3 collective-permute-start.12
  46.0 0.5 shard_map.153.own_part
  46.5 0.5 %collective-permute-done.12.peer_ref = bf16[4,5376]{1,0:T(4,128)(2,1)S(1)} collective-permute-done((bf16[4,5376]{1,0:T(4,128)(2,1)S(1)}, bf16[4,5376]{1,0:T(4,128)(2,1)S(1)}, u32[]{:S(2)}, u32[]{:S(2)}) %collective-permute-start.12) | collective-permute-done | bytes 43040 | tf_op jit(solution)/shard_map/ppermute | solution.py:28
  47.0 0.4 shard_map.154
  47.4 1.6 %collective-permute-start.13 = (f32[4,256]{1,0:T(4,128)S(1)}, f32[4,256]{1,0:T(4,128)S(1)}, u32[]{:S(2)}, u32[]{:S(2)}) collective-permute-start(f32[4,256]{1,0:T(4,128)S(1)} %shard_map.154), channel_id=1, source_target_pairs={{0,1},{1,0},{2,3},{3,2},{4,5},{5,4},{6,7},{7,6},{8,9},{9,8},{10,11... | collective-permute-start | bytes 12296 | tf_op jit(solution)/shard_map/ppermute | solution.py:28
  49.0 2.1 %collective-permute-done.13 = f32[4,256]{1,0:T(4,128)S(1)} collective-permute-done((f32[4,256]{1,0:T(4,128)S(1)}, f32[4,256]{1,0:T(4,128)S(1)}, u32[]{:S(2)}, u32[]{:S(2)}) %collective-permute-start.13) | collective-permute-done | bytes 4128 | tf_op jit(solution)/shard_map/ppermute | solution.py:28
  51.1 0.6 %add_convert_fusion = bf16[4,256]{1,0:T(4,128)(2,1)} fusion(f32[4,256]{1,0:T(4,128)S(1)} %get-tuple-element.45, f32[4,256]{1,0:T(4,128)S(1)} %shard_map.154, f32[4,256]{1,0:T(4,128)S(1)} %collective-permute-done.13), kind=kLoop, calls=%fused_computation | loop fusion | flops 3072 | bytes 14336 | tf_op jit(solution)/shard_map/convert_element_type | solution.py:769
  (28 shorter events, 0.2 us)
Async XLA Ops:
  0.0 1.4 %copy-start = (bf16[256,2048]{1,0:T(8,128)(2,1)S(1)}, bf16[256,2048]{1,0:T(8,128)(2,1)}, u32[]{:S(2)}) copy-start(bf16[256,2048]{1,0:T(8,128)(2,1)} %wq_ref.3) | copy-start | bytes 3145732
  0.0 1.5 %copy-start.2 = (bf16[256,512]{1,0:T(8,128)(2,1)S(1)}, bf16[256,512]{1,0:T(8,128)(2,1)}, u32[]{:S(2)}) copy-start(bf16[256,512]{1,0:T(8,128)(2,1)} %wk_ref.3) | copy-start | bytes 786436
  0.0 1.6 %copy-start.3 = (bf16[256,512]{1,0:T(8,128)(2,1)S(1)}, bf16[256,512]{1,0:T(8,128)(2,1)}, u32[]{:S(2)}) copy-start(bf16[256,512]{1,0:T(8,128)(2,1)} %wv_ref.3) | copy-start | bytes 786436
  1.6 1.7 %copy-start.1 = (bf16[2048,256]{1,0:T(8,128)(2,1)S(1)}, bf16[2048,256]{1,0:T(8,128)(2,1)}, u32[]{:S(2)}) copy-start(bf16[2048,256]{1,0:T(8,128)(2,1)} %w_ref.5) | copy-start | bytes 3145732
  1.6 15.9 %copy-start.4 = (bf16[4,128,512]{2,1,0:T(8,128)(2,1)S(1)}, bf16[4,128,512]{2,1,0:T(8,128)(2,1)}, u32[]{:S(2)}) copy-start(bf16[4,128,512]{2,1,0:T(8,128)(2,1)} %key_own.1) | copy-start | bytes 1572868
  1.6 15.9 %copy-start.5 = (bf16[4,128,512]{2,1,0:T(8,128)(2,1)S(1)}, bf16[4,128,512]{2,1,0:T(8,128)(2,1)}, u32[]{:S(2)}) copy-start(bf16[4,128,512]{2,1,0:T(8,128)(2,1)} %value_own.1) | copy-start | bytes 1572868
  1.8 1.3 %collective-permute-start = (f32[4,1792]{1,0:T(4,128)S(1)}, f32[4,1792]{1,0:T(4,128)S(1)}, u32[]{:S(2)}, u32[]{:S(2)}) collective-permute-start(f32[4,1792]{1,0:T(4,128)S(1)} %shard_map.138), channel_id=1, source_target_pairs={{0,2},{2,0},{1,3},{3,1},{4,6},{6,4},{5,7},{7,5},{8,10},{10,8},{9,1... | collective-permute-start | bytes 86024 | tf_op jit(solution)/shard_map/ppermute | solution.py:28
  3.2 14.9 %collective-permute-start.2 = (bf16[2048,256]{1,0:T(8,128)(2,1)S(1)}, bf16[2048,256]{1,0:T(8,128)(2,1)S(1)}, u32[]{:S(2)}, u32[]{:S(2)}) collective-permute-start(bf16[2048,256]{1,0:T(8,128)(2,1)S(1)} %copy-done.1), channel_id=1, source_target_pairs={{0,2},{2,0},{1,3},{3,1},{4,6},{6,4},{5,7},{7,5},{8,10},{10,8},{9,1... | collective-permute-start | bytes 3145736 | tf_op jit(solution)/shard_map/ppermute | solution.py:28
  3.7 13.8 %collective-permute-start.1 = (bf16[2,4,128,256]{3,2,1,0:T(8,128)(2,1)S(1)}, bf16[2,4,128,256]{3,2,1,0:T(8,128)(2,1)S(1)}, u32[]{:S(2)}, u32[]{:S(2)}) collective-permute-start(bf16[2,4,128,256]{3,2,1,0:T(8,128)(2,1)S(1)} %get-tuple-element.39), channel_id=1, source_target_pairs={{0,2},{2,0},{1,3},{3,1},{4,6},{6,4},{5,7},{7,5},{8,10},{10,8},{9,1... | collective-permute-start | bytes 1572872 | tf_op jit(solution)/shard_map/ppermute | solution.py:28
  17.4 14.9 %slice-start = ((s8[5505024]{0:T(1024)(128)(4,1)}), s8[4194304]{0:T(1024)(128)(4,1)S(1)}, s32[]{:S(2)}) async-start(s8[5505024]{0:T(1024)(128)(4,1)} %bitcast.2), calls=%async_computation.2 | async-start | bytes 8388608
  17.5 14.9 %slice-start.1 = ((s8[5505024]{0:T(1024)(128)(4,1)}), s8[1310720]{0:T(1024)(128)(4,1)S(1)}, s32[]{:S(2)}) async-start(s8[5505024]{0:T(1024)(128)(4,1)} %bitcast.2), calls=%async_computation.3 | async-start | bytes 2621440
  27.6 1.5 %collective-permute-start.3 = (bf16[4,1024]{1,0:T(4,128)(2,1)S(1)}, bf16[4,1024]{1,0:T(4,128)(2,1)S(1)}, u32[]{:S(2)}, u32[]{:S(2)}) collective-permute-start(bf16[4,1024]{1,0:T(4,128)(2,1)S(1)} %shard_map.141.own_ref), channel_id=1, source_target_pairs={{0,2},{2,0},{1,3},{3,1},{4,6},{6,4},{5,7},{7,5},{8,10},{10,8},{9,1... | collective-permute-start | bytes 24584 | tf_op jit(solution)/shard_map/ppermute | solution.py:28
  29.3 3.0 %collective-permute-start.4 = (f32[4,256]{1,0:T(4,128)S(1)}, f32[4,256]{1,0:T(4,128)S(1)}, u32[]{:S(2)}, u32[]{:S(2)}) collective-permute-start(f32[4,256]{1,0:T(4,128)S(1)} %shard_map.144), channel_id=1, source_target_pairs={{0,3},{1,2},{2,1},{3,0},{4,7},{5,6},{6,5},{7,4},{8,11},{9,10},{10,... | collective-permute-start | bytes 12296 | tf_op jit(solution)/shard_map/ppermute | solution.py:32
  30.7 15.3 %slice-start.2 = ((s8[5505024]{0:T(1024)(128)(4,1)}), s8[4194304]{0:T(1024)(128)(4,1)S(1)}, s32[]{:S(2)}) async-start(s8[5505024]{0:T(1024)(128)(4,1)} %bitcast.4), calls=%async_computation.4 | async-start | bytes 8388608
  32.3 13.7 %slice-start.3 = ((s8[5505024]{0:T(1024)(128)(4,1)}), s8[1310720]{0:T(1024)(128)(4,1)S(1)}, s32[]{:S(2)}) async-start(s8[5505024]{0:T(1024)(128)(4,1)} %bitcast.4), calls=%async_computation.5 | async-start | bytes 2621440
  32.8 1.3 %collective-permute-start.5 = (f32[4,5504]{1,0:T(4,128)S(1)}, f32[4,5504]{1,0:T(4,128)S(1)}, u32[]{:S(2)}, u32[]{:S(2)}) collective-permute-start(f32[4,5504]{1,0:T(4,128)S(1)} %get-tuple-element.48), channel_id=1, source_target_pairs={{0,2},{2,0},{1,3},{3,1},{4,6},{6,4},{5,7},{7,5},{8,10},{10,8},{9,1... | collective-permute-start | bytes 264200 | tf_op jit(solution)/shard_map/ppermute | solution.py:28
  34.2 3.3 %collective-permute-start.9 = (bf16[4,2816]{1,0:T(4,128)(2,1)S(1)}, bf16[4,2816]{1,0:T(4,128)(2,1)S(1)}, u32[]{:S(2)}, u32[]{:S(2)}) collective-permute-start(bf16[4,2816]{1,0:T(4,128)(2,1)S(1)} %get-tuple-element.56), channel_id=1, source_target_pairs={{0,10},{2,8},{4,14},{6,12},{8,2},{10,0},{12,6},{14,4},{16,26},{18,... | collective-permute-start | bytes 67592 | tf_op jit(solution)/shard_map/ppermute | solution.py:37
  34.7 4.1 %collective-permute-start.6 = (bf16[4,2688]{1,0:T(4,128)(2,1)S(1)}, bf16[4,2688]{1,0:T(4,128)(2,1)S(1)}, u32[]{:S(2)}, u32[]{:S(2)}) collective-permute-start(bf16[4,2688]{1,0:T(4,128)(2,1)S(1)} %get-tuple-element.50), channel_id=1, source_target_pairs={{0,18},{2,16},{4,22},{6,20},{8,26},{10,24},{12,30},{14,28},{16,2},... | collective-permute-start | bytes 64520 | tf_op jit(solution)/shard_map/ppermute | solution.py:37
  37.6 3.2 %collective-permute-start.10 = (bf16[4,2816]{1,0:T(4,128)(2,1)S(1)}, bf16[4,2816]{1,0:T(4,128)(2,1)S(1)}, u32[]{:S(2)}, u32[]{:S(2)}) collective-permute-start(bf16[4,2816]{1,0:T(4,128)(2,1)S(1)} %get-tuple-element.58), channel_id=1, source_target_pairs={{0,6},{2,4},{4,2},{6,0},{8,14},{10,12},{12,10},{14,8},{16,22},{18,... | collective-permute-start | bytes 67592 | tf_op jit(solution)/shard_map/ppermute | solution.py:37
  38.8 3.3 %collective-permute-start.7 = (bf16[4,2688]{1,0:T(4,128)(2,1)S(1)}, bf16[4,2688]{1,0:T(4,128)(2,1)S(1)}, u32[]{:S(2)}, u32[]{:S(2)}) collective-permute-start(bf16[4,2688]{1,0:T(4,128)(2,1)S(1)} %get-tuple-element.52), channel_id=1, source_target_pairs={{0,10},{2,8},{4,14},{6,12},{8,2},{10,0},{12,6},{14,4},{16,26},{18,... | collective-permute-start | bytes 64520 | tf_op jit(solution)/shard_map/ppermute | solution.py:37
  40.9 4.6 %collective-permute-start.11 = (bf16[4,2816]{1,0:T(4,128)(2,1)S(1)}, bf16[4,2816]{1,0:T(4,128)(2,1)S(1)}, u32[]{:S(2)}, u32[]{:S(2)}) collective-permute-start(bf16[4,2816]{1,0:T(4,128)(2,1)S(1)} %get-tuple-element.60), channel_id=1, source_target_pairs={{0,18},{2,16},{4,22},{6,20},{8,26},{10,24},{12,30},{14,28},{16,2},... | collective-permute-start | bytes 67592 | tf_op jit(solution)/shard_map/ppermute | solution.py:37
  42.1 3.3 %collective-permute-start.8 = (bf16[4,2688]{1,0:T(4,128)(2,1)S(1)}, bf16[4,2688]{1,0:T(4,128)(2,1)S(1)}, u32[]{:S(2)}, u32[]{:S(2)}) collective-permute-start(bf16[4,2688]{1,0:T(4,128)(2,1)S(1)} %get-tuple-element.54), channel_id=1, source_target_pairs={{0,6},{2,4},{4,2},{6,0},{8,14},{10,12},{12,10},{14,8},{16,22},{18,... | collective-permute-start | bytes 64520 | tf_op jit(solution)/shard_map/ppermute | solution.py:37
  45.7 1.3 %collective-permute-start.12 = (bf16[4,5376]{1,0:T(4,128)(2,1)S(1)}, bf16[4,5376]{1,0:T(4,128)(2,1)S(1)}, u32[]{:S(2)}, u32[]{:S(2)}) collective-permute-start(bf16[4,5376]{1,0:T(4,128)(2,1)S(1)} %shard_map.152.own_ref), channel_id=1, source_target_pairs={{0,2},{2,0},{1,3},{3,1},{4,6},{6,4},{5,7},{7,5},{8,10},{10,8},{9,1... | collective-permute-start | bytes 129032 | tf_op jit(solution)/shard_map/ppermute | solution.py:28
  47.4 3.7 %collective-permute-start.13 = (f32[4,256]{1,0:T(4,128)S(1)}, f32[4,256]{1,0:T(4,128)S(1)}, u32[]{:S(2)}, u32[]{:S(2)}) collective-permute-start(f32[4,256]{1,0:T(4,128)S(1)} %shard_map.154), channel_id=1, source_target_pairs={{0,1},{1,0},{2,3},{3,2},{4,5},{5,4},{6,7},{7,6},{8,9},{9,8},{10,11... | collective-permute-start | bytes 12296 | tf_op jit(solution)/shard_map/ppermute | solution.py:28

commit v12 on v11

--- a/solution.py
+++ b/solution.py
@@ -1,3 +1,4 @@
+import functools
 import math
 
 import jax
@@ -520,34 +521,25 @@
     up_columns(scaled_ref[...], w_ref, up_half(), mine_ref)
 
 
-def squares_tile(squares):
+def up_pair_kernel(mine_ref, arrived_ref, total_a, sent_a, total_b, sent_b):
+    half = mine_ref.shape[1] - LANES
+    start = total_a.shape[1]
+    total = mine_ref[:, :half] + arrived_ref[:, :half]
+    squares = mine_ref[:, half:] + arrived_ref[:, half:]
     lane = lax.broadcasted_iota(jnp.int32, squares.shape, 1)
     tile = jnp.zeros_like(squares)
     for p, piece in enumerate(pieces_of(squares)):
         tile = jnp.where(lane == p, piece, tile)
-    return tile.astype(jnp.bfloat16)
-
-
-def send_sum(total, sent_ref):
-    half = sent_ref.shape[1] - LANES
-    sent_ref[:, :half] = total[:, :half].astype(jnp.bfloat16)
-    sent_ref[:, half:] = squares_tile(total[:, half:])
-
-
-def add_arrived(total, arrived):
-    half = total.shape[1] - LANES
-    arrived = arrived.astype(jnp.float32)
-    squares = jnp.sum(arrived[:, half:], axis=1, keepdims=True)
-    return total[:, :half] + arrived[:, :half], total[:, half:] + squares
-
-
-def up_pair_kernel(mine_ref, arrived_ref, total_a, sent_a, total_b, sent_b):
-    total = mine_ref[...] + arrived_ref[...]
-    width = total_a.shape[1]
-    total_a[...] = total[:, :width]
-    sent_a[...] = total[:, :width].astype(jnp.bfloat16)
-    total_b[...] = total[:, width:]
-    send_sum(total[:, width:], sent_b)
+    total_a[...] = total[:, :start]
+    sent_a[...] = total[:, :start].astype(jnp.bfloat16)
+    put_b(total[:, start:], tile, total_b, sent_b)
+
+
+def put_b(total, tile, total_ref, sent_ref):
+    width = total.shape[1]
+    for at, value in ((slice(0, width), total), (slice(width, None), tile)):
+        total_ref[:, at] = value
+        sent_ref[:, at] = value.astype(jnp.bfloat16)
 
 
 def up_add_a_kernel(part_ref, arrived_ref, total_ref, sent_ref):
@@ -556,19 +548,22 @@
     sent_ref[...] = total.astype(jnp.bfloat16)
 
 
-def up_add_b_kernel(part_ref, arrived_ref, total_ref, sent_ref):
-    total = jnp.concatenate(add_arrived(part_ref[...], arrived_ref[...]), axis=1)
-    total_ref[...] = total
-    send_sum(total, sent_ref)
+def up_add_b_kernel(shift, part_ref, arrived_ref, total_ref, sent_ref):
+    width = part_ref.shape[1] - LANES
+    total = part_ref[:, :width] + arrived_ref[:, :width].astype(jnp.float32)
+    pieces = pltpu.roll(arrived_ref[:, width:].astype(jnp.float32), shift, 1)
+    put_b(total, part_ref[:, width:] + pieces, total_ref, sent_ref)
 
 
 def activate_kernel(part_a, arrived_a, part_b, arrived_b, out_ref):
-    width = part_a.shape[1]
+    start, width = part_a.shape[1], part_b.shape[1] - LANES
+    pieces = part_b[:, width:] + arrived_b[:, width:].astype(jnp.float32)
+    squares = jnp.sum(pieces, axis=1, keepdims=True)
+    inv_mlp = lax.rsqrt(squares / D + NORM_EPS)
     total_a = part_a[...] + arrived_a[...].astype(jnp.float32)
-    total_b, squares = add_arrived(part_b[...], arrived_b[...])
-    inv_mlp = lax.rsqrt(squares[:, :1] / D + NORM_EPS)
-    out_ref[:, :width] = squared_relu(total_a * inv_mlp).astype(jnp.bfloat16)
-    out_ref[:, width:] = squared_relu(total_b * inv_mlp).astype(jnp.bfloat16)
+    out_ref[:, :start] = squared_relu(total_a * inv_mlp).astype(jnp.bfloat16)
+    total_b = part_b[:, :width] + arrived_b[:, :width].astype(jnp.float32)
+    out_ref[:, start:] = squared_relu(total_b * inv_mlp).astype(jnp.bfloat16)
 
 
 def down_own_kernel(own_ref, w_ref, out_ref):
@@ -736,10 +731,11 @@
         flops=up_mine.size,
     )
     parts = [pair[:2], pair[2:]]
-    orders = [[2, 1, 0], [1, 0, 2]]
+    orders = [(2, 1, 0), (1, 0, 2)]
     arrived = [swap_chips(part[1], order[0]) for part, order in zip(parts, orders)]
     for step in range(1, chip_bits()):
-        for i, kernel in enumerate((up_add_a_kernel, up_add_b_kernel)):
+        add_b = functools.partial(up_add_b_kernel, 3 * 2 ** (step - 1))
+        for i, kernel in enumerate((up_add_a_kernel, add_b)):
             parts[i] = local_kernel(
                 kernel, sums[i], [parts[i][0], arrived[i]], flops=n_req * widths[i]
             )

time: 51.9 us -> 51.8 us (level)
  no operation moved by 1% of the time
where the time goes in v12:
time: 51.8 us; the launch traced here: 51.6 us
  blocking collectives  22.7 us (44%)
  waiting for transfers between devices  12.1 us (23%)
  starting transfers between devices  10.1 us (19%)
  Pallas kernels  5.55 us (11%)
  other arithmetic  0.63 us (1%)
    all_to_all x1, blocking collectives, per_device(): lax.all_to_all(jnp.broadcast_to(qkv_message[None], (n_chips,) + qkv_messa...  13.6 us
    all_to_all x1, blocking collectives, per_device(): lax.all_to_all(message, ('chip', 'core'), 0, 0, axis_index_groups=sides)  9.09 us
    ppermute x6, waiting for transfers between devices, swap_chips(): lax.ppermute(values_in, ('chip', 'core'), [(i, i ^ 2 << bit ^ 1) for i in...  6.45 us
    pallas_call x19, Pallas kernels, local_kernel(): pl.pallas_call(kernel, out_shape=outs, in_specs=in_specs, out_specs=[IN_V...  5.55 us
    ppermute x6, starting transfers between devices, swap_chips(): lax.ppermute(values_in, ('chip', 'core'), [(i, i ^ 2 << bit ^ 1) for i in...  4.67 us
    ppermute x7, waiting for transfers between devices, swap(): return lax.ppermute(values_in, axis, [(i, i ^ 1) for i in range(n)])  4.38 us
    ppermute x7, starting transfers between devices, swap(): return lax.ppermute(values_in, axis, [(i, i ^ 1) for i in range(n)])  4 us
    ppermute x1, starting transfers between devices, swap_diagonal(): lax.ppermute(values_in, ('core', 'tp'), [(i, 3 - i) for i in range(4)])  1.48 us
  transfers between devices with their start and end apart: 14, of which 12 were waited for; matrix products, arithmetic and copies ran while one was open for 0% of the time, Pallas kernels for 5%

profile of v12, /device:TPU:0, one launch (start us, length us, event | category | flops | bytes accessed | tf_op | source)
XLA Modules:
  0.0 51.6 jit_solution(8380456836325951273)
XLA Ops:
  0.0 1.3 %shard_map.136 = (bf16[4,256]{1,0:T(4,128)(2,1)S(1)}, f32[4,128]{1,0:T(4,128)S(1)}, f32[4,128]{1,0:T(4,128)S(1)}, bf16[4,256]{1,0:T(4,128)(2,1)S(1)}, f32[1,256]...) custom-call(bf16[4,256]{1,0:T(4,128)(2,1)} %x_hbm.1, f32[1,256]{1,0:T(1,128)} %bitcast.6, f32[1,256]{1,0:T(1,128)} %bitcast.7, ...), custom_call_target="tpu_custom_call" | custom-call | flops 4000000000 | bytes 1054752 | tf_op jit(solution)/shard_map/pallas_call | solution.py:255
  1.3 0.2 copy-done
  1.4 0.0 copy-done.2
  1.5 0.1 copy-done.3
  1.6 0.2 shard_map.138
  1.8 0.5 collective-permute-start
  2.3 0.2 shard_map.137.mine_ref
  2.5 0.7 %collective-permute-done.arrived_ref = f32[4,1792]{1,0:T(4,128)S(1)} collective-permute-done((f32[4,1792]{1,0:T(4,128)S(1)}, f32[4,1792]{1,0:T(4,128)S(1)}, u32[]{:S(2)}, u32[]{:S(2)}) %collective-permute-start) | collective-permute-done | bytes 28704 | tf_op jit(solution)/shard_map/ppermute | solution.py:29
  3.1 0.1 shard_map.139
  3.2 0.4 collective-permute-start.2
  3.7 0.2 collective-permute-start.1
  3.9 13.6 %all_to_all.10 = f16[8,4,1664]{2,1,0:T(4,128)(2,1)S(1)} all-to-all(f16[8,4,1664]{2,1,0:T(4,128)(2,1)S(1)} %broadcast_in_dim.2), channel_id=1, replica_groups={{0,4,10,14,16,20,26,30},{2,6,8,12,18,22,24,28},{1,5,11,15,17,21,27,31},..., dimensions={0} | all-to-all | bytes 212992 | tf_op jit(solution)/shard_map/all_to_all | solution.py:657
  17.5 0.6 %shard_map.140 = bf16[8,8,640]{2,1,0:T(8,128)(2,1)S(1)} custom-call(f32[8,4,1664]{2,1,0:T(4,128)S(1)} %convert_element_type.10.arrived_ref, bf16[4,128,512]{2,1,0:T(8,128)(2,1)S(1)} %copy-done.4, bf16[4,128,512]{2,1,0:T(8,128)(2,1)S(1)} %copy-done.5, bf16[2,4,128,256]{3,2,1,0:T(8,128)(2,1)S(1)} %collective-permute-done.1.cache_peer, ...), custom_call_target="tpu_custom_call" | custom-call | flops 4000000000 | bytes 1789952 | tf_op jit(solution)/shard_map/pallas_call | solution.py:255
  18.2 9.1 %all_to_all.11.arrived_ref = bf16[8,8,640]{2,1,0:T(8,128)(2,1)S(1)} all-to-all(bf16[8,8,640]{2,1,0:T(8,128)(2,1)S(1)} %shard_map.140), channel_id=1, replica_groups={{0,4,10,14,16,20,26,30},{2,6,8,12,18,22,24,28},{1,5,11,15,17,21,27,31},..., dimensions={0} | all-to-all | bytes 163840 | tf_op jit(solution)/shard_map/all_to_all | solution.py:677
  27.3 0.3 shard_map.141.own_ref
  27.6 0.7 %collective-permute-start.3 = (bf16[4,1024]{1,0:T(4,128)(2,1)S(1)}, bf16[4,1024]{1,0:T(4,128)(2,1)S(1)}, u32[]{:S(2)}, u32[]{:S(2)}) collective-permute-start(bf16[4,1024]{1,0:T(4,128)(2,1)S(1)} %shard_map.141.own_ref), channel_id=1, source_target_pairs={{0,2},{2,0},{1,3},{3,1},{4,6},{6,4},{5,7},{7,5},{8,10},{10,8},{9,1... | collective-permute-start | bytes 24584 | tf_op jit(solution)/shard_map/ppermute | solution.py:29
  28.3 0.2 shard_map.143.own_part
  28.4 0.6 %collective-permute-done.3.peer_ref = bf16[4,1024]{1,0:T(4,128)(2,1)S(1)} collective-permute-done((bf16[4,1024]{1,0:T(4,128)(2,1)S(1)}, bf16[4,1024]{1,0:T(4,128)(2,1)S(1)}, u32[]{:S(2)}, u32[]{:S(2)}) %collective-permute-start.3) | collective-permute-done | bytes 8224 | tf_op jit(solution)/shard_map/ppermute | solution.py:29
  29.1 0.2 shard_map.144
  29.3 1.5 %collective-permute-start.4 = (f32[4,256]{1,0:T(4,128)S(1)}, f32[4,256]{1,0:T(4,128)S(1)}, u32[]{:S(2)}, u32[]{:S(2)}) collective-permute-start(f32[4,256]{1,0:T(4,128)S(1)} %shard_map.144), channel_id=1, source_target_pairs={{0,3},{1,2},{2,1},{3,0},{4,7},{5,6},{6,5},{7,4},{8,11},{9,10},{10,... | collective-permute-start | bytes 12296 | tf_op jit(solution)/shard_map/ppermute | solution.py:33
  30.8 0.2 shard_map.142.part_ref
  31.0 1.3 %collective-permute-done.4.peer_ref = f32[4,256]{1,0:T(4,128)S(1)} collective-permute-done((f32[4,256]{1,0:T(4,128)S(1)}, f32[4,256]{1,0:T(4,128)S(1)}, u32[]{:S(2)}, u32[]{:S(2)}) %collective-permute-start.4) | collective-permute-done | bytes 4128 | tf_op jit(solution)/shard_map/ppermute | solution.py:33
  32.3 0.5 shard_map.145
  32.8 0.4 collective-permute-start.5
  33.2 0.5 shard_map.146.mine_ref
  33.7 0.5 collective-permute-done.5.arrived_ref
  34.2 0.5 collective-permute-start.9
  34.7 0.7 %collective-permute-start.6 = (bf16[4,2688]{1,0:T(4,128)(2,1)S(1)}, bf16[4,2688]{1,0:T(4,128)(2,1)S(1)}, u32[]{:S(2)}, u32[]{:S(2)}) collective-permute-start(bf16[4,2688]{1,0:T(4,128)(2,1)S(1)} %get-tuple-element.50), channel_id=1, source_target_pairs={{0,18},{2,16},{4,22},{6,20},{8,26},{10,24},{12,30},{14,28},{16,2},... | collective-permute-start | bytes 64520 | tf_op jit(solution)/shard_map/ppermute | solution.py:38
  35.4 2.1 %collective-permute-done.9.arrived_ref = bf16[4,2816]{1,0:T(4,128)(2,1)S(1)} collective-permute-done((bf16[4,2816]{1,0:T(4,128)(2,1)S(1)}, bf16[4,2816]{1,0:T(4,128)(2,1)S(1)}, u32[]{:S(2)}, u32[]{:S(2)}) %collective-permute-start.9) | collective-permute-done | bytes 22560 | tf_op jit(solution)/shard_map/ppermute | solution.py:38
  37.5 0.1 shard_map.150
  37.6 0.3 collective-permute-start.10
  37.9 0.9 %collective-permute-done.6.arrived_ref = bf16[4,2688]{1,0:T(4,128)(2,1)S(1)} collective-permute-done((bf16[4,2688]{1,0:T(4,128)(2,1)S(1)}, bf16[4,2688]{1,0:T(4,128)(2,1)S(1)}, u32[]{:S(2)}, u32[]{:S(2)}) %collective-permute-start.6) | collective-permute-done | bytes 21536 | tf_op jit(solution)/shard_map/ppermute | solution.py:38
  38.8 1.4 %collective-permute-start.7 = (bf16[4,2688]{1,0:T(4,128)(2,1)S(1)}, bf16[4,2688]{1,0:T(4,128)(2,1)S(1)}, u32[]{:S(2)}, u32[]{:S(2)}) collective-permute-start(bf16[4,2688]{1,0:T(4,128)(2,1)S(1)} %get-tuple-element.52), channel_id=1, source_target_pairs={{0,10},{2,8},{4,14},{6,12},{8,2},{10,0},{12,6},{14,4},{16,26},{18,... | collective-permute-start | bytes 64520 | tf_op jit(solution)/shard_map/ppermute | solution.py:38
  40.2 0.6 %collective-permute-done.10.arrived_ref = bf16[4,2816]{1,0:T(4,128)(2,1)S(1)} collective-permute-done((bf16[4,2816]{1,0:T(4,128)(2,1)S(1)}, bf16[4,2816]{1,0:T(4,128)(2,1)S(1)}, u32[]{:S(2)}, u32[]{:S(2)}) %collective-permute-start.10) | collective-permute-done | bytes 22560 | tf_op jit(solution)/shard_map/ppermute | solution.py:38
  40.8 0.1 shard_map.151
  40.9 0.4 collective-permute-start.11
  41.3 0.8 %collective-permute-done.7.arrived_ref = bf16[4,2688]{1,0:T(4,128)(2,1)S(1)} collective-permute-done((bf16[4,2688]{1,0:T(4,128)(2,1)S(1)}, bf16[4,2688]{1,0:T(4,128)(2,1)S(1)}, u32[]{:S(2)}, u32[]{:S(2)}) %collective-permute-start.7) | collective-permute-done | bytes 21536 | tf_op jit(solution)/shard_map/ppermute | solution.py:38
  42.1 1.4 %collective-permute-start.8 = (bf16[4,2688]{1,0:T(4,128)(2,1)S(1)}, bf16[4,2688]{1,0:T(4,128)(2,1)S(1)}, u32[]{:S(2)}, u32[]{:S(2)}) collective-permute-start(bf16[4,2688]{1,0:T(4,128)(2,1)S(1)} %get-tuple-element.54), channel_id=1, source_target_pairs={{0,6},{2,4},{4,2},{6,0},{8,14},{10,12},{12,10},{14,8},{16,22},{18,... | collective-permute-start | bytes 64520 | tf_op jit(solution)/shard_map/ppermute | solution.py:38
  43.5 1.9 %collective-permute-done.8.arrived_a = bf16[4,2688]{1,0:T(4,128)(2,1)S(1)} collective-permute-done((bf16[4,2688]{1,0:T(4,128)(2,1)S(1)}, bf16[4,2688]{1,0:T(4,128)(2,1)S(1)}, u32[]{:S(2)}, u32[]{:S(2)}) %collective-permute-start.8) | collective-permute-done | bytes 21536 | tf_op jit(solution)/shard_map/ppermute | solution.py:38
  45.4 0.1 collective-permute-done.11.arrived_b
  45.5 0.1 shard_map.152.own_ref
  45.6 0.3 collective-permute-start.12
  45.9 0.5 shard_map.153.own_part
  46.4 0.5 collective-permute-done.12.peer_ref
  46.9 0.4 shard_map.154
  47.4 1.6 %collective-permute-start.13 = (f32[4,256]{1,0:T(4,128)S(1)}, f32[4,256]{1,0:T(4,128)S(1)}, u32[]{:S(2)}, u32[]{:S(2)}) collective-permute-start(f32[4,256]{1,0:T(4,128)S(1)} %shard_map.154), channel_id=1, source_target_pairs={{0,1},{1,0},{2,3},{3,2},{4,5},{5,4},{6,7},{7,6},{8,9},{9,8},{10,11... | collective-permute-start | bytes 12296 | tf_op jit(solution)/shard_map/ppermute | solution.py:29
  48.9 2.1 %collective-permute-done.13 = f32[4,256]{1,0:T(4,128)S(1)} collective-permute-done((f32[4,256]{1,0:T(4,128)S(1)}, f32[4,256]{1,0:T(4,128)S(1)}, u32[]{:S(2)}, u32[]{:S(2)}) %collective-permute-start.13) | collective-permute-done | bytes 4128 | tf_op jit(solution)/shard_map/ppermute | solution.py:29
  51.0 0.6 %add_convert_fusion = bf16[4,256]{1,0:T(4,128)(2,1)} fusion(f32[4,256]{1,0:T(4,128)S(1)} %get-tuple-element.45, f32[4,256]{1,0:T(4,128)S(1)} %shard_map.154, f32[4,256]{1,0:T(4,128)S(1)} %collective-permute-done.13), kind=kLoop, calls=%fused_computation | loop fusion | flops 3072 | bytes 14336 | tf_op jit(solution)/shard_map/convert_element_type | solution.py:765
  (28 shorter events, 0.2 us)
Async XLA Ops:
  0.0 1.4 %copy-start = (bf16[256,2048]{1,0:T(8,128)(2,1)S(1)}, bf16[256,2048]{1,0:T(8,128)(2,1)}, u32[]{:S(2)}) copy-start(bf16[256,2048]{1,0:T(8,128)(2,1)} %wq_ref.3) | copy-start | bytes 3145732
  0.0 1.5 %copy-start.2 = (bf16[256,512]{1,0:T(8,128)(2,1)S(1)}, bf16[256,512]{1,0:T(8,128)(2,1)}, u32[]{:S(2)}) copy-start(bf16[256,512]{1,0:T(8,128)(2,1)} %wk_ref.3) | copy-start | bytes 786436
  0.0 1.6 %copy-start.3 = (bf16[256,512]{1,0:T(8,128)(2,1)S(1)}, bf16[256,512]{1,0:T(8,128)(2,1)}, u32[]{:S(2)}) copy-start(bf16[256,512]{1,0:T(8,128)(2,1)} %wv_ref.3) | copy-start | bytes 786436
  1.6 1.7 %copy-start.1 = (bf16[2048,256]{1,0:T(8,128)(2,1)S(1)}, bf16[2048,256]{1,0:T(8,128)(2,1)}, u32[]{:S(2)}) copy-start(bf16[2048,256]{1,0:T(8,128)(2,1)} %w_ref.5) | copy-start | bytes 3145732
  1.6 15.9 %copy-start.4 = (bf16[4,128,512]{2,1,0:T(8,128)(2,1)S(1)}, bf16[4,128,512]{2,1,0:T(8,128)(2,1)}, u32[]{:S(2)}) copy-start(bf16[4,128,512]{2,1,0:T(8,128)(2,1)} %key_own.1) | copy-start | bytes 1572868
  1.6 15.9 %copy-start.5 = (bf16[4,128,512]{2,1,0:T(8,128)(2,1)S(1)}, bf16[4,128,512]{2,1,0:T(8,128)(2,1)}, u32[]{:S(2)}) copy-start(bf16[4,128,512]{2,1,0:T(8,128)(2,1)} %value_own.1) | copy-start | bytes 1572868
  1.8 1.3 %collective-permute-start = (f32[4,1792]{1,0:T(4,128)S(1)}, f32[4,1792]{1,0:T(4,128)S(1)}, u32[]{:S(2)}, u32[]{:S(2)}) collective-permute-start(f32[4,1792]{1,0:T(4,128)S(1)} %shard_map.138), channel_id=1, source_target_pairs={{0,2},{2,0},{1,3},{3,1},{4,6},{6,4},{5,7},{7,5},{8,10},{10,8},{9,1... | collective-permute-start | bytes 86024 | tf_op jit(solution)/shard_map/ppermute | solution.py:29
  3.2 14.9 %collective-permute-start.2 = (bf16[2048,256]{1,0:T(8,128)(2,1)S(1)}, bf16[2048,256]{1,0:T(8,128)(2,1)S(1)}, u32[]{:S(2)}, u32[]{:S(2)}) collective-permute-start(bf16[2048,256]{1,0:T(8,128)(2,1)S(1)} %copy-done.1), channel_id=1, source_target_pairs={{0,2},{2,0},{1,3},{3,1},{4,6},{6,4},{5,7},{7,5},{8,10},{10,8},{9,1... | collective-permute-start | bytes 3145736 | tf_op jit(solution)/shard_map/ppermute | solution.py:29
  3.7 13.8 %collective-permute-start.1 = (bf16[2,4,128,256]{3,2,1,0:T(8,128)(2,1)S(1)}, bf16[2,4,128,256]{3,2,1,0:T(8,128)(2,1)S(1)}, u32[]{:S(2)}, u32[]{:S(2)}) collective-permute-start(bf16[2,4,128,256]{3,2,1,0:T(8,128)(2,1)S(1)} %get-tuple-element.39), channel_id=1, source_target_pairs={{0,2},{2,0},{1,3},{3,1},{4,6},{6,4},{5,7},{7,5},{8,10},{10,8},{9,1... | collective-permute-start | bytes 1572872 | tf_op jit(solution)/shard_map/ppermute | solution.py:29
  17.4 14.9 %slice-start = ((s8[5505024]{0:T(1024)(128)(4,1)}), s8[4194304]{0:T(1024)(128)(4,1)S(1)}, s32[]{:S(2)}) async-start(s8[5505024]{0:T(1024)(128)(4,1)} %bitcast.2), calls=%async_computation.2 | async-start | bytes 8388608
  17.5 14.9 %slice-start.1 = ((s8[5505024]{0:T(1024)(128)(4,1)}), s8[1310720]{0:T(1024)(128)(4,1)S(1)}, s32[]{:S(2)}) async-start(s8[5505024]{0:T(1024)(128)(4,1)} %bitcast.2), calls=%async_computation.3 | async-start | bytes 2621440
  27.6 1.5 %collective-permute-start.3 = (bf16[4,1024]{1,0:T(4,128)(2,1)S(1)}, bf16[4,1024]{1,0:T(4,128)(2,1)S(1)}, u32[]{:S(2)}, u32[]{:S(2)}) collective-permute-start(bf16[4,1024]{1,0:T(4,128)(2,1)S(1)} %shard_map.141.own_ref), channel_id=1, source_target_pairs={{0,2},{2,0},{1,3},{3,1},{4,6},{6,4},{5,7},{7,5},{8,10},{10,8},{9,1... | collective-permute-start | bytes 24584 | tf_op jit(solution)/shard_map/ppermute | solution.py:29
  29.3 3.0 %collective-permute-start.4 = (f32[4,256]{1,0:T(4,128)S(1)}, f32[4,256]{1,0:T(4,128)S(1)}, u32[]{:S(2)}, u32[]{:S(2)}) collective-permute-start(f32[4,256]{1,0:T(4,128)S(1)} %shard_map.144), channel_id=1, source_target_pairs={{0,3},{1,2},{2,1},{3,0},{4,7},{5,6},{6,5},{7,4},{8,11},{9,10},{10,... | collective-permute-start | bytes 12296 | tf_op jit(solution)/shard_map/ppermute | solution.py:33
  30.7 15.2 %slice-start.2 = ((s8[5505024]{0:T(1024)(128)(4,1)}), s8[4194304]{0:T(1024)(128)(4,1)S(1)}, s32[]{:S(2)}) async-start(s8[5505024]{0:T(1024)(128)(4,1)} %bitcast.4), calls=%async_computation.4 | async-start | bytes 8388608
  32.3 13.6 %slice-start.3 = ((s8[5505024]{0:T(1024)(128)(4,1)}), s8[1310720]{0:T(1024)(128)(4,1)S(1)}, s32[]{:S(2)}) async-start(s8[5505024]{0:T(1024)(128)(4,1)} %bitcast.4), calls=%async_computation.5 | async-start | bytes 2621440
  32.8 1.3 %collective-permute-start.5 = (f32[4,5504]{1,0:T(4,128)S(1)}, f32[4,5504]{1,0:T(4,128)S(1)}, u32[]{:S(2)}, u32[]{:S(2)}) collective-permute-start(f32[4,5504]{1,0:T(4,128)S(1)} %get-tuple-element.48), channel_id=1, source_target_pairs={{0,2},{2,0},{1,3},{3,1},{4,6},{6,4},{5,7},{7,5},{8,10},{10,8},{9,1... | collective-permute-start | bytes 264200 | tf_op jit(solution)/shard_map/ppermute | solution.py:29
  34.2 3.3 %collective-permute-start.9 = (bf16[4,2816]{1,0:T(4,128)(2,1)S(1)}, bf16[4,2816]{1,0:T(4,128)(2,1)S(1)}, u32[]{:S(2)}, u32[]{:S(2)}) collective-permute-start(bf16[4,2816]{1,0:T(4,128)(2,1)S(1)} %get-tuple-element.56), channel_id=1, source_target_pairs={{0,10},{2,8},{4,14},{6,12},{8,2},{10,0},{12,6},{14,4},{16,26},{18,... | collective-permute-start | bytes 67592 | tf_op jit(solution)/shard_map/ppermute | solution.py:38
  34.7 4.1 %collective-permute-start.6 = (bf16[4,2688]{1,0:T(4,128)(2,1)S(1)}, bf16[4,2688]{1,0:T(4,128)(2,1)S(1)}, u32[]{:S(2)}, u32[]{:S(2)}) collective-permute-start(bf16[4,2688]{1,0:T(4,128)(2,1)S(1)} %get-tuple-element.50), channel_id=1, source_target_pairs={{0,18},{2,16},{4,22},{6,20},{8,26},{10,24},{12,30},{14,28},{16,2},... | collective-permute-start | bytes 64520 | tf_op jit(solution)/shard_map/ppermute | solution.py:38
  37.6 3.2 %collective-permute-start.10 = (bf16[4,2816]{1,0:T(4,128)(2,1)S(1)}, bf16[4,2816]{1,0:T(4,128)(2,1)S(1)}, u32[]{:S(2)}, u32[]{:S(2)}) collective-permute-start(bf16[4,2816]{1,0:T(4,128)(2,1)S(1)} %get-tuple-element.58), channel_id=1, source_target_pairs={{0,6},{2,4},{4,2},{6,0},{8,14},{10,12},{12,10},{14,8},{16,22},{18,... | collective-permute-start | bytes 67592 | tf_op jit(solution)/shard_map/ppermute | solution.py:38
  38.8 3.3 %collective-permute-start.7 = (bf16[4,2688]{1,0:T(4,128)(2,1)S(1)}, bf16[4,2688]{1,0:T(4,128)(2,1)S(1)}, u32[]{:S(2)}, u32[]{:S(2)}) collective-permute-start(bf16[4,2688]{1,0:T(4,128)(2,1)S(1)} %get-tuple-element.52), channel_id=1, source_target_pairs={{0,10},{2,8},{4,14},{6,12},{8,2},{10,0},{12,6},{14,4},{16,26},{18,... | collective-permute-start | bytes 64520 | tf_op jit(solution)/shard_map/ppermute | solution.py:38
  40.9 4.6 %collective-permute-start.11 = (bf16[4,2816]{1,0:T(4,128)(2,1)S(1)}, bf16[4,2816]{1,0:T(4,128)(2,1)S(1)}, u32[]{:S(2)}, u32[]{:S(2)}) collective-permute-start(bf16[4,2816]{1,0:T(4,128)(2,1)S(1)} %get-tuple-element.60), channel_id=1, source_target_pairs={{0,18},{2,16},{4,22},{6,20},{8,26},{10,24},{12,30},{14,28},{16,2},... | collective-permute-start | bytes 67592 | tf_op jit(solution)/shard_map/ppermute | solution.py:38
  42.1 3.3 %collective-permute-start.8 = (bf16[4,2688]{1,0:T(4,128)(2,1)S(1)}, bf16[4,2688]{1,0:T(4,128)(2,1)S(1)}, u32[]{:S(2)}, u32[]{:S(2)}) collective-permute-start(bf16[4,2688]{1,0:T(4,128)(2,1)S(1)} %get-tuple-element.54), channel_id=1, source_target_pairs={{0,6},{2,4},{4,2},{6,0},{8,14},{10,12},{12,10},{14,8},{16,22},{18,... | collective-permute-start | bytes 64520 | tf_op jit(solution)/shard_map/ppermute | solution.py:38
  45.6 1.3 %collective-permute-start.12 = (bf16[4,5376]{1,0:T(4,128)(2,1)S(1)}, bf16[4,5376]{1,0:T(4,128)(2,1)S(1)}, u32[]{:S(2)}, u32[]{:S(2)}) collective-permute-start(bf16[4,5376]{1,0:T(4,128)(2,1)S(1)} %shard_map.152.own_ref), channel_id=1, source_target_pairs={{0,2},{2,0},{1,3},{3,1},{4,6},{6,4},{5,7},{7,5},{8,10},{10,8},{9,1... | collective-permute-start | bytes 129032 | tf_op jit(solution)/shard_map/ppermute | solution.py:29
  47.4 3.7 %collective-permute-start.13 = (f32[4,256]{1,0:T(4,128)S(1)}, f32[4,256]{1,0:T(4,128)S(1)}, u32[]{:S(2)}, u32[]{:S(2)}) collective-permute-start(f32[4,256]{1,0:T(4,128)S(1)} %shard_map.154), channel_id=1, source_target_pairs={{0,1},{1,0},{2,3},{3,2},{4,5},{5,4},{6,7},{7,6},{8,9},{9,8},{10,11... | collective-permute-start | bytes 12296 | tf_op jit(solution)/shard_map/ppermute | solution.py:29

commit v13 on v12

--- a/solution.py
+++ b/solution.py
@@ -1,4 +1,3 @@
-import functools
 import math
 
 import jax
@@ -528,8 +527,9 @@
     squares = mine_ref[:, half:] + arrived_ref[:, half:]
     lane = lax.broadcasted_iota(jnp.int32, squares.shape, 1)
     tile = jnp.zeros_like(squares)
+    first = 3 * lax.axis_index("chip")
     for p, piece in enumerate(pieces_of(squares)):
-        tile = jnp.where(lane == p, piece, tile)
+        tile = jnp.where(lane == first + p, piece, tile)
     total_a[...] = total[:, :start]
     sent_a[...] = total[:, :start].astype(jnp.bfloat16)
     put_b(total[:, start:], tile, total_b, sent_b)
@@ -542,17 +542,10 @@
         sent_ref[:, at] = value.astype(jnp.bfloat16)
 
 
-def up_add_a_kernel(part_ref, arrived_ref, total_ref, sent_ref):
+def up_add_kernel(part_ref, arrived_ref, total_ref, sent_ref):
     total = part_ref[...] + arrived_ref[...].astype(jnp.float32)
     total_ref[...] = total
     sent_ref[...] = total.astype(jnp.bfloat16)
-
-
-def up_add_b_kernel(shift, part_ref, arrived_ref, total_ref, sent_ref):
-    width = part_ref.shape[1] - LANES
-    total = part_ref[:, :width] + arrived_ref[:, :width].astype(jnp.float32)
-    pieces = pltpu.roll(arrived_ref[:, width:].astype(jnp.float32), shift, 1)
-    put_b(total, part_ref[:, width:] + pieces, total_ref, sent_ref)
 
 
 def activate_kernel(part_a, arrived_a, part_b, arrived_b, out_ref):
@@ -734,10 +727,9 @@
     orders = [(2, 1, 0), (1, 0, 2)]
     arrived = [swap_chips(part[1], order[0]) for part, order in zip(parts, orders)]
     for step in range(1, chip_bits()):
-        add_b = functools.partial(up_add_b_kernel, 3 * 2 ** (step - 1))
-        for i, kernel in enumerate((up_add_a_kernel, add_b)):
+        for i in range(2):
             parts[i] = local_kernel(
-                kernel, sums[i], [parts[i][0], arrived[i]], flops=n_req * widths[i]
+                up_add_kernel, sums[i], [parts[i][0], arrived[i]], flops=n_req * widths[i]
             )
             arrived[i] = swap_chips(parts[i][1], orders[i][step])
     (active_half,) = local_kernel(

time: 51.8 us -> 51.8 us (level)
  transfers between devices with their start and end apart: 14 -> 14, of which waited for: 12 -> 12; matrix products, arithmetic and copies ran while one was open for 0% -> 0% of each run, Pallas kernels for 5% -> 4%
where the time goes in v13:
time: 51.8 us; the launch traced here: 51.6 us
  blocking collectives  22.7 us (44%)
  waiting for transfers between devices  12.1 us (23%)
  starting transfers between devices  10.3 us (20%)
  Pallas kernels  5.43 us (10%)
  other arithmetic  0.63 us (1%)
    all_to_all x1, blocking collectives, per_device(): lax.all_to_all(jnp.broadcast_to(qkv_message[None], (n_chips,) + qkv_messa...  13.6 us
    all_to_all x1, blocking collectives, per_device(): lax.all_to_all(message, ('chip', 'core'), 0, 0, axis_index_groups=sides)  9.09 us
    ppermute x6, waiting for transfers between devices, swap_chips(): lax.ppermute(values_in, ('chip', 'core'), [(i, i ^ 2 << bit ^ 1) for i in...  6.45 us
    pallas_call x19, Pallas kernels, local_kernel(): pl.pallas_call(kernel, out_shape=outs, in_specs=in_specs, out_specs=[IN_V...  5.43 us
    ppermute x6, starting transfers between devices, swap_chips(): lax.ppermute(values_in, ('chip', 'core'), [(i, i ^ 2 << bit ^ 1) for i in...  4.79 us
    ppermute x7, waiting for transfers between devices, swap(): return lax.ppermute(values_in, axis, [(i, i ^ 1) for i in range(n)])  4.38 us
    ppermute x7, starting transfers between devices, swap(): return lax.ppermute(values_in, axis, [(i, i ^ 1) for i in range(n)])  4 us
    ppermute x1, starting transfers between devices, swap_diagonal(): lax.ppermute(values_in, ('core', 'tp'), [(i, 3 - i) for i in range(4)])  1.48 us
  transfers between devices with their start and end apart: 14, of which 12 were waited for; matrix products, arithmetic and copies ran while one was open for 0% of the time, Pallas kernels for 4%

profile of v13, /device:TPU:0, one launch (start us, length us, event | category | flops | bytes accessed | tf_op | source)
XLA Modules:
  0.0 51.6 jit_solution(9632400009382277521)
XLA Ops:
  0.0 1.3 %shard_map.136 = (bf16[4,256]{1,0:T(4,128)(2,1)S(1)}, f32[4,128]{1,0:T(4,128)S(1)}, f32[4,128]{1,0:T(4,128)S(1)}, bf16[4,256]{1,0:T(4,128)(2,1)S(1)}, f32[1,256]...) custom-call(bf16[4,256]{1,0:T(4,128)(2,1)} %x_hbm.1, f32[1,256]{1,0:T(1,128)} %bitcast.6, f32[1,256]{1,0:T(1,128)} %bitcast.7, ...), custom_call_target="tpu_custom_call" | custom-call | flops 4000000000 | bytes 1054752 | tf_op jit(solution)/shard_map/pallas_call | solution.py:254
  1.3 0.2 copy-done
  1.4 0.0 copy-done.2
  1.5 0.1 copy-done.3
  1.6 0.2 shard_map.138
  1.8 0.5 collective-permute-start
  2.3 0.2 shard_map.137.mine_ref
  2.5 0.7 %collective-permute-done.arrived_ref = f32[4,1792]{1,0:T(4,128)S(1)} collective-permute-done((f32[4,1792]{1,0:T(4,128)S(1)}, f32[4,1792]{1,0:T(4,128)S(1)}, u32[]{:S(2)}, u32[]{:S(2)}) %collective-permute-start) | collective-permute-done | bytes 28704 | tf_op jit(solution)/shard_map/ppermute | solution.py:28
  3.1 0.1 shard_map.139
  3.2 0.4 collective-permute-start.2
  3.7 0.2 collective-permute-start.1
  3.9 13.6 %all_to_all.10 = f16[8,4,1664]{2,1,0:T(4,128)(2,1)S(1)} all-to-all(f16[8,4,1664]{2,1,0:T(4,128)(2,1)S(1)} %broadcast_in_dim.2), channel_id=1, replica_groups={{0,4,10,14,16,20,26,30},{2,6,8,12,18,22,24,28},{1,5,11,15,17,21,27,31},..., dimensions={0} | all-to-all | bytes 212992 | tf_op jit(solution)/shard_map/all_to_all | solution.py:650
  17.5 0.0 slice-start.1
  17.5 0.0 collective-permute-done.1.cache_peer
  17.5 0.6 %shard_map.140 = bf16[8,8,640]{2,1,0:T(8,128)(2,1)S(1)} custom-call(f32[8,4,1664]{2,1,0:T(4,128)S(1)} %convert_element_type.10.arrived_ref, bf16[4,128,512]{2,1,0:T(8,128)(2,1)S(1)} %copy-done.4, bf16[4,128,512]{2,1,0:T(8,128)(2,1)S(1)} %copy-done.5, bf16[2,4,128,256]{3,2,1,0:T(8,128)(2,1)S(1)} %collective-permute-done.1.cache_peer, ...), custom_call_target="tpu_custom_call" | custom-call | flops 4000000000 | bytes 1789952 | tf_op jit(solution)/shard_map/pallas_call | solution.py:254
  18.2 9.1 %all_to_all.11.arrived_ref = bf16[8,8,640]{2,1,0:T(8,128)(2,1)S(1)} all-to-all(bf16[8,8,640]{2,1,0:T(8,128)(2,1)S(1)} %shard_map.140), channel_id=1, replica_groups={{0,4,10,14,16,20,26,30},{2,6,8,12,18,22,24,28},{1,5,11,15,17,21,27,31},..., dimensions={0} | all-to-all | bytes 163840 | tf_op jit(solution)/shard_map/all_to_all | solution.py:670
  27.3 0.3 shard_map.141.own_ref
  27.6 0.7 %collective-permute-start.3 = (bf16[4,1024]{1,0:T(4,128)(2,1)S(1)}, bf16[4,1024]{1,0:T(4,128)(2,1)S(1)}, u32[]{:S(2)}, u32[]{:S(2)}) collective-permute-start(bf16[4,1024]{1,0:T(4,128)(2,1)S(1)} %shard_map.141.own_ref), channel_id=1, source_target_pairs={{0,2},{2,0},{1,3},{3,1},{4,6},{6,4},{5,7},{7,5},{8,10},{10,8},{9,1... | collective-permute-start | bytes 24584 | tf_op jit(solution)/shard_map/ppermute | solution.py:28
  28.3 0.2 shard_map.143.own_part
  28.4 0.6 %collective-permute-done.3.peer_ref = bf16[4,1024]{1,0:T(4,128)(2,1)S(1)} collective-permute-done((bf16[4,1024]{1,0:T(4,128)(2,1)S(1)}, bf16[4,1024]{1,0:T(4,128)(2,1)S(1)}, u32[]{:S(2)}, u32[]{:S(2)}) %collective-permute-start.3) | collective-permute-done | bytes 8224 | tf_op jit(solution)/shard_map/ppermute | solution.py:28
  29.1 0.2 shard_map.144
  29.3 1.5 %collective-permute-start.4 = (f32[4,256]{1,0:T(4,128)S(1)}, f32[4,256]{1,0:T(4,128)S(1)}, u32[]{:S(2)}, u32[]{:S(2)}) collective-permute-start(f32[4,256]{1,0:T(4,128)S(1)} %shard_map.144), channel_id=1, source_target_pairs={{0,3},{1,2},{2,1},{3,0},{4,7},{5,6},{6,5},{7,4},{8,11},{9,10},{10,... | collective-permute-start | bytes 12296 | tf_op jit(solution)/shard_map/ppermute | solution.py:32
  30.8 0.2 shard_map.142.part_ref
  31.0 1.3 %collective-permute-done.4.peer_ref = f32[4,256]{1,0:T(4,128)S(1)} collective-permute-done((f32[4,256]{1,0:T(4,128)S(1)}, f32[4,256]{1,0:T(4,128)S(1)}, u32[]{:S(2)}, u32[]{:S(2)}) %collective-permute-start.4) | collective-permute-done | bytes 4128 | tf_op jit(solution)/shard_map/ppermute | solution.py:32
  32.3 0.5 shard_map.145
  32.8 0.4 collective-permute-start.5
  33.2 0.5 shard_map.146.mine_ref
  33.7 0.5 collective-permute-done.5.arrived_ref
  34.2 0.5 collective-permute-start.9
  34.7 0.7 %collective-permute-start.6 = (bf16[4,2688]{1,0:T(4,128)(2,1)S(1)}, bf16[4,2688]{1,0:T(4,128)(2,1)S(1)}, u32[]{:S(2)}, u32[]{:S(2)}) collective-permute-start(bf16[4,2688]{1,0:T(4,128)(2,1)S(1)} %get-tuple-element.50), channel_id=1, source_target_pairs={{0,18},{2,16},{4,22},{6,20},{8,26},{10,24},{12,30},{14,28},{16,2},... | collective-permute-start | bytes 64520 | tf_op jit(solution)/shard_map/ppermute | solution.py:37
  35.4 2.1 %collective-permute-done.9.arrived_ref = bf16[4,2816]{1,0:T(4,128)(2,1)S(1)} collective-permute-done((bf16[4,2816]{1,0:T(4,128)(2,1)S(1)}, bf16[4,2816]{1,0:T(4,128)(2,1)S(1)}, u32[]{:S(2)}, u32[]{:S(2)}) %collective-permute-start.9) | collective-permute-done | bytes 22560 | tf_op jit(solution)/shard_map/ppermute | solution.py:37
  37.5 0.4 collective-permute-start.10
  37.9 0.9 %collective-permute-done.6.arrived_ref = bf16[4,2688]{1,0:T(4,128)(2,1)S(1)} collective-permute-done((bf16[4,2688]{1,0:T(4,128)(2,1)S(1)}, bf16[4,2688]{1,0:T(4,128)(2,1)S(1)}, u32[]{:S(2)}, u32[]{:S(2)}) %collective-permute-start.6) | collective-permute-done | bytes 21536 | tf_op jit(solution)/shard_map/ppermute | solution.py:37
  38.8 1.4 %collective-permute-start.7 = (bf16[4,2688]{1,0:T(4,128)(2,1)S(1)}, bf16[4,2688]{1,0:T(4,128)(2,1)S(1)}, u32[]{:S(2)}, u32[]{:S(2)}) collective-permute-start(bf16[4,2688]{1,0:T(4,128)(2,1)S(1)} %get-tuple-element.52), channel_id=1, source_target_pairs={{0,10},{2,8},{4,14},{6,12},{8,2},{10,0},{12,6},{14,4},{16,26},{18,... | collective-permute-start | bytes 64520 | tf_op jit(solution)/shard_map/ppermute | solution.py:37
  40.2 0.6 %collective-permute-done.10.arrived_ref = bf16[4,2816]{1,0:T(4,128)(2,1)S(1)} collective-permute-done((bf16[4,2816]{1,0:T(4,128)(2,1)S(1)}, bf16[4,2816]{1,0:T(4,128)(2,1)S(1)}, u32[]{:S(2)}, u32[]{:S(2)}) %collective-permute-start.10) | collective-permute-done | bytes 22560 | tf_op jit(solution)/shard_map/ppermute | solution.py:37
  40.8 0.5 collective-permute-start.11
  41.3 0.8 %collective-permute-done.7.arrived_ref = bf16[4,2688]{1,0:T(4,128)(2,1)S(1)} collective-permute-done((bf16[4,2688]{1,0:T(4,128)(2,1)S(1)}, bf16[4,2688]{1,0:T(4,128)(2,1)S(1)}, u32[]{:S(2)}, u32[]{:S(2)}) %collective-permute-start.7) | collective-permute-done | bytes 21536 | tf_op jit(solution)/shard_map/ppermute | solution.py:37
  42.1 1.4 %collective-permute-start.8 = (bf16[4,2688]{1,0:T(4,128)(2,1)S(1)}, bf16[4,2688]{1,0:T(4,128)(2,1)S(1)}, u32[]{:S(2)}, u32[]{:S(2)}) collective-permute-start(bf16[4,2688]{1,0:T(4,128)(2,1)S(1)} %get-tuple-element.54), channel_id=1, source_target_pairs={{0,6},{2,4},{4,2},{6,0},{8,14},{10,12},{12,10},{14,8},{16,22},{18,... | collective-permute-start | bytes 64520 | tf_op jit(solution)/shard_map/ppermute | solution.py:37
  43.5 1.9 %collective-permute-done.8.arrived_a = bf16[4,2688]{1,0:T(4,128)(2,1)S(1)} collective-permute-done((bf16[4,2688]{1,0:T(4,128)(2,1)S(1)}, bf16[4,2688]{1,0:T(4,128)(2,1)S(1)}, u32[]{:S(2)}, u32[]{:S(2)}) %collective-permute-start.8) | collective-permute-done | bytes 21536 | tf_op jit(solution)/shard_map/ppermute | solution.py:37
  45.4 0.1 collective-permute-done.11.arrived_b
  45.5 0.1 shard_map.152.own_ref
  45.6 0.3 collective-permute-start.12
  45.9 0.5 shard_map.153.own_part
  46.4 0.5 collective-permute-done.12.peer_ref
  46.9 0.4 shard_map.154
  47.4 1.6 %collective-permute-start.13 = (f32[4,256]{1,0:T(4,128)S(1)}, f32[4,256]{1,0:T(4,128)S(1)}, u32[]{:S(2)}, u32[]{:S(2)}) collective-permute-start(f32[4,256]{1,0:T(4,128)S(1)} %shard_map.154), channel_id=1, source_target_pairs={{0,1},{1,0},{2,3},{3,2},{4,5},{5,4},{6,7},{7,6},{8,9},{9,8},{10,11... | collective-permute-start | bytes 12296 | tf_op jit(solution)/shard_map/ppermute | solution.py:28
  48.9 2.1 %collective-permute-done.13 = f32[4,256]{1,0:T(4,128)S(1)} collective-permute-done((f32[4,256]{1,0:T(4,128)S(1)}, f32[4,256]{1,0:T(4,128)S(1)}, u32[]{:S(2)}, u32[]{:S(2)}) %collective-permute-start.13) | collective-permute-done | bytes 4128 | tf_op jit(solution)/shard_map/ppermute | solution.py:28
  51.0 0.6 %add_convert_fusion = bf16[4,256]{1,0:T(4,128)(2,1)} fusion(f32[4,256]{1,0:T(4,128)S(1)} %get-tuple-element.45, f32[4,256]{1,0:T(4,128)S(1)} %shard_map.154, f32[4,256]{1,0:T(4,128)S(1)} %collective-permute-done.13), kind=kLoop, calls=%fused_computation | loop fusion | flops 3072 | bytes 14336 | tf_op jit(solution)/shard_map/convert_element_type | solution.py:757
  (28 shorter events, 0.2 us)
Async XLA Ops:
  0.0 1.4 %copy-start = (bf16[256,2048]{1,0:T(8,128)(2,1)S(1)}, bf16[256,2048]{1,0:T(8,128)(2,1)}, u32[]{:S(2)}) copy-start(bf16[256,2048]{1,0:T(8,128)(2,1)} %wq_ref.3) | copy-start | bytes 3145732
  0.0 1.5 %copy-start.2 = (bf16[256,512]{1,0:T(8,128)(2,1)S(1)}, bf16[256,512]{1,0:T(8,128)(2,1)}, u32[]{:S(2)}) copy-start(bf16[256,512]{1,0:T(8,128)(2,1)} %wk_ref.3) | copy-start | bytes 786436
  0.0 1.6 %copy-start.3 = (bf16[256,512]{1,0:T(8,128)(2,1)S(1)}, bf16[256,512]{1,0:T(8,128)(2,1)}, u32[]{:S(2)}) copy-start(bf16[256,512]{1,0:T(8,128)(2,1)} %wv_ref.3) | copy-start | bytes 786436
  1.6 1.7 %copy-start.1 = (bf16[2048,256]{1,0:T(8,128)(2,1)S(1)}, bf16[2048,256]{1,0:T(8,128)(2,1)}, u32[]{:S(2)}) copy-start(bf16[2048,256]{1,0:T(8,128)(2,1)} %w_ref.5) | copy-start | bytes 3145732
  1.6 15.9 %copy-start.4 = (bf16[4,128,512]{2,1,0:T(8,128)(2,1)S(1)}, bf16[4,128,512]{2,1,0:T(8,128)(2,1)}, u32[]{:S(2)}) copy-start(bf16[4,128,512]{2,1,0:T(8,128)(2,1)} %key_own.1) | copy-start | bytes 1572868
  1.6 15.9 %copy-start.5 = (bf16[4,128,512]{2,1,0:T(8,128)(2,1)S(1)}, bf16[4,128,512]{2,1,0:T(8,128)(2,1)}, u32[]{:S(2)}) copy-start(bf16[4,128,512]{2,1,0:T(8,128)(2,1)} %value_own.1) | copy-start | bytes 1572868
  1.8 1.3 %collective-permute-start = (f32[4,1792]{1,0:T(4,128)S(1)}, f32[4,1792]{1,0:T(4,128)S(1)}, u32[]{:S(2)}, u32[]{:S(2)}) collective-permute-start(f32[4,1792]{1,0:T(4,128)S(1)} %shard_map.138), channel_id=1, source_target_pairs={{0,2},{2,0},{1,3},{3,1},{4,6},{6,4},{5,7},{7,5},{8,10},{10,8},{9,1... | collective-permute-start | bytes 86024 | tf_op jit(solution)/shard_map/ppermute | solution.py:28
  3.2 14.9 %collective-permute-start.2 = (bf16[2048,256]{1,0:T(8,128)(2,1)S(1)}, bf16[2048,256]{1,0:T(8,128)(2,1)S(1)}, u32[]{:S(2)}, u32[]{:S(2)}) collective-permute-start(bf16[2048,256]{1,0:T(8,128)(2,1)S(1)} %copy-done.1), channel_id=1, source_target_pairs={{0,2},{2,0},{1,3},{3,1},{4,6},{6,4},{5,7},{7,5},{8,10},{10,8},{9,1... | collective-permute-start | bytes 3145736 | tf_op jit(solution)/shard_map/ppermute | solution.py:28
  3.7 13.8 %collective-permute-start.1 = (bf16[2,4,128,256]{3,2,1,0:T(8,128)(2,1)S(1)}, bf16[2,4,128,256]{3,2,1,0:T(8,128)(2,1)S(1)}, u32[]{:S(2)}, u32[]{:S(2)}) collective-permute-start(bf16[2,4,128,256]{3,2,1,0:T(8,128)(2,1)S(1)} %get-tuple-element.39), channel_id=1, source_target_pairs={{0,2},{2,0},{1,3},{3,1},{4,6},{6,4},{5,7},{7,5},{8,10},{10,8},{9,1... | collective-permute-start | bytes 1572872 | tf_op jit(solution)/shard_map/ppermute | solution.py:28
  17.4 14.9 %slice-start = ((s8[5505024]{0:T(1024)(128)(4,1)}), s8[4194304]{0:T(1024)(128)(4,1)S(1)}, s32[]{:S(2)}) async-start(s8[5505024]{0:T(1024)(128)(4,1)} %bitcast.2), calls=%async_computation.2 | async-start | bytes 8388608
  17.5 14.9 %slice-start.1 = ((s8[5505024]{0:T(1024)(128)(4,1)}), s8[1310720]{0:T(1024)(128)(4,1)S(1)}, s32[]{:S(2)}) async-start(s8[5505024]{0:T(1024)(128)(4,1)} %bitcast.2), calls=%async_computation.3 | async-start | bytes 2621440
  27.6 1.5 %collective-permute-start.3 = (bf16[4,1024]{1,0:T(4,128)(2,1)S(1)}, bf16[4,1024]{1,0:T(4,128)(2,1)S(1)}, u32[]{:S(2)}, u32[]{:S(2)}) collective-permute-start(bf16[4,1024]{1,0:T(4,128)(2,1)S(1)} %shard_map.141.own_ref), channel_id=1, source_target_pairs={{0,2},{2,0},{1,3},{3,1},{4,6},{6,4},{5,7},{7,5},{8,10},{10,8},{9,1... | collective-permute-start | bytes 24584 | tf_op jit(solution)/shard_map/ppermute | solution.py:28
  29.3 3.0 %collective-permute-start.4 = (f32[4,256]{1,0:T(4,128)S(1)}, f32[4,256]{1,0:T(4,128)S(1)}, u32[]{:S(2)}, u32[]{:S(2)}) collective-permute-start(f32[4,256]{1,0:T(4,128)S(1)} %shard_map.144), channel_id=1, source_target_pairs={{0,3},{1,2},{2,1},{3,0},{4,7},{5,6},{6,5},{7,4},{8,11},{9,10},{10,... | collective-permute-start | bytes 12296 | tf_op jit(solution)/shard_map/ppermute | solution.py:32
  30.7 15.2 %slice-start.2 = ((s8[5505024]{0:T(1024)(128)(4,1)}), s8[4194304]{0:T(1024)(128)(4,1)S(1)}, s32[]{:S(2)}) async-start(s8[5505024]{0:T(1024)(128)(4,1)} %bitcast.4), calls=%async_computation.4 | async-start | bytes 8388608
  32.3 13.6 %slice-start.3 = ((s8[5505024]{0:T(1024)(128)(4,1)}), s8[1310720]{0:T(1024)(128)(4,1)S(1)}, s32[]{:S(2)}) async-start(s8[5505024]{0:T(1024)(128)(4,1)} %bitcast.4), calls=%async_computation.5 | async-start | bytes 2621440
  32.8 1.3 %collective-permute-start.5 = (f32[4,5504]{1,0:T(4,128)S(1)}, f32[4,5504]{1,0:T(4,128)S(1)}, u32[]{:S(2)}, u32[]{:S(2)}) collective-permute-start(f32[4,5504]{1,0:T(4,128)S(1)} %get-tuple-element.48), channel_id=1, source_target_pairs={{0,2},{2,0},{1,3},{3,1},{4,6},{6,4},{5,7},{7,5},{8,10},{10,8},{9,1... | collective-permute-start | bytes 264200 | tf_op jit(solution)/shard_map/ppermute | solution.py:28
  34.2 3.3 %collective-permute-start.9 = (bf16[4,2816]{1,0:T(4,128)(2,1)S(1)}, bf16[4,2816]{1,0:T(4,128)(2,1)S(1)}, u32[]{:S(2)}, u32[]{:S(2)}) collective-permute-start(bf16[4,2816]{1,0:T(4,128)(2,1)S(1)} %get-tuple-element.56), channel_id=1, source_target_pairs={{0,10},{2,8},{4,14},{6,12},{8,2},{10,0},{12,6},{14,4},{16,26},{18,... | collective-permute-start | bytes 67592 | tf_op jit(solution)/shard_map/ppermute | solution.py:37
  34.7 4.1 %collective-permute-start.6 = (bf16[4,2688]{1,0:T(4,128)(2,1)S(1)}, bf16[4,2688]{1,0:T(4,128)(2,1)S(1)}, u32[]{:S(2)}, u32[]{:S(2)}) collective-permute-start(bf16[4,2688]{1,0:T(4,128)(2,1)S(1)} %get-tuple-element.50), channel_id=1, source_target_pairs={{0,18},{2,16},{4,22},{6,20},{8,26},{10,24},{12,30},{14,28},{16,2},... | collective-permute-start | bytes 64520 | tf_op jit(solution)/shard_map/ppermute | solution.py:37
  37.5 3.3 %collective-permute-start.10 = (bf16[4,2816]{1,0:T(4,128)(2,1)S(1)}, bf16[4,2816]{1,0:T(4,128)(2,1)S(1)}, u32[]{:S(2)}, u32[]{:S(2)}) collective-permute-start(bf16[4,2816]{1,0:T(4,128)(2,1)S(1)} %get-tuple-element.58), channel_id=1, source_target_pairs={{0,6},{2,4},{4,2},{6,0},{8,14},{10,12},{12,10},{14,8},{16,22},{18,... | collective-permute-start | bytes 67592 | tf_op jit(solution)/shard_map/ppermute | solution.py:37
  38.8 3.3 %collective-permute-start.7 = (bf16[4,2688]{1,0:T(4,128)(2,1)S(1)}, bf16[4,2688]{1,0:T(4,128)(2,1)S(1)}, u32[]{:S(2)}, u32[]{:S(2)}) collective-permute-start(bf16[4,2688]{1,0:T(4,128)(2,1)S(1)} %get-tuple-element.52), channel_id=1, source_target_pairs={{0,10},{2,8},{4,14},{6,12},{8,2},{10,0},{12,6},{14,4},{16,26},{18,... | collective-permute-start | bytes 64520 | tf_op jit(solution)/shard_map/ppermute | solution.py:37
  40.8 4.7 %collective-permute-start.11 = (bf16[4,2816]{1,0:T(4,128)(2,1)S(1)}, bf16[4,2816]{1,0:T(4,128)(2,1)S(1)}, u32[]{:S(2)}, u32[]{:S(2)}) collective-permute-start(bf16[4,2816]{1,0:T(4,128)(2,1)S(1)} %get-tuple-element.60), channel_id=1, source_target_pairs={{0,18},{2,16},{4,22},{6,20},{8,26},{10,24},{12,30},{14,28},{16,2},... | collective-permute-start | bytes 67592 | tf_op jit(solution)/shard_map/ppermute | solution.py:37
  42.1 3.3 %collective-permute-start.8 = (bf16[4,2688]{1,0:T(4,128)(2,1)S(1)}, bf16[4,2688]{1,0:T(4,128)(2,1)S(1)}, u32[]{:S(2)}, u32[]{:S(2)}) collective-permute-start(bf16[4,2688]{1,0:T(4,128)(2,1)S(1)} %get-tuple-element.54), channel_id=1, source_target_pairs={{0,6},{2,4},{4,2},{6,0},{8,14},{10,12},{12,10},{14,8},{16,22},{18,... | collective-permute-start | bytes 64520 | tf_op jit(solution)/shard_map/ppermute | solution.py:37
  45.6 1.3 %collective-permute-start.12 = (bf16[4,5376]{1,0:T(4,128)(2,1)S(1)}, bf16[4,5376]{1,0:T(4,128)(2,1)S(1)}, u32[]{:S(2)}, u32[]{:S(2)}) collective-permute-start(bf16[4,5376]{1,0:T(4,128)(2,1)S(1)} %shard_map.152.own_ref), channel_id=1, source_target_pairs={{0,2},{2,0},{1,3},{3,1},{4,6},{6,4},{5,7},{7,5},{8,10},{10,8},{9,1... | collective-permute-start | bytes 129032 | tf_op jit(solution)/shard_map/ppermute | solution.py:28
  47.4 3.7 %collective-permute-start.13 = (f32[4,256]{1,0:T(4,128)S(1)}, f32[4,256]{1,0:T(4,128)S(1)}, u32[]{:S(2)}, u32[]{:S(2)}) collective-permute-start(f32[4,256]{1,0:T(4,128)S(1)} %shard_map.154), channel_id=1, source_target_pairs={{0,1},{1,0},{2,3},{3,2},{4,5},{5,4},{6,7},{7,6},{8,9},{9,8},{10,11... | collective-permute-start | bytes 12296 | tf_op jit(solution)/shard_map/ppermute | solution.py:28

commit v14 on v13

--- a/solution.py
+++ b/solution.py
@@ -497,11 +497,12 @@
 def up_columns(scaled_mlp, w_ref, side, out_ref):
     half = out_ref.shape[1] - LANES
     mine = pl.ds(pl.multiple_of(side * half, LANES), half)
-    out_ref[:, :half] = jnp.dot(scaled_mlp, w_ref[:, mine], preferred_element_type=jnp.float32)
+    columns = jnp.dot(scaled_mlp, w_ref[:, mine], preferred_element_type=jnp.float32)
+    out_ref[:, :half] = columns.astype(out_ref.dtype)
 
 
 def up_other_kernel(
-    x_ref, part_ref, peer_ref, gain_ref, w_ref, hidden_ref, scaled_ref, squares_ref, other_ref
+    x_ref, part_ref, peer_ref, gain_ref, w_ref, hidden_ref, scaled_ref, tile_ref, other_ref
 ):
     attn_out = part_ref[...] + peer_ref[...]
     hidden_state = (x_ref[...].astype(jnp.float32) + attn_out).astype(jnp.bfloat16)
@@ -510,36 +511,28 @@
     scaled_mlp = (resid_rows * gain_ref[...]).astype(jnp.bfloat16)
     scaled_ref[...] = scaled_mlp
     squares = jnp.sum(resid_rows * resid_rows, axis=1, keepdims=True)
-    squares_ref[...] = jnp.broadcast_to(squares, squares_ref.shape)
-    other_ref[:, other_ref.shape[1] - LANES :] = squares_ref[...]
-    up_columns(scaled_mlp, w_ref, 1 - up_half(), other_ref)
-
-
-def up_mine_kernel(scaled_ref, squares_ref, w_ref, mine_ref):
-    mine_ref[:, mine_ref.shape[1] - LANES :] = squares_ref[...]
-    up_columns(scaled_ref[...], w_ref, up_half(), mine_ref)
-
-
-def up_pair_kernel(mine_ref, arrived_ref, total_a, sent_a, total_b, sent_b):
-    half = mine_ref.shape[1] - LANES
-    start = total_a.shape[1]
-    total = mine_ref[:, :half] + arrived_ref[:, :half]
-    squares = mine_ref[:, half:] + arrived_ref[:, half:]
-    lane = lax.broadcasted_iota(jnp.int32, squares.shape, 1)
-    tile = jnp.zeros_like(squares)
-    first = 3 * lax.axis_index("chip")
+    first = 3 * (2 * lax.axis_index("chip") + lax.axis_index("core"))
+    lane = lax.broadcasted_iota(jnp.int32, tile_ref.shape, 1)
+    tile = jnp.zeros(tile_ref.shape, jnp.float32)
     for p, piece in enumerate(pieces_of(squares)):
         tile = jnp.where(lane == first + p, piece, tile)
+    tile_ref[...] = tile
+    other_ref[:, other_ref.shape[1] - LANES :] = tile.astype(jnp.bfloat16)
+    up_columns(scaled_mlp, w_ref, 1 - up_half(), other_ref)
+
+
+def up_mine_kernel(scaled_ref, tile_ref, w_ref, mine_ref):
+    mine_ref[:, mine_ref.shape[1] - LANES :] = tile_ref[...]
+    up_columns(scaled_ref[...], w_ref, up_half(), mine_ref)
+
+
+def up_pair_kernel(mine_ref, arrived_ref, total_a, sent_a, total_b, sent_b):
+    total = mine_ref[...] + arrived_ref[...].astype(jnp.float32)
+    start = total_a.shape[1]
     total_a[...] = total[:, :start]
     sent_a[...] = total[:, :start].astype(jnp.bfloat16)
-    put_b(total[:, start:], tile, total_b, sent_b)
-
-
-def put_b(total, tile, total_ref, sent_ref):
-    width = total.shape[1]
-    for at, value in ((slice(0, width), total), (slice(width, None), tile)):
-        total_ref[:, at] = value
-        sent_ref[:, at] = value.astype(jnp.bfloat16)
+    total_b[...] = total[:, start:]
+    sent_b[...] = total[:, start:].astype(jnp.bfloat16)
 
 
 def up_add_kernel(part_ref, arrived_ref, total_ref, sent_ref):
@@ -695,13 +688,13 @@
         flops=2 * n_req * out_weight.size,
     )
 
-    resid_rows, scaled_mlp, squares, up_other = local_kernel(
+    resid_rows, scaled_mlp, tile, up_other = local_kernel(
         up_other_kernel,
         [
             f32(n_req, d_here),
             bf16(n_req, d_here),
             f32(n_req, LANES),
-            f32(n_req, half_up + LANES),
+            bf16(n_req, half_up + LANES),
         ],
         [x_rows, head_part, head_peer, gain, up_weight],
         flops=n_req * up_weight.size,
@@ -710,7 +703,7 @@
     (up_mine,) = local_kernel(
         up_mine_kernel,
         [f32(n_req, half_up + LANES)],
-        [scaled_mlp, squares, up_weight],
+        [scaled_mlp, tile, up_weight],
         flops=n_req * up_weight.size,
         anywhere=(2,),
     )

time: 51.8 us -> 51.7 us (level)
  no operation moved by 1% of the time
where the time goes in v14:
time: 51.7 us; the launch traced here: 51.5 us
  blocking collectives  22.7 us (44%)
  waiting for transfers between devices  12.1 us (23%)
  starting transfers between devices  10.3 us (20%)
  Pallas kernels  5.42 us (10%)
  other arithmetic  0.63 us (1%)
    all_to_all x1, blocking collectives, per_device(): lax.all_to_all(jnp.broadcast_to(qkv_message[None], (n_chips,) + qkv_messa...  13.6 us
    all_to_all x1, blocking collectives, per_device(): lax.all_to_all(message, ('chip', 'core'), 0, 0, axis_index_groups=sides)  9.09 us
    ppermute x6, waiting for transfers between devices, swap_chips(): lax.ppermute(values_in, ('chip', 'core'), [(i, i ^ 2 << bit ^ 1) for i in...  6.45 us
    pallas_call x19, Pallas kernels, local_kernel(): pl.pallas_call(kernel, out_shape=outs, in_specs=in_specs, out_specs=[IN_V...  5.42 us
    ppermute x6, starting transfers between devices, swap_chips(): lax.ppermute(values_in, ('chip', 'core'), [(i, i ^ 2 << bit ^ 1) for i in...  4.79 us
    ppermute x7, waiting for transfers between devices, swap(): return lax.ppermute(values_in, axis, [(i, i ^ 1) for i in range(n)])  4.31 us
    ppermute x7, starting transfers between devices, swap(): return lax.ppermute(values_in, axis, [(i, i ^ 1) for i in range(n)])  3.99 us
    ppermute x1, starting transfers between devices, swap_diagonal(): lax.ppermute(values_in, ('core', 'tp'), [(i, 3 - i) for i in range(4)])  1.48 us
  transfers between devices with their start and end apart: 14, of which 12 were waited for; matrix products, arithmetic and copies ran while one was open for 0% of the time, Pallas kernels for 4%

profile of v14, /device:TPU:0, one launch (start us, length us, event | category | flops | bytes accessed | tf_op | source)
XLA Modules:
  0.0 51.5 jit_solution(3545594190666291430)
XLA Ops:
  0.0 1.3 %shard_map.136 = (bf16[4,256]{1,0:T(4,128)(2,1)S(1)}, f32[4,128]{1,0:T(4,128)S(1)}, f32[4,128]{1,0:T(4,128)S(1)}, bf16[4,256]{1,0:T(4,128)(2,1)S(1)}, f32[1,256]...) custom-call(bf16[4,256]{1,0:T(4,128)(2,1)} %x_hbm.1, f32[1,256]{1,0:T(1,128)} %bitcast.6, f32[1,256]{1,0:T(1,128)} %bitcast.7, ...), custom_call_target="tpu_custom_call" | custom-call | flops 4000000000 | bytes 1054752 | tf_op jit(solution)/shard_map/pallas_call | solution.py:254
  1.3 0.2 copy-done
  1.4 0.0 copy-done.2
  1.5 0.1 copy-done.3
  1.6 0.2 shard_map.138
  1.8 0.5 collective-permute-start
  2.3 0.2 shard_map.137.mine_ref
  2.5 0.7 %collective-permute-done.arrived_ref = f32[4,1792]{1,0:T(4,128)S(1)} collective-permute-done((f32[4,1792]{1,0:T(4,128)S(1)}, f32[4,1792]{1,0:T(4,128)S(1)}, u32[]{:S(2)}, u32[]{:S(2)}) %collective-permute-start) | collective-permute-done | bytes 28704 | tf_op jit(solution)/shard_map/ppermute | solution.py:28
  3.1 0.1 shard_map.139
  3.2 0.4 collective-permute-start.2
  3.7 0.2 collective-permute-start.1
  3.9 13.6 %all_to_all.10 = f16[8,4,1664]{2,1,0:T(4,128)(2,1)S(1)} all-to-all(f16[8,4,1664]{2,1,0:T(4,128)(2,1)S(1)} %broadcast_in_dim.2), channel_id=1, replica_groups={{0,4,10,14,16,20,26,30},{2,6,8,12,18,22,24,28},{1,5,11,15,17,21,27,31},..., dimensions={0} | all-to-all | bytes 212992 | tf_op jit(solution)/shard_map/all_to_all | solution.py:643
  17.5 0.0 slice-start.1
  17.5 0.0 collective-permute-done.1.cache_peer
  17.5 0.6 %shard_map.140 = bf16[8,8,640]{2,1,0:T(8,128)(2,1)S(1)} custom-call(f32[8,4,1664]{2,1,0:T(4,128)S(1)} %convert_element_type.10.arrived_ref, bf16[4,128,512]{2,1,0:T(8,128)(2,1)S(1)} %copy-done.4, bf16[4,128,512]{2,1,0:T(8,128)(2,1)S(1)} %copy-done.5, bf16[2,4,128,256]{3,2,1,0:T(8,128)(2,1)S(1)} %collective-permute-done.1.cache_peer, ...), custom_call_target="tpu_custom_call" | custom-call | flops 4000000000 | bytes 1789952 | tf_op jit(solution)/shard_map/pallas_call | solution.py:254
  18.2 9.1 %all_to_all.11.arrived_ref = bf16[8,8,640]{2,1,0:T(8,128)(2,1)S(1)} all-to-all(bf16[8,8,640]{2,1,0:T(8,128)(2,1)S(1)} %shard_map.140), channel_id=1, replica_groups={{0,4,10,14,16,20,26,30},{2,6,8,12,18,22,24,28},{1,5,11,15,17,21,27,31},..., dimensions={0} | all-to-all | bytes 163840 | tf_op jit(solution)/shard_map/all_to_all | solution.py:663
  27.3 0.3 shard_map.141.own_ref
  27.6 0.7 %collective-permute-start.3 = (bf16[4,1024]{1,0:T(4,128)(2,1)S(1)}, bf16[4,1024]{1,0:T(4,128)(2,1)S(1)}, u32[]{:S(2)}, u32[]{:S(2)}) collective-permute-start(bf16[4,1024]{1,0:T(4,128)(2,1)S(1)} %shard_map.141.own_ref), channel_id=1, source_target_pairs={{0,2},{2,0},{1,3},{3,1},{4,6},{6,4},{5,7},{7,5},{8,10},{10,8},{9,1... | collective-permute-start | bytes 24584 | tf_op jit(solution)/shard_map/ppermute | solution.py:28
  28.3 0.2 shard_map.143.own_part
  28.4 0.6 %collective-permute-done.3.peer_ref = bf16[4,1024]{1,0:T(4,128)(2,1)S(1)} collective-permute-done((bf16[4,1024]{1,0:T(4,128)(2,1)S(1)}, bf16[4,1024]{1,0:T(4,128)(2,1)S(1)}, u32[]{:S(2)}, u32[]{:S(2)}) %collective-permute-start.3) | collective-permute-done | bytes 8224 | tf_op jit(solution)/shard_map/ppermute | solution.py:28
  29.1 0.2 shard_map.144
  29.3 1.5 %collective-permute-start.4 = (f32[4,256]{1,0:T(4,128)S(1)}, f32[4,256]{1,0:T(4,128)S(1)}, u32[]{:S(2)}, u32[]{:S(2)}) collective-permute-start(f32[4,256]{1,0:T(4,128)S(1)} %shard_map.144), channel_id=1, source_target_pairs={{0,3},{1,2},{2,1},{3,0},{4,7},{5,6},{6,5},{7,4},{8,11},{9,10},{10,... | collective-permute-start | bytes 12296 | tf_op jit(solution)/shard_map/ppermute | solution.py:32
  30.8 0.2 shard_map.142.part_ref
  31.0 1.3 %collective-permute-done.4.peer_ref = f32[4,256]{1,0:T(4,128)S(1)} collective-permute-done((f32[4,256]{1,0:T(4,128)S(1)}, f32[4,256]{1,0:T(4,128)S(1)}, u32[]{:S(2)}, u32[]{:S(2)}) %collective-permute-start.4) | collective-permute-done | bytes 4128 | tf_op jit(solution)/shard_map/ppermute | solution.py:32
  32.3 0.5 shard_map.145
  32.8 0.4 collective-permute-start.5
  33.2 0.5 shard_map.146.mine_ref
  33.7 0.4 collective-permute-done.5.arrived_ref
  34.1 0.5 collective-permute-start.9
  34.6 0.7 %collective-permute-start.6 = (bf16[4,2688]{1,0:T(4,128)(2,1)S(1)}, bf16[4,2688]{1,0:T(4,128)(2,1)S(1)}, u32[]{:S(2)}, u32[]{:S(2)}) collective-permute-start(bf16[4,2688]{1,0:T(4,128)(2,1)S(1)} %get-tuple-element.50), channel_id=1, source_target_pairs={{0,18},{2,16},{4,22},{6,20},{8,26},{10,24},{12,30},{14,28},{16,2},... | collective-permute-start | bytes 64520 | tf_op jit(solution)/shard_map/ppermute | solution.py:37
  35.3 2.1 %collective-permute-done.9.arrived_ref = bf16[4,2816]{1,0:T(4,128)(2,1)S(1)} collective-permute-done((bf16[4,2816]{1,0:T(4,128)(2,1)S(1)}, bf16[4,2816]{1,0:T(4,128)(2,1)S(1)}, u32[]{:S(2)}, u32[]{:S(2)}) %collective-permute-start.9) | collective-permute-done | bytes 22560 | tf_op jit(solution)/shard_map/ppermute | solution.py:37
  37.4 0.4 collective-permute-start.10
  37.8 0.9 %collective-permute-done.6.arrived_ref = bf16[4,2688]{1,0:T(4,128)(2,1)S(1)} collective-permute-done((bf16[4,2688]{1,0:T(4,128)(2,1)S(1)}, bf16[4,2688]{1,0:T(4,128)(2,1)S(1)}, u32[]{:S(2)}, u32[]{:S(2)}) %collective-permute-start.6) | collective-permute-done | bytes 21536 | tf_op jit(solution)/shard_map/ppermute | solution.py:37
  38.7 1.4 %collective-permute-start.7 = (bf16[4,2688]{1,0:T(4,128)(2,1)S(1)}, bf16[4,2688]{1,0:T(4,128)(2,1)S(1)}, u32[]{:S(2)}, u32[]{:S(2)}) collective-permute-start(bf16[4,2688]{1,0:T(4,128)(2,1)S(1)} %get-tuple-element.52), channel_id=1, source_target_pairs={{0,10},{2,8},{4,14},{6,12},{8,2},{10,0},{12,6},{14,4},{16,26},{18,... | collective-permute-start | bytes 64520 | tf_op jit(solution)/shard_map/ppermute | solution.py:37
  40.1 0.6 %collective-permute-done.10.arrived_ref = bf16[4,2816]{1,0:T(4,128)(2,1)S(1)} collective-permute-done((bf16[4,2816]{1,0:T(4,128)(2,1)S(1)}, bf16[4,2816]{1,0:T(4,128)(2,1)S(1)}, u32[]{:S(2)}, u32[]{:S(2)}) %collective-permute-start.10) | collective-permute-done | bytes 22560 | tf_op jit(solution)/shard_map/ppermute | solution.py:37
  40.7 0.5 collective-permute-start.11
  41.2 0.8 %collective-permute-done.7.arrived_ref = bf16[4,2688]{1,0:T(4,128)(2,1)S(1)} collective-permute-done((bf16[4,2688]{1,0:T(4,128)(2,1)S(1)}, bf16[4,2688]{1,0:T(4,128)(2,1)S(1)}, u32[]{:S(2)}, u32[]{:S(2)}) %collective-permute-start.7) | collective-permute-done | bytes 21536 | tf_op jit(solution)/shard_map/ppermute | solution.py:37
  42.0 1.4 %collective-permute-start.8 = (bf16[4,2688]{1,0:T(4,128)(2,1)S(1)}, bf16[4,2688]{1,0:T(4,128)(2,1)S(1)}, u32[]{:S(2)}, u32[]{:S(2)}) collective-permute-start(bf16[4,2688]{1,0:T(4,128)(2,1)S(1)} %get-tuple-element.54), channel_id=1, source_target_pairs={{0,6},{2,4},{4,2},{6,0},{8,14},{10,12},{12,10},{14,8},{16,22},{18,... | collective-permute-start | bytes 64520 | tf_op jit(solution)/shard_map/ppermute | solution.py:37
  43.4 1.9 %collective-permute-done.8.arrived_a = bf16[4,2688]{1,0:T(4,128)(2,1)S(1)} collective-permute-done((bf16[4,2688]{1,0:T(4,128)(2,1)S(1)}, bf16[4,2688]{1,0:T(4,128)(2,1)S(1)}, u32[]{:S(2)}, u32[]{:S(2)}) %collective-permute-start.8) | collective-permute-done | bytes 21536 | tf_op jit(solution)/shard_map/ppermute | solution.py:37
  45.3 0.1 collective-permute-done.11.arrived_b
  45.4 0.1 shard_map.152.own_ref
  45.5 0.3 collective-permute-start.12
  45.9 0.5 shard_map.153.own_part
  46.3 0.5 collective-permute-done.12.peer_ref
  46.8 0.4 shard_map.154
  47.3 1.6 %collective-permute-start.13 = (f32[4,256]{1,0:T(4,128)S(1)}, f32[4,256]{1,0:T(4,128)S(1)}, u32[]{:S(2)}, u32[]{:S(2)}) collective-permute-start(f32[4,256]{1,0:T(4,128)S(1)} %shard_map.154), channel_id=1, source_target_pairs={{0,1},{1,0},{2,3},{3,2},{4,5},{5,4},{6,7},{7,6},{8,9},{9,8},{10,11... | collective-permute-start | bytes 12296 | tf_op jit(solution)/shard_map/ppermute | solution.py:28
  48.9 2.1 %collective-permute-done.13 = f32[4,256]{1,0:T(4,128)S(1)} collective-permute-done((f32[4,256]{1,0:T(4,128)S(1)}, f32[4,256]{1,0:T(4,128)S(1)}, u32[]{:S(2)}, u32[]{:S(2)}) %collective-permute-start.13) | collective-permute-done | bytes 4128 | tf_op jit(solution)/shard_map/ppermute | solution.py:28
  50.9 0.6 %add_convert_fusion = bf16[4,256]{1,0:T(4,128)(2,1)} fusion(f32[4,256]{1,0:T(4,128)S(1)} %get-tuple-element.45, f32[4,256]{1,0:T(4,128)S(1)} %shard_map.154, f32[4,256]{1,0:T(4,128)S(1)} %collective-permute-done.13), kind=kLoop, calls=%fused_computation | loop fusion | flops 3072 | bytes 14336 | tf_op jit(solution)/shard_map/convert_element_type | solution.py:750
  (28 shorter events, 0.2 us)
Async XLA Ops:
  0.0 1.4 %copy-start = (bf16[256,2048]{1,0:T(8,128)(2,1)S(1)}, bf16[256,2048]{1,0:T(8,128)(2,1)}, u32[]{:S(2)}) copy-start(bf16[256,2048]{1,0:T(8,128)(2,1)} %wq_ref.3) | copy-start | bytes 3145732
  0.0 1.5 %copy-start.2 = (bf16[256,512]{1,0:T(8,128)(2,1)S(1)}, bf16[256,512]{1,0:T(8,128)(2,1)}, u32[]{:S(2)}) copy-start(bf16[256,512]{1,0:T(8,128)(2,1)} %wk_ref.3) | copy-start | bytes 786436
  0.0 1.6 %copy-start.3 = (bf16[256,512]{1,0:T(8,128)(2,1)S(1)}, bf16[256,512]{1,0:T(8,128)(2,1)}, u32[]{:S(2)}) copy-start(bf16[256,512]{1,0:T(8,128)(2,1)} %wv_ref.3) | copy-start | bytes 786436
  1.6 1.7 %copy-start.1 = (bf16[2048,256]{1,0:T(8,128)(2,1)S(1)}, bf16[2048,256]{1,0:T(8,128)(2,1)}, u32[]{:S(2)}) copy-start(bf16[2048,256]{1,0:T(8,128)(2,1)} %w_ref.5) | copy-start | bytes 3145732
  1.6 15.9 %copy-start.4 = (bf16[4,128,512]{2,1,0:T(8,128)(2,1)S(1)}, bf16[4,128,512]{2,1,0:T(8,128)(2,1)}, u32[]{:S(2)}) copy-start(bf16[4,128,512]{2,1,0:T(8,128)(2,1)} %key_own.1) | copy-start | bytes 1572868
  1.6 15.9 %copy-start.5 = (bf16[4,128,512]{2,1,0:T(8,128)(2,1)S(1)}, bf16[4,128,512]{2,1,0:T(8,128)(2,1)}, u32[]{:S(2)}) copy-start(bf16[4,128,512]{2,1,0:T(8,128)(2,1)} %value_own.1) | copy-start | bytes 1572868
  1.8 1.3 %collective-permute-start = (f32[4,1792]{1,0:T(4,128)S(1)}, f32[4,1792]{1,0:T(4,128)S(1)}, u32[]{:S(2)}, u32[]{:S(2)}) collective-permute-start(f32[4,1792]{1,0:T(4,128)S(1)} %shard_map.138), channel_id=1, source_target_pairs={{0,2},{2,0},{1,3},{3,1},{4,6},{6,4},{5,7},{7,5},{8,10},{10,8},{9,1... | collective-permute-start | bytes 86024 | tf_op jit(solution)/shard_map/ppermute | solution.py:28
  3.2 14.9 %collective-permute-start.2 = (bf16[2048,256]{1,0:T(8,128)(2,1)S(1)}, bf16[2048,256]{1,0:T(8,128)(2,1)S(1)}, u32[]{:S(2)}, u32[]{:S(2)}) collective-permute-start(bf16[2048,256]{1,0:T(8,128)(2,1)S(1)} %copy-done.1), channel_id=1, source_target_pairs={{0,2},{2,0},{1,3},{3,1},{4,6},{6,4},{5,7},{7,5},{8,10},{10,8},{9,1... | collective-permute-start | bytes 3145736 | tf_op jit(solution)/shard_map/ppermute | solution.py:28
  3.7 13.8 %collective-permute-start.1 = (bf16[2,4,128,256]{3,2,1,0:T(8,128)(2,1)S(1)}, bf16[2,4,128,256]{3,2,1,0:T(8,128)(2,1)S(1)}, u32[]{:S(2)}, u32[]{:S(2)}) collective-permute-start(bf16[2,4,128,256]{3,2,1,0:T(8,128)(2,1)S(1)} %get-tuple-element.39), channel_id=1, source_target_pairs={{0,2},{2,0},{1,3},{3,1},{4,6},{6,4},{5,7},{7,5},{8,10},{10,8},{9,1... | collective-permute-start | bytes 1572872 | tf_op jit(solution)/shard_map/ppermute | solution.py:28
  17.4 14.9 %slice-start = ((s8[5505024]{0:T(1024)(128)(4,1)}), s8[4194304]{0:T(1024)(128)(4,1)S(1)}, s32[]{:S(2)}) async-start(s8[5505024]{0:T(1024)(128)(4,1)} %bitcast.2), calls=%async_computation.2 | async-start | bytes 8388608
  17.5 14.9 %slice-start.1 = ((s8[5505024]{0:T(1024)(128)(4,1)}), s8[1310720]{0:T(1024)(128)(4,1)S(1)}, s32[]{:S(2)}) async-start(s8[5505024]{0:T(1024)(128)(4,1)} %bitcast.2), calls=%async_computation.3 | async-start | bytes 2621440
  27.6 1.5 %collective-permute-start.3 = (bf16[4,1024]{1,0:T(4,128)(2,1)S(1)}, bf16[4,1024]{1,0:T(4,128)(2,1)S(1)}, u32[]{:S(2)}, u32[]{:S(2)}) collective-permute-start(bf16[4,1024]{1,0:T(4,128)(2,1)S(1)} %shard_map.141.own_ref), channel_id=1, source_target_pairs={{0,2},{2,0},{1,3},{3,1},{4,6},{6,4},{5,7},{7,5},{8,10},{10,8},{9,1... | collective-permute-start | bytes 24584 | tf_op jit(solution)/shard_map/ppermute | solution.py:28
  29.3 3.0 %collective-permute-start.4 = (f32[4,256]{1,0:T(4,128)S(1)}, f32[4,256]{1,0:T(4,128)S(1)}, u32[]{:S(2)}, u32[]{:S(2)}) collective-permute-start(f32[4,256]{1,0:T(4,128)S(1)} %shard_map.144), channel_id=1, source_target_pairs={{0,3},{1,2},{2,1},{3,0},{4,7},{5,6},{6,5},{7,4},{8,11},{9,10},{10,... | collective-permute-start | bytes 12296 | tf_op jit(solution)/shard_map/ppermute | solution.py:32
  30.7 15.1 %slice-start.2 = ((s8[5505024]{0:T(1024)(128)(4,1)}), s8[4194304]{0:T(1024)(128)(4,1)S(1)}, s32[]{:S(2)}) async-start(s8[5505024]{0:T(1024)(128)(4,1)} %bitcast.4), calls=%async_computation.4 | async-start | bytes 8388608
  32.3 13.5 %slice-start.3 = ((s8[5505024]{0:T(1024)(128)(4,1)}), s8[1310720]{0:T(1024)(128)(4,1)S(1)}, s32[]{:S(2)}) async-start(s8[5505024]{0:T(1024)(128)(4,1)} %bitcast.4), calls=%async_computation.5 | async-start | bytes 2621440
  32.8 1.2 %collective-permute-start.5 = (bf16[4,5504]{1,0:T(4,128)(2,1)S(1)}, bf16[4,5504]{1,0:T(4,128)(2,1)S(1)}, u32[]{:S(2)}, u32[]{:S(2)}) collective-permute-start(bf16[4,5504]{1,0:T(4,128)(2,1)S(1)} %get-tuple-element.48), channel_id=1, source_target_pairs={{0,2},{2,0},{1,3},{3,1},{4,6},{6,4},{5,7},{7,5},{8,10},{10,8},{9,1... | collective-permute-start | bytes 132104 | tf_op jit(solution)/shard_map/ppermute | solution.py:28
  34.1 3.3 %collective-permute-start.9 = (bf16[4,2816]{1,0:T(4,128)(2,1)S(1)}, bf16[4,2816]{1,0:T(4,128)(2,1)S(1)}, u32[]{:S(2)}, u32[]{:S(2)}) collective-permute-start(bf16[4,2816]{1,0:T(4,128)(2,1)S(1)} %get-tuple-element.56), channel_id=1, source_target_pairs={{0,10},{2,8},{4,14},{6,12},{8,2},{10,0},{12,6},{14,4},{16,26},{18,... | collective-permute-start | bytes 67592 | tf_op jit(solution)/shard_map/ppermute | solution.py:37
  34.6 4.1 %collective-permute-start.6 = (bf16[4,2688]{1,0:T(4,128)(2,1)S(1)}, bf16[4,2688]{1,0:T(4,128)(2,1)S(1)}, u32[]{:S(2)}, u32[]{:S(2)}) collective-permute-start(bf16[4,2688]{1,0:T(4,128)(2,1)S(1)} %get-tuple-element.50), channel_id=1, source_target_pairs={{0,18},{2,16},{4,22},{6,20},{8,26},{10,24},{12,30},{14,28},{16,2},... | collective-permute-start | bytes 64520 | tf_op jit(solution)/shard_map/ppermute | solution.py:37
  37.4 3.3 %collective-permute-start.10 = (bf16[4,2816]{1,0:T(4,128)(2,1)S(1)}, bf16[4,2816]{1,0:T(4,128)(2,1)S(1)}, u32[]{:S(2)}, u32[]{:S(2)}) collective-permute-start(bf16[4,2816]{1,0:T(4,128)(2,1)S(1)} %get-tuple-element.58), channel_id=1, source_target_pairs={{0,6},{2,4},{4,2},{6,0},{8,14},{10,12},{12,10},{14,8},{16,22},{18,... | collective-permute-start | bytes 67592 | tf_op jit(solution)/shard_map/ppermute | solution.py:37
  38.7 3.3 %collective-permute-start.7 = (bf16[4,2688]{1,0:T(4,128)(2,1)S(1)}, bf16[4,2688]{1,0:T(4,128)(2,1)S(1)}, u32[]{:S(2)}, u32[]{:S(2)}) collective-permute-start(bf16[4,2688]{1,0:T(4,128)(2,1)S(1)} %get-tuple-element.52), channel_id=1, source_target_pairs={{0,10},{2,8},{4,14},{6,12},{8,2},{10,0},{12,6},{14,4},{16,26},{18,... | collective-permute-start | bytes 64520 | tf_op jit(solution)/shard_map/ppermute | solution.py:37
  40.7 4.7 %collective-permute-start.11 = (bf16[4,2816]{1,0:T(4,128)(2,1)S(1)}, bf16[4,2816]{1,0:T(4,128)(2,1)S(1)}, u32[]{:S(2)}, u32[]{:S(2)}) collective-permute-start(bf16[4,2816]{1,0:T(4,128)(2,1)S(1)} %get-tuple-element.60), channel_id=1, source_target_pairs={{0,18},{2,16},{4,22},{6,20},{8,26},{10,24},{12,30},{14,28},{16,2},... | collective-permute-start | bytes 67592 | tf_op jit(solution)/shard_map/ppermute | solution.py:37
  42.0 3.3 %collective-permute-start.8 = (bf16[4,2688]{1,0:T(4,128)(2,1)S(1)}, bf16[4,2688]{1,0:T(4,128)(2,1)S(1)}, u32[]{:S(2)}, u32[]{:S(2)}) collective-permute-start(bf16[4,2688]{1,0:T(4,128)(2,1)S(1)} %get-tuple-element.54), channel_id=1, source_target_pairs={{0,6},{2,4},{4,2},{6,0},{8,14},{10,12},{12,10},{14,8},{16,22},{18,... | collective-permute-start | bytes 64520 | tf_op jit(solution)/shard_map/ppermute | solution.py:37
  45.5 1.3 %collective-permute-start.12 = (bf16[4,5376]{1,0:T(4,128)(2,1)S(1)}, bf16[4,5376]{1,0:T(4,128)(2,1)S(1)}, u32[]{:S(2)}, u32[]{:S(2)}) collective-permute-start(bf16[4,5376]{1,0:T(4,128)(2,1)S(1)} %shard_map.152.own_ref), channel_id=1, source_target_pairs={{0,2},{2,0},{1,3},{3,1},{4,6},{6,4},{5,7},{7,5},{8,10},{10,8},{9,1... | collective-permute-start | bytes 129032 | tf_op jit(solution)/shard_map/ppermute | solution.py:28
  47.3 3.7 %collective-permute-start.13 = (f32[4,256]{1,0:T(4,128)S(1)}, f32[4,256]{1,0:T(4,128)S(1)}, u32[]{:S(2)}, u32[]{:S(2)}) collective-permute-start(f32[4,256]{1,0:T(4,128)S(1)} %shard_map.154), channel_id=1, source_target_pairs={{0,1},{1,0},{2,3},{3,2},{4,5},{5,4},{6,7},{7,6},{8,9},{9,8},{10,11... | collective-permute-start | bytes 12296 | tf_op jit(solution)/shard_map/ppermute | solution.py:28
